TPU v7x, 128 devices: a whole 4x4x4 slice. The times are simulated.
128 devices in a mesh: gx: 8 (over y, core), gy: 16 (over x, z).
Axes of the slice: x: 4, y: 4, z: 4, core: 2. Of those that a mesh axis runs over, the one named last changes fastest.
Arguments:
- source: float32 [16, 256, 2048], P(None, 'gx', 'gy'), may hold values from -6 to 6
- absorption: float32 [16, 256, 2048], P(None, 'gx', 'gy'), may hold values from 0.05 to 2
- basis: bfloat16 [32, 16, 256, 2048], P(None, None, 'gx', 'gy'), may hold values from -0.0234375 to 0.0234375
- coarse_inverse: float32 [4096, 4096], P(('gx', 'gy')), as said below
- margin_width: int32 [8, 16], P('gx', 'gy'), may hold values from 1 to 8, as said below
- coarse_slot: int32 [8, 16, 32], P('gx', 'gy'), may hold values from 0 to 4095, as said below
Outputs:
- concentration: float32 [16, 256, 2048], P(None, 'gx', 'gy')
- residual: float32 [16, 256, 2048], P(None, 'gx', 'gy')
Inputs may be any that keep to these rules, and one draw needn't show every extreme that they name: `margin_width`: some subdomain has margin width exactly 8. `coarse_slot`: each number of 0 to 4095 appears exactly once. `coarse_inverse`: symmetric and positive definite.
All inputs are finite; a program needn't handle non-finite values.
Results may differ from a plain program's by a relative error of at most 0.01.
Values sent between devices are 32-bit elements; how exact they have to be, the bound alone decides.
No kernel may reach another device: no remote copies, remote signals or barrier semaphores. Data moves between devices by JAX's collectives and lax.ppermute only.
A program may use at most 64 MiB of HBM per device.

v0:
```python
import jax
import jax.numpy as jnp
from jax import lax
from jax.sharding import PartitionSpec as P

WMAX = 8
KCHEB = 9
ITERS = 2


lowest_rate = 0.05
highest_rate = 18.5
vertical = 2.0


def extended_2(block, sides, width):
    for axis, dim in sides:
        count = lax.axis_size(axis)
        forward = [(i, i + 1) for i in range(count - 1)]
        backward = [(target, source) for source, target in forward]
        low = lax.ppermute(
            lax.slice_in_dim(block, block.shape[dim] - width, None, axis=dim), axis, forward
        )
        high = lax.ppermute(lax.slice_in_dim(block, 0, width, axis=dim), axis, backward)
        block = jnp.concatenate([low, block, high], axis=dim)
    return block


def apply_stencil(padded, coefficient):
    center = padded[:, 1:-1, 1:-1]
    stacked = jnp.pad(center, ((1, 1), (0, 0), (0, 0)))
    beside = padded[:, 2:, 1:-1] + padded[:, :-2, 1:-1] + padded[:, 1:-1, 2:] + padded[:, 1:-1, :-2]
    above = stacked[2:] + stacked[:-2]
    return (coefficient + (4.0 + 2.0 * vertical)) * center - beside - vertical * above


def pad_sides(field, width):
    return jnp.pad(field, ((0, 0), (width, width), (width, width)))


def window_of(row_start, col_start, margin, block_x, block_y, total_x, total_y, reach):
    row_local = jnp.arange(block_x + 2 * reach, dtype=jnp.int32)
    col_local = jnp.arange(block_y + 2 * reach, dtype=jnp.int32)
    row_global = row_start + row_local - reach
    col_global = col_start + col_local - reach
    row_inside = (
        (row_global >= 0)
        & (row_global < total_x)
        & (row_local >= reach - margin)
        & (row_local < block_x + reach + margin)
    )
    col_inside = (
        (col_global >= 0)
        & (col_global < total_y)
        & (col_local >= reach - margin)
        & (col_local < block_y + reach + margin)
    )
    return (row_inside[:, None] & col_inside[None, :]).astype(jnp.float32)[None]


def local_solve(source_window, coefficient, window, steps_count):
    theta = 0.5 * (highest_rate + lowest_rate)
    delta = 0.5 * (highest_rate - lowest_rate)
    ratio = theta / delta
    guess = source_window / theta
    update = guess
    rho_old = 1.0 / ratio
    for sweep in range(steps_count - 1):
        applied = window * apply_stencil(pad_sides(guess, 1), coefficient)
        defect = source_window - applied
        rho_new = 1.0 / (2.0 * ratio - rho_old)
        update = rho_new * rho_old * update + 2.0 * rho_new / delta * defect
        guess = guess + update
        rho_old = rho_new
    return guess


def extend(field):
    return extended_2(field, (("gx", 1), ("gy", 2)), WMAX)


def fold_window(extended, reach, block_x, block_y):
    row_rims = jnp.concatenate((extended[:, :reach], extended[:, block_x + reach :]), axis=1)
    arrived = extended_2(row_rims, (("gx", 1),), reach)
    middle = extended[:, reach : block_x + reach]
    middle = middle.at[:, :reach].add(arrived[:, :reach])
    middle = middle.at[:, block_x - reach :].add(arrived[:, 3 * reach :])
    col_rims = jnp.concatenate((middle[:, :, :reach], middle[:, :, block_y + reach :]), axis=2)
    arrived = extended_2(col_rims, (("gy", 2),), reach)
    inner = middle[:, :, reach : block_y + reach]
    inner = inner.at[:, :, :reach].add(arrived[:, :, :reach])
    return inner.at[:, :, block_y - reach :].add(arrived[:, :, 3 * reach :])


def precondition(resid_ext, resid, coef_ext, window, basis_flat, inverse_rows, slots):
    levels, block_x, block_y = resid.shape
    coarse_count = inverse_rows.shape[1]
    resid_b = resid.astype(jnp.bfloat16).reshape(-1)
    projected = jnp.dot(basis_flat, resid_b, preferred_element_type=jnp.float32)
    placed = jnp.zeros((coarse_count,), jnp.float32).at[slots].set(projected)
    projection = lax.psum(placed, ("gx", "gy"))
    result = local_solve(window * resid_ext, coef_ext, window, KCHEB)
    smoothed = fold_window(result, WMAX, block_x, block_y)
    smooth_total = lax.psum(jnp.sum(resid * smoothed), ("gx", "gy"))
    coarse_rows = jnp.dot(inverse_rows, projection, precision=lax.Precision.HIGHEST)
    coarse = lax.all_gather(coarse_rows, ("gx", "gy"), axis=0, tiled=True)
    coefficient = coarse[slots].astype(jnp.bfloat16)
    correction = jnp.dot(
        coefficient[None, :], basis_flat, preferred_element_type=jnp.float32
    ).reshape(levels, block_x, block_y)
    weight = smooth_total + jnp.dot(projection, coarse, precision=lax.Precision.HIGHEST)
    return (smoothed + correction, weight)


def shards(source, absorption, basis, coarse_inverse, margin_width, coarse_slot):
    levels, block_x, block_y = source.shape
    reach = WMAX
    slots = coarse_slot.reshape(-1)
    basis_flat = basis.reshape(basis.shape[0], -1)
    coef_ext = extend(absorption)
    row_start = lax.axis_index("gx") * block_x
    col_start = lax.axis_index("gy") * block_y
    window = window_of(
        row_start,
        col_start,
        margin_width[0, 0],
        block_x,
        block_y,
        block_x * lax.axis_size("gx"),
        block_y * lax.axis_size("gy"),
        reach,
    )
    concentration = jnp.zeros_like(source)
    residual = source
    resid_ext = extend(residual)
    preconditioned, rz_value = precondition(
        resid_ext, residual, coef_ext, window, basis_flat, coarse_inverse, slots
    )
    direction = preconditioned
    for iteration in range(ITERS):
        direction_pad = extended_2(direction, (("gx", 1), ("gy", 2)), 1)
        image = apply_stencil(direction_pad, absorption)
        curvature = lax.psum(jnp.sum(direction * image), ("gx", "gy"))
        step_size = rz_value / curvature
        concentration = concentration + step_size * direction
        residual = residual - step_size * image
        if iteration + 1 < ITERS:
            resid_ext = extend(residual)
            preconditioned, weight = precondition(
                resid_ext, residual, coef_ext, window, basis_flat, coarse_inverse, slots
            )
            direction = preconditioned + weight / rz_value * direction
            rz_value = weight
    return (concentration, residual)


def solution(mesh):
    return jax.shard_map(
        shards,
        mesh=mesh,
        in_specs=(
            P(None, "gx", "gy"),
            P(None, "gx", "gy"),
            P(None, None, "gx", "gy"),
            P(("gx", "gy"), None),
            P("gx", "gy"),
            P("gx", "gy", None),
        ),
        out_specs=(P(None, "gx", "gy"), P(None, "gx", "gy")),
        check_vma=False,
    )
```

profile of v0, /device:TPU:1, one launch (start us, length us, event | category | flops | bytes accessed | tf_op | source)
XLA Modules:
  0.0 598.1 jit_solution(6924895944958216073)
XLA Ops:
  1.6 3.3 collective-permute-start.1
  4.9 3.2 collective-permute-start
  9.0 1.9 collective-permute-start.5
  10.9 3.6 collective-permute-start.4
  15.9 4.9 copy.41
  20.8 2.9 copy.23
  23.9 4.7 fusion.8
  29.6 4.3 collective-permute-start.2
  36.2 4.0 collective-permute-start.6
  42.2 70.4 %psum.43 = f32[4096]{0:T(1024)S(1)} all-reduce(f32[4096]{0:T(1024)S(1)} %scatter_custom_fusion), channel_id=1, replica_groups=mesh['gx'=8,'gy'=16] {'gx','gy'}, use_global_device_ids=true, to_apply=%region_3.4 | all-reduce | flops 4096 | bytes 32768 | tf_op jit(solution)/shard_map/psum | solution.py:101
  120.7 3.0 collective-permute-start.8
  124.4 63.3 %all-reduce.34 = f32[4096]{0:T(1024)S(1)} all-reduce(f32[4096]{0:T(1024)S(1)} %dynamic-update-slice.24), channel_id=1, replica_groups=mesh['gx'=8,'gy'=16] {'gx','gy'}, use_global_device_ids=true, to_apply=%add.34 | all-reduce | flops 4096 | bytes 32768
  188.5 2.8 collective-permute-start.9
  191.3 3.4 collective-permute-done.9
  194.9 1.9 collective-permute-start.10
  196.8 4.6 fusion.2
  203.4 6.3 %collective-permute-done.11 = f32[16,32,8]{2,1,0:T(8,128)S(1)} collective-permute-done((f32[16,32,8]{2,1,0:T(8,128)S(1)}, f32[16,32,8]{2,1,0:T(8,128)S(1)}, u32[]{:S(2)}, u32[]{:S(2)}) %collective-permute-start.11) | collective-permute-done | bytes 16416 | tf_op jit(solution)/shard_map/ppermute | solution.py:24
  209.9 2.7 scatter-add.31
  213.3 4.6 collective-permute-start.13
  218.0 1.9 collective-permute-start.12
  219.9 3.0 collective-permute-done.12
  224.4 4.0 collective-permute-start.15
  229.0 4.0 collective-permute-done.14
  233.0 1.8 collective-permute-done.15
  235.7 71.1 %all-reduce.37 = (f32[]{:T(128)}, f32[]{:T(128)}) all-reduce(f32[]{:T(128)} %get-tuple-element.163, f32[]{:T(128)} %get-tuple-element.122), channel_id=1, replica_groups=mesh['gx'=8,'gy'=16] {'gx','gy'}, use_global_device_ids=true, to_apply=%region_1.0 | all-reduce | flops 2 | bytes 16 | tf_op jit(solution)/shard_map/psum | solution.py:104
  308.8 4.6 collective-permute-start.16
  313.4 1.9 collective-permute-start.17
  315.4 3.6 collective-permute-done.17
  322.3 4.9 collective-permute-done.18
  327.2 4.1 collective-permute-done.19
  338.1 4.7 collective-permute-start.20
  342.8 2.8 fusion.11
  346.3 65.6 %psum.46 = f32[4096]{0:T(1024)S(1)} all-reduce(f32[4096]{0:T(1024)S(1)} %scatter_custom_fusion.1), channel_id=1, replica_groups=mesh['gx'=8,'gy'=16] {'gx','gy'}, use_global_device_ids=true, to_apply=%region_9.10 | all-reduce | flops 4096 | bytes 32768 | tf_op jit(solution)/shard_map/psum | solution.py:101
  412.0 2.8 collective-permute-start.21
  414.8 3.6 collective-permute-done.21
  418.6 1.7 collective-permute-start.22
  422.7 2.2 collective-permute-done.22
  425.4 4.4 collective-permute-done.23
  430.0 2.7 scatter-add.39
  433.4 67.2 %all-reduce.36 = (f32[4096]{0:T(1024)S(1)}, f32[]{:T(128)}) all-reduce(f32[4096]{0:T(1024)S(1)} %dynamic-update-slice.25, f32[]{:T(128)} %multiply_reduce_fusion.1), channel_id=1, replica_groups=mesh['gx'=8,'gy'=16] {'gx','gy'}, use_global_device_ids=true, to_apply=%add.35 | all-reduce | flops 4097 | bytes 32776
  503.2 4.6 fusion
  507.9 3.9 collective-permute-start.25
  511.8 1.9 collective-permute-start.24
  513.8 3.0 collective-permute-done.24
  518.3 4.0 collective-permute-start.27
  522.3 4.6 collective-permute-done.26
  526.9 1.8 collective-permute-done.27
  529.6 66.8 %psum.47 = f32[]{:T(128)} all-reduce(f32[]{:T(128)} %get-tuple-element.102), channel_id=1, replica_groups=mesh['gx'=8,'gy'=16] {'gx','gy'}, use_global_device_ids=true, to_apply=%region_11.12 | all-reduce | flops 1 | bytes 8 | tf_op jit(solution)/shard_map/psum | solution.py:143
  (109 shorter events, 42.7 us)
Async XLA Ops:
  0.6 123.0 %copy-start = (f32[32,4096]{1,0:T(8,128)S(1)}, f32[32,4096]{1,0:T(8,128)}, u32[]{:S(2)}) copy-start(f32[32,4096]{1,0:T(8,128)} %param.25) | copy-start | bytes 1572868
  1.6 27.0 %collective-permute-start.1 = (f32[16,8,128]{2,1,0:T(8,128)S(1)}, f32[16,8,128]{2,1,0:T(8,128)S(1)}, u32[]{:S(2)}, u32[]{:S(2)}) collective-permute-start(f32[16,8,128]{2,1,0:T(8,128)S(1)} %get-tuple-element.171), channel_id=1, source_target_pairs={{16,0},{32,16},{48,32},{64,48},{80,64},{96,80},{112,96},{17,1},{33... | collective-permute-start | bytes 196616 | tf_op jit(solution)/shard_map/ppermute | solution.py:24
  4.9 18.9 %collective-permute-start = (f32[16,8,128]{2,1,0:T(8,128)S(1)}, f32[16,8,128]{2,1,0:T(8,128)S(1)}, u32[]{:S(2)}, u32[]{:S(2)}) collective-permute-start(f32[16,8,128]{2,1,0:T(8,128)S(1)} %get-tuple-element.172), channel_id=1, source_target_pairs={{0,16},{16,32},{32,48},{48,64},{64,80},{80,96},{96,112},{1,17},{17... | collective-permute-start | bytes 196616 | tf_op jit(solution)/shard_map/ppermute | solution.py:21
  9.0 26.2 %collective-permute-start.5 = (f32[16,8,128]{2,1,0:T(8,128)S(1)}, f32[16,8,128]{2,1,0:T(8,128)S(1)}, u32[]{:S(2)}, u32[]{:S(2)}) collective-permute-start(f32[16,8,128]{2,1,0:T(8,128)S(1)} %get-tuple-element.169), channel_id=1, source_target_pairs={{16,0},{32,16},{48,32},{64,48},{80,64},{96,80},{112,96},{17,1},{33... | collective-permute-start | bytes 196616 | tf_op jit(solution)/shard_map/ppermute | solution.py:24
  10.9 24.2 %collective-permute-start.4 = (f32[16,8,128]{2,1,0:T(8,128)S(1)}, f32[16,8,128]{2,1,0:T(8,128)S(1)}, u32[]{:S(2)}, u32[]{:S(2)}) collective-permute-start(f32[16,8,128]{2,1,0:T(8,128)S(1)} %get-tuple-element.170), channel_id=1, source_target_pairs={{0,16},{16,32},{32,48},{48,64},{64,80},{80,96},{96,112},{1,17},{17... | collective-permute-start | bytes 196616 | tf_op jit(solution)/shard_map/ppermute | solution.py:21
  20.8 3.0 copy-start.2
  23.9 11.3 %copy-start.3 = (f32[16,32,128]{2,1,0:T(8,128)S(1)}, f32[16,32,128]{2,1,0:T(8,128)}, u32[]{:S(2)}) copy-start(f32[16,32,128]{2,1,0:T(8,128)} %param.23) | copy-start | bytes 786436
  29.6 83.1 %collective-permute-start.2 = (f32[16,48,8]{2,1,0:T(8,128)}, f32[16,48,8]{2,1,0:T(8,128)}, u32[]{:S(2)}, u32[]{:S(2)}) collective-permute-start(f32[16,48,8]{2,1,0:T(8,128)} %get-tuple-element.153), channel_id=1, source_target_pairs={{0,1},{1,2},{2,3},{3,4},{4,5},{5,6},{6,7},{7,8},{8,9},{9,10},{10,1... | collective-permute-start | bytes 73736 | tf_op jit(solution)/shard_map/ppermute | solution.py:21
  33.9 78.8 %collective-permute-start.3 = (f32[16,48,8]{2,1,0:T(8,128)S(1)}, f32[16,48,8]{2,1,0:T(8,128)}, u32[]{:S(2)}, u32[]{:S(2)}) collective-permute-start(f32[16,48,8]{2,1,0:T(8,128)S(1)} %get-tuple-element.154), channel_id=1, source_target_pairs={{1,0},{2,1},{3,2},{4,3},{5,4},{6,5},{7,6},{8,7},{9,8},{10,9},{11,1... | collective-permute-start | bytes 73736 | tf_op jit(solution)/shard_map/ppermute | solution.py:24
  36.2 77.9 %collective-permute-start.6 = (f32[16,48,8]{2,1,0:T(8,128)}, f32[16,48,8]{2,1,0:T(8,128)S(1)}, u32[]{:S(2)}, u32[]{:S(2)}) collective-permute-start(f32[16,48,8]{2,1,0:T(8,128)} %get-tuple-element.151), channel_id=1, source_target_pairs={{0,1},{1,2},{2,3},{3,4},{4,5},{5,6},{6,7},{7,8},{8,9},{9,10},{10,1... | collective-permute-start | bytes 73736 | tf_op jit(solution)/shard_map/ppermute | solution.py:21
  40.2 73.9 %collective-permute-start.7 = (f32[16,48,8]{2,1,0:T(8,128)}, f32[16,48,8]{2,1,0:T(8,128)S(1)}, u32[]{:S(2)}, u32[]{:S(2)}) collective-permute-start(f32[16,48,8]{2,1,0:T(8,128)} %get-tuple-element.152), channel_id=1, source_target_pairs={{1,0},{2,1},{3,2},{4,3},{5,4},{6,5},{7,6},{8,7},{9,8},{10,9},{11,1... | collective-permute-start | bytes 73736 | tf_op jit(solution)/shard_map/ppermute | solution.py:24
  120.7 70.6 %collective-permute-start.8 = (f32[16,8,144]{2,1,0:T(8,128)S(1)}, f32[16,8,144]{2,1,0:T(8,128)S(1)}, u32[]{:S(2)}, u32[]{:S(2)}) collective-permute-start(f32[16,8,144]{2,1,0:T(8,128)S(1)} %get-tuple-element.144), channel_id=1, source_target_pairs={{0,16},{16,32},{32,48},{48,64},{64,80},{80,96},{96,112},{1,17},{17... | collective-permute-start | bytes 221192 | tf_op jit(solution)/shard_map/ppermute | solution.py:21
  188.5 6.3 %collective-permute-start.9 = (f32[16,8,144]{2,1,0:T(8,128)S(1)}, f32[16,8,144]{2,1,0:T(8,128)S(1)}, u32[]{:S(2)}, u32[]{:S(2)}) collective-permute-start(f32[16,8,144]{2,1,0:T(8,128)S(1)} %get-tuple-element.143), channel_id=1, source_target_pairs={{16,0},{32,16},{48,32},{64,48},{80,64},{96,80},{112,96},{17,1},{33... | collective-permute-start | bytes 221192 | tf_op jit(solution)/shard_map/ppermute | solution.py:24
  194.9 7.9 %collective-permute-start.10 = (f32[16,32,8]{2,1,0:T(8,128)S(1)}, f32[16,32,8]{2,1,0:T(8,128)S(1)}, u32[]{:S(2)}, u32[]{:S(2)}) collective-permute-start(f32[16,32,8]{2,1,0:T(8,128)S(1)} %get-tuple-element.148), channel_id=1, source_target_pairs={{0,1},{1,2},{2,3},{3,4},{4,5},{5,6},{6,7},{7,8},{8,9},{9,10},{10,1... | collective-permute-start | bytes 49160 | tf_op jit(solution)/shard_map/ppermute | solution.py:21
  201.5 8.2 %collective-permute-start.11 = (f32[16,32,8]{2,1,0:T(8,128)S(1)}, f32[16,32,8]{2,1,0:T(8,128)S(1)}, u32[]{:S(2)}, u32[]{:S(2)}) collective-permute-start(f32[16,32,8]{2,1,0:T(8,128)S(1)} %get-tuple-element.147), channel_id=1, source_target_pairs={{1,0},{2,1},{3,2},{4,3},{5,4},{6,5},{7,6},{8,7},{9,8},{10,9},{11,1... | collective-permute-start | bytes 49160 | tf_op jit(solution)/shard_map/ppermute | solution.py:24
  213.3 6.6 %collective-permute-start.13 = (f32[16,1,128]{2,1,0:T(1,128)S(1)}, f32[16,1,128]{2,1,0:T(1,128)S(1)}, u32[]{:S(2)}, u32[]{:S(2)}) collective-permute-start(f32[16,1,128]{2,1,0:T(1,128)S(1)} %get-tuple-element.165), channel_id=1, source_target_pairs={{0,16},{16,32},{32,48},{48,64},{64,80},{80,96},{96,112},{1,17},{17... | collective-permute-start | bytes 24584 | tf_op jit(solution)/shard_map/ppermute | solution.py:21
  218.0 5.0 collective-permute-start.12
  223.1 9.9 %collective-permute-start.14 = (f32[16,34,1]{2,1,0:T(8,128)S(1)}, f32[16,34,1]{2,1,0:T(8,128)S(1)}, u32[]{:S(2)}, u32[]{:S(2)}) collective-permute-start(f32[16,34,1]{2,1,0:T(8,128)S(1)} %get-tuple-element.157), channel_id=1, source_target_pairs={{1,0},{2,1},{3,2},{4,3},{5,4},{6,5},{7,6},{8,7},{9,8},{10,9},{11,1... | collective-permute-start | bytes 6536 | tf_op jit(solution)/shard_map/ppermute | solution.py:24
  224.4 10.4 %collective-permute-start.15 = (f32[16,34,1]{2,1,0:T(8,128)S(1)}, f32[16,34,1]{2,1,0:T(8,128)S(1)}, u32[]{:S(2)}, u32[]{:S(2)}) collective-permute-start(f32[16,34,1]{2,1,0:T(8,128)S(1)} %get-tuple-element.158), channel_id=1, source_target_pairs={{0,1},{1,2},{2,3},{3,4},{4,5},{5,6},{6,7},{7,8},{8,9},{9,10},{10,1... | collective-permute-start | bytes 6536 | tf_op jit(solution)/shard_map/ppermute | solution.py:21
  308.8 6.5 %collective-permute-start.16 = (f32[16,8,128]{2,1,0:T(8,128)S(1)}, f32[16,8,128]{2,1,0:T(8,128)S(1)}, u32[]{:S(2)}, u32[]{:S(2)}) collective-permute-start(f32[16,8,128]{2,1,0:T(8,128)S(1)} %get-tuple-element.161), channel_id=1, source_target_pairs={{0,16},{16,32},{32,48},{48,64},{64,80},{80,96},{96,112},{1,17},{17... | collective-permute-start | bytes 196616 | tf_op jit(solution)/shard_map/ppermute | solution.py:21
  313.4 5.6 collective-permute-start.17
  319.2 8.0 %collective-permute-start.18 = (f32[16,48,8]{2,1,0:T(8,128)S(1)}, f32[16,48,8]{2,1,0:T(8,128)S(1)}, u32[]{:S(2)}, u32[]{:S(2)}) collective-permute-start(f32[16,48,8]{2,1,0:T(8,128)S(1)} %get-tuple-element.149), channel_id=1, source_target_pairs={{0,1},{1,2},{2,3},{3,4},{4,5},{5,6},{6,7},{7,8},{8,9},{9,10},{10,1... | collective-permute-start | bytes 73736 | tf_op jit(solution)/shard_map/ppermute | solution.py:21
  320.5 10.8 %collective-permute-start.19 = (f32[16,48,8]{2,1,0:T(8,128)S(1)}, f32[16,48,8]{2,1,0:T(8,128)S(1)}, u32[]{:S(2)}, u32[]{:S(2)}) collective-permute-start(f32[16,48,8]{2,1,0:T(8,128)S(1)} %get-tuple-element.150), channel_id=1, source_target_pairs={{1,0},{2,1},{3,2},{4,3},{5,4},{6,5},{7,6},{8,7},{9,8},{10,9},{11,1... | collective-permute-start | bytes 73736 | tf_op jit(solution)/shard_map/ppermute | solution.py:24
  336.5 6.3 %copy-start.1 = (bf16[32,16,32,128]{3,2,1,0:T(8,128)(2,1)S(1)}, bf16[32,16,32,128]{3,2,1,0:T(8,128)(2,1)}, u32[]{:S(2)}) copy-start(bf16[32,16,32,128]{3,2,1,0:T(8,128)(2,1)} %param.24) | copy-start | bytes 12582916
  338.1 76.7 %collective-permute-start.20 = (f32[16,8,144]{2,1,0:T(8,128)S(1)}, f32[16,8,144]{2,1,0:T(8,128)S(1)}, u32[]{:S(2)}, u32[]{:S(2)}) collective-permute-start(f32[16,8,144]{2,1,0:T(8,128)S(1)} %get-tuple-element.142), channel_id=1, source_target_pairs={{0,16},{16,32},{32,48},{48,64},{64,80},{80,96},{96,112},{1,17},{17... | collective-permute-start | bytes 221192 | tf_op jit(solution)/shard_map/ppermute | solution.py:21
  412.0 6.4 %collective-permute-start.21 = (f32[16,8,144]{2,1,0:T(8,128)S(1)}, f32[16,8,144]{2,1,0:T(8,128)S(1)}, u32[]{:S(2)}, u32[]{:S(2)}) collective-permute-start(f32[16,8,144]{2,1,0:T(8,128)S(1)} %get-tuple-element.141), channel_id=1, source_target_pairs={{16,0},{32,16},{48,32},{64,48},{80,64},{96,80},{112,96},{17,1},{33... | collective-permute-start | bytes 221192 | tf_op jit(solution)/shard_map/ppermute | solution.py:24
  418.6 6.3 %collective-permute-start.22 = (f32[16,32,8]{2,1,0:T(8,128)S(1)}, f32[16,32,8]{2,1,0:T(8,128)S(1)}, u32[]{:S(2)}, u32[]{:S(2)}) collective-permute-start(f32[16,32,8]{2,1,0:T(8,128)S(1)} %get-tuple-element.146), channel_id=1, source_target_pairs={{0,1},{1,2},{2,3},{3,4},{4,5},{5,6},{6,7},{7,8},{8,9},{9,10},{10,1... | collective-permute-start | bytes 49160 | tf_op jit(solution)/shard_map/ppermute | solution.py:21
  421.2 8.6 %collective-permute-start.23 = (f32[16,32,8]{2,1,0:T(8,128)S(1)}, f32[16,32,8]{2,1,0:T(8,128)S(1)}, u32[]{:S(2)}, u32[]{:S(2)}) collective-permute-start(f32[16,32,8]{2,1,0:T(8,128)S(1)} %get-tuple-element.145), channel_id=1, source_target_pairs={{1,0},{2,1},{3,2},{4,3},{5,4},{6,5},{7,6},{8,7},{9,8},{10,9},{11,1... | collective-permute-start | bytes 49160 | tf_op jit(solution)/shard_map/ppermute | solution.py:24
  507.9 5.8 collective-permute-start.25
  511.8 5.0 collective-permute-start.24
  517.0 9.9 %collective-permute-start.26 = (f32[16,34,1]{2,1,0:T(8,128)S(1)}, f32[16,34,1]{2,1,0:T(8,128)S(1)}, u32[]{:S(2)}, u32[]{:S(2)}) collective-permute-start(f32[16,34,1]{2,1,0:T(8,128)S(1)} %get-tuple-element.155), channel_id=1, source_target_pairs={{1,0},{2,1},{3,2},{4,3},{5,4},{6,5},{7,6},{8,7},{9,8},{10,9},{11,1... | collective-permute-start | bytes 6536 | tf_op jit(solution)/shard_map/ppermute | solution.py:24
  518.3 10.4 %collective-permute-start.27 = (f32[16,34,1]{2,1,0:T(8,128)S(1)}, f32[16,34,1]{2,1,0:T(8,128)S(1)}, u32[]{:S(2)}, u32[]{:S(2)}) collective-permute-start(f32[16,34,1]{2,1,0:T(8,128)S(1)} %get-tuple-element.156), channel_id=1, source_target_pairs={{0,1},{1,2},{2,3},{3,4},{4,5},{5,6},{6,7},{7,8},{8,9},{9,10},{10,1... | collective-permute-start | bytes 6536 | tf_op jit(solution)/shard_map/ppermute | solution.py:21
where the time goes:
time: 606 us; the launch traced here: 598 us
  blocking collectives  404 us (67%)
  starting transfers between devices  75.1 us (12%)
  waiting for transfers between devices  50.8 us (8%)
  local copies, waits for them, and re-layouts  22.3 us (4%)
  other arithmetic  21.6 us (4%)
  matrix products  17.8 us (3%)
  between operations  6.16 us (1%)
    psum x2, blocking collectives, precondition(): projection = lax.psum(placed, ('gx', 'gy'))  136 us
    unnamed x2, blocking collectives  131 us
    psum x1, blocking collectives, precondition(): smooth_total = lax.psum(jnp.sum(resid * smoothed), ('gx', 'gy'))  71.1 us
    psum x1, blocking collectives, shards(): curvature = lax.psum(jnp.sum(direction * image), ('gx', 'gy'))  66.8 us
    ppermute x14, starting transfers between devices, extended_2(): lax.ppermute(lax.slice_in_dim(block, block.shape[dim] - width, None, axis...  48.8 us
    ppermute x14, waiting for transfers between devices, extended_2(): lax.ppermute(lax.slice_in_dim(block, 0, width, axis=dim), axis, backward)  40.1 us
    ppermute x14, starting transfers between devices, extended_2(): lax.ppermute(lax.slice_in_dim(block, 0, width, axis=dim), axis, backward)  26.3 us
    add x16, other arithmetic, local_solve(): guess = guess + update  12.7 us
  transfers between devices with their start and end apart: 28, of which 14 were waited for; matrix products, arithmetic and copies ran while one was open for 5% of the time, Pallas kernels for 0%

commit v1 on v0

v1 whole, which is shorter than its diff:
```python
import functools

import jax
import jax.numpy as jnp
from jax import lax
from jax.experimental import pallas as pl
from jax.experimental.pallas import tpu as pltpu
from jax.sharding import PartitionSpec as P

KCHEB = 9
AXES = ("gx", "gy")
LEVELS = 16
ROWS = 32
COLS = 128
VECTORS = 32
EDGE = 16
TALL = ROWS + 2 * EDGE
HIGHEST = lax.Precision.HIGHEST

lowest_rate = 0.05
highest_rate = 18.5
vertical = 2.0
theta = 0.5 * (highest_rate + lowest_rate)
delta = 0.5 * (highest_rate - lowest_rate)
VMEM_LIMIT = 44 * 1024 * 1024


def chebyshev_table():
    ratio = theta / delta
    rho_old = 1.0 / ratio
    table = []
    for _ in range(KCHEB - 1):
        rho_new = 1.0 / (2.0 * ratio - rho_old)
        table.append((rho_new * rho_old, 2.0 * rho_new / delta))
        rho_old = rho_new
    return table


def iota(shape, dim):
    return lax.broadcasted_iota(jnp.int32, shape, dim)


def roll(value, shift):
    return pltpu.roll(value, shift % COLS, 1)


def exchange(forward_value, backward_value, axis):
    count = lax.axis_size(axis)
    forward = [(i, i + 1) for i in range(count - 1)]
    backward = [(target, source) for source, target in forward]
    return lax.ppermute(forward_value, axis, forward), lax.ppermute(backward_value, axis, backward)


def everyone(rows):
    return lax.all_to_all(rows, AXES, 0, 0, tiled=True)


def row_of_sums(sums):
    padded = jnp.concatenate([sums, jnp.zeros((COLS - VECTORS, COLS), jnp.float32)], 0)
    ones = jnp.ones((COLS, COLS), jnp.float32)
    return lax.dot_general(
        ones, padded, (((1,), (1,)), ((), ())), precision=HIGHEST, preferred_element_type=jnp.float32
    )


def first_kernel(field_ref, basis_ref, told_ref, out_ref, up_ref, down_ref, left_ref, right_ref, sums_ref):
    step = pl.program_id(0)
    group = basis_ref.shape[0]
    lane = iota((ROWS, COLS), 1)

    @pl.when(step == 0)
    def _():
        left_ref[...] = jnp.zeros_like(left_ref)
        right_ref[...] = jnp.zeros_like(right_ref)

    def level(z, sums):
        field = field_ref[z]
        low = left_ref[z]
        high = right_ref[z]
        new = []
        for j in range(group):
            values = basis_ref[j, z].astype(jnp.float32)
            product = values * field
            new.append(
                sums[j] + product[0:8] + product[8:16] + product[16:24] + product[24:32]
            )
            up_ref[j, pl.ds(z, 1), :] = values[0:1]
            down_ref[j, pl.ds(z, 1), :] = values[ROWS - 1 : ROWS]
            k = step * group + j
            turned = pltpu.roll(values, k, 1)
            low = jnp.where(lane == k, turned, low)
            turned = pltpu.roll(values, k + 1, 1)
            high = jnp.where(lane == k, turned, high)
        left_ref[z] = low
        right_ref[z] = high
        return tuple(new)

    zero = jnp.zeros((8, COLS), jnp.float32)
    sums = lax.fori_loop(0, LEVELS, level, (zero,) * group)
    for j in range(group):
        sums_ref[pl.ds(step * group + j, 1), :] = jnp.sum(sums[j], axis=0, keepdims=True)

    @pl.when(step == pl.num_programs(0) - 1)
    def _():
        out_ref[...] = row_of_sums(sums_ref[...]) + told_ref[...]


def first_projection(field, basis, told_row):
    group = 8
    edge_rows = jax.ShapeDtypeStruct((VECTORS, LEVELS, COLS), jnp.float32)
    edge_cols = jax.ShapeDtypeStruct((LEVELS, ROWS, COLS), jnp.float32)
    rows_spec = pl.BlockSpec((group, LEVELS, COLS), lambda i: (i, 0, 0))
    cols_spec = pl.BlockSpec((LEVELS, ROWS, COLS), lambda i: (0, 0, 0))
    return pl.pallas_call(
        first_kernel,
        grid=(VECTORS // group,),
        in_specs=[
            pl.BlockSpec((LEVELS, ROWS, COLS), lambda i: (0, 0, 0)),
            pl.BlockSpec((group, LEVELS, ROWS, COLS), lambda i: (i, 0, 0, 0)),
            pl.BlockSpec((1, COLS), lambda i: (0, 0)),
        ],
        out_specs=[
            pl.BlockSpec((COLS, COLS), lambda i: (0, 0)),
            rows_spec,
            rows_spec,
            cols_spec,
            cols_spec,
        ],
        out_shape=[jax.ShapeDtypeStruct((COLS, COLS), jnp.float32), edge_rows, edge_rows, edge_cols, edge_cols],
        scratch_shapes=[pltpu.VMEM((VECTORS, COLS), jnp.float32)],
        compiler_params=pltpu.CompilerParams(vmem_limit_bytes=VMEM_LIMIT),
        name="first_projection",
    )(field, basis, told_row)


def coarse_rows(told_ref, slots_ref, inverse_ref, out_ref):
    told = told_ref[...]
    slots = slots_ref[...]
    turned = told.T
    slots_turned = slots.T
    lane = iota((COLS, COLS), 1)
    sub = iota((VECTORS, COLS), 0)
    placed = jnp.zeros((3 * VECTORS, COLS), jnp.float32)
    for k in range(VECTORS):
        slot_column = slots[:, VECTORS + k : VECTORS + k + 1].astype(jnp.int32)
        ones = jnp.where((slot_column & 127) == lane, 1.0, 0.0).astype(jnp.bfloat16)
        slot_row = slots_turned[VECTORS + k : VECTORS + k + 1, :].astype(jnp.int32)
        values = turned[k : k + 1, :]
        spread = jnp.where((slot_row >> 7) == sub, values, 0.0)
        first = spread.astype(jnp.bfloat16)
        rest = spread - first.astype(jnp.float32)
        second = rest.astype(jnp.bfloat16)
        third = (rest - second.astype(jnp.float32)).astype(jnp.bfloat16)
        parts = jnp.concatenate([first, second, third], 0)
        placed = placed + jnp.dot(parts, ones, preferred_element_type=jnp.float32)
    placed = placed[:VECTORS] + placed[VECTORS : 2 * VECTORS] + placed[2 * VECTORS :]
    total = jnp.zeros((VECTORS, COLS), jnp.float32)
    for high in range(VECTORS):
        total = total + inverse_ref[:, high * COLS : (high + 1) * COLS] * placed[high : high + 1]
    out_ref[...] = row_of_sums(total)


def pack_strips(parts, forward_ref, backward_ref, at):
    for group in range(LEVELS // 8):
        row = 0
        for part in parts:
            height = part.shape[1]
            lane = iota((height, COLS), 1)
            ahead = jnp.zeros((height, COLS), jnp.float32)
            behind = ahead
            for j in range(8):
                value = part[group * 8 + j]
                mine = (lane >= EDGE * j) & (lane < EDGE * (j + 1))
                ahead = jnp.where(mine, roll(value, EDGE * j - (COLS - EDGE)), ahead)
                behind = jnp.where(mine, roll(value, EDGE * j), behind)
            forward_ref[at + group, row : row + height, :] = ahead
            backward_ref[at + group, row : row + height, :] = behind
            row += height


def middle_kernel(fields, told_ref, slots_ref, inverse_ref, *refs):
    ins = refs[: 3 * fields]
    out_ref, forward_ref, backward_ref = refs[3 * fields :]
    for f in range(fields):
        pack_strips(ins[3 * f : 3 * f + 3], forward_ref, backward_ref, 2 * f)
    coarse_rows(told_ref, slots_ref, inverse_ref, out_ref)


def middle(told, slots_told, inverse_rows, fields):
    strips = jax.ShapeDtypeStruct((2 * len(fields), TALL, COLS), jnp.float32)
    flat = [part for field in fields for part in field]
    return pl.pallas_call(
        functools.partial(middle_kernel, len(fields)),
        out_shape=[jax.ShapeDtypeStruct((COLS, COLS), jnp.float32), strips, strips],
        compiler_params=pltpu.CompilerParams(vmem_limit_bytes=VMEM_LIMIT),
        name="coarse_rows",
    )(told, slots_told, inverse_rows, *flat)


class Place:
    def __init__(self, place_ref, told_ref):
        self.row = place_ref[0]
        self.col = place_ref[1]
        self.rows = place_ref[2]
        self.cols = place_ref[3]
        self.told_ref = told_ref

    def index(self, down, right):
        row = jnp.clip(self.row + down, 0, self.rows - 1)
        col = jnp.clip(self.col + right, 0, self.cols - 1)
        return row * self.cols + col

    def margin(self, down, right):
        row, col = self.row + down, self.col + right
        real = (row >= 0) & (row < self.rows) & (col >= 0) & (col < self.cols)
        margin = self.told_ref[pl.ds(self.index(down, right), 1), :][:, 64:65]
        return jnp.where(real, margin.astype(jnp.int32), -4096)


def masks(place, own_ref, beside_ref, strip_ref):
    shape = (TALL, COLS)
    row = iota(shape, 0) - EDGE
    lane = iota(shape, 1)
    top, bottom = -ROWS * place.row, ROWS * (place.rows - place.row)
    first, last = -COLS * place.col, COLS * (place.cols - place.col)
    row_real = (row >= top) & (row < bottom)
    m = {(i, j): place.margin(i, j) for i in (-1, 0, 1) for j in (-1, 0, 1)}
    upper, lower = row < 8, row >= ROWS - 8
    for tile in range(2):
        col = lane if tile == 0 else jnp.where(lane < 64, lane + COLS, lane - COLS)
        real = row_real & (col >= first) & (col < last)
        if tile == 1:
            real = real & ((lane < EDGE) | (lane >= COLS - EDGE))

        def across(margin):
            return (col >= -margin) & (col < COLS + margin)

        own = m[0, 0]
        inside = real & (row >= -own) & (row < ROWS + own) & across(own)
        own_ref[tile] = jnp.where(inside, 1.0, 0.0)
        above, below = m[-1, 0], m[1, 0]
        inside = (upper & (row < above) & across(above)) | (lower & (row >= ROWS - below) & across(below))
        beside_ref[tile] = jnp.where(real & inside, 1.0, 0.0)
    group = ((lane + EDGE) & 127) >> 5
    away = ((lane + EDGE) & 31) - EDGE
    inside = row < -4096
    for place_of, side in ((0, -1), (2, 1)):
        col = away if side < 0 else away + COLS
        real = row_real & (col >= first) & (col < last)

        def reached(margin):
            return (away < margin) if side < 0 else (away >= -margin)

        level = m[0, side]
        inside = inside | (
            (group == place_of) & real & (row >= -level) & (row < ROWS + level) & reached(level)
        )
        above, below = m[-1, side], m[1, side]
        corner = (upper & (row < above) & reached(above)) | (
            lower & (row >= ROWS - below) & reached(below)
        )
        inside = inside | ((group == place_of + 1) & real & corner)
    strip_ref[...] = jnp.where(inside, 1.0, 0.0)


def rows_of(parts, z, i):
    low, block, high = parts
    if i < 2:
        return low[z, i * 8 : i * 8 + 8, :]
    if i < 6:
        return block[z, (i - 2) * 8 : (i - 2) * 8 + 8, :]
    return high[z, (i - 6) * 8 : (i - 6) * 8 + 8, :]


def tiles_of(parts, from_left, from_right, at, z, i):
    lane = iota((8, COLS), 1)
    center = rows_of(parts, z, i)
    group, j = divmod(z, 8)
    left = roll(from_left[at + group, i * 8 : i * 8 + 8, :], (COLS - EDGE) - EDGE * j)
    right = roll(from_right[at + group, i * 8 : i * 8 + 8, :], -EDGE * j)
    margin = jnp.where(lane >= COLS - EDGE, left, jnp.where(lane < EDGE, right, 0.0))
    at_left = jnp.where(lane >= 64, margin, center)
    at_right = jnp.where(lane < 64, margin, center)
    near = (lane < EDGE) | (lane >= COLS - EDGE)
    packed = jnp.where(
        near,
        at_left,
        jnp.where(
            lane < 48, roll(at_left, 32), jnp.where(lane < 80, roll(at_right, 64), roll(at_right, 96))
        ),
    )
    return center, margin, packed


def smooth(place, field, coefficient, strips, table_ref, scratch):
    (own_m, beside_m, strip_m, own, beside, strip, diag, strip_diag) = scratch
    masks(place, own_m, beside_m, strip_m)
    own_a, own_b, own_d, own_r = own
    bes_a, bes_b, bes_d, bes_r = beside
    str_a, str_b, str_d, str_r = strip
    left, right, left_c, right_c, at_c = strips
    base = 4.0 + 2.0 * vertical
    zero = jnp.zeros((8, COLS), jnp.float32)
    for i in range(8):
        s = slice(i * 8, i * 8 + 8)
        for z in range(LEVELS):
            tiles = tiles_of(field, left, right, 0, z, i)
            for t in range(2):
                lanes = slice(t * COLS, (t + 1) * COLS)
                value = tiles[t] * own_m[t, s]
                own_r[z, s, lanes] = value
                own_a[z, s, lanes] = value * (1.0 / theta)
                own_d[z, s, lanes] = value * (1.0 / theta)
                value = tiles[t] * beside_m[t, s]
                bes_r[z, s, lanes] = value
                bes_a[z, s, lanes] = value * (1.0 / theta)
                bes_d[z, s, lanes] = value * (1.0 / theta)
                if i in (0, 7):
                    own_b[z, s, lanes] = zero
                if i in (0, 3, 4, 7):
                    bes_b[z, s, lanes] = zero
            value = tiles[2] * strip_m[s]
            str_r[z, s] = value
            str_a[z, s] = value * (1.0 / theta)
            str_d[z, s] = value * (1.0 / theta)
            if i in (0, 7):
                str_b[z, s] = zero
            else:
                tiles = tiles_of(coefficient, left_c, right_c, at_c, z, i)
                diag[z, s, 0:COLS] = tiles[0] + base
                diag[z, s, COLS : 2 * COLS] = tiles[1] + base
                strip_diag[z, s] = tiles[2] + base

    lane = iota((8, COLS), 1)
    at_first, at_last = lane == 0, lane == COLS - 1

    def step(x, y, d, r, a, mask, width, i, keep, scale):
        s = slice(i * 8, i * 8 + 8)
        up, down = slice(i * 8 - 1, i * 8 + 7), slice(i * 8 + 1, i * 8 + 9)
        lanes = [slice(t * COLS, (t + 1) * COLS) for t in range(width)]
        before = [zero] * width
        now = [x[0, s, lanes[t]] for t in range(width)]
        for z in range(LEVELS):
            after = [x[z + 1, s, lanes[t]] for t in range(width)] if z + 1 < LEVELS else [zero] * width
            back = [roll(v, 1) for v in now]
            fore = [roll(v, -1) for v in now]
            if width == 2:
                back = [jnp.where(at_first, back[1], back[0]), jnp.where(at_first, back[0], back[1])]
                fore = [jnp.where(at_last, fore[1], fore[0]), jnp.where(at_last, fore[0], fore[1])]
            for t in range(width):
                high = before[t] + after[t]
                around = (x[z, up, lanes[t]] + x[z, down, lanes[t]]) + (back[t] + fore[t])
                around = around + (high + high)
                defect = r[z, s, lanes[t]] - a[z, s, lanes[t]] * now[t] + around
                move = keep * d[z, s, lanes[t]] + scale * defect
                if mask[t] is not None:
                    move = move * mask[t]
                d[z, s, lanes[t]] = move
                y[z, s, lanes[t]] = now[t] + move
            before, now = now, after

    def sweep(n, x, y, which):
        keep, scale = table_ref[0, n], table_ref[1, n]
        for i in range(1, 7):
            s = slice(i * 8, i * 8 + 8)
            free = 2 <= i < 6
            step(
                own[which], own[1 - which], own_d, own_r, diag,
                [None if free else own_m[0, s], own_m[1, s]], 2, i, keep, scale,
            )
            if i in (1, 2, 5, 6):
                step(
                    beside[which], beside[1 - which], bes_d, bes_r, diag,
                    [beside_m[0, s], beside_m[1, s]], 2, i, keep, scale,
                )
            step(
                strip[which], strip[1 - which], str_d, str_r, strip_diag, [strip_m[s]], 1, i, keep, scale
            )

    def pair(n, carry):
        sweep(2 * n, None, None, 0)
        sweep(2 * n + 1, None, None, 1)
        return carry

    lax.fori_loop(0, (KCHEB - 1) // 2, pair, 0)
    near_first, near_last = lane < EDGE, lane >= COLS - EDGE
    for i in range(1, 7):
        s = slice(i * 8, i * 8 + 8)
        for z in range(LEVELS):
            value = str_a[z, s]
            at_left = value + roll(value, -32)
            at_right = roll(at_left, 64)
            first = jnp.where(near_first, at_left, jnp.where(near_last, at_right, 0.0))
            second = jnp.where(near_last, at_left, jnp.where(near_first, at_right, 0.0))
            first = first + own_a[z, s, 0:COLS]
            second = second + own_a[z, s, COLS : 2 * COLS]
            if i in (1, 2, 5, 6):
                first = first + bes_a[z, s, 0:COLS]
                second = second + bes_a[z, s, COLS : 2 * COLS]
            own_a[z, s, 0:COLS] = first
            own_a[z, s, COLS : 2 * COLS] = second
    return own_a


def coarse_row(place, told_ref, coarse_turned, down, right):
    slots = roll(told_ref[pl.ds(place.index(down, right), 1), :], -VECTORS).astype(jnp.int32)
    lane = iota((1, COLS), 1)
    slots = jnp.where(lane < VECTORS, slots, 0)
    pick = jnp.where(iota((COLS, COLS), 0) == (slots >> 5), 1.0, 0.0)
    found = jnp.dot(coarse_turned, pick, precision=HIGHEST, preferred_element_type=jnp.float32)
    found = jnp.where(iota((VECTORS, COLS), 0) == (slots & 31), found, 0.0)
    return jnp.where(lane < VECTORS, jnp.sum(found, axis=0, keepdims=True), 0.0)


def add_coarse(place, told_ref, coarse_ref, basis_ref, edges, x, column_ref):
    from_up, from_down, from_left, from_right = edges
    turned = coarse_ref[...].T[:VECTORS]
    row_own = coarse_row(place, told_ref, turned, 0, 0)
    lane = iota((8, COLS), 1)

    def columns(row):
        column_ref[...] = jnp.broadcast_to(row, (COLS, COLS)).T[:VECTORS]

    for edge, down, at in ((from_up, -1, EDGE - 1), (from_down, 1, EDGE + ROWS)):
        columns(coarse_row(place, told_ref, turned, down, 0))
        total = jnp.zeros((LEVELS, COLS), jnp.float32)
        for k in range(VECTORS):
            total = total + edge[k] * column_ref[k : k + 1]
        for z in range(LEVELS):
            x[z, at : at + 1, 0:COLS] = x[z, at : at + 1, 0:COLS] + total[z : z + 1]
    row_left = coarse_row(place, told_ref, turned, 0, -1)
    row_right = coarse_row(place, told_ref, turned, 0, 1)
    for z in range(LEVELS):
        for i in range(ROWS // 8):
            s = slice(i * 8, i * 8 + 8)
            t = slice(EDGE + i * 8, EDGE + i * 8 + 8)
            left = jnp.sum(from_left[z, s] * row_left, axis=1, keepdims=True)
            right = jnp.sum(from_right[z, s] * row_right, axis=1, keepdims=True)
            value = x[z, t, COLS : 2 * COLS]
            value = value + jnp.where(lane == COLS - 1, left, jnp.where(lane == 0, right, 0.0))
            x[z, t, COLS : 2 * COLS] = value
    columns(row_own)

    def level(z, carry):
        total = x[z, EDGE : EDGE + ROWS, 0:COLS]
        for k in range(VECTORS):
            total = total + basis_ref[k, z].astype(jnp.float32) * column_ref[k : k + 1]
        x[z, EDGE : EDGE + ROWS, 0:COLS] = total
        return carry

    lax.fori_loop(0, LEVELS, level, 0)
    return row_own


def image_of(x, diag, put):
    lane = iota((8, COLS), 1)
    zero = jnp.zeros((8, COLS), jnp.float32)
    for i in range(2, 6):
        s = slice(i * 8, i * 8 + 8)
        up, down = slice(i * 8 - 1, i * 8 + 7), slice(i * 8 + 1, i * 8 + 9)
        for z in range(LEVELS):
            now = x[z, s, 0:COLS]
            margin = x[z, s, COLS : 2 * COLS]
            back = jnp.where(lane == 0, roll(margin, 1), roll(now, 1))
            fore = jnp.where(lane == COLS - 1, roll(margin, -1), roll(now, -1))
            high = (x[z - 1, s, 0:COLS] if z else zero) + (x[z + 1, s, 0:COLS] if z + 1 < LEVELS else zero)
            around = x[z, up, 0:COLS] + x[z, down, 0:COLS] + back + fore
            put(z, i - 2, now, diag[z, s, 0:COLS] * now - around - vertical * high)


def total_of(value):
    return jnp.sum(jnp.sum(value, axis=0, keepdims=True), axis=1, keepdims=True)


def gather_scratch(refs):
    own_m, beside_m, strip_m = refs[:3]
    own, beside, strip = refs[3:7], refs[7:11], refs[11:15]
    return (own_m, beside_m, strip_m, own, beside, strip, refs[15], refs[16])


def solve_kernel(
    place_ref, table_ref, told_ref, coarse_ref, basis_ref, r_up, r_own, r_down, c_up, c_own, c_down,
    left_ref, right_ref, e_up, e_down, e_left, e_right,
    direction_ref, smooth_ref, image_ref, ahead_ref, behind_ref, out_ref, *refs,
):
    column_ref, sums_ref = refs[:2]
    scratch = gather_scratch(refs[2:])
    place = Place(place_ref, told_ref)
    x = smooth(
        place, (r_up, r_own, r_down), (c_up, c_own, c_down),
        (left_ref, right_ref, left_ref, right_ref, 2), table_ref, scratch,
    )
    smooth_ref[...] = x[:, EDGE : EDGE + ROWS, 0:COLS]
    row = add_coarse(place, told_ref, coarse_ref, basis_ref, (e_up, e_down, e_left, e_right), x, column_ref)
    zero = jnp.zeros((8, COLS), jnp.float32)
    weight = [zero]
    curve = [zero]

    def put(z, i, now, image):
        s = slice(i * 8, i * 8 + 8)
        direction_ref[z, s] = now
        image_ref[z, s] = image
        if i >= 2:
            ahead_ref[z, (i - 2) * 8 : (i - 1) * 8] = image
        else:
            behind_ref[z, s] = image
        weight[0] = weight[0] + r_own[z, s] * smooth_ref[z, s]
        curve[0] = curve[0] + now * image

    image_of(x, scratch[6], put)
    mine = told_ref[pl.ds(place.index(0, 0), 1), :]
    weight_part = total_of(weight[0]) + total_of(row * mine)
    curve_part = total_of(curve[0])
    half = VECTORS // 2
    for part in range(2):

        def level(z, sums):
            image = image_ref[z]
            new = []
            for k in range(half):
                product = basis_ref[part * half + k, z].astype(jnp.float32) * image
                new.append(sums[k] + product[0:8] + product[8:16] + product[16:24] + product[24:32])
            return tuple(new)

        sums = lax.fori_loop(0, LEVELS, level, (zero,) * half)
        for k in range(half):
            sums_ref[part * half + k : part * half + k + 1] = jnp.sum(sums[k], axis=0, keepdims=True)
    lane = iota((1, COLS), 1)
    told = roll(row, VECTORS)
    told = told + jnp.where(lane == 64, weight_part, 0.0) + jnp.where(lane == 65, curve_part, 0.0)
    out_ref[...] = row_of_sums(sums_ref[...]) + told


def scalars(told_ref):
    totals = jnp.sum(told_ref[...], axis=0, keepdims=True)
    return totals[:, 64:65], totals[:, 65:66]


def again_kernel(
    place_ref, table_ref, told_ref, again_ref, coarse_ref, basis_ref, w_up, w_own, w_down, c_up, c_own, c_down,
    left_ref, right_ref, left_c, right_c, e_up, e_down, e_left, e_right, source_ref, direction_ref, smooth_ref,
    residual_ref, precond_ref, image_ref, out_ref, *refs,
):
    column_ref, more_ref = refs[:2]
    scratch = gather_scratch(refs[2:])
    place = Place(place_ref, told_ref)
    x = smooth(
        place, (w_up, w_own, w_down), (c_up, c_own, c_down), (left_ref, right_ref, left_c, right_c, 2),
        table_ref, scratch,
    )
    more_ref[...] = x[:, EDGE : EDGE + ROWS, 0:COLS]
    row = add_coarse(place, told_ref, coarse_ref, basis_ref, (e_up, e_down, e_left, e_right), x, column_ref)
    weight0, curve0 = scalars(again_ref)
    step = weight0 / curve0
    zero = jnp.zeros((8, COLS), jnp.float32)
    sums = [zero, zero, zero]

    def put(z, i, now, image):
        s = slice(i * 8, i * 8 + 8)
        direction, first = direction_ref[z, s], w_own[z, s]
        residual = source_ref[z, s] - step * first
        precond = direction - step * now
        image = first - step * image
        residual_ref[z, s] = residual
        precond_ref[z, s] = precond
        image_ref[z, s] = image
        sums[0] = sums[0] + residual * (smooth_ref[z, s] - step * more_ref[z, s])
        sums[1] = sums[1] + precond * image
        sums[2] = sums[2] + (precond * first + direction * image)

    image_of(x, scratch[6], put)
    mine = pl.ds(place.index(0, 0), 1)
    lane = iota((1, COLS), 1)
    again = again_ref[mine, :]
    projected = told_ref[mine, :] - step * again
    coarse = roll(again, -VECTORS) - step * row
    both = jnp.where(lane < VECTORS, projected * coarse, 0.0)
    told = jnp.where(lane == 0, total_of(sums[0]) + total_of(both), 0.0)
    told = told + jnp.where(lane == 1, total_of(sums[1]), 0.0) + jnp.where(lane == 2, total_of(sums[2]), 0.0)
    out_ref[...] = jnp.broadcast_to(told, (COLS, COLS))


def last_kernel(again_ref, last_ref, direction_ref, first_ref, residual_ref, precond_ref, image_ref, x_ref, r_ref):
    weight0, curve0 = scalars(again_ref)
    step0 = weight0 / curve0
    totals = jnp.sum(last_ref[...], axis=0, keepdims=True)
    weight1, own, cross = totals[:, 0:1], totals[:, 1:2], totals[:, 2:3]
    ratio = weight1 / weight0
    step1 = weight1 / (own + ratio * (cross + ratio * curve0))

    def level(z, carry):
        direction = direction_ref[z]
        x_ref[z] = step0 * direction + step1 * (precond_ref[z] + ratio * direction)
        r_ref[z] = residual_ref[z] - step1 * (image_ref[z] + ratio * first_ref[z])
        return carry

    lax.fori_loop(0, LEVELS, level, 0)


def smoother_scratch():
    wide = pltpu.VMEM((LEVELS, TALL, 2 * COLS), jnp.float32)
    thin = pltpu.VMEM((LEVELS, TALL, COLS), jnp.float32)
    pair = pltpu.VMEM((2, TALL, COLS), jnp.float32)
    return [pair, pair, pltpu.VMEM((TALL, COLS), jnp.float32)] + [wide] * 8 + [thin] * 4 + [wide, thin]


def shards(source, absorption, basis, coarse_inverse, margin_width, coarse_slot):
    block = jax.ShapeDtypeStruct((LEVELS, ROWS, COLS), jnp.float32)
    slab = jax.ShapeDtypeStruct((LEVELS, EDGE, COLS), jnp.float32)
    message = jax.ShapeDtypeStruct((COLS, COLS), jnp.float32)
    params = pltpu.CompilerParams(vmem_limit_bytes=VMEM_LIMIT)
    smem = pl.BlockSpec(memory_space=pltpu.SMEM)
    vmem = pl.BlockSpec(memory_space=pltpu.VMEM)
    place = jnp.stack(
        [lax.axis_index("gx"), lax.axis_index("gy"), lax.axis_size("gx"), lax.axis_size("gy")]
    ).astype(jnp.int32)
    table = jnp.array(list(zip(*chebyshev_table())), jnp.float32)
    told_row = jnp.concatenate(
        [
            jnp.zeros((1, VECTORS), jnp.float32),
            coarse_slot.reshape(1, -1).astype(jnp.float32),
            margin_width.astype(jnp.float32),
            jnp.zeros((1, COLS - 65), jnp.float32),
        ],
        axis=1,
    )
    both = [
        jnp.concatenate([source[:, ROWS - EDGE :], absorption[:, ROWS - EDGE :]]),
        jnp.concatenate([source[:, :EDGE], absorption[:, :EDGE]]),
    ]
    low, high = exchange(both[0], both[1], "gx")
    rows, e_first, e_last, e_left, e_right = first_projection(source, basis, told_row)
    told = everyone(rows)
    r_parts = (low[:LEVELS], source, high[:LEVELS])
    c_parts = (low[LEVELS:], absorption, high[LEVELS:])
    rows, ahead, behind = middle(told, told, coarse_inverse, [r_parts, c_parts])
    left, right = exchange(ahead, behind, "gy")
    coarse = everyone(rows)
    from_up, from_down = exchange(e_last, e_first, "gx")
    from_left, from_right = exchange(e_right, e_left, "gy")
    edges = (from_up, from_down, from_left, from_right)
    direction, smoothed, image, ahead, behind, rows = pl.pallas_call(
        solve_kernel,
        in_specs=[smem] * 2 + [vmem] * 15,
        out_shape=[block, block, block, slab, slab, message],
        scratch_shapes=[pltpu.VMEM((VECTORS, COLS), jnp.float32)] * 2 + smoother_scratch(),
        compiler_params=params,
        name="precondition",
    )(place, table, told, coarse, basis, *r_parts, *c_parts, left, right, *edges)
    low, high = exchange(ahead, behind, "gx")
    again = everyone(rows)
    w_parts = (low, image, high)
    rows, ahead, behind = middle(again, told, coarse_inverse, [w_parts])
    left_w, right_w = exchange(ahead, behind, "gy")
    coarse = everyone(rows)
    residual, precond, precond_image, rows = pl.pallas_call(
        again_kernel,
        in_specs=[smem] * 2 + [vmem] * 21,
        out_shape=[block, block, block, message],
        scratch_shapes=[pltpu.VMEM((VECTORS, COLS), jnp.float32), pltpu.VMEM(block.shape, jnp.float32)]
        + smoother_scratch(),
        compiler_params=params,
        name="precondition_image",
    )(
        place, table, told, again, coarse, basis, *w_parts, *c_parts, left_w, right_w, left, right, *edges,
        source, direction, smoothed,
    )
    last = everyone(rows)
    concentration, residual = pl.pallas_call(
        last_kernel, out_shape=[block, block], compiler_params=params, name="update"
    )(again, last, direction, image, residual, precond, precond_image)
    return (concentration, residual)


def solution(mesh):
    return jax.shard_map(
        shards,
        mesh=mesh,
        in_specs=(
            P(None, "gx", "gy"),
            P(None, "gx", "gy"),
            P(None, None, "gx", "gy"),
            P(("gx", "gy"), None),
            P("gx", "gy"),
            P("gx", "gy", None),
        ),
        out_specs=(P(None, "gx", "gy"), P(None, "gx", "gy")),
        check_vma=False,
    )
```

time: 606 us -> 199 us (0.33); the launches traced: 598 us -> 198 us
  blocking collectives: 404 us -> 45.3 us
  Pallas kernels: 0 us -> 78 us
  waiting for transfers between devices: 50.8 us -> 9.45 us
  starting transfers between devices: 75.1 us -> 54.2 us
  other arithmetic: 21.6 us -> 1.55 us
  matrix products: 17.8 us -> 0 us
  local copies, waits for them, and re-layouts: 22.3 us -> 8.43 us
    psum x4 -> x0, blocking collectives: 274 us -> none  [the longest x2 136 us: precondition(): projection = lax.psum(placed, ('gx', 'gy'))]
    unnamed x2 -> x0, blocking collectives: 131 us -> none
    pallas_call x0 -> x6, Pallas kernels: none -> 78 us  [the longest x1 31.9 us: shards(): pl.pallas_call(solve_kernel, in_specs=[smem] * 2 + [vmem] * 15, out_shape...]
    ppermute x28 -> x12, waiting for transfers between devices: 50.8 us -> 0.03 us  [the longest x6 0.02 us: exchange(): lax.ppermute(backward_value, axis, backward)]
    all_to_all x0 -> x3, blocking collectives: none -> 45.3 us  [everyone(): return lax.all_to_all(rows, AXES, 0, 0, tiled=True)]
    ppermute x28 -> x12, starting transfers between devices: 75.1 us -> 30.7 us  [the longest x6 21.1 us: exchange(): lax.ppermute(forward_value, axis, forward)]
    all_to_all x0 -> x2, starting transfers between devices: none -> 23.5 us  [everyone(): return lax.all_to_all(rows, AXES, 0, 0, tiled=True)]
    dot_general x6 -> x0, matrix products: 17.8 us -> none  [the longest x2 9.2 us: precondition(): jnp.dot(coefficient[None, :], basis_flat, preferred_element_type=jnp.floa...]
  transfers between devices with their start and end apart: 28 -> 14, of which waited for: 14 -> 1; matrix products, arithmetic and copies ran while one was open for 5% -> 1% of each run, Pallas kernels for 0% -> 5%
where the time goes in v1:
time: 199 us; the launch traced here: 198 us
  Pallas kernels  78 us (39%)
  starting transfers between devices  54.2 us (27%)
  blocking collectives  45.3 us (23%)
  waiting for transfers between devices  9.45 us (5%)
  local copies, waits for them, and re-layouts  8.43 us (4%)
    all_to_all x3, blocking collectives, everyone(): return lax.all_to_all(rows, AXES, 0, 0, tiled=True)  45.3 us
    pallas_call x1, Pallas kernels, shards(): pl.pallas_call(solve_kernel, in_specs=[smem] * 2 + [vmem] * 15, out_shape...  31.9 us
    pallas_call x1, Pallas kernels, shards(): pl.pallas_call(again_kernel, in_specs=[smem] * 2 + [vmem] * 21, out_shape...  31.7 us
    all_to_all x2, starting transfers between devices, everyone(): return lax.all_to_all(rows, AXES, 0, 0, tiled=True)  23.5 us
    ppermute x6, starting transfers between devices, exchange(): lax.ppermute(forward_value, axis, forward)  21.1 us
    ppermute x6, starting transfers between devices, exchange(): lax.ppermute(backward_value, axis, backward)  9.63 us
    all_to_all x2, waiting for transfers between devices, everyone(): return lax.all_to_all(rows, AXES, 0, 0, tiled=True)  9.42 us
    pallas_call x1, Pallas kernels, first_projection(): pl.pallas_call(first_kernel, grid=(VECTORS // group,), in_specs=[pl.Block...  7.67 us
  transfers between devices with their start and end apart: 14, of which 1 were waited for; matrix products, arithmetic and copies ran while one was open for 1% of the time, Pallas kernels for 5%

profile of v1, /device:TPU:1, one launch (start us, length us, event | category | flops | bytes accessed | tf_op | source)
XLA Modules:
  0.0 198.5 jit_solution(12706110964213765732)
XLA Ops:
  0.6 0.0 copy-start.4
  0.7 1.1 fusion.4
  1.7 1.0 fusion.3
  2.7 0.0 copy-start.7
  2.8 4.6 %collective-permute-start = (f32[32,16,128]{2,1,0:T(8,128)S(1)}, f32[32,16,128]{2,1,0:T(8,128)S(1)}, u32[]{:S(2)}, u32[]{:S(2)}) collective-permute-start(f32[32,16,128]{2,1,0:T(8,128)S(1)} %pad_maximum_fusion), channel_id=1, source_target_pairs={{0,16},{16,32},{32,48},{48,64},{64,80},{80,96},{96,112},{1,17},{17... | collective-permute-start | bytes 786440 | tf_op jit(solution)/shard_map/ppermute | solution.py:51
  7.4 0.7 pad_maximum_fusion.1
  8.1 1.9 collective-permute-start.1
  10.7 0.7 convert_bitcast_fusion
  11.3 0.1 bitcast_maximum_fusion.told_ref
  11.4 2.2 %copy-done = bf16[32,16,32,128]{3,2,1,0:T(8,128)(2,1)S(1)} copy-done((bf16[32,16,32,128]{3,2,1,0:T(8,128)(2,1)S(1)}, bf16[32,16,32,128]{3,2,1,0:T(8,128)(2,1)}, u32[]{:S(2)}) %copy-start) | copy-done | bytes 4194328
  13.6 0.9 copy-done.3
  14.5 7.7 %first_projection.1 = (f32[128,128]{1,0:T(8,128)}, f32[32,16,128]{2,1,0:T(8,128)}, f32[32,16,128]{2,1,0:T(8,128)}, f32[16,32,128]{2,1,0:T(8,128)S(1)}, f32[16,32,128]{2,1,0:T(8,128)S(1)}) custom-call(f32[16,32,128]{2,1,0:T(8,128)S(1)} %copy-done.3, bf16[32,16,32,128]{3,2,1,0:T(8,128)(2,1)S(1)} %copy-done, f32[1,128]{1,0:T(1,128)S(1)} %bitcast_maximum_fusion.told_ref), custom_call_target="tpu_custom_call" | custom-call | tf_op jit(solution)/shard_map/first_projection/pallas_call | solution.py:114
  22.2 10.5 %all-to-all-start = ((f32[128,1,128]{2,1,0:T(1,128)}), f32[128,1,128]{2,1,0:T(1,128)S(1)}, u32[]{:S(2)}, u32[]{:S(2)}) async-start(f32[128,1,128]{2,1,0:T(1,128)} %bitcast.4), calls=%async_computation | async-start | bytes 131072 | tf_op jit(solution)/shard_map/all_to_all | solution.py:55
  32.8 3.5 %collective-permute-start.4 = (f32[32,16,128]{2,1,0:T(8,128)}, f32[32,16,128]{2,1,0:T(8,128)S(1)}, u32[]{:S(2)}, u32[]{:S(2)}) collective-permute-start(f32[32,16,128]{2,1,0:T(8,128)} %get-tuple-element.27), channel_id=1, source_target_pairs={{0,16},{16,32},{32,48},{48,64},{64,80},{80,96},{96,112},{1,17},{17... | collective-permute-start | bytes 786440 | tf_op jit(solution)/shard_map/ppermute | solution.py:51
  36.3 1.9 collective-permute-start.5
  38.2 3.3 %collective-permute-start.6 = (f32[16,32,128]{2,1,0:T(8,128)S(1)}, f32[16,32,128]{2,1,0:T(8,128)S(1)}, u32[]{:S(2)}, u32[]{:S(2)}) collective-permute-start(f32[16,32,128]{2,1,0:T(8,128)S(1)} %get-tuple-element.29), channel_id=1, source_target_pairs={{0,1},{1,2},{2,3},{3,4},{4,5},{5,6},{6,7},{7,8},{8,9},{9,10},{10,1... | collective-permute-start | bytes 786440 | tf_op jit(solution)/shard_map/ppermute | solution.py:51
  41.5 0.0 collective-permute-done
  41.6 1.3 collective-permute-start.7
  42.9 0.0 collective-permute-done.1
  42.9 1.0 fusion.1
  43.9 0.0 all-to-all-done
  43.9 2.3 %coarse_rows.2 = (f32[128,128]{1,0:T(8,128)}, f32[4,64,128]{2,1,0:T(8,128)}, f32[4,64,128]{2,1,0:T(8,128)}) custom-call(f32[128,128]{1,0:T(8,128)S(1)} %bitcast.32, f32[128,128]{1,0:T(8,128)S(1)} %bitcast.33, f32[32,4096]{1,0:T(8,128)S(1)} %copy-done.6, f32[16,16,128]{2,1,0:T(8,128)S(1)} %get-tuple-element.47.refs_0_.r_up, f32[16,32,128]{2,1,0:T(8,128)S(1)} %copy-done.4, ...), custom_call_target="tpu_custom_call" | custom-call | tf_op jit(solution)/shard_map/coarse_rows/pallas_call | solution.py:192
  46.2 4.0 %collective-permute-start.2 = (f32[4,64,128]{2,1,0:T(8,128)}, f32[4,64,128]{2,1,0:T(8,128)S(1)}, u32[]{:S(2)}, u32[]{:S(2)}) collective-permute-start(f32[4,64,128]{2,1,0:T(8,128)} %get-tuple-element.25), channel_id=1, source_target_pairs={{0,1},{1,2},{2,3},{3,4},{4,5},{5,6},{6,7},{7,8},{8,9},{9,10},{10,1... | collective-permute-start | bytes 393224 | tf_op jit(solution)/shard_map/ppermute | solution.py:51
  50.2 0.0 collective-permute-done.4.e_up
  50.2 1.3 collective-permute-start.3
  51.5 13.0 %all-to-all-start.1 = ((f32[128,1,128]{2,1,0:T(1,128)}), f32[128,1,128]{2,1,0:T(1,128)S(1)}, u32[]{:S(2)}, u32[]{:S(2)}) async-start(f32[128,1,128]{2,1,0:T(1,128)} %bitcast.7), calls=%async_computation.1 | async-start | bytes 131072 | tf_op jit(solution)/shard_map/all_to_all | solution.py:55
  64.5 0.1 pad_add_fusion.place_ref
  64.6 0.0 collective-permute-done.5.e_down
  64.6 0.0 collective-permute-done.6.e_left
  64.6 0.0 collective-permute-done.7.e_right
  64.6 9.4 %all-to-all-done.1 = f32[128,1,128]{2,1,0:T(1,128)S(1)} async-done(((f32[128,1,128]{2,1,0:T(1,128)}), f32[128,1,128]{2,1,0:T(1,128)S(1)}, u32[]{:S(2)}, u32[]{:S(2)}) %all-to-all-start.1) | async-done | bytes 65568 | tf_op jit(solution)/shard_map/all_to_all | solution.py:55
  74.0 0.0 collective-permute-done.2.left_ref.left_c
  74.0 0.0 collective-permute-done.3.right_ref.right_c
  74.0 0.0 copy-start.1
  74.0 2.2 %copy-done.1 = bf16[32,16,32,128]{3,2,1,0:T(8,128)(2,1)S(1)} copy-done((bf16[32,16,32,128]{3,2,1,0:T(8,128)(2,1)S(1)}, bf16[32,16,32,128]{3,2,1,0:T(8,128)(2,1)}, u32[]{:S(2)}) %copy-start.1) | copy-done | bytes 4194328
  76.2 31.9 %precondition.1 = (f32[16,32,128]{2,1,0:T(8,128)S(1)}, f32[16,32,128]{2,1,0:T(8,128)S(1)}, f32[16,32,128]{2,1,0:T(8,128)S(1)}, f32[16,16,128]{2,1,0:T(8,128)S(1)...) custom-call(s32[4]{0:T(128)S(1)} %pad_add_fusion.place_ref, f32[2,8]{1,0:T(2,128)S(1)} %copy-done.7, ...), custom_call_target="tpu_custom_call" | custom-call | tf_op jit(solution)/shard_map/precondition/pallas_call | solution.py:642
  108.2 3.2 %collective-permute-start.8 = (f32[16,16,128]{2,1,0:T(8,128)S(1)}, f32[16,16,128]{2,1,0:T(8,128)S(1)}, u32[]{:S(2)}, u32[]{:S(2)}) collective-permute-start(f32[16,16,128]{2,1,0:T(8,128)S(1)} %get-tuple-element.32), channel_id=1, source_target_pairs={{0,16},{16,32},{32,48},{48,64},{64,80},{80,96},{96,112},{1,17},{17... | collective-permute-start | bytes 393224 | tf_op jit(solution)/shard_map/ppermute | solution.py:51
  111.4 1.9 collective-permute-start.9
  113.3 14.3 %all_to_all.55 = f32[128,1,128]{2,1,0:T(1,128)S(1)} all-to-all(f32[128,1,128]{2,1,0:T(1,128)S(1)} %bitcast.44), channel_id=1, replica_groups=mesh['gx'=8,'gy'=16] {'gx','gy'}, dimensions={0} | all-to-all | bytes 131072 | tf_op jit(solution)/shard_map/all_to_all | solution.py:55
  127.6 0.0 collective-permute-done.8.refs_0_.w_up
  127.6 0.0 collective-permute-done.9.refs_2_.w_down
  127.6 1.4 coarse_rows.3
  129.1 2.5 %collective-permute-start.10 = (f32[2,64,128]{2,1,0:T(8,128)S(1)}, f32[2,64,128]{2,1,0:T(8,128)S(1)}, u32[]{:S(2)}, u32[]{:S(2)}) collective-permute-start(f32[2,64,128]{2,1,0:T(8,128)S(1)} %get-tuple-element.36), channel_id=1, source_target_pairs={{0,1},{1,2},{2,3},{3,4},{4,5},{5,6},{6,7},{7,8},{8,9},{9,10},{10,1... | collective-permute-start | bytes 196616 | tf_op jit(solution)/shard_map/ppermute | solution.py:51
  131.6 1.3 collective-permute-start.11
  132.9 17.1 %all_to_all.56 = f32[128,1,128]{2,1,0:T(1,128)S(1)} all-to-all(f32[128,1,128]{2,1,0:T(1,128)S(1)} %bitcast.45), channel_id=1, replica_groups=mesh['gx'=8,'gy'=16] {'gx','gy'}, dimensions={0} | all-to-all | bytes 131072 | tf_op jit(solution)/shard_map/all_to_all | solution.py:55
  150.0 31.7 %precondition_image.1 = (f32[16,32,128]{2,1,0:T(8,128)S(1)}, f32[16,32,128]{2,1,0:T(8,128)S(1)}, f32[16,32,128]{2,1,0:T(8,128)S(1)}, f32[128,128]{1,0:T(8,128)S(1)}) custom-call(s32[4]{0:T(128)S(1)} %pad_add_fusion.place_ref, f32[2,8]{1,0:T(2,128)S(1)} %copy-done.7, f32[128,128]{1,0:T(8,128)S(1)} %bitcast.36, f32[128,128]{1,0:T(8,128)S(1)} %bitcast.38, ...), custom_call_target="tpu_custom_call" | custom-call | tf_op jit(solution)/shard_map/precondition_image/pallas_call | solution.py:656
  181.7 13.9 %all_to_all.57 = f32[128,1,128]{2,1,0:T(1,128)S(1)} all-to-all(f32[128,1,128]{2,1,0:T(1,128)S(1)} %bitcast.43), channel_id=1, replica_groups=mesh['gx'=8,'gy'=16] {'gx','gy'}, dimensions={0} | all-to-all | bytes 131072 | tf_op jit(solution)/shard_map/all_to_all | solution.py:55
  195.6 2.9 %update.1 = (f32[16,32,128]{2,1,0:T(8,128)}, f32[16,32,128]{2,1,0:T(8,128)}) custom-call(f32[128,128]{1,0:T(8,128)S(1)} %bitcast.39, f32[128,128]{1,0:T(8,128)S(1)} %bitcast.42, f32[16,32,128]{2,1,0:T(8,128)S(1)} %get-tuple-element.38.direction_ref, f32[16,32,128]{2,1,0:T(8,128)S(1)} %get-tuple-element.33.refs_1_.w_own.first_ref, ...), custom_call_target="tpu_custom_call" | custom-call | tf_op jit(solution)/shard_map/update/pallas_call | solution.py:669
  (16 shorter events, 0.1 us)
Async XLA Ops:
  0.6 43.3 %copy-start.5 = (f32[16,32,128]{2,1,0:T(8,128)S(1)}, f32[16,32,128]{2,1,0:T(8,128)}, u32[]{:S(2)}) copy-start(f32[16,32,128]{2,1,0:T(8,128)} %c_own.3) | copy-start | bytes 786436
  0.6 43.3 %copy-start.4 = (f32[16,32,128]{2,1,0:T(8,128)S(1)}, f32[16,32,128]{2,1,0:T(8,128)}, u32[]{:S(2)}) copy-start(f32[16,32,128]{2,1,0:T(8,128)} %source_ref.1) | copy-start | bytes 786436
  0.7 43.3 %copy-start.6 = (f32[32,4096]{1,0:T(8,128)S(1)}, f32[32,4096]{1,0:T(8,128)}, u32[]{:S(2)}) copy-start(f32[32,4096]{1,0:T(8,128)} %inverse_ref.3) | copy-start | bytes 1572868
  2.7 71.3 %copy-start.7 = (f32[2,8]{1,0:T(2,128)S(1)}, f32[2,8]{1,0:T(2,128)}, u32[]{:S(2)}) copy-start(f32[2,8]{1,0:T(2,128)} %constant.18.clone.table_ref) | copy-start | bytes 196
  2.8 38.8 %collective-permute-start = (f32[32,16,128]{2,1,0:T(8,128)S(1)}, f32[32,16,128]{2,1,0:T(8,128)S(1)}, u32[]{:S(2)}, u32[]{:S(2)}) collective-permute-start(f32[32,16,128]{2,1,0:T(8,128)S(1)} %pad_maximum_fusion), channel_id=1, source_target_pairs={{0,16},{16,32},{32,48},{48,64},{64,80},{80,96},{96,112},{1,17},{17... | collective-permute-start | bytes 786440 | tf_op jit(solution)/shard_map/ppermute | solution.py:51
  8.1 34.8 %collective-permute-start.1 = (f32[32,16,128]{2,1,0:T(8,128)}, f32[32,16,128]{2,1,0:T(8,128)}, u32[]{:S(2)}, u32[]{:S(2)}) collective-permute-start(f32[32,16,128]{2,1,0:T(8,128)} %pad_maximum_fusion.1), channel_id=1, source_target_pairs={{16,0},{32,16},{48,32},{64,48},{80,64},{96,80},{112,96},{17,1},{33... | collective-permute-start | bytes 786440 | tf_op jit(solution)/shard_map/ppermute | solution.py:51
  11.4 2.2 %copy-start = (bf16[32,16,32,128]{3,2,1,0:T(8,128)(2,1)S(1)}, bf16[32,16,32,128]{3,2,1,0:T(8,128)(2,1)}, u32[]{:S(2)}) copy-start(bf16[32,16,32,128]{3,2,1,0:T(8,128)(2,1)} %basis_ref.5) | copy-start | bytes 12582916
  13.6 0.9 copy-start.3
  22.2 21.7 %all-to-all-start = ((f32[128,1,128]{2,1,0:T(1,128)}), f32[128,1,128]{2,1,0:T(1,128)S(1)}, u32[]{:S(2)}, u32[]{:S(2)}) async-start(f32[128,1,128]{2,1,0:T(1,128)} %bitcast.4), calls=%async_computation | async-start | bytes 131072 | tf_op jit(solution)/shard_map/all_to_all | solution.py:55
  32.8 17.5 %collective-permute-start.4 = (f32[32,16,128]{2,1,0:T(8,128)}, f32[32,16,128]{2,1,0:T(8,128)S(1)}, u32[]{:S(2)}, u32[]{:S(2)}) collective-permute-start(f32[32,16,128]{2,1,0:T(8,128)} %get-tuple-element.27), channel_id=1, source_target_pairs={{0,16},{16,32},{32,48},{48,64},{64,80},{80,96},{96,112},{1,17},{17... | collective-permute-start | bytes 786440 | tf_op jit(solution)/shard_map/ppermute | solution.py:51
  36.3 28.3 %collective-permute-start.5 = (f32[32,16,128]{2,1,0:T(8,128)}, f32[32,16,128]{2,1,0:T(8,128)S(1)}, u32[]{:S(2)}, u32[]{:S(2)}) collective-permute-start(f32[32,16,128]{2,1,0:T(8,128)} %get-tuple-element.28), channel_id=1, source_target_pairs={{16,0},{32,16},{48,32},{64,48},{80,64},{96,80},{112,96},{17,1},{33... | collective-permute-start | bytes 786440 | tf_op jit(solution)/shard_map/ppermute | solution.py:51
  38.2 26.3 %collective-permute-start.6 = (f32[16,32,128]{2,1,0:T(8,128)S(1)}, f32[16,32,128]{2,1,0:T(8,128)S(1)}, u32[]{:S(2)}, u32[]{:S(2)}) collective-permute-start(f32[16,32,128]{2,1,0:T(8,128)S(1)} %get-tuple-element.29), channel_id=1, source_target_pairs={{0,1},{1,2},{2,3},{3,4},{4,5},{5,6},{6,7},{7,8},{8,9},{9,10},{10,1... | collective-permute-start | bytes 786440 | tf_op jit(solution)/shard_map/ppermute | solution.py:51
  41.6 23.0 %collective-permute-start.7 = (f32[16,32,128]{2,1,0:T(8,128)S(1)}, f32[16,32,128]{2,1,0:T(8,128)S(1)}, u32[]{:S(2)}, u32[]{:S(2)}) collective-permute-start(f32[16,32,128]{2,1,0:T(8,128)S(1)} %get-tuple-element.30), channel_id=1, source_target_pairs={{1,0},{2,1},{3,2},{4,3},{5,4},{6,5},{7,6},{8,7},{9,8},{10,9},{11,1... | collective-permute-start | bytes 786440 | tf_op jit(solution)/shard_map/ppermute | solution.py:51
  46.2 27.8 %collective-permute-start.2 = (f32[4,64,128]{2,1,0:T(8,128)}, f32[4,64,128]{2,1,0:T(8,128)S(1)}, u32[]{:S(2)}, u32[]{:S(2)}) collective-permute-start(f32[4,64,128]{2,1,0:T(8,128)} %get-tuple-element.25), channel_id=1, source_target_pairs={{0,1},{1,2},{2,3},{3,4},{4,5},{5,6},{6,7},{7,8},{8,9},{9,10},{10,1... | collective-permute-start | bytes 393224 | tf_op jit(solution)/shard_map/ppermute | solution.py:51
  50.2 23.8 %collective-permute-start.3 = (f32[4,64,128]{2,1,0:T(8,128)}, f32[4,64,128]{2,1,0:T(8,128)S(1)}, u32[]{:S(2)}, u32[]{:S(2)}) collective-permute-start(f32[4,64,128]{2,1,0:T(8,128)} %get-tuple-element.26), channel_id=1, source_target_pairs={{1,0},{2,1},{3,2},{4,3},{5,4},{6,5},{7,6},{8,7},{9,8},{10,9},{11,1... | collective-permute-start | bytes 393224 | tf_op jit(solution)/shard_map/ppermute | solution.py:51
  51.5 22.5 %all-to-all-start.1 = ((f32[128,1,128]{2,1,0:T(1,128)}), f32[128,1,128]{2,1,0:T(1,128)S(1)}, u32[]{:S(2)}, u32[]{:S(2)}) async-start(f32[128,1,128]{2,1,0:T(1,128)} %bitcast.7), calls=%async_computation.1 | async-start | bytes 131072 | tf_op jit(solution)/shard_map/all_to_all | solution.py:55
  74.0 2.2 %copy-start.1 = (bf16[32,16,32,128]{3,2,1,0:T(8,128)(2,1)S(1)}, bf16[32,16,32,128]{3,2,1,0:T(8,128)(2,1)}, u32[]{:S(2)}) copy-start(bf16[32,16,32,128]{3,2,1,0:T(8,128)(2,1)} %basis_ref.5) | copy-start | bytes 12582916
  76.2 73.8 %copy-start.2 = (bf16[32,16,32,128]{3,2,1,0:T(8,128)(2,1)S(1)}, bf16[32,16,32,128]{3,2,1,0:T(8,128)(2,1)}, u32[]{:S(2)}) copy-start(bf16[32,16,32,128]{3,2,1,0:T(8,128)(2,1)} %basis_ref.5) | copy-start | bytes 12582916
  108.2 19.5 %collective-permute-start.8 = (f32[16,16,128]{2,1,0:T(8,128)S(1)}, f32[16,16,128]{2,1,0:T(8,128)S(1)}, u32[]{:S(2)}, u32[]{:S(2)}) collective-permute-start(f32[16,16,128]{2,1,0:T(8,128)S(1)} %get-tuple-element.32), channel_id=1, source_target_pairs={{0,16},{16,32},{32,48},{48,64},{64,80},{80,96},{96,112},{1,17},{17... | collective-permute-start | bytes 393224 | tf_op jit(solution)/shard_map/ppermute | solution.py:51
  111.4 16.3 %collective-permute-start.9 = (f32[16,16,128]{2,1,0:T(8,128)S(1)}, f32[16,16,128]{2,1,0:T(8,128)S(1)}, u32[]{:S(2)}, u32[]{:S(2)}) collective-permute-start(f32[16,16,128]{2,1,0:T(8,128)S(1)} %get-tuple-element.34), channel_id=1, source_target_pairs={{16,0},{32,16},{48,32},{64,48},{80,64},{96,80},{112,96},{17,1},{33... | collective-permute-start | bytes 393224 | tf_op jit(solution)/shard_map/ppermute | solution.py:51
  129.1 20.9 %collective-permute-start.10 = (f32[2,64,128]{2,1,0:T(8,128)S(1)}, f32[2,64,128]{2,1,0:T(8,128)S(1)}, u32[]{:S(2)}, u32[]{:S(2)}) collective-permute-start(f32[2,64,128]{2,1,0:T(8,128)S(1)} %get-tuple-element.36), channel_id=1, source_target_pairs={{0,1},{1,2},{2,3},{3,4},{4,5},{5,6},{6,7},{7,8},{8,9},{9,10},{10,1... | collective-permute-start | bytes 196616 | tf_op jit(solution)/shard_map/ppermute | solution.py:51
  131.6 18.4 %collective-permute-start.11 = (f32[2,64,128]{2,1,0:T(8,128)S(1)}, f32[2,64,128]{2,1,0:T(8,128)S(1)}, u32[]{:S(2)}, u32[]{:S(2)}) collective-permute-start(f32[2,64,128]{2,1,0:T(8,128)S(1)} %get-tuple-element.37), channel_id=1, source_target_pairs={{1,0},{2,1},{3,2},{4,3},{5,4},{6,5},{7,6},{8,7},{9,8},{10,9},{11,1... | collective-permute-start | bytes 196616 | tf_op jit(solution)/shard_map/ppermute | solution.py:51

commit v2 on v1

v2 whole, which is shorter than its diff:
```python
import functools

import jax
import jax.numpy as jnp
from jax import lax
from jax.experimental import pallas as pl
from jax.experimental.pallas import tpu as pltpu
from jax.sharding import PartitionSpec as P

KCHEB = 9
AXES = ("gx", "gy")
LEVELS = 16
ROWS = 32
COLS = 128
VECTORS = 32
EDGE = 16
TALL = ROWS + 2 * EDGE
HIGHEST = lax.Precision.HIGHEST

lowest_rate = 0.05
highest_rate = 18.5
vertical = 2.0
theta = 0.5 * (highest_rate + lowest_rate)
delta = 0.5 * (highest_rate - lowest_rate)
VMEM_LIMIT = 24 * 1024 * 1024
FIRST_LIMIT = 58 * 1024 * 1024


def chebyshev_table():
    ratio = theta / delta
    rho_old = 1.0 / ratio
    table = []
    for _ in range(KCHEB - 1):
        rho_new = 1.0 / (2.0 * ratio - rho_old)
        table.append((rho_new * rho_old, 2.0 * rho_new / delta))
        rho_old = rho_new
    return table


def iota(shape, dim):
    return lax.broadcasted_iota(jnp.int32, shape, dim)


def roll(value, shift):
    return pltpu.roll(value, shift % COLS, 1)


def exchange(forward_value, backward_value, axis):
    count = lax.axis_size(axis)
    forward = [(i, i + 1) for i in range(count - 1)]
    backward = [(target, source) for source, target in forward]
    return lax.ppermute(forward_value, axis, forward), lax.ppermute(backward_value, axis, backward)


def everyone(rows):
    return lax.all_to_all(rows, AXES, 0, 0, tiled=True)


def row_of_sums(sums):
    padded = jnp.concatenate([sums, jnp.zeros((COLS - VECTORS, COLS), jnp.float32)], 0)
    ones = jnp.ones((COLS, COLS), jnp.float32)
    return lax.dot_general(
        ones, padded, (((1,), (1,)), ((), ())), precision=HIGHEST, preferred_element_type=jnp.float32
    )


def fold_rows(product):
    return (product[0:8] + product[8:16]) + (product[16:24] + product[24:32])


def first_kernel(
    field_ref, coefficient_ref, basis_ref, told_ref, out_ref, ahead_ref, behind_ref, left_ref, right_ref, sums_ref
):
    step = pl.program_id(0)
    group = basis_ref.shape[0]
    lane = iota((ROWS, COLS), 1)

    @pl.when(step == 0)
    def _():
        left_ref[...] = jnp.zeros_like(left_ref)
        right_ref[...] = jnp.zeros_like(right_ref)

        def level(z, carry):
            ahead_ref[z] = field_ref[z, ROWS - EDGE :, :]
            behind_ref[z] = field_ref[z, :EDGE, :]
            ahead_ref[LEVELS + z] = coefficient_ref[z, ROWS - EDGE :, :]
            behind_ref[LEVELS + z] = coefficient_ref[z, :EDGE, :]
            return carry

        lax.fori_loop(0, LEVELS, level, 0)

    def level(z, sums):
        field = field_ref[z]
        low = left_ref[z >> 2]
        high = right_ref[z >> 2]
        new = []
        for j in range(group):
            values = basis_ref[j, z].astype(jnp.float32)
            new.append(sums[j] + fold_rows(values * field))
            at = 2 * LEVELS + step * group + j
            behind_ref[at, pl.ds(z, 1), :] = values[0:1]
            ahead_ref[at, pl.ds(z, 1), :] = values[ROWS - 1 : ROWS]
            k = step * group + j + VECTORS * (z & 3)
            turned = pltpu.roll(values, k, 1)
            low = jnp.where(lane == k, turned, low)
            high = jnp.where(lane == ((k + COLS - 1) & (COLS - 1)), turned, high)
        left_ref[z >> 2] = low
        right_ref[z >> 2] = high
        return tuple(new)

    zero = jnp.zeros((8, COLS), jnp.float32)
    sums = lax.fori_loop(0, LEVELS, level, (zero,) * group)
    for j in range(group):
        sums_ref[pl.ds(step * group + j, 1), :] = jnp.sum(sums[j], axis=0, keepdims=True)

    @pl.when(step == pl.num_programs(0) - 1)
    def _():
        out_ref[...] = row_of_sums(sums_ref[...]) + told_ref[...]


def first_projection(field, coefficient, basis, told_row):
    group = 8
    rows = 2 * LEVELS + VECTORS
    edge_rows = jax.ShapeDtypeStruct((rows, LEVELS, COLS), jnp.float32)
    edge_cols = jax.ShapeDtypeStruct((LEVELS // 4, ROWS, COLS), jnp.float32)
    block_spec = pl.BlockSpec((LEVELS, ROWS, COLS), lambda i: (0, 0, 0))
    rows_spec = pl.BlockSpec(edge_rows.shape, lambda i: (0, 0, 0))
    cols_spec = pl.BlockSpec(edge_cols.shape, lambda i: (0, 0, 0))
    return pl.pallas_call(
        first_kernel,
        grid=(VECTORS // group,),
        in_specs=[
            block_spec,
            block_spec,
            pl.BlockSpec((group, LEVELS, ROWS, COLS), lambda i: (i, 0, 0, 0)),
            pl.BlockSpec((1, COLS), lambda i: (0, 0)),
        ],
        out_specs=[pl.BlockSpec((COLS, COLS), lambda i: (0, 0)), rows_spec, rows_spec, cols_spec, cols_spec],
        out_shape=[jax.ShapeDtypeStruct((COLS, COLS), jnp.float32), edge_rows, edge_rows, edge_cols, edge_cols],
        scratch_shapes=[pltpu.VMEM((VECTORS, COLS), jnp.float32)],
        compiler_params=pltpu.CompilerParams(vmem_limit_bytes=FIRST_LIMIT),
        name="first_projection",
    )(field, coefficient, basis, told_row)


def coarse_rows(told_ref, slots_ref, inverse_ref, out_ref):
    told = told_ref[...]
    slots = slots_ref[...]
    turned = told.T
    slots_turned = slots.T
    lane = iota((COLS, COLS), 1)
    sub = iota((VECTORS, COLS), 0)
    placed = jnp.zeros((3 * VECTORS, COLS), jnp.float32)
    for k in range(VECTORS):
        slot_column = slots[:, VECTORS + k : VECTORS + k + 1].astype(jnp.int32)
        ones = jnp.where((slot_column & 127) == lane, 1.0, 0.0).astype(jnp.bfloat16)
        slot_row = slots_turned[VECTORS + k : VECTORS + k + 1, :].astype(jnp.int32)
        values = turned[k : k + 1, :]
        spread = jnp.where((slot_row >> 7) == sub, values, 0.0)
        first = spread.astype(jnp.bfloat16)
        rest = spread - first.astype(jnp.float32)
        second = rest.astype(jnp.bfloat16)
        third = (rest - second.astype(jnp.float32)).astype(jnp.bfloat16)
        parts = jnp.concatenate([first, second, third], 0)
        placed = placed + jnp.dot(parts, ones, preferred_element_type=jnp.float32)
    placed = placed[:VECTORS] + placed[VECTORS : 2 * VECTORS] + placed[2 * VECTORS :]
    total = jnp.zeros((VECTORS, COLS), jnp.float32)
    for high in range(VECTORS):
        total = total + inverse_ref[:, high * COLS : (high + 1) * COLS] * placed[high : high + 1]
    out_ref[...] = row_of_sums(total)


def pack_strips(parts, forward_ref, backward_ref, at):
    def levels(group, carry):
        row = 0
        for part, start in parts:
            height = EDGE if part.shape[1] == EDGE else ROWS
            lane = iota((height, COLS), 1)
            ahead = jnp.zeros((height, COLS), jnp.float32)
            behind = ahead
            for j in range(8):
                value = part[start + group * 8 + j]
                mine = (lane >= EDGE * j) & (lane < EDGE * (j + 1))
                ahead = jnp.where(mine, roll(value, EDGE * j - (COLS - EDGE)), ahead)
                behind = jnp.where(mine, roll(value, EDGE * j), behind)
            forward_ref[at + group, row : row + height, :] = ahead
            backward_ref[at + group, row : row + height, :] = behind
            row += height
        return carry

    lax.fori_loop(0, LEVELS // 8, levels, 0)


def first_middle_kernel(
    told_ref, inverse_ref, source_ref, absorption_ref, low_ref, high_ref, left_ref, right_ref,
    out_ref, forward_ref, backward_ref,
):
    for f, block in enumerate((source_ref, absorption_ref)):
        pack_strips(((low_ref, LEVELS * f), (block, 0), (high_ref, LEVELS * f)), forward_ref, backward_ref, 2 * f)
    for n in range(LEVELS // 8):
        for half in range(2):
            rows = slice(half * ROWS, (half + 1) * ROWS)
            forward_ref[4 + n, rows, :] = right_ref[2 * n + half]
            backward_ref[4 + n, rows, :] = left_ref[2 * n + half]
    coarse_rows(told_ref, told_ref, inverse_ref, out_ref)


def middle_kernel(told_ref, slots_ref, inverse_ref, block_ref, low_ref, high_ref, out_ref, forward_ref, backward_ref):
    pack_strips(((low_ref, 0), (block_ref, 0), (high_ref, 0)), forward_ref, backward_ref, 0)
    coarse_rows(told_ref, slots_ref, inverse_ref, out_ref)


def middle(kernel, strips, *operands):
    strips = jax.ShapeDtypeStruct((strips, TALL, COLS), jnp.float32)
    return pl.pallas_call(
        kernel,
        out_shape=[jax.ShapeDtypeStruct((COLS, COLS), jnp.float32), strips, strips],
        compiler_params=pltpu.CompilerParams(vmem_limit_bytes=VMEM_LIMIT),
        name="coarse_rows",
    )(*operands)


class Place:
    def __init__(self, place_ref, told_ref):
        self.row = place_ref[0]
        self.col = place_ref[1]
        self.rows = place_ref[2]
        self.cols = place_ref[3]
        self.told_ref = told_ref

    def index(self, down, right):
        row = jnp.clip(self.row + down, 0, self.rows - 1)
        col = jnp.clip(self.col + right, 0, self.cols - 1)
        return row * self.cols + col

    def margin(self, down, right):
        row, col = self.row + down, self.col + right
        real = (row >= 0) & (row < self.rows) & (col >= 0) & (col < self.cols)
        margin = self.told_ref[pl.ds(self.index(down, right), 1), :][:, 64:65]
        return jnp.where(real, margin.astype(jnp.int32), -4096)


def masks(place, own_ref, beside_ref, strip_ref):
    shape = (TALL, COLS)
    row = iota(shape, 0) - EDGE
    lane = iota(shape, 1)
    top, bottom = -ROWS * place.row, ROWS * (place.rows - place.row)
    first, last = -COLS * place.col, COLS * (place.cols - place.col)
    row_real = (row >= top) & (row < bottom)
    m = {(i, j): place.margin(i, j) for i in (-1, 0, 1) for j in (-1, 0, 1)}
    upper, lower = row < 8, row >= ROWS - 8
    for tile in range(2):
        col = lane if tile == 0 else jnp.where(lane < 64, lane + COLS, lane - COLS)
        real = row_real & (col >= first) & (col < last)
        if tile == 1:
            real = real & ((lane < EDGE) | (lane >= COLS - EDGE))

        def across(margin):
            return (col >= -margin) & (col < COLS + margin)

        own = m[0, 0]
        inside = real & (row >= -own) & (row < ROWS + own) & across(own)
        own_ref[tile] = jnp.where(inside, 1.0, 0.0)
        above, below = m[-1, 0], m[1, 0]
        inside = (upper & (row < above) & across(above)) | (lower & (row >= ROWS - below) & across(below))
        beside_ref[tile] = jnp.where(real & inside, 1.0, 0.0)
    group = ((lane + EDGE) & 127) >> 5
    away = ((lane + EDGE) & 31) - EDGE
    inside = row < -4096
    for place_of, side in ((0, -1), (2, 1)):
        col = away if side < 0 else away + COLS
        real = row_real & (col >= first) & (col < last)

        def reached(margin):
            return (away < margin) if side < 0 else (away >= -margin)

        level = m[0, side]
        inside = inside | (
            (group == place_of) & real & (row >= -level) & (row < ROWS + level) & reached(level)
        )
        above, below = m[-1, side], m[1, side]
        corner = (upper & (row < above) & reached(above)) | (
            lower & (row >= ROWS - below) & reached(below)
        )
        inside = inside | ((group == place_of + 1) & real & corner)
    strip_ref[...] = jnp.where(inside, 1.0, 0.0)


def tiles_of(parts, start, strips, at, z, i):
    low, block, high = parts
    from_left, from_right = strips
    lane = iota((8, COLS), 1)
    if i < 2:
        center = low[start + z, i * 8 : i * 8 + 8, :]
    elif i < 6:
        center = block[z, (i - 2) * 8 : (i - 2) * 8 + 8, :]
    else:
        center = high[start + z, (i - 6) * 8 : (i - 6) * 8 + 8, :]
    s = slice(i * 8, i * 8 + 8)
    group, shift = at + (z >> 3), EDGE * (z & 7)
    left = pltpu.roll(from_left[group, s, :], (COLS - EDGE) - shift, 1)
    right = pltpu.roll(from_right[group, s, :], (COLS - shift) & (COLS - 1), 1)
    margin = jnp.where(lane >= COLS - EDGE, left, jnp.where(lane < EDGE, right, 0.0))
    at_left = jnp.where(lane >= 64, margin, center)
    at_right = jnp.where(lane < 64, margin, center)
    near = (lane < EDGE) | (lane >= COLS - EDGE)
    others = jnp.where(lane < 80, roll(at_right, 64), roll(at_right, 96))
    packed = jnp.where(near, at_left, jnp.where(lane < 48, roll(at_left, 32), others))
    return center, margin, packed


PLANES = LEVELS + 2
BESIDE_TILES = (1, 2, 5, 6)


def smooth_kernel(
    starts, place_ref, table_ref, told_ref, block_ref, low_ref, high_ref, left_ref, right_ref,
    absorption_ref, low_c, high_c, left_c, right_c, out_ref,
    own_m, beside_m, strip_m, own, beside, strip, own_d, beside_d, strip_d, own_r, beside_r, strip_r, diag, strip_diag,
):
    field_start, coef_start, coef_at = starts
    masks(Place(place_ref, told_ref), own_m, beside_m, strip_m)
    base = 4.0 + 2.0 * vertical
    zero = jnp.zeros((8, COLS), jnp.float32)
    lane = iota((8, COLS), 1)
    lanes = [slice(0, COLS), slice(COLS, 2 * COLS)]

    def clear(n, carry):
        at = (n & 1) * (PLANES - 1) + (n >> 1) * PLANES
        for i in range(8):
            s = slice(i * 8, i * 8 + 8)
            for t in range(2):
                own[at, s, lanes[t]] = zero
                beside[at, s, lanes[t]] = zero
            strip[at, s] = zero
        return carry

    lax.fori_loop(0, 4, clear, 0)

    def begin(z, carry):
        at = z + 1
        for i in range(8):
            s = slice(i * 8, i * 8 + 8)
            tiles = tiles_of((low_ref, block_ref, high_ref), field_start, (left_ref, right_ref), 0, z, i)
            inner = 1 <= i < 7
            for t in range(2):
                value = tiles[t] * own_m[t, s]
                if inner:
                    own_r[z, s, lanes[t]] = value
                    own_d[z, s, lanes[t]] = value * (1.0 / theta)
                else:
                    own[at + PLANES, s, lanes[t]] = zero
                own[at, s, lanes[t]] = value * (1.0 / theta)
                value = tiles[t] * beside_m[t, s]
                if i in BESIDE_TILES:
                    beside_r[z, s, lanes[t]] = value
                    beside_d[z, s, lanes[t]] = value * (1.0 / theta)
                else:
                    beside[at + PLANES, s, lanes[t]] = zero
                beside[at, s, lanes[t]] = value * (1.0 / theta)
            value = tiles[2] * strip_m[s]
            strip[at, s] = value * (1.0 / theta)
            if inner:
                strip_r[z, s] = value
                strip_d[z, s] = value * (1.0 / theta)
                tiles = tiles_of((low_c, absorption_ref, high_c), coef_start, (left_c, right_c), coef_at, z, i)
                diag[z, s, lanes[0]] = tiles[0] + base
                diag[z, s, lanes[1]] = tiles[1] + base
                strip_diag[z, s] = tiles[2] + base
            else:
                strip[at + PLANES, s] = zero
        return carry

    lax.fori_loop(0, LEVELS, begin, 0)
    at_first, at_last = lane == 0, lane == COLS - 1

    def sweep(n, carry):
        keep, scale = table_ref[0, n], table_ref[1, n]
        source = (n & 1) * PLANES + 1
        target = (PLANES + 2) - source

        def step(z, x, d, r, a, mask, width, i):
            s = slice(i * 8, i * 8 + 8)
            up, down = slice(i * 8 - 1, i * 8 + 7), slice(i * 8 + 1, i * 8 + 9)
            here = source + z
            now = [x[here, s, lanes[t]] for t in range(width)]
            back = [roll(v, 1) for v in now]
            fore = [roll(v, -1) for v in now]
            if width == 2:
                back = [jnp.where(at_first, back[1], back[0]), jnp.where(at_first, back[0], back[1])]
                fore = [jnp.where(at_last, fore[1], fore[0]), jnp.where(at_last, fore[0], fore[1])]
            for t in range(width):
                high = x[here - 1, s, lanes[t]] + x[here + 1, s, lanes[t]]
                around = (x[here, up, lanes[t]] + x[here, down, lanes[t]]) + (back[t] + fore[t])
                around = around + (high + high)
                defect = r[z, s, lanes[t]] - a[z, s, lanes[t]] * now[t] + around
                move = keep * d[z, s, lanes[t]] + scale * defect
                if mask[t] is not None:
                    move = move * mask[t]
                d[z, s, lanes[t]] = move
                x[target + z, s, lanes[t]] = now[t] + move

        def level(z, carry):
            for i in range(1, 7):
                s = slice(i * 8, i * 8 + 8)
                first = None if 2 <= i < 6 else own_m[0, s]
                step(z, own, own_d, own_r, diag, [first, own_m[1, s]], 2, i)
                if i in BESIDE_TILES:
                    step(z, beside, beside_d, beside_r, diag, [beside_m[0, s], beside_m[1, s]], 2, i)
                step(z, strip, strip_d, strip_r, strip_diag, [strip_m[s]], 1, i)
            return carry

        return lax.fori_loop(0, LEVELS, level, carry)

    lax.fori_loop(0, KCHEB - 1, sweep, 0)
    near_first, near_last = lane < EDGE, lane >= COLS - EDGE

    def finish(z, carry):
        at = z + 1
        for i in range(1, 7):
            s = slice(i * 8, i * 8 + 8)
            out = slice(i * 8 - 8, i * 8)
            value = strip[at, s]
            at_left = value + roll(value, -32)
            at_right = roll(at_left, 64)
            first = jnp.where(near_first, at_left, jnp.where(near_last, at_right, 0.0))
            second = jnp.where(near_last, at_left, jnp.where(near_first, at_right, 0.0))
            first = first + own[at, s, lanes[0]]
            second = second + own[at, s, lanes[1]]
            if i in BESIDE_TILES:
                first = first + beside[at, s, lanes[0]]
                second = second + beside[at, s, lanes[1]]
            out_ref[z, out, lanes[0]] = first
            out_ref[z, out, lanes[1]] = second
        return carry

    lax.fori_loop(0, LEVELS, finish, 0)


def smooth(starts, place, table, told, block, low, high, strips, absorption, low_c, high_c, strips_c):
    wide = (TALL, 2 * COLS)
    thin = (TALL, COLS)

    def scratch(*shape):
        return pltpu.VMEM(shape, jnp.float32)

    smem = pl.BlockSpec(memory_space=pltpu.SMEM)
    vmem = pl.BlockSpec(memory_space=pltpu.VMEM)
    return pl.pallas_call(
        functools.partial(smooth_kernel, starts),
        in_specs=[smem] * 2 + [vmem] * 11,
        out_shape=jax.ShapeDtypeStruct((LEVELS, INNER, 2 * COLS), jnp.float32),
        scratch_shapes=[
            scratch(2, *thin), scratch(2, *thin), scratch(*thin),
            scratch(2 * PLANES, *wide), scratch(2 * PLANES, *wide), scratch(2 * PLANES, *thin),
            scratch(LEVELS, *wide), scratch(LEVELS, *wide), scratch(LEVELS, *thin),
            scratch(LEVELS, *wide), scratch(LEVELS, *wide), scratch(LEVELS, *thin),
            scratch(LEVELS, *wide), scratch(LEVELS, *thin),
        ],
        compiler_params=pltpu.CompilerParams(vmem_limit_bytes=VMEM_LIMIT),
        cost_estimate=pl.CostEstimate(flops=60000000, bytes_accessed=4000000, transcendentals=0),
        name="smoother",
    )(place, table, told, block, low, high, *strips, absorption, low_c, high_c, *strips_c)


INNER = ROWS + 16


def slots_of(place, told_ref, moves):
    lane = iota((1, COLS), 1)
    slots = jnp.zeros((1, COLS), jnp.float32)
    for n, (down, right) in enumerate(moves):
        row = roll(told_ref[pl.ds(place.index(down, right), 1), :], VECTORS * (n - 1))
        slots = jnp.where((lane >> 5) == n, row, slots)
    return slots.astype(jnp.int32)


def coarse_at(coarse_turned, slots):
    pick = jnp.where(iota((COLS, COLS), 0) == (slots >> 5), 1.0, 0.0)
    found = jnp.dot(coarse_turned, pick, precision=HIGHEST, preferred_element_type=jnp.float32)
    found = jnp.where(iota((VECTORS, COLS), 0) == (slots & 31), found, 0.0)
    return jnp.sum(found, axis=0, keepdims=True)


def add_coarse(place, told_ref, coarse_ref, basis_ref, low_ref, high_ref, left_ref, right_ref, at, sum_ref, x,
               own_c, edge_c, ring_ref, side_ref):
    turned = coarse_ref[...].T[:VECTORS]
    row = coarse_at(turned, slots_of(place, told_ref, ((0, 0), (-1, 0), (1, 0), (0, -1))))
    other = coarse_at(turned, slots_of(place, told_ref, ((0, 1),)))
    lane = iota((8, COLS), 1)
    lane_row = iota((1, COLS), 1)
    column = jnp.broadcast_to(row, (COLS, COLS)).T
    own_c[...] = column[:VECTORS]
    edge_c[...] = column[VECTORS : 3 * VECTORS]
    for n, edge in ((0, low_ref), (1, high_ref)):

        def vector(k, total):
            return total + edge[2 * LEVELS + k] * edge_c[pl.ds(n * VECTORS + k, 1), :]

        ring_ref[n] = lax.fori_loop(0, VECTORS, vector, jnp.zeros((LEVELS, COLS), jnp.float32))
    for n, (edge, values, shift) in enumerate(((left_ref, roll(row, VECTORS), -1), (right_ref, other, 0))):
        values = jnp.where(lane_row < VECTORS, values, 0.0)
        values = values + roll(values, 32) + roll(values, 64) + roll(values, 96)
        weights = jnp.broadcast_to(roll(values, shift), (COLS, COLS)).T
        which = ((iota((COLS, COLS), 0) - shift) & (COLS - 1)) >> 5
        weights = jnp.where(iota((COLS, COLS), 1) == which, weights, 0.0)
        parts = edge[at : at + 2].reshape(2 * TALL, COLS)
        side_ref[n] = jnp.dot(parts, weights, precision=HIGHEST, preferred_element_type=jnp.float32)

    def level(z, carry):
        total = sum_ref[z, 8 : 8 + ROWS, 0:COLS]
        for k in range(VECTORS):
            total = total + basis_ref[k, z].astype(jnp.float32) * own_c[k : k + 1]
        here = z + 1
        x[here, 8 : 8 + ROWS, 0:COLS] = total
        rows = pl.ds(z, 1)
        x[here, 7:8, 0:COLS] = sum_ref[z, 7:8, 0:COLS] + ring_ref[0, rows, :]
        x[here, 8 + ROWS : 9 + ROWS, 0:COLS] = sum_ref[z, 8 + ROWS : 9 + ROWS, 0:COLS] + ring_ref[1, rows, :]
        q = z & 3
        for i in range(ROWS // 8):
            s = pl.ds(pl.multiple_of((z >> 2) * ROWS + i * 8, 8), 8)
            left = pltpu.roll(side_ref[0, s, :], (COLS - 1) - q, 1)
            right = pltpu.roll(side_ref[1, s, :], (COLS - q) & (COLS - 1), 1)
            t = slice(8 + i * 8, 16 + i * 8)
            value = jnp.where(lane == COLS - 1, left, jnp.where(lane == 0, right, 0.0))
            x[here, t, COLS : 2 * COLS] = sum_ref[z, t, COLS : 2 * COLS] + value
        return carry

    lax.fori_loop(0, LEVELS, level, 0)
    zero = jnp.zeros((ROWS, COLS), jnp.float32)
    x[0, 8 : 8 + ROWS, 0:COLS] = zero
    x[PLANES - 1, 8 : 8 + ROWS, 0:COLS] = zero
    return row


def image_at(x, absorption_ref, z, i):
    lane = iota((8, COLS), 1)
    here = z + 1
    s = slice(8 + i * 8, 16 + i * 8)
    up, down = slice(7 + i * 8, 15 + i * 8), slice(9 + i * 8, 17 + i * 8)
    now = x[here, s, 0:COLS]
    margin = x[here, s, COLS : 2 * COLS]
    back = jnp.where(lane == 0, roll(margin, 1), roll(now, 1))
    fore = jnp.where(lane == COLS - 1, roll(margin, -1), roll(now, -1))
    high = x[here - 1, s, 0:COLS] + x[here + 1, s, 0:COLS]
    around = (x[here, up, 0:COLS] + x[here, down, 0:COLS]) + (back + fore)
    diagonal = absorption_ref[z, i * 8 : i * 8 + 8, :] + (4.0 + 2.0 * vertical)
    return now, diagonal * now - around - vertical * high


def total_of(value):
    return jnp.sum(jnp.sum(value, axis=0, keepdims=True), axis=1, keepdims=True)


def scalars(told_ref):
    totals = jnp.sum(told_ref[...], axis=0, keepdims=True)
    return totals[:, 64:65], totals[:, 65:66]


def first_coarse_kernel(
    place_ref, told_ref, coarse_ref, basis_ref, low_ref, high_ref, left_ref, right_ref, sum_ref, source_ref, absorption_ref,
    direction_ref, image_ref, ahead_ref, behind_ref, out_ref, x, own_c, edge_c, ring_ref, side_ref, sums_ref,
):
    place = Place(place_ref, told_ref)
    row = add_coarse(place, told_ref, coarse_ref, basis_ref, low_ref, high_ref, left_ref, right_ref, 4, sum_ref, x,
                     own_c, edge_c, ring_ref, side_ref)
    zero = jnp.zeros((8, COLS), jnp.float32)

    def images(z, carry):
        weight, curve = carry
        for i in range(ROWS // 8):
            s = slice(i * 8, i * 8 + 8)
            now, image = image_at(x, absorption_ref, z, i)
            direction_ref[z, s] = now
            image_ref[z, s] = image
            if i >= 2:
                ahead_ref[z, (i - 2) * 8 : (i - 1) * 8] = image
            else:
                behind_ref[z, s] = image
            weight = weight + source_ref[z, s] * sum_ref[z, 8 + i * 8 : 16 + i * 8, 0:COLS]
            curve = curve + now * image
        return weight, curve

    weight, curve = lax.fori_loop(0, LEVELS, images, (zero, zero))
    half = VECTORS // 2
    for part in range(2):

        def level(z, sums):
            image = image_ref[z]
            return tuple(
                sums[k] + fold_rows(basis_ref[part * half + k, z].astype(jnp.float32) * image) for k in range(half)
            )

        sums = lax.fori_loop(0, LEVELS, level, (zero,) * half)
        for k in range(half):
            sums_ref[part * half + k : part * half + k + 1] = jnp.sum(sums[k], axis=0, keepdims=True)
    lane = iota((1, COLS), 1)
    row = jnp.where(lane < VECTORS, row, 0.0)
    mine = told_ref[pl.ds(place.index(0, 0), 1), :]
    told = roll(row, VECTORS)
    told = told + jnp.where(lane == 64, total_of(weight) + total_of(row * mine), 0.0)
    told = told + jnp.where(lane == 65, total_of(curve), 0.0)
    out_ref[...] = row_of_sums(sums_ref[...]) + told


def second_coarse_kernel(
    place_ref, told_ref, coarse_ref, basis_ref, low_ref, high_ref, left_ref, right_ref, sum_ref, source_ref, absorption_ref,
    again_ref, first_sum_ref, direction_ref, first_ref,
    residual_ref, precond_ref, image_ref, out_ref, x, own_c, edge_c, ring_ref, side_ref,
):
    place = Place(place_ref, told_ref)
    row = add_coarse(place, told_ref, coarse_ref, basis_ref, low_ref, high_ref, left_ref, right_ref, 4, sum_ref, x,
                     own_c, edge_c, ring_ref, side_ref)
    weight0, curve0 = scalars(again_ref)
    step = weight0 / curve0
    zero = jnp.zeros((8, COLS), jnp.float32)

    def images(z, sums):
        weight, own, cross = sums
        for i in range(ROWS // 8):
            s = slice(i * 8, i * 8 + 8)
            t = slice(8 + i * 8, 16 + i * 8)
            now, image = image_at(x, absorption_ref, z, i)
            direction, first = direction_ref[z, s], first_ref[z, s]
            residual = source_ref[z, s] - step * first
            precond = direction - step * now
            image = first - step * image
            residual_ref[z, s] = residual
            precond_ref[z, s] = precond
            image_ref[z, s] = image
            weight = weight + residual * (first_sum_ref[z, t, 0:COLS] - step * sum_ref[z, t, 0:COLS])
            own = own + precond * image
            cross = cross + (precond * first + direction * image)
        return weight, own, cross

    weight, own, cross = lax.fori_loop(0, LEVELS, images, (zero, zero, zero))
    mine = pl.ds(place.index(0, 0), 1)
    lane = iota((1, COLS), 1)
    again = again_ref[mine, :]
    projected = told_ref[mine, :] - step * again
    coarse = roll(again, -VECTORS) - step * row
    both = jnp.where(lane < VECTORS, projected * coarse, 0.0)
    told = jnp.where(lane == 0, total_of(weight) + total_of(both), 0.0)
    told = told + jnp.where(lane == 1, total_of(own), 0.0) + jnp.where(lane == 2, total_of(cross), 0.0)
    out_ref[...] = jnp.broadcast_to(told, (COLS, COLS))


def last_kernel(again_ref, last_ref, direction_ref, first_ref, residual_ref, precond_ref, image_ref, x_ref, r_ref):
    weight0, curve0 = scalars(again_ref)
    step0 = weight0 / curve0
    totals = jnp.sum(last_ref[...], axis=0, keepdims=True)
    weight1, own, cross = totals[:, 0:1], totals[:, 1:2], totals[:, 2:3]
    ratio = weight1 / weight0
    step1 = weight1 / (own + ratio * (cross + ratio * curve0))

    def level(z, carry):
        direction = direction_ref[z]
        x_ref[z] = step0 * direction + step1 * (precond_ref[z] + ratio * direction)
        r_ref[z] = residual_ref[z] - step1 * (image_ref[z] + ratio * first_ref[z])
        return carry

    lax.fori_loop(0, LEVELS, level, 0)


def shards(source, absorption, basis, coarse_inverse, margin_width, coarse_slot):
    block = jax.ShapeDtypeStruct((LEVELS, ROWS, COLS), jnp.float32)
    slab = jax.ShapeDtypeStruct((LEVELS, EDGE, COLS), jnp.float32)
    message = jax.ShapeDtypeStruct((COLS, COLS), jnp.float32)
    params = pltpu.CompilerParams(vmem_limit_bytes=VMEM_LIMIT)
    smem = pl.BlockSpec(memory_space=pltpu.SMEM)
    vmem = pl.BlockSpec(memory_space=pltpu.VMEM)

    def scratch(*shape):
        return pltpu.VMEM(shape, jnp.float32)

    coarse_scratch = [
        scratch(PLANES, INNER, 2 * COLS), scratch(VECTORS, COLS), scratch(2 * VECTORS, COLS),
        scratch(2, LEVELS, COLS), scratch(2, 2 * TALL, COLS),
    ]
    place = jnp.stack(
        [lax.axis_index("gx"), lax.axis_index("gy"), lax.axis_size("gx"), lax.axis_size("gy")]
    ).astype(jnp.int32)
    table = jnp.array(list(zip(*chebyshev_table())), jnp.float32)
    told_row = jnp.concatenate(
        [
            jnp.zeros((1, VECTORS), jnp.float32),
            coarse_slot.reshape(1, -1).astype(jnp.float32),
            margin_width.astype(jnp.float32),
            jnp.zeros((1, COLS - 65), jnp.float32),
        ],
        axis=1,
    )
    rows, ahead, behind, left_edge, right_edge = first_projection(source, absorption, basis, told_row)
    low, high = exchange(ahead, behind, "gx")
    told = everyone(rows)
    rows, ahead, behind = middle(
        first_middle_kernel, 6, told, coarse_inverse, source, absorption, low, high, left_edge, right_edge
    )
    strips = exchange(ahead, behind, "gy")
    coarse = everyone(rows)
    coef = (absorption, low, high, strips)
    first_sum = smooth((0, LEVELS, 2), place, table, told, source, low, high, strips, *coef)
    edges = (low, high, *strips)
    direction, image, ahead, behind, rows = pl.pallas_call(
        first_coarse_kernel,
        in_specs=[smem] + [vmem] * 10,
        out_shape=[block, block, slab, slab, message],
        scratch_shapes=coarse_scratch + [scratch(VECTORS, COLS)],
        compiler_params=params,
        name="direction_and_image",
    )(place, told, coarse, basis, *edges, first_sum, source, absorption)
    low_w, high_w = exchange(ahead, behind, "gx")
    again = everyone(rows)
    rows, ahead, behind = middle(middle_kernel, 2, again, told, coarse_inverse, image, low_w, high_w)
    strips_w = exchange(ahead, behind, "gy")
    coarse = everyone(rows)
    second_sum = smooth((0, LEVELS, 2), place, table, told, image, low_w, high_w, strips_w, *coef)
    residual, precond, precond_image, rows = pl.pallas_call(
        second_coarse_kernel,
        in_specs=[smem] + [vmem] * 14,
        out_shape=[block, block, block, message],
        scratch_shapes=coarse_scratch,
        compiler_params=params,
        name="second_images",
    )(place, told, coarse, basis, *edges, second_sum, source, absorption, again, first_sum, direction, image)
    last = everyone(rows)
    concentration, residual = pl.pallas_call(
        last_kernel, out_shape=[block, block], compiler_params=params, name="update"
    )(again, last, direction, image, residual, precond, precond_image)
    return (concentration, residual)


def solution(mesh):
    return jax.shard_map(
        shards,
        mesh=mesh,
        in_specs=(
            P(None, "gx", "gy"),
            P(None, "gx", "gy"),
            P(None, None, "gx", "gy"),
            P(("gx", "gy"), None),
            P("gx", "gy"),
            P("gx", "gy", None),
        ),
        out_specs=(P(None, "gx", "gy"), P(None, "gx", "gy")),
        check_vma=False,
    )
```

time: 199 us -> 305 us (1.53)
  Pallas kernels: 78 us -> 198 us
  starting transfers between devices: 54.2 us -> 35.5 us
  blocking collectives: 45.3 us -> 58.3 us
  waiting for transfers between devices: 9.45 us -> 0.03 us
    pallas_call x5 -> x7, Pallas kernels: 75.1 us -> 195 us  [the longest x2 171 us: smooth(): pl.pallas_call(functools.partial(smooth_kernel, starts), in_specs=[smem]...]
    all_to_all x3, blocking collectives: 45.3 us -> 58.3 us  [everyone(): return lax.all_to_all(rows, AXES, 0, 0, tiled=True)]
    all_to_all x2, waiting for transfers between devices: 9.42 us -> 0.01 us  [everyone(): return lax.all_to_all(rows, AXES, 0, 0, tiled=True)]
    all_to_all x2, starting transfers between devices: 23.5 us -> 15.4 us  [everyone(): return lax.all_to_all(rows, AXES, 0, 0, tiled=True)]
    ppermute x6 -> x4, starting transfers between devices: 21.1 us -> 13.7 us  [exchange(): lax.ppermute(forward_value, axis, forward)]
    unnamed x16 -> x28, local copies, waits for them, and re-layouts: 5.35 us -> 9.62 us
    ppermute x6 -> x4, starting transfers between devices: 9.63 us -> 6.41 us  [exchange(): lax.ppermute(backward_value, axis, backward)]
    slice x4 -> x0, local copies, waits for them, and re-layouts: 3.08 us -> none  [the longest x1 1.08 us: shards(): absorption[:, :EDGE]]
  transfers between devices with their start and end apart: 14 -> 10, of which waited for: 1 -> 0; matrix products, arithmetic and copies ran while one was open for 1% -> 0% of each run, Pallas kernels for 5% -> 56%
where the time goes in v2:
time: 305 us; the launch traced here: 304 us
  Pallas kernels  198 us (65%)
  blocking collectives  58.3 us (19%)
  starting transfers between devices  35.5 us (12%)
  local copies, waits for them, and re-layouts  9.62 us (3%)
    pallas_call x2, Pallas kernels, smooth(): pl.pallas_call(functools.partial(smooth_kernel, starts), in_specs=[smem]...  171 us
    all_to_all x3, blocking collectives, everyone(): return lax.all_to_all(rows, AXES, 0, 0, tiled=True)  58.3 us
    all_to_all x2, starting transfers between devices, everyone(): return lax.all_to_all(rows, AXES, 0, 0, tiled=True)  15.4 us
    ppermute x4, starting transfers between devices, exchange(): lax.ppermute(forward_value, axis, forward)  13.7 us
    unnamed x28, local copies, waits for them, and re-layouts  9.62 us
    pallas_call x1, Pallas kernels, first_projection(): pl.pallas_call(first_kernel, grid=(VECTORS // group,), in_specs=[block_sp...  8.53 us
    ppermute x4, starting transfers between devices, exchange(): lax.ppermute(backward_value, axis, backward)  6.41 us
  transfers between devices with their start and end apart: 10, of which 0 were waited for; matrix products, arithmetic and copies ran while one was open for 0% of the time, Pallas kernels for 56%

profile of v2, /device:TPU:1, one launch (start us, length us, event | category | flops | bytes accessed | tf_op | source)
XLA Modules:
  0.0 304.4 jit_solution(489824116792791267)
XLA Ops:
  0.6 0.0 copy-start.13
  0.6 0.0 copy-start.2
  0.7 0.0 copy-start.3
  0.7 0.0 copy-start.6
  1.4 0.7 convert_bitcast_fusion
  2.1 0.7 bitcast_maximum_fusion.told_ref
  2.7 8.5 %first_projection.1 = (f32[128,128]{1,0:T(8,128)}, f32[64,16,128]{2,1,0:T(8,128)}, f32[64,16,128]{2,1,0:T(8,128)}, f32[4,32,128]{2,1,0:T(8,128)}, f32[4,32,128]{2,1,0:T(8,128)}) custom-call(f32[16,32,128]{2,1,0:T(8,128)} %source_ref.5, f32[16,32,128]{2,1,0:T(8,128)} %absorption_ref.9, bf16[32,16,32,128]{3,2,1,0:T(8,128)(2,1)} %basis_ref.5, ...), custom_call_target="tpu_custom_call" | custom-call | tf_op jit(solution)/shard_map/first_projection/pallas_call | solution.py:129
  11.3 4.6 %collective-permute-start = (f32[64,16,128]{2,1,0:T(8,128)}, f32[64,16,128]{2,1,0:T(8,128)S(1)}, u32[]{:S(2)}, u32[]{:S(2)}) collective-permute-start(f32[64,16,128]{2,1,0:T(8,128)} %get-tuple-element.23), channel_id=1, source_target_pairs={{0,16},{16,32},{32,48},{48,64},{64,80},{80,96},{96,112},{1,17},{17... | collective-permute-start | bytes 1572872 | tf_op jit(solution)/shard_map/ppermute | solution.py:52
  15.8 1.9 collective-permute-start.1
  17.8 20.0 %all_to_all.55 = f32[128,1,128]{2,1,0:T(1,128)S(1)} all-to-all(f32[128,1,128]{2,1,0:T(1,128)} %bitcast.46), channel_id=1, replica_groups=mesh['gx'=8,'gy'=16] {'gx','gy'}, dimensions={0} | all-to-all | bytes 131072 | tf_op jit(solution)/shard_map/all_to_all | solution.py:56
  37.8 0.0 collective-permute-done.low_ref.low_c
  37.8 0.0 collective-permute-done.1.high_ref.high_c
  37.8 0.0 copy-start.10
  37.8 0.8 copy-done.10
  38.7 0.8 copy-done.11
  39.5 2.5 coarse_rows.2
  42.0 2.5 collective-permute-start.2
  44.5 1.3 collective-permute-start.3
  45.8 7.8 %all-to-all-start.1 = ((f32[128,1,128]{2,1,0:T(1,128)}), f32[128,1,128]{2,1,0:T(1,128)S(1)}, u32[]{:S(2)}, u32[]{:S(2)}) async-start(f32[128,1,128]{2,1,0:T(1,128)} %bitcast.7), calls=%async_computation.1 | async-start | bytes 131072 | tf_op jit(solution)/shard_map/all_to_all | solution.py:56
  53.6 0.1 pad_add_fusion.place_ref
  53.7 0.0 collective-permute-done.2.left_ref.left_c
  53.7 0.0 collective-permute-done.3.right_ref.right_c
  53.7 85.1 %smoother.2.sum_ref.first_sum_ref = f32[16,48,256]{2,1,0:T(8,128)S(1)} custom-call(s32[4]{0:T(128)S(1)} %pad_add_fusion.place_ref, f32[2,8]{1,0:T(2,128)S(1)} %copy-done.13, f32[128,128]{1,0:T(8,128)S(1)} %bitcast.33, f32[16,32,128]{2,1,0:T(8,128)S(1)} %copy-done.3, f32[64,16,128]{2,1,0:T(8,128)S(1)} %collective-permute-done.low_ref.low_c, ...), custom_call_target="tpu_custom_call" | custom-call | flops 60000000 | bytes 4000000 | tf_op jit(solution)/shard_map/smoother/pallas_call | solution.py:449
  138.8 0.0 all-to-all-done.1
  138.8 0.0 copy-start
  138.8 2.2 copy-done
  141.0 6.0 %direction_and_image.1 = (f32[16,32,128]{2,1,0:T(8,128)S(1)}, f32[16,32,128]{2,1,0:T(8,128)S(1)}, f32[16,16,128]{2,1,0:T(8,128)S(1)}, f32[16,16,128]{2,1,0:T(8,128)S(1)}, f32[128,128]{1,0:T(8,128)S(1)}) custom-call(s32[4]{0:T(128)S(1)} %pad_add_fusion.place_ref, f32[128,128]{1,0:T(8,128)S(1)} %bitcast.34, f32[128,128]{1,0:T(8,128)S(1)} %bitcast.41, ...), custom_call_target="tpu_custom_call" | custom-call | tf_op jit(solution)/shard_map/direction_and_image/pallas_call | solution.py:704
  147.0 3.5 %collective-permute-start.4 = (f32[16,16,128]{2,1,0:T(8,128)S(1)}, f32[16,16,128]{2,1,0:T(8,128)S(1)}, u32[]{:S(2)}, u32[]{:S(2)}) collective-permute-start(f32[16,16,128]{2,1,0:T(8,128)S(1)} %get-tuple-element.32), channel_id=1, source_target_pairs={{0,16},{16,32},{32,48},{48,64},{64,80},{80,96},{96,112},{1,17},{17... | collective-permute-start | bytes 393224 | tf_op jit(solution)/shard_map/ppermute | solution.py:52
  150.6 1.9 collective-permute-start.5
  152.5 19.2 %all_to_all.56 = f32[128,1,128]{2,1,0:T(1,128)S(1)} all-to-all(f32[128,1,128]{2,1,0:T(1,128)S(1)} %bitcast.44), channel_id=1, replica_groups=mesh['gx'=8,'gy'=16] {'gx','gy'}, dimensions={0} | all-to-all | bytes 131072 | tf_op jit(solution)/shard_map/all_to_all | solution.py:56
  171.7 0.0 collective-permute-done.4.low_ref
  171.7 0.0 collective-permute-done.5.high_ref
  171.7 2.0 coarse_rows.3
  173.7 0.6 copy-done.12
  174.3 3.1 %collective-permute-start.6 = (f32[2,64,128]{2,1,0:T(8,128)}, f32[2,64,128]{2,1,0:T(8,128)}, u32[]{:S(2)}, u32[]{:S(2)}) collective-permute-start(f32[2,64,128]{2,1,0:T(8,128)} %get-tuple-element.35), channel_id=1, source_target_pairs={{0,1},{1,2},{2,3},{3,4},{4,5},{5,6},{6,7},{7,8},{8,9},{9,10},{10,1... | collective-permute-start | bytes 196616 | tf_op jit(solution)/shard_map/ppermute | solution.py:52
  177.4 1.3 collective-permute-start.7
  178.6 7.6 %all-to-all-start.3 = ((f32[128,1,128]{2,1,0:T(1,128)}), f32[128,1,128]{2,1,0:T(1,128)}, u32[]{:S(2)}, u32[]{:S(2)}) async-start(f32[128,1,128]{2,1,0:T(1,128)} %bitcast.43), calls=%async_computation.3 | async-start | bytes 131072 | tf_op jit(solution)/shard_map/all_to_all | solution.py:56
  186.3 0.0 collective-permute-done.6.left_ref
  186.3 0.0 collective-permute-done.7.right_ref
  186.3 0.0 copy-start.9
  186.3 0.9 copy-done.9
  187.2 85.4 %smoother.3.sum_ref = f32[16,48,256]{2,1,0:T(8,128)S(1)} custom-call(s32[4]{0:T(128)S(1)} %pad_add_fusion.place_ref, f32[2,8]{1,0:T(2,128)S(1)} %copy-done.13, f32[128,128]{1,0:T(8,128)S(1)} %bitcast.36, f32[16,32,128]{2,1,0:T(8,128)S(1)} %get-tuple-element.31.block_ref.first_ref, f32[16,16,128]{2,1,0:T(8,128)S(1)} %collective-permute-done.4.low_ref, ...), custom_call_target="tpu_custom_call" | custom-call | flops 60000000 | bytes 4000000 | tf_op jit(solution)/shard_map/smoother/pallas_call | solution.py:449
  272.7 0.9 copy-done.4
  273.6 2.2 copy-done.1
  275.8 1.1 copy-done.5
  276.9 5.5 %second_images.1 = (f32[16,32,128]{2,1,0:T(8,128)S(1)}, f32[16,32,128]{2,1,0:T(8,128)S(1)}, f32[16,32,128]{2,1,0:T(8,128)S(1)}, f32[128,128]{1,0:T(8,128)S(1)}) custom-call(s32[4]{0:T(128)S(1)} %pad_add_fusion.place_ref, f32[128,128]{1,0:T(8,128)S(1)} %bitcast.37, f32[128,128]{1,0:T(8,128)} %bitcast.14.coarse_ref, bf16[32,16,32,128]{3,2,1,0:T(8,128)(2,1)S(1)} %copy-done.1, ...), custom_call_target="tpu_custom_call" | custom-call | tf_op jit(solution)/shard_map/second_images/pallas_call | solution.py:718
  282.4 19.1 %all_to_all.57 = f32[128,1,128]{2,1,0:T(1,128)S(1)} all-to-all(f32[128,1,128]{2,1,0:T(1,128)S(1)} %bitcast.45), channel_id=1, replica_groups=mesh['gx'=8,'gy'=16] {'gx','gy'}, dimensions={0} | all-to-all | bytes 131072 | tf_op jit(solution)/shard_map/all_to_all | solution.py:56
  301.5 2.9 update.1
  (16 shorter events, 0.0 us)
Async XLA Ops:
  0.6 53.0 %copy-start.13 = (f32[2,8]{1,0:T(2,128)S(1)}, f32[2,8]{1,0:T(2,128)}, u32[]{:S(2)}) copy-start(f32[2,8]{1,0:T(2,128)} %constant.18.clone.table_ref) | copy-start | bytes 196
  0.6 37.2 %copy-start.2 = (f32[16,32,128]{2,1,0:T(8,128)S(1)}, f32[16,32,128]{2,1,0:T(8,128)}, u32[]{:S(2)}) copy-start(f32[16,32,128]{2,1,0:T(8,128)} %absorption_ref.9) | copy-start | bytes 786436
  0.7 37.1 %copy-start.3 = (f32[16,32,128]{2,1,0:T(8,128)S(1)}, f32[16,32,128]{2,1,0:T(8,128)}, u32[]{:S(2)}) copy-start(f32[16,32,128]{2,1,0:T(8,128)} %source_ref.5) | copy-start | bytes 786436
  0.7 37.1 %copy-start.6 = (f32[32,4096]{1,0:T(8,128)S(1)}, f32[32,4096]{1,0:T(8,128)}, u32[]{:S(2)}) copy-start(f32[32,4096]{1,0:T(8,128)} %inverse_ref.3) | copy-start | bytes 1572868
  11.3 26.5 %collective-permute-start = (f32[64,16,128]{2,1,0:T(8,128)}, f32[64,16,128]{2,1,0:T(8,128)S(1)}, u32[]{:S(2)}, u32[]{:S(2)}) collective-permute-start(f32[64,16,128]{2,1,0:T(8,128)} %get-tuple-element.23), channel_id=1, source_target_pairs={{0,16},{16,32},{32,48},{48,64},{64,80},{80,96},{96,112},{1,17},{17... | collective-permute-start | bytes 1572872 | tf_op jit(solution)/shard_map/ppermute | solution.py:52
  15.8 21.9 %collective-permute-start.1 = (f32[64,16,128]{2,1,0:T(8,128)}, f32[64,16,128]{2,1,0:T(8,128)S(1)}, u32[]{:S(2)}, u32[]{:S(2)}) collective-permute-start(f32[64,16,128]{2,1,0:T(8,128)} %get-tuple-element.24), channel_id=1, source_target_pairs={{16,0},{32,16},{48,32},{64,48},{80,64},{96,80},{112,96},{17,1},{33... | collective-permute-start | bytes 1572872 | tf_op jit(solution)/shard_map/ppermute | solution.py:52
  37.8 0.8 copy-start.10
  38.7 0.8 copy-start.11
  42.0 11.6 %collective-permute-start.2 = (f32[6,64,128]{2,1,0:T(8,128)S(1)}, f32[6,64,128]{2,1,0:T(8,128)S(1)}, u32[]{:S(2)}, u32[]{:S(2)}) collective-permute-start(f32[6,64,128]{2,1,0:T(8,128)S(1)} %get-tuple-element.28), channel_id=1, source_target_pairs={{0,1},{1,2},{2,3},{3,4},{4,5},{5,6},{6,7},{7,8},{8,9},{9,10},{10,1... | collective-permute-start | bytes 589832 | tf_op jit(solution)/shard_map/ppermute | solution.py:52
  44.5 9.2 %collective-permute-start.3 = (f32[6,64,128]{2,1,0:T(8,128)S(1)}, f32[6,64,128]{2,1,0:T(8,128)S(1)}, u32[]{:S(2)}, u32[]{:S(2)}) collective-permute-start(f32[6,64,128]{2,1,0:T(8,128)S(1)} %get-tuple-element.29), channel_id=1, source_target_pairs={{1,0},{2,1},{3,2},{4,3},{5,4},{6,5},{7,6},{8,7},{9,8},{10,9},{11,1... | collective-permute-start | bytes 589832 | tf_op jit(solution)/shard_map/ppermute | solution.py:52
  45.8 93.0 %all-to-all-start.1 = ((f32[128,1,128]{2,1,0:T(1,128)}), f32[128,1,128]{2,1,0:T(1,128)S(1)}, u32[]{:S(2)}, u32[]{:S(2)}) async-start(f32[128,1,128]{2,1,0:T(1,128)} %bitcast.7), calls=%async_computation.1 | async-start | bytes 131072 | tf_op jit(solution)/shard_map/all_to_all | solution.py:56
  138.8 2.2 copy-start
  141.0 30.7 %copy-start.7 = (f32[32,4096]{1,0:T(8,128)S(1)}, f32[32,4096]{1,0:T(8,128)}, u32[]{:S(2)}) copy-start(f32[32,4096]{1,0:T(8,128)} %inverse_ref.3) | copy-start | bytes 1572868
  147.0 24.7 %collective-permute-start.4 = (f32[16,16,128]{2,1,0:T(8,128)S(1)}, f32[16,16,128]{2,1,0:T(8,128)S(1)}, u32[]{:S(2)}, u32[]{:S(2)}) collective-permute-start(f32[16,16,128]{2,1,0:T(8,128)S(1)} %get-tuple-element.32), channel_id=1, source_target_pairs={{0,16},{16,32},{32,48},{48,64},{64,80},{80,96},{96,112},{1,17},{17... | collective-permute-start | bytes 393224 | tf_op jit(solution)/shard_map/ppermute | solution.py:52
  150.6 21.1 %collective-permute-start.5 = (f32[16,16,128]{2,1,0:T(8,128)S(1)}, f32[16,16,128]{2,1,0:T(8,128)S(1)}, u32[]{:S(2)}, u32[]{:S(2)}) collective-permute-start(f32[16,16,128]{2,1,0:T(8,128)S(1)} %get-tuple-element.33), channel_id=1, source_target_pairs={{16,0},{32,16},{48,32},{64,48},{80,64},{96,80},{112,96},{17,1},{33... | collective-permute-start | bytes 393224 | tf_op jit(solution)/shard_map/ppermute | solution.py:52
  171.7 2.0 copy-start.8
  173.7 0.6 copy-start.12
  174.3 12.0 %collective-permute-start.6 = (f32[2,64,128]{2,1,0:T(8,128)}, f32[2,64,128]{2,1,0:T(8,128)}, u32[]{:S(2)}, u32[]{:S(2)}) collective-permute-start(f32[2,64,128]{2,1,0:T(8,128)} %get-tuple-element.35), channel_id=1, source_target_pairs={{0,1},{1,2},{2,3},{3,4},{4,5},{5,6},{6,7},{7,8},{8,9},{9,10},{10,1... | collective-permute-start | bytes 196616 | tf_op jit(solution)/shard_map/ppermute | solution.py:52
  177.4 8.9 %collective-permute-start.7 = (f32[2,64,128]{2,1,0:T(8,128)}, f32[2,64,128]{2,1,0:T(8,128)}, u32[]{:S(2)}, u32[]{:S(2)}) collective-permute-start(f32[2,64,128]{2,1,0:T(8,128)} %get-tuple-element.36), channel_id=1, source_target_pairs={{1,0},{2,1},{3,2},{4,3},{5,4},{6,5},{7,6},{8,7},{9,8},{10,9},{11,1... | collective-permute-start | bytes 196616 | tf_op jit(solution)/shard_map/ppermute | solution.py:52
  178.6 94.9 %all-to-all-start.3 = ((f32[128,1,128]{2,1,0:T(1,128)}), f32[128,1,128]{2,1,0:T(1,128)}, u32[]{:S(2)}, u32[]{:S(2)}) async-start(f32[128,1,128]{2,1,0:T(1,128)} %bitcast.43), calls=%async_computation.3 | async-start | bytes 131072 | tf_op jit(solution)/shard_map/all_to_all | solution.py:56
  186.3 0.9 copy-start.9
  272.7 0.9 copy-start.4
  273.6 2.2 copy-start.1
  275.8 1.1 copy-start.5

commit v3 on v2

--- a/solution.py
+++ b/solution.py
@@ -22,7 +22,7 @@
 vertical = 2.0
 theta = 0.5 * (highest_rate + lowest_rate)
 delta = 0.5 * (highest_rate - lowest_rate)
-VMEM_LIMIT = 24 * 1024 * 1024
+VMEM_LIMIT = 30 * 1024 * 1024
 FIRST_LIMIT = 58 * 1024 * 1024
 
 
@@ -309,6 +309,7 @@
     return center, margin, packed
 
 
+UNROLL = 4
 PLANES = LEVELS + 2
 BESIDE_TILES = (1, 2, 5, 6)
 
@@ -316,7 +317,8 @@
 def smooth_kernel(
     starts, place_ref, table_ref, told_ref, block_ref, low_ref, high_ref, left_ref, right_ref,
     absorption_ref, low_c, high_c, left_c, right_c, out_ref,
-    own_m, beside_m, strip_m, own, beside, strip, own_d, beside_d, strip_d, own_r, beside_r, strip_r, diag, strip_diag,
+    own_m, beside_m, strip_m, own, beside, strip, own_y, beside_y, strip_y, own_d, beside_d, strip_d,
+    own_e, beside_e, strip_e, own_r, beside_r, strip_r, diag, strip_diag,
 ):
     field_start, coef_start, coef_at = starts
     masks(Place(place_ref, told_ref), own_m, beside_m, strip_m)
@@ -326,16 +328,17 @@
     lanes = [slice(0, COLS), slice(COLS, 2 * COLS)]
 
     def clear(n, carry):
-        at = (n & 1) * (PLANES - 1) + (n >> 1) * PLANES
+        at = n * (PLANES - 1)
         for i in range(8):
             s = slice(i * 8, i * 8 + 8)
             for t in range(2):
-                own[at, s, lanes[t]] = zero
-                beside[at, s, lanes[t]] = zero
+                for x in (own, own_y, beside, beside_y):
+                    x[at, s, lanes[t]] = zero
             strip[at, s] = zero
+            strip_y[at, s] = zero
         return carry
 
-    lax.fori_loop(0, 4, clear, 0)
+    lax.fori_loop(0, 2, clear, 0)
 
     def begin(z, carry):
         at = z + 1
@@ -349,14 +352,14 @@
                     own_r[z, s, lanes[t]] = value
                     own_d[z, s, lanes[t]] = value * (1.0 / theta)
                 else:
-                    own[at + PLANES, s, lanes[t]] = zero
+                    own_y[at, s, lanes[t]] = zero
                 own[at, s, lanes[t]] = value * (1.0 / theta)
                 value = tiles[t] * beside_m[t, s]
                 if i in BESIDE_TILES:
                     beside_r[z, s, lanes[t]] = value
                     beside_d[z, s, lanes[t]] = value * (1.0 / theta)
                 else:
-                    beside[at + PLANES, s, lanes[t]] = zero
+                    beside_y[at, s, lanes[t]] = zero
                 beside[at, s, lanes[t]] = value * (1.0 / theta)
             value = tiles[2] * strip_m[s]
             strip[at, s] = value * (1.0 / theta)
@@ -368,51 +371,59 @@
                 diag[z, s, lanes[1]] = tiles[1] + base
                 strip_diag[z, s] = tiles[2] + base
             else:
-                strip[at + PLANES, s] = zero
+                strip_y[at, s] = zero
         return carry
 
     lax.fori_loop(0, LEVELS, begin, 0)
     at_first, at_last = lane == 0, lane == COLS - 1
 
-    def sweep(n, carry):
+    def step(here, x, y, d, e, r, a, mask, width, i, keep, scale):
+        s = slice(i * 8, i * 8 + 8)
+        up, down = slice(i * 8 - 1, i * 8 + 7), slice(i * 8 + 1, i * 8 + 9)
+        z = here - 1
+        now = [x[here, s, lanes[t]] for t in range(width)]
+        back = [roll(v, 1) for v in now]
+        fore = [roll(v, -1) for v in now]
+        if width == 2:
+            back = [jnp.where(at_first, back[1], back[0]), jnp.where(at_first, back[0], back[1])]
+            fore = [jnp.where(at_last, fore[1], fore[0]), jnp.where(at_last, fore[0], fore[1])]
+        for t in range(width):
+            high = x[here - 1, s, lanes[t]] + x[here + 1, s, lanes[t]]
+            around = (x[here, up, lanes[t]] + x[here, down, lanes[t]]) + (back[t] + fore[t])
+            around = around + (high + high)
+            defect = r[z, s, lanes[t]] - a[z, s, lanes[t]] * now[t] + around
+            move = keep * d[z, s, lanes[t]] + scale * defect
+            if mask[t] is not None:
+                move = move * mask[t]
+            e[z, s, lanes[t]] = move
+            y[here, s, lanes[t]] = now[t] + move
+
+    first = ((own, own_y, own_d, own_e), (beside, beside_y, beside_d, beside_e), (strip, strip_y, strip_d, strip_e))
+    second = tuple((y, x, e, d) for x, y, d, e in first)
+
+    def sweep(n, arrays):
         keep, scale = table_ref[0, n], table_ref[1, n]
-        source = (n & 1) * PLANES + 1
-        target = (PLANES + 2) - source
-
-        def step(z, x, d, r, a, mask, width, i):
-            s = slice(i * 8, i * 8 + 8)
-            up, down = slice(i * 8 - 1, i * 8 + 7), slice(i * 8 + 1, i * 8 + 9)
-            here = source + z
-            now = [x[here, s, lanes[t]] for t in range(width)]
-            back = [roll(v, 1) for v in now]
-            fore = [roll(v, -1) for v in now]
-            if width == 2:
-                back = [jnp.where(at_first, back[1], back[0]), jnp.where(at_first, back[0], back[1])]
-                fore = [jnp.where(at_last, fore[1], fore[0]), jnp.where(at_last, fore[0], fore[1])]
-            for t in range(width):
-                high = x[here - 1, s, lanes[t]] + x[here + 1, s, lanes[t]]
-                around = (x[here, up, lanes[t]] + x[here, down, lanes[t]]) + (back[t] + fore[t])
-                around = around + (high + high)
-                defect = r[z, s, lanes[t]] - a[z, s, lanes[t]] * now[t] + around
-                move = keep * d[z, s, lanes[t]] + scale * defect
-                if mask[t] is not None:
-                    move = move * mask[t]
-                d[z, s, lanes[t]] = move
-                x[target + z, s, lanes[t]] = now[t] + move
+        own, beside, strip = arrays
 
         def level(z, carry):
+            here = z + 1
             for i in range(1, 7):
                 s = slice(i * 8, i * 8 + 8)
-                first = None if 2 <= i < 6 else own_m[0, s]
-                step(z, own, own_d, own_r, diag, [first, own_m[1, s]], 2, i)
+                free = None if 2 <= i < 6 else own_m[0, s]
+                step(here, *own, own_r, diag, [free, own_m[1, s]], 2, i, keep, scale)
                 if i in BESIDE_TILES:
-                    step(z, beside, beside_d, beside_r, diag, [beside_m[0, s], beside_m[1, s]], 2, i)
-                step(z, strip, strip_d, strip_r, strip_diag, [strip_m[s]], 1, i)
+                    step(here, *beside, beside_r, diag, [beside_m[0, s], beside_m[1, s]], 2, i, keep, scale)
+                step(here, *strip, strip_r, strip_diag, [strip_m[s]], 1, i, keep, scale)
             return carry
 
-        return lax.fori_loop(0, LEVELS, level, carry)
-
-    lax.fori_loop(0, KCHEB - 1, sweep, 0)
+        lax.fori_loop(0, LEVELS, level, 0, unroll=UNROLL)
+
+    def pair(n, carry):
+        sweep(2 * n, first)
+        sweep(2 * n + 1, second)
+        return carry
+
+    lax.fori_loop(0, (KCHEB - 1) // 2, pair, 0)
     near_first, near_last = lane < EDGE, lane >= COLS - EDGE
 
     def finish(z, carry):
@@ -452,7 +463,9 @@
         out_shape=jax.ShapeDtypeStruct((LEVELS, INNER, 2 * COLS), jnp.float32),
         scratch_shapes=[
             scratch(2, *thin), scratch(2, *thin), scratch(*thin),
-            scratch(2 * PLANES, *wide), scratch(2 * PLANES, *wide), scratch(2 * PLANES, *thin),
+            scratch(PLANES, *wide), scratch(PLANES, *wide), scratch(PLANES, *thin),
+            scratch(PLANES, *wide), scratch(PLANES, *wide), scratch(PLANES, *thin),
+            scratch(LEVELS, *wide), scratch(LEVELS, *wide), scratch(LEVELS, *thin),
             scratch(LEVELS, *wide), scratch(LEVELS, *wide), scratch(LEVELS, *thin),
             scratch(LEVELS, *wide), scratch(LEVELS, *wide), scratch(LEVELS, *thin),
             scratch(LEVELS, *wide), scratch(LEVELS, *thin),

time: 305 us -> 172 us (0.56)
  Pallas kernels: 198 us -> 64.9 us
    pallas_call x2, Pallas kernels: 171 us -> 37.4 us  [smooth(): pl.pallas_call(functools.partial(smooth_kernel, starts), in_specs=[smem]...]
  transfers between devices with their start and end apart: 10 -> 10, of which waited for: 0 -> 0; matrix products, arithmetic and copies ran while one was open for 0% -> 0% of each run, Pallas kernels for 56% -> 22%
where the time goes in v3:
time: 172 us; the launch traced here: 171 us
  Pallas kernels  64.9 us (38%)
  blocking collectives  58.3 us (34%)
  starting transfers between devices  35.5 us (21%)
  local copies, waits for them, and re-layouts  9.62 us (6%)
    all_to_all x3, blocking collectives, everyone(): return lax.all_to_all(rows, AXES, 0, 0, tiled=True)  58.3 us
    pallas_call x2, Pallas kernels, smooth(): pl.pallas_call(functools.partial(smooth_kernel, starts), in_specs=[smem]...  37.4 us
    all_to_all x2, starting transfers between devices, everyone(): return lax.all_to_all(rows, AXES, 0, 0, tiled=True)  15.4 us
    ppermute x4, starting transfers between devices, exchange(): lax.ppermute(forward_value, axis, forward)  13.7 us
    unnamed x28, local copies, waits for them, and re-layouts  9.62 us
    pallas_call x1, Pallas kernels, first_projection(): pl.pallas_call(first_kernel, grid=(VECTORS // group,), in_specs=[block_sp...  8.53 us
    ppermute x4, starting transfers between devices, exchange(): lax.ppermute(backward_value, axis, backward)  6.41 us
    pallas_call x1, Pallas kernels, shards(): pl.pallas_call(first_coarse_kernel, in_specs=[smem] + [vmem] * 10, out_sh...  6 us
  transfers between devices with their start and end apart: 10, of which 0 were waited for; matrix products, arithmetic and copies ran while one was open for 0% of the time, Pallas kernels for 22%

profile of v3, /device:TPU:1, one launch (start us, length us, event | category | flops | bytes accessed | tf_op | source)
XLA Modules:
  0.0 171.3 jit_solution(13918116852583131717)
XLA Ops:
  0.6 0.0 copy-start.13
  0.6 0.0 copy-start.2
  0.7 0.0 copy-start.3
  0.7 0.0 copy-start.6
  1.4 0.7 convert_bitcast_fusion
  2.1 0.7 bitcast_maximum_fusion.told_ref
  2.7 8.5 %first_projection.1 = (f32[128,128]{1,0:T(8,128)}, f32[64,16,128]{2,1,0:T(8,128)}, f32[64,16,128]{2,1,0:T(8,128)}, f32[4,32,128]{2,1,0:T(8,128)}, f32[4,32,128]{2,1,0:T(8,128)}) custom-call(f32[16,32,128]{2,1,0:T(8,128)} %source_ref.5, f32[16,32,128]{2,1,0:T(8,128)} %absorption_ref.9, bf16[32,16,32,128]{3,2,1,0:T(8,128)(2,1)} %basis_ref.5, ...), custom_call_target="tpu_custom_call" | custom-call | tf_op jit(solution)/shard_map/first_projection/pallas_call | solution.py:129
  11.3 4.6 %collective-permute-start = (f32[64,16,128]{2,1,0:T(8,128)}, f32[64,16,128]{2,1,0:T(8,128)S(1)}, u32[]{:S(2)}, u32[]{:S(2)}) collective-permute-start(f32[64,16,128]{2,1,0:T(8,128)} %get-tuple-element.23), channel_id=1, source_target_pairs={{0,16},{16,32},{32,48},{48,64},{64,80},{80,96},{96,112},{1,17},{17... | collective-permute-start | bytes 1572872 | tf_op jit(solution)/shard_map/ppermute | solution.py:52
  15.8 1.9 %collective-permute-start.1 = (f32[64,16,128]{2,1,0:T(8,128)}, f32[64,16,128]{2,1,0:T(8,128)S(1)}, u32[]{:S(2)}, u32[]{:S(2)}) collective-permute-start(f32[64,16,128]{2,1,0:T(8,128)} %get-tuple-element.24), channel_id=1, source_target_pairs={{16,0},{32,16},{48,32},{64,48},{80,64},{96,80},{112,96},{17,1},{33... | collective-permute-start | bytes 1572872 | tf_op jit(solution)/shard_map/ppermute | solution.py:52
  17.8 20.0 %all_to_all.55 = f32[128,1,128]{2,1,0:T(1,128)S(1)} all-to-all(f32[128,1,128]{2,1,0:T(1,128)} %bitcast.46), channel_id=1, replica_groups=mesh['gx'=8,'gy'=16] {'gx','gy'}, dimensions={0} | all-to-all | bytes 131072 | tf_op jit(solution)/shard_map/all_to_all | solution.py:56
  37.8 0.0 collective-permute-done.low_ref.low_c
  37.8 0.0 collective-permute-done.1.high_ref.high_c
  37.8 0.0 copy-start.10
  37.8 0.8 copy-done.10
  38.7 0.8 copy-done.11
  39.5 2.5 %coarse_rows.2 = (f32[128,128]{1,0:T(8,128)}, f32[6,64,128]{2,1,0:T(8,128)S(1)}, f32[6,64,128]{2,1,0:T(8,128)S(1)}) custom-call(f32[128,128]{1,0:T(8,128)S(1)} %bitcast.32, f32[32,4096]{1,0:T(8,128)S(1)} %copy-done.6, f32[16,32,128]{2,1,0:T(8,128)S(1)} %copy-done.3, f32[16,32,128]{2,1,0:T(8,128)S(1)} %copy-done.2, ...), custom_call_target="tpu_custom_call" | custom-call | tf_op jit(solution)/shard_map/coarse_rows/pallas_call | solution.py:215
  42.0 2.5 %collective-permute-start.2 = (f32[6,64,128]{2,1,0:T(8,128)S(1)}, f32[6,64,128]{2,1,0:T(8,128)S(1)}, u32[]{:S(2)}, u32[]{:S(2)}) collective-permute-start(f32[6,64,128]{2,1,0:T(8,128)S(1)} %get-tuple-element.28), channel_id=1, source_target_pairs={{0,1},{1,2},{2,3},{3,4},{4,5},{5,6},{6,7},{7,8},{8,9},{9,10},{10,1... | collective-permute-start | bytes 589832 | tf_op jit(solution)/shard_map/ppermute | solution.py:52
  44.5 1.3 collective-permute-start.3
  45.8 7.8 %all-to-all-start.1 = ((f32[128,1,128]{2,1,0:T(1,128)}), f32[128,1,128]{2,1,0:T(1,128)S(1)}, u32[]{:S(2)}, u32[]{:S(2)}) async-start(f32[128,1,128]{2,1,0:T(1,128)} %bitcast.7), calls=%async_computation.1 | async-start | bytes 131072 | tf_op jit(solution)/shard_map/all_to_all | solution.py:56
  53.6 0.1 pad_add_fusion.place_ref
  53.7 0.0 collective-permute-done.2.left_ref.left_c
  53.7 0.0 collective-permute-done.3.right_ref.right_c
  53.7 18.6 %smoother.2.sum_ref.first_sum_ref = f32[16,48,256]{2,1,0:T(8,128)S(1)} custom-call(s32[4]{0:T(128)S(1)} %pad_add_fusion.place_ref, f32[2,8]{1,0:T(2,128)S(1)} %copy-done.13, f32[128,128]{1,0:T(8,128)S(1)} %bitcast.33, f32[16,32,128]{2,1,0:T(8,128)S(1)} %copy-done.3, f32[64,16,128]{2,1,0:T(8,128)S(1)} %collective-permute-done.low_ref.low_c, ...), custom_call_target="tpu_custom_call" | custom-call | flops 60000000 | bytes 4000000 | tf_op jit(solution)/shard_map/smoother/pallas_call | solution.py:460
  72.2 0.0 all-to-all-done.1
  72.3 0.0 copy-start
  72.3 2.2 %copy-done = bf16[32,16,32,128]{3,2,1,0:T(8,128)(2,1)S(1)} copy-done((bf16[32,16,32,128]{3,2,1,0:T(8,128)(2,1)S(1)}, bf16[32,16,32,128]{3,2,1,0:T(8,128)(2,1)}, u32[]{:S(2)}) %copy-start) | copy-done | bytes 4194328
  74.5 6.0 %direction_and_image.1 = (f32[16,32,128]{2,1,0:T(8,128)S(1)}, f32[16,32,128]{2,1,0:T(8,128)S(1)}, f32[16,16,128]{2,1,0:T(8,128)S(1)}, f32[16,16,128]{2,1,0:T(8,128)S(1)}, f32[128,128]{1,0:T(8,128)S(1)}) custom-call(s32[4]{0:T(128)S(1)} %pad_add_fusion.place_ref, f32[128,128]{1,0:T(8,128)S(1)} %bitcast.34, f32[128,128]{1,0:T(8,128)S(1)} %bitcast.41, ...), custom_call_target="tpu_custom_call" | custom-call | tf_op jit(solution)/shard_map/direction_and_image/pallas_call | solution.py:717
  80.5 3.5 %collective-permute-start.4 = (f32[16,16,128]{2,1,0:T(8,128)S(1)}, f32[16,16,128]{2,1,0:T(8,128)S(1)}, u32[]{:S(2)}, u32[]{:S(2)}) collective-permute-start(f32[16,16,128]{2,1,0:T(8,128)S(1)} %get-tuple-element.32), channel_id=1, source_target_pairs={{0,16},{16,32},{32,48},{48,64},{64,80},{80,96},{96,112},{1,17},{17... | collective-permute-start | bytes 393224 | tf_op jit(solution)/shard_map/ppermute | solution.py:52
  84.0 1.9 %collective-permute-start.5 = (f32[16,16,128]{2,1,0:T(8,128)S(1)}, f32[16,16,128]{2,1,0:T(8,128)S(1)}, u32[]{:S(2)}, u32[]{:S(2)}) collective-permute-start(f32[16,16,128]{2,1,0:T(8,128)S(1)} %get-tuple-element.33), channel_id=1, source_target_pairs={{16,0},{32,16},{48,32},{64,48},{80,64},{96,80},{112,96},{17,1},{33... | collective-permute-start | bytes 393224 | tf_op jit(solution)/shard_map/ppermute | solution.py:52
  85.9 19.2 %all_to_all.56 = f32[128,1,128]{2,1,0:T(1,128)S(1)} all-to-all(f32[128,1,128]{2,1,0:T(1,128)S(1)} %bitcast.44), channel_id=1, replica_groups=mesh['gx'=8,'gy'=16] {'gx','gy'}, dimensions={0} | all-to-all | bytes 131072 | tf_op jit(solution)/shard_map/all_to_all | solution.py:56
  105.1 0.0 collective-permute-done.4.low_ref
  105.1 0.0 collective-permute-done.5.high_ref
  105.2 2.0 %coarse_rows.3 = (f32[128,128]{1,0:T(8,128)S(1)}, f32[2,64,128]{2,1,0:T(8,128)}, f32[2,64,128]{2,1,0:T(8,128)}) custom-call(f32[128,128]{1,0:T(8,128)S(1)} %bitcast.38, f32[128,128]{1,0:T(8,128)S(1)} %bitcast.35, f32[32,4096]{1,0:T(8,128)S(1)} %copy-done.7, f32[16,32,128]{2,1,0:T(8,128)S(1)} %get-tuple-element.31.block_ref.first_ref, ...), custom_call_target="tpu_custom_call" | custom-call | tf_op jit(solution)/shard_map/coarse_rows/pallas_call | solution.py:215
  107.1 0.6 copy-done.12
  107.7 3.1 %collective-permute-start.6 = (f32[2,64,128]{2,1,0:T(8,128)}, f32[2,64,128]{2,1,0:T(8,128)}, u32[]{:S(2)}, u32[]{:S(2)}) collective-permute-start(f32[2,64,128]{2,1,0:T(8,128)} %get-tuple-element.35), channel_id=1, source_target_pairs={{0,1},{1,2},{2,3},{3,4},{4,5},{5,6},{6,7},{7,8},{8,9},{9,10},{10,1... | collective-permute-start | bytes 196616 | tf_op jit(solution)/shard_map/ppermute | solution.py:52
  110.8 1.3 collective-permute-start.7
  112.1 7.6 %all-to-all-start.3 = ((f32[128,1,128]{2,1,0:T(1,128)}), f32[128,1,128]{2,1,0:T(1,128)}, u32[]{:S(2)}, u32[]{:S(2)}) async-start(f32[128,1,128]{2,1,0:T(1,128)} %bitcast.43), calls=%async_computation.3 | async-start | bytes 131072 | tf_op jit(solution)/shard_map/all_to_all | solution.py:56
  119.7 0.0 collective-permute-done.6.left_ref
  119.8 0.0 collective-permute-done.7.right_ref
  119.8 0.0 copy-start.9
  119.8 0.9 copy-done.9
  120.7 18.9 %smoother.3.sum_ref = f32[16,48,256]{2,1,0:T(8,128)S(1)} custom-call(s32[4]{0:T(128)S(1)} %pad_add_fusion.place_ref, f32[2,8]{1,0:T(2,128)S(1)} %copy-done.13, f32[128,128]{1,0:T(8,128)S(1)} %bitcast.36, f32[16,32,128]{2,1,0:T(8,128)S(1)} %get-tuple-element.31.block_ref.first_ref, f32[16,16,128]{2,1,0:T(8,128)S(1)} %collective-permute-done.4.low_ref, ...), custom_call_target="tpu_custom_call" | custom-call | flops 60000000 | bytes 4000000 | tf_op jit(solution)/shard_map/smoother/pallas_call | solution.py:460
  139.6 0.9 copy-done.4
  140.5 2.2 %copy-done.1 = bf16[32,16,32,128]{3,2,1,0:T(8,128)(2,1)S(1)} copy-done((bf16[32,16,32,128]{3,2,1,0:T(8,128)(2,1)S(1)}, bf16[32,16,32,128]{3,2,1,0:T(8,128)(2,1)}, u32[]{:S(2)}) %copy-start.1) | copy-done | bytes 4194328
  142.7 1.1 copy-done.5
  143.8 5.5 %second_images.1 = (f32[16,32,128]{2,1,0:T(8,128)S(1)}, f32[16,32,128]{2,1,0:T(8,128)S(1)}, f32[16,32,128]{2,1,0:T(8,128)S(1)}, f32[128,128]{1,0:T(8,128)S(1)}) custom-call(s32[4]{0:T(128)S(1)} %pad_add_fusion.place_ref, f32[128,128]{1,0:T(8,128)S(1)} %bitcast.37, f32[128,128]{1,0:T(8,128)} %bitcast.14.coarse_ref, bf16[32,16,32,128]{3,2,1,0:T(8,128)(2,1)S(1)} %copy-done.1, ...), custom_call_target="tpu_custom_call" | custom-call | tf_op jit(solution)/shard_map/second_images/pallas_call | solution.py:731
  149.3 19.1 %all_to_all.57 = f32[128,1,128]{2,1,0:T(1,128)S(1)} all-to-all(f32[128,1,128]{2,1,0:T(1,128)S(1)} %bitcast.45), channel_id=1, replica_groups=mesh['gx'=8,'gy'=16] {'gx','gy'}, dimensions={0} | all-to-all | bytes 131072 | tf_op jit(solution)/shard_map/all_to_all | solution.py:56
  168.4 2.9 %update.1 = (f32[16,32,128]{2,1,0:T(8,128)}, f32[16,32,128]{2,1,0:T(8,128)}) custom-call(f32[128,128]{1,0:T(8,128)S(1)} %bitcast.40, f32[128,128]{1,0:T(8,128)S(1)} %bitcast.42, f32[16,32,128]{2,1,0:T(8,128)S(1)} %get-tuple-element.37.direction_ref, f32[16,32,128]{2,1,0:T(8,128)S(1)} %get-tuple-element.31.block_ref.first_ref, ...), custom_call_target="tpu_custom_call" | custom-call | tf_op jit(solution)/shard_map/update/pallas_call | solution.py:740
  (16 shorter events, 0.0 us)
Async XLA Ops:
  0.6 53.0 %copy-start.13 = (f32[2,8]{1,0:T(2,128)S(1)}, f32[2,8]{1,0:T(2,128)}, u32[]{:S(2)}) copy-start(f32[2,8]{1,0:T(2,128)} %constant.18.clone.table_ref) | copy-start | bytes 196
  0.6 37.2 %copy-start.2 = (f32[16,32,128]{2,1,0:T(8,128)S(1)}, f32[16,32,128]{2,1,0:T(8,128)}, u32[]{:S(2)}) copy-start(f32[16,32,128]{2,1,0:T(8,128)} %absorption_ref.9) | copy-start | bytes 786436
  0.7 37.1 %copy-start.3 = (f32[16,32,128]{2,1,0:T(8,128)S(1)}, f32[16,32,128]{2,1,0:T(8,128)}, u32[]{:S(2)}) copy-start(f32[16,32,128]{2,1,0:T(8,128)} %source_ref.5) | copy-start | bytes 786436
  0.7 37.1 %copy-start.6 = (f32[32,4096]{1,0:T(8,128)S(1)}, f32[32,4096]{1,0:T(8,128)}, u32[]{:S(2)}) copy-start(f32[32,4096]{1,0:T(8,128)} %inverse_ref.3) | copy-start | bytes 1572868
  11.3 26.5 %collective-permute-start = (f32[64,16,128]{2,1,0:T(8,128)}, f32[64,16,128]{2,1,0:T(8,128)S(1)}, u32[]{:S(2)}, u32[]{:S(2)}) collective-permute-start(f32[64,16,128]{2,1,0:T(8,128)} %get-tuple-element.23), channel_id=1, source_target_pairs={{0,16},{16,32},{32,48},{48,64},{64,80},{80,96},{96,112},{1,17},{17... | collective-permute-start | bytes 1572872 | tf_op jit(solution)/shard_map/ppermute | solution.py:52
  15.8 21.9 %collective-permute-start.1 = (f32[64,16,128]{2,1,0:T(8,128)}, f32[64,16,128]{2,1,0:T(8,128)S(1)}, u32[]{:S(2)}, u32[]{:S(2)}) collective-permute-start(f32[64,16,128]{2,1,0:T(8,128)} %get-tuple-element.24), channel_id=1, source_target_pairs={{16,0},{32,16},{48,32},{64,48},{80,64},{96,80},{112,96},{17,1},{33... | collective-permute-start | bytes 1572872 | tf_op jit(solution)/shard_map/ppermute | solution.py:52
  37.8 0.8 copy-start.10
  38.7 0.8 copy-start.11
  42.0 11.6 %collective-permute-start.2 = (f32[6,64,128]{2,1,0:T(8,128)S(1)}, f32[6,64,128]{2,1,0:T(8,128)S(1)}, u32[]{:S(2)}, u32[]{:S(2)}) collective-permute-start(f32[6,64,128]{2,1,0:T(8,128)S(1)} %get-tuple-element.28), channel_id=1, source_target_pairs={{0,1},{1,2},{2,3},{3,4},{4,5},{5,6},{6,7},{7,8},{8,9},{9,10},{10,1... | collective-permute-start | bytes 589832 | tf_op jit(solution)/shard_map/ppermute | solution.py:52
  44.5 9.2 %collective-permute-start.3 = (f32[6,64,128]{2,1,0:T(8,128)S(1)}, f32[6,64,128]{2,1,0:T(8,128)S(1)}, u32[]{:S(2)}, u32[]{:S(2)}) collective-permute-start(f32[6,64,128]{2,1,0:T(8,128)S(1)} %get-tuple-element.29), channel_id=1, source_target_pairs={{1,0},{2,1},{3,2},{4,3},{5,4},{6,5},{7,6},{8,7},{9,8},{10,9},{11,1... | collective-permute-start | bytes 589832 | tf_op jit(solution)/shard_map/ppermute | solution.py:52
  45.8 26.4 %all-to-all-start.1 = ((f32[128,1,128]{2,1,0:T(1,128)}), f32[128,1,128]{2,1,0:T(1,128)S(1)}, u32[]{:S(2)}, u32[]{:S(2)}) async-start(f32[128,1,128]{2,1,0:T(1,128)} %bitcast.7), calls=%async_computation.1 | async-start | bytes 131072 | tf_op jit(solution)/shard_map/all_to_all | solution.py:56
  72.3 2.2 %copy-start = (bf16[32,16,32,128]{3,2,1,0:T(8,128)(2,1)S(1)}, bf16[32,16,32,128]{3,2,1,0:T(8,128)(2,1)}, u32[]{:S(2)}) copy-start(bf16[32,16,32,128]{3,2,1,0:T(8,128)(2,1)} %basis_ref.5) | copy-start | bytes 12582916
  74.5 30.7 %copy-start.7 = (f32[32,4096]{1,0:T(8,128)S(1)}, f32[32,4096]{1,0:T(8,128)}, u32[]{:S(2)}) copy-start(f32[32,4096]{1,0:T(8,128)} %inverse_ref.3) | copy-start | bytes 1572868
  80.5 24.7 %collective-permute-start.4 = (f32[16,16,128]{2,1,0:T(8,128)S(1)}, f32[16,16,128]{2,1,0:T(8,128)S(1)}, u32[]{:S(2)}, u32[]{:S(2)}) collective-permute-start(f32[16,16,128]{2,1,0:T(8,128)S(1)} %get-tuple-element.32), channel_id=1, source_target_pairs={{0,16},{16,32},{32,48},{48,64},{64,80},{80,96},{96,112},{1,17},{17... | collective-permute-start | bytes 393224 | tf_op jit(solution)/shard_map/ppermute | solution.py:52
  84.0 21.1 %collective-permute-start.5 = (f32[16,16,128]{2,1,0:T(8,128)S(1)}, f32[16,16,128]{2,1,0:T(8,128)S(1)}, u32[]{:S(2)}, u32[]{:S(2)}) collective-permute-start(f32[16,16,128]{2,1,0:T(8,128)S(1)} %get-tuple-element.33), channel_id=1, source_target_pairs={{16,0},{32,16},{48,32},{64,48},{80,64},{96,80},{112,96},{17,1},{33... | collective-permute-start | bytes 393224 | tf_op jit(solution)/shard_map/ppermute | solution.py:52
  105.1 2.0 %copy-start.8 = (f32[16,16,128]{2,1,0:T(8,128)}, f32[16,16,128]{2,1,0:T(8,128)S(1)}, u32[]{:S(2)}) copy-start(f32[16,16,128]{2,1,0:T(8,128)S(1)} %collective-permute-done.5.high_ref) | copy-start | bytes 393220
  107.1 0.6 copy-start.12
  107.7 12.0 %collective-permute-start.6 = (f32[2,64,128]{2,1,0:T(8,128)}, f32[2,64,128]{2,1,0:T(8,128)}, u32[]{:S(2)}, u32[]{:S(2)}) collective-permute-start(f32[2,64,128]{2,1,0:T(8,128)} %get-tuple-element.35), channel_id=1, source_target_pairs={{0,1},{1,2},{2,3},{3,4},{4,5},{5,6},{6,7},{7,8},{8,9},{9,10},{10,1... | collective-permute-start | bytes 196616 | tf_op jit(solution)/shard_map/ppermute | solution.py:52
  110.8 8.9 %collective-permute-start.7 = (f32[2,64,128]{2,1,0:T(8,128)}, f32[2,64,128]{2,1,0:T(8,128)}, u32[]{:S(2)}, u32[]{:S(2)}) collective-permute-start(f32[2,64,128]{2,1,0:T(8,128)} %get-tuple-element.36), channel_id=1, source_target_pairs={{1,0},{2,1},{3,2},{4,3},{5,4},{6,5},{7,6},{8,7},{9,8},{10,9},{11,1... | collective-permute-start | bytes 196616 | tf_op jit(solution)/shard_map/ppermute | solution.py:52
  112.1 28.4 %all-to-all-start.3 = ((f32[128,1,128]{2,1,0:T(1,128)}), f32[128,1,128]{2,1,0:T(1,128)}, u32[]{:S(2)}, u32[]{:S(2)}) async-start(f32[128,1,128]{2,1,0:T(1,128)} %bitcast.43), calls=%async_computation.3 | async-start | bytes 131072 | tf_op jit(solution)/shard_map/all_to_all | solution.py:56
  119.8 0.9 copy-start.9
  139.6 0.9 copy-start.4
  140.5 2.2 %copy-start.1 = (bf16[32,16,32,128]{3,2,1,0:T(8,128)(2,1)S(1)}, bf16[32,16,32,128]{3,2,1,0:T(8,128)(2,1)}, u32[]{:S(2)}) copy-start(bf16[32,16,32,128]{3,2,1,0:T(8,128)(2,1)} %basis_ref.5) | copy-start | bytes 12582916
  142.7 1.1 copy-start.5

commit v4 on v3

--- a/solution.py
+++ b/solution.py
@@ -69,16 +69,15 @@
 
 
 def first_kernel(
-    field_ref, coefficient_ref, basis_ref, told_ref, out_ref, ahead_ref, behind_ref, left_ref, right_ref, sums_ref
+    field_ref, coefficient_ref, basis_ref, slots_ref, margin_ref,
+    out_ref, ahead_ref, behind_ref, left_ref, right_ref, sums_ref, edges_ref,
 ):
     step = pl.program_id(0)
     group = basis_ref.shape[0]
-    lane = iota((ROWS, COLS), 1)
 
     @pl.when(step == 0)
     def _():
-        left_ref[...] = jnp.zeros_like(left_ref)
-        right_ref[...] = jnp.zeros_like(right_ref)
+        edges_ref[...] = jnp.zeros_like(edges_ref)
 
         def level(z, carry):
             ahead_ref[z] = field_ref[z, ROWS - EDGE :, :]
@@ -91,8 +90,6 @@
 
     def level(z, sums):
         field = field_ref[z]
-        low = left_ref[z >> 2]
-        high = right_ref[z >> 2]
         new = []
         for j in range(group):
             values = basis_ref[j, z].astype(jnp.float32)
@@ -100,25 +97,47 @@
             at = 2 * LEVELS + step * group + j
             behind_ref[at, pl.ds(z, 1), :] = values[0:1]
             ahead_ref[at, pl.ds(z, 1), :] = values[ROWS - 1 : ROWS]
-            k = step * group + j + VECTORS * (z & 3)
-            turned = pltpu.roll(values, k, 1)
-            low = jnp.where(lane == k, turned, low)
-            high = jnp.where(lane == ((k + COLS - 1) & (COLS - 1)), turned, high)
-        left_ref[z >> 2] = low
-        right_ref[z >> 2] = high
         return tuple(new)
 
     zero = jnp.zeros((8, COLS), jnp.float32)
-    sums = lax.fori_loop(0, LEVELS, level, (zero,) * group)
+    sums = lax.fori_loop(0, LEVELS, level, (zero,) * group, unroll=2)
     for j in range(group):
         sums_ref[pl.ds(step * group + j, 1), :] = jnp.sum(sums[j], axis=0, keepdims=True)
+    from_lane, to_lane = iota((COLS, COLS), 0), iota((COLS, COLS), 1)
+    picks = []
+    for j in range(group):
+        k = step * group + j
+        pick = ((from_lane == 0) & (to_lane == k)) | ((from_lane == COLS - 1) & (to_lane == VECTORS + k))
+        picks.append(jnp.where(pick, 1.0, 0.0).astype(jnp.bfloat16))
+    values = jnp.concatenate([basis_ref[j].reshape(LEVELS * ROWS, COLS) for j in range(group)], axis=1)
+    edges_ref[...] += jnp.dot(values, jnp.concatenate(picks, 0), preferred_element_type=jnp.float32)
 
     @pl.when(step == pl.num_programs(0) - 1)
     def _():
-        out_ref[...] = row_of_sums(sums_ref[...]) + told_ref[...]
-
-
-def first_projection(field, coefficient, basis, told_row):
+        told = jnp.concatenate(
+            [
+                jnp.zeros((1, VECTORS), jnp.float32),
+                slots_ref[0].astype(jnp.float32),
+                margin_ref[...].astype(jnp.float32),
+                jnp.zeros((1, COLS - 65), jnp.float32),
+            ],
+            axis=1,
+        )
+        out_ref[...] = row_of_sums(sums_ref[...]) + told
+        place = iota((ROWS, COLS), 1) >> 5
+        for n in range(LEVELS // 4):
+            left = jnp.zeros((ROWS, COLS), jnp.float32)
+            right = left
+            for q in range(4):
+                z = 4 * n + q
+                value = edges_ref[z * ROWS : (z + 1) * ROWS]
+                left = jnp.where(place == q, roll(value, VECTORS * q), left)
+                right = jnp.where(place == q, roll(value, VECTORS * (q - 1)), right)
+            left_ref[n] = left
+            right_ref[n] = right
+
+
+def first_projection(field, coefficient, basis, slots, margin):
     group = 8
     rows = 2 * LEVELS + VECTORS
     edge_rows = jax.ShapeDtypeStruct((rows, LEVELS, COLS), jnp.float32)
@@ -133,14 +152,17 @@
             block_spec,
             block_spec,
             pl.BlockSpec((group, LEVELS, ROWS, COLS), lambda i: (i, 0, 0, 0)),
-            pl.BlockSpec((1, COLS), lambda i: (0, 0)),
+            pl.BlockSpec(slots.shape, lambda i: (0, 0, 0)),
+            pl.BlockSpec(margin.shape, lambda i: (0, 0)),
         ],
         out_specs=[pl.BlockSpec((COLS, COLS), lambda i: (0, 0)), rows_spec, rows_spec, cols_spec, cols_spec],
         out_shape=[jax.ShapeDtypeStruct((COLS, COLS), jnp.float32), edge_rows, edge_rows, edge_cols, edge_cols],
-        scratch_shapes=[pltpu.VMEM((VECTORS, COLS), jnp.float32)],
+        scratch_shapes=[
+            pltpu.VMEM((VECTORS, COLS), jnp.float32), pltpu.VMEM((LEVELS * ROWS, COLS), jnp.float32)
+        ],
         compiler_params=pltpu.CompilerParams(vmem_limit_bytes=FIRST_LIMIT),
         name="first_projection",
-    )(field, coefficient, basis, told_row)
+    )(field, coefficient, basis, slots, margin)
 
 
 def coarse_rows(told_ref, slots_ref, inverse_ref, out_ref):
@@ -191,9 +213,8 @@
     lax.fori_loop(0, LEVELS // 8, levels, 0)
 
 
-def first_middle_kernel(
-    told_ref, inverse_ref, source_ref, absorption_ref, low_ref, high_ref, left_ref, right_ref,
-    out_ref, forward_ref, backward_ref,
+def first_pack_kernel(
+    source_ref, absorption_ref, low_ref, high_ref, left_ref, right_ref, forward_ref, backward_ref
 ):
     for f, block in enumerate((source_ref, absorption_ref)):
         pack_strips(((low_ref, LEVELS * f), (block, 0), (high_ref, LEVELS * f)), forward_ref, backward_ref, 2 * f)
@@ -202,19 +223,34 @@
             rows = slice(half * ROWS, (half + 1) * ROWS)
             forward_ref[4 + n, rows, :] = right_ref[2 * n + half]
             backward_ref[4 + n, rows, :] = left_ref[2 * n + half]
-    coarse_rows(told_ref, told_ref, inverse_ref, out_ref)
-
-
-def middle_kernel(told_ref, slots_ref, inverse_ref, block_ref, low_ref, high_ref, out_ref, forward_ref, backward_ref):
+
+
+def pack_kernel(block_ref, low_ref, high_ref, forward_ref, backward_ref):
     pack_strips(((low_ref, 0), (block_ref, 0), (high_ref, 0)), forward_ref, backward_ref, 0)
-    coarse_rows(told_ref, slots_ref, inverse_ref, out_ref)
-
-
-def middle(kernel, strips, *operands):
+
+
+FIELDS_SPEC = pl.BlockSpec((2 * LEVELS, EDGE, COLS), lambda i: (0, 0, 0))
+VMEM_SPEC = pl.BlockSpec(memory_space=pltpu.VMEM)
+SMEM_SPEC = pl.BlockSpec(memory_space=pltpu.SMEM)
+
+
+def pack(kernel, specs, strips, *operands):
     strips = jax.ShapeDtypeStruct((strips, TALL, COLS), jnp.float32)
     return pl.pallas_call(
         kernel,
-        out_shape=[jax.ShapeDtypeStruct((COLS, COLS), jnp.float32), strips, strips],
+        grid=(1,),
+        in_specs=specs,
+        out_shape=[strips, strips],
+        compiler_params=pltpu.CompilerParams(vmem_limit_bytes=VMEM_LIMIT),
+        cost_estimate=pl.CostEstimate(flops=2000000, bytes_accessed=2000000, transcendentals=0),
+        name="strips",
+    )(*operands)
+
+
+def solve_rows(*operands):
+    return pl.pallas_call(
+        coarse_rows,
+        out_shape=jax.ShapeDtypeStruct((COLS, COLS), jnp.float32),
         compiler_params=pltpu.CompilerParams(vmem_limit_bytes=VMEM_LIMIT),
         name="coarse_rows",
     )(*operands)
@@ -309,18 +345,24 @@
     return center, margin, packed
 
 
-UNROLL = 4
+UNROLL = 8
+UNROLL_BEGIN = 2
+UNROLL_FINISH = 2
 PLANES = LEVELS + 2
 BESIDE_TILES = (1, 2, 5, 6)
 
 
-def smooth_kernel(
-    starts, place_ref, table_ref, told_ref, block_ref, low_ref, high_ref, left_ref, right_ref,
-    absorption_ref, low_c, high_c, left_c, right_c, out_ref,
-    own_m, beside_m, strip_m, own, beside, strip, own_y, beside_y, strip_y, own_d, beside_d, strip_d,
-    own_e, beside_e, strip_e, own_r, beside_r, strip_r, diag, strip_diag,
-):
-    field_start, coef_start, coef_at = starts
+def smooth_kernel(same, place_ref, table_ref, told_ref, block_ref, low_ref, high_ref, left_ref, right_ref, absorption_ref, *refs):
+    if same:
+        low_c, high_c, left_c, right_c = low_ref, high_ref, left_ref, right_ref
+    else:
+        low_c, high_c, left_c, right_c = refs[:4]
+        refs = refs[4:]
+    (
+        out_ref, own_m, beside_m, strip_m, own, beside, strip, own_y, beside_y, strip_y,
+        wide_r, strip_r, diag, strip_diag,
+    ) = refs
+    field_start, coef_start, coef_at = 0, LEVELS, 2
     masks(Place(place_ref, told_ref), own_m, beside_m, strip_m)
     base = 4.0 + 2.0 * vertical
     zero = jnp.zeros((8, COLS), jnp.float32)
@@ -333,9 +375,9 @@
             s = slice(i * 8, i * 8 + 8)
             for t in range(2):
                 for x in (own, own_y, beside, beside_y):
-                    x[at, s, lanes[t]] = zero
-            strip[at, s] = zero
-            strip_y[at, s] = zero
+                    x[at, t, s] = zero
+            strip[at, 0, s] = zero
+            strip_y[at, 0, s] = zero
         return carry
 
     lax.fori_loop(0, 2, clear, 0)
@@ -347,59 +389,50 @@
             tiles = tiles_of((low_ref, block_ref, high_ref), field_start, (left_ref, right_ref), 0, z, i)
             inner = 1 <= i < 7
             for t in range(2):
-                value = tiles[t] * own_m[t, s]
+                guess = tiles[t] * (1.0 / theta)
+                value = guess if t == 0 and 2 <= i < 6 else guess * own_m[t, s]
+                own[at, t, s] = value
+                own_y[at, t, s] = zero
                 if inner:
-                    own_r[z, s, lanes[t]] = value
-                    own_d[z, s, lanes[t]] = value * (1.0 / theta)
-                else:
-                    own_y[at, s, lanes[t]] = zero
-                own[at, s, lanes[t]] = value * (1.0 / theta)
-                value = tiles[t] * beside_m[t, s]
-                if i in BESIDE_TILES:
-                    beside_r[z, s, lanes[t]] = value
-                    beside_d[z, s, lanes[t]] = value * (1.0 / theta)
-                else:
-                    beside_y[at, s, lanes[t]] = zero
-                beside[at, s, lanes[t]] = value * (1.0 / theta)
-            value = tiles[2] * strip_m[s]
-            strip[at, s] = value * (1.0 / theta)
+                    wide_r[z, t, s] = tiles[t]
+                beside_y[at, t, s] = zero
+                beside[at, t, s] = zero if i in (3, 4) else guess * beside_m[t, s]
+            strip[at, 0, s] = tiles[2] * (strip_m[s] * (1.0 / theta))
+            strip_y[at, 0, s] = zero
             if inner:
-                strip_r[z, s] = value
-                strip_d[z, s] = value * (1.0 / theta)
+                strip_r[z, 0, s] = tiles[2]
                 tiles = tiles_of((low_c, absorption_ref, high_c), coef_start, (left_c, right_c), coef_at, z, i)
-                diag[z, s, lanes[0]] = tiles[0] + base
-                diag[z, s, lanes[1]] = tiles[1] + base
-                strip_diag[z, s] = tiles[2] + base
-            else:
-                strip_y[at, s] = zero
+                diag[z, 0, s] = tiles[0] + base
+                diag[z, 1, s] = tiles[1] + base
+                strip_diag[z, 0, s] = tiles[2] + base
         return carry
 
-    lax.fori_loop(0, LEVELS, begin, 0)
+    lax.fori_loop(0, LEVELS, begin, 0, unroll=UNROLL_BEGIN)
     at_first, at_last = lane == 0, lane == COLS - 1
 
-    def step(here, x, y, d, e, r, a, mask, width, i, keep, scale):
+    def step(here, x, y, r, a, mask, width, i, keep, scale):
         s = slice(i * 8, i * 8 + 8)
         up, down = slice(i * 8 - 1, i * 8 + 7), slice(i * 8 + 1, i * 8 + 9)
         z = here - 1
-        now = [x[here, s, lanes[t]] for t in range(width)]
+        now = [x[here, t, s] for t in range(width)]
         back = [roll(v, 1) for v in now]
         fore = [roll(v, -1) for v in now]
         if width == 2:
             back = [jnp.where(at_first, back[1], back[0]), jnp.where(at_first, back[0], back[1])]
             fore = [jnp.where(at_last, fore[1], fore[0]), jnp.where(at_last, fore[0], fore[1])]
         for t in range(width):
-            high = x[here - 1, s, lanes[t]] + x[here + 1, s, lanes[t]]
-            around = (x[here, up, lanes[t]] + x[here, down, lanes[t]]) + (back[t] + fore[t])
+            high = x[here - 1, t, s] + x[here + 1, t, s]
+            around = (x[here, t, up] + x[here, t, down]) + (back[t] + fore[t])
             around = around + (high + high)
-            defect = r[z, s, lanes[t]] - a[z, s, lanes[t]] * now[t] + around
-            move = keep * d[z, s, lanes[t]] + scale * defect
+            defect = (r[z, t, s] + around) - a[z, t, s] * now[t]
+            move = keep * (now[t] - y[here, t, s]) + scale * defect
+            after = now[t] + move
             if mask[t] is not None:
-                move = move * mask[t]
-            e[z, s, lanes[t]] = move
-            y[here, s, lanes[t]] = now[t] + move
-
-    first = ((own, own_y, own_d, own_e), (beside, beside_y, beside_d, beside_e), (strip, strip_y, strip_d, strip_e))
-    second = tuple((y, x, e, d) for x, y, d, e in first)
+                after = after * mask[t]
+            y[here, t, s] = after
+
+    first = ((own, own_y), (beside, beside_y), (strip, strip_y))
+    second = tuple((y, x) for x, y in first)
 
     def sweep(n, arrays):
         keep, scale = table_ref[0, n], table_ref[1, n]
@@ -410,9 +443,9 @@
             for i in range(1, 7):
                 s = slice(i * 8, i * 8 + 8)
                 free = None if 2 <= i < 6 else own_m[0, s]
-                step(here, *own, own_r, diag, [free, own_m[1, s]], 2, i, keep, scale)
+                step(here, *own, wide_r, diag, [free, own_m[1, s]], 2, i, keep, scale)
                 if i in BESIDE_TILES:
-                    step(here, *beside, beside_r, diag, [beside_m[0, s], beside_m[1, s]], 2, i, keep, scale)
+                    step(here, *beside, wide_r, diag, [beside_m[0, s], beside_m[1, s]], 2, i, keep, scale)
                 step(here, *strip, strip_r, strip_diag, [strip_m[s]], 1, i, keep, scale)
             return carry
 
@@ -431,49 +464,50 @@
         for i in range(1, 7):
             s = slice(i * 8, i * 8 + 8)
             out = slice(i * 8 - 8, i * 8)
-            value = strip[at, s]
+            value = strip[at, 0, s]
             at_left = value + roll(value, -32)
             at_right = roll(at_left, 64)
             first = jnp.where(near_first, at_left, jnp.where(near_last, at_right, 0.0))
             second = jnp.where(near_last, at_left, jnp.where(near_first, at_right, 0.0))
-            first = first + own[at, s, lanes[0]]
-            second = second + own[at, s, lanes[1]]
+            first = first + own[at, 0, s]
+            second = second + own[at, 1, s]
             if i in BESIDE_TILES:
-                first = first + beside[at, s, lanes[0]]
-                second = second + beside[at, s, lanes[1]]
+                first = first + beside[at, 0, s]
+                second = second + beside[at, 1, s]
             out_ref[z, out, lanes[0]] = first
             out_ref[z, out, lanes[1]] = second
         return carry
 
-    lax.fori_loop(0, LEVELS, finish, 0)
-
-
-def smooth(starts, place, table, told, block, low, high, strips, absorption, low_c, high_c, strips_c):
-    wide = (TALL, 2 * COLS)
-    thin = (TALL, COLS)
+    lax.fori_loop(0, LEVELS, finish, 0, unroll=UNROLL_FINISH)
+
+
+def smooth(place, table, told, block, low, high, strips, absorption, coefficient=None):
+    wide = (2, TALL, COLS)
+    thin = (1, TALL, COLS)
 
     def scratch(*shape):
         return pltpu.VMEM(shape, jnp.float32)
 
-    smem = pl.BlockSpec(memory_space=pltpu.SMEM)
-    vmem = pl.BlockSpec(memory_space=pltpu.VMEM)
+    more = () if coefficient is None else coefficient
+    specs = [SMEM_SPEC] * 2 + [VMEM_SPEC] * 2 + [VMEM_SPEC if more else FIELDS_SPEC] * 2 + [VMEM_SPEC] * 3
+    if more:
+        specs += [FIELDS_SPEC] * 2 + [VMEM_SPEC] * 2
     return pl.pallas_call(
-        functools.partial(smooth_kernel, starts),
-        in_specs=[smem] * 2 + [vmem] * 11,
+        functools.partial(smooth_kernel, not more),
+        grid=(1,),
+        in_specs=specs,
         out_shape=jax.ShapeDtypeStruct((LEVELS, INNER, 2 * COLS), jnp.float32),
         scratch_shapes=[
-            scratch(2, *thin), scratch(2, *thin), scratch(*thin),
+            scratch(*wide), scratch(*wide), scratch(TALL, COLS),
             scratch(PLANES, *wide), scratch(PLANES, *wide), scratch(PLANES, *thin),
             scratch(PLANES, *wide), scratch(PLANES, *wide), scratch(PLANES, *thin),
-            scratch(LEVELS, *wide), scratch(LEVELS, *wide), scratch(LEVELS, *thin),
-            scratch(LEVELS, *wide), scratch(LEVELS, *wide), scratch(LEVELS, *thin),
-            scratch(LEVELS, *wide), scratch(LEVELS, *wide), scratch(LEVELS, *thin),
+            scratch(LEVELS, *wide), scratch(LEVELS, *thin),
             scratch(LEVELS, *wide), scratch(LEVELS, *thin),
         ],
         compiler_params=pltpu.CompilerParams(vmem_limit_bytes=VMEM_LIMIT),
         cost_estimate=pl.CostEstimate(flops=60000000, bytes_accessed=4000000, transcendentals=0),
         name="smoother",
-    )(place, table, told, block, low, high, *strips, absorption, low_c, high_c, *strips_c)
+    )(place, table, told, block, low, high, *strips, absorption, *more)
 
 
 INNER = ROWS + 16
@@ -495,8 +529,14 @@
     return jnp.sum(found, axis=0, keepdims=True)
 
 
-def add_coarse(place, told_ref, coarse_ref, basis_ref, low_ref, high_ref, left_ref, right_ref, at, sum_ref, x,
+def add_coarse(place, told_ref, coarse_ref, basis_hbm, basis_ref, sems, low_ref, high_ref, left_ref, right_ref, at, sum_ref, x,
                own_c, edge_c, ring_ref, side_ref):
+    def part(q):
+        levels = pl.ds(q * 4, 4)
+        return pltpu.make_async_copy(basis_hbm.at[:, levels], basis_ref.at[:, levels], sems.at[q])
+
+    for q in range(LEVELS // 4):
+        part(q).start()
     turned = coarse_ref[...].T[:VECTORS]
     row = coarse_at(turned, slots_of(place, told_ref, ((0, 0), (-1, 0), (1, 0), (0, -1))))
     other = coarse_at(turned, slots_of(place, told_ref, ((0, 1),)))
@@ -511,11 +551,11 @@
             return total + edge[2 * LEVELS + k] * edge_c[pl.ds(n * VECTORS + k, 1), :]
 
         ring_ref[n] = lax.fori_loop(0, VECTORS, vector, jnp.zeros((LEVELS, COLS), jnp.float32))
-    for n, (edge, values, shift) in enumerate(((left_ref, roll(row, VECTORS), -1), (right_ref, other, 0))):
+    which = iota((COLS, COLS), 0) >> 5
+    for n, (edge, values) in enumerate(((left_ref, roll(row, VECTORS)), (right_ref, other))):
         values = jnp.where(lane_row < VECTORS, values, 0.0)
         values = values + roll(values, 32) + roll(values, 64) + roll(values, 96)
-        weights = jnp.broadcast_to(roll(values, shift), (COLS, COLS)).T
-        which = ((iota((COLS, COLS), 0) - shift) & (COLS - 1)) >> 5
+        weights = jnp.broadcast_to(values, (COLS, COLS)).T
         weights = jnp.where(iota((COLS, COLS), 1) == which, weights, 0.0)
         parts = edge[at : at + 2].reshape(2 * TALL, COLS)
         side_ref[n] = jnp.dot(parts, weights, precision=HIGHEST, preferred_element_type=jnp.float32)
@@ -539,7 +579,11 @@
             x[here, t, COLS : 2 * COLS] = sum_ref[z, t, COLS : 2 * COLS] + value
         return carry
 
-    lax.fori_loop(0, LEVELS, level, 0)
+    def levels(q, carry):
+        part(q).wait()
+        return lax.fori_loop(4 * q, 4 * q + 4, level, carry)
+
+    lax.fori_loop(0, LEVELS // 4, levels, 0)
     zero = jnp.zeros((ROWS, COLS), jnp.float32)
     x[0, 8 : 8 + ROWS, 0:COLS] = zero
     x[PLANES - 1, 8 : 8 + ROWS, 0:COLS] = zero
@@ -571,11 +615,11 @@
 
 
 def first_coarse_kernel(
-    place_ref, told_ref, coarse_ref, basis_ref, low_ref, high_ref, left_ref, right_ref, sum_ref, source_ref, absorption_ref,
-    direction_ref, image_ref, ahead_ref, behind_ref, out_ref, x, own_c, edge_c, ring_ref, side_ref, sums_ref,
+    place_ref, told_ref, coarse_ref, basis_hbm, low_ref, high_ref, left_ref, right_ref, sum_ref, source_ref, absorption_ref,
+    direction_ref, image_ref, ahead_ref, behind_ref, out_ref, x, own_c, edge_c, ring_ref, side_ref, basis_ref, sems, sums_ref,
 ):
     place = Place(place_ref, told_ref)
-    row = add_coarse(place, told_ref, coarse_ref, basis_ref, low_ref, high_ref, left_ref, right_ref, 4, sum_ref, x,
+    row = add_coarse(place, told_ref, coarse_ref, basis_hbm, basis_ref, sems, low_ref, high_ref, left_ref, right_ref, 4, sum_ref, x,
                      own_c, edge_c, ring_ref, side_ref)
     zero = jnp.zeros((8, COLS), jnp.float32)
 
@@ -617,12 +661,12 @@
 
 
 def second_coarse_kernel(
-    place_ref, told_ref, coarse_ref, basis_ref, low_ref, high_ref, left_ref, right_ref, sum_ref, source_ref, absorption_ref,
+    place_ref, told_ref, coarse_ref, basis_hbm, low_ref, high_ref, left_ref, right_ref, sum_ref, source_ref, absorption_ref,
     again_ref, first_sum_ref, direction_ref, first_ref,
-    residual_ref, precond_ref, image_ref, out_ref, x, own_c, edge_c, ring_ref, side_ref,
+    residual_ref, precond_ref, image_ref, out_ref, x, own_c, edge_c, ring_ref, side_ref, basis_ref, sems,
 ):
     place = Place(place_ref, told_ref)
-    row = add_coarse(place, told_ref, coarse_ref, basis_ref, low_ref, high_ref, left_ref, right_ref, 4, sum_ref, x,
+    row = add_coarse(place, told_ref, coarse_ref, basis_hbm, basis_ref, sems, low_ref, high_ref, left_ref, right_ref, 4, sum_ref, x,
                      own_c, edge_c, ring_ref, side_ref)
     weight0, curve0 = scalars(again_ref)
     step = weight0 / curve0
@@ -680,8 +724,7 @@
     slab = jax.ShapeDtypeStruct((LEVELS, EDGE, COLS), jnp.float32)
     message = jax.ShapeDtypeStruct((COLS, COLS), jnp.float32)
     params = pltpu.CompilerParams(vmem_limit_bytes=VMEM_LIMIT)
-    smem = pl.BlockSpec(memory_space=pltpu.SMEM)
-    vmem = pl.BlockSpec(memory_space=pltpu.VMEM)
+    hbm = pl.BlockSpec(memory_space=pltpu.HBM)
 
     def scratch(*shape):
         return pltpu.VMEM(shape, jnp.float32)
@@ -689,34 +732,27 @@
     coarse_scratch = [
         scratch(PLANES, INNER, 2 * COLS), scratch(VECTORS, COLS), scratch(2 * VECTORS, COLS),
         scratch(2, LEVELS, COLS), scratch(2, 2 * TALL, COLS),
+        pltpu.VMEM(basis.shape, basis.dtype), pltpu.SemaphoreType.DMA((LEVELS // 4,)),
     ]
     place = jnp.stack(
         [lax.axis_index("gx"), lax.axis_index("gy"), lax.axis_size("gx"), lax.axis_size("gy")]
     ).astype(jnp.int32)
     table = jnp.array(list(zip(*chebyshev_table())), jnp.float32)
-    told_row = jnp.concatenate(
-        [
-            jnp.zeros((1, VECTORS), jnp.float32),
-            coarse_slot.reshape(1, -1).astype(jnp.float32),
-            margin_width.astype(jnp.float32),
-            jnp.zeros((1, COLS - 65), jnp.float32),
-        ],
-        axis=1,
+    rows, ahead, behind, left_edge, right_edge = first_projection(
+        source, absorption, basis, coarse_slot, margin_width
     )
-    rows, ahead, behind, left_edge, right_edge = first_projection(source, absorption, basis, told_row)
     low, high = exchange(ahead, behind, "gx")
     told = everyone(rows)
-    rows, ahead, behind = middle(
-        first_middle_kernel, 6, told, coarse_inverse, source, absorption, low, high, left_edge, right_edge
+    fields = [VMEM_SPEC] * 2 + [FIELDS_SPEC] * 2 + [VMEM_SPEC] * 2
+    strips = exchange(
+        *pack(first_pack_kernel, fields, 6, source, absorption, low, high, left_edge, right_edge), "gy"
     )
-    strips = exchange(ahead, behind, "gy")
-    coarse = everyone(rows)
-    coef = (absorption, low, high, strips)
-    first_sum = smooth((0, LEVELS, 2), place, table, told, source, low, high, strips, *coef)
+    coarse = everyone(solve_rows(told, told, coarse_inverse))
+    first_sum = smooth(place, table, told, source, low, high, strips, absorption)
     edges = (low, high, *strips)
     direction, image, ahead, behind, rows = pl.pallas_call(
         first_coarse_kernel,
-        in_specs=[smem] + [vmem] * 10,
+        in_specs=[SMEM_SPEC] + [VMEM_SPEC] * 2 + [hbm] + [VMEM_SPEC] * 7,
         out_shape=[block, block, slab, slab, message],
         scratch_shapes=coarse_scratch + [scratch(VECTORS, COLS)],
         compiler_params=params,
@@ -724,13 +760,12 @@
     )(place, told, coarse, basis, *edges, first_sum, source, absorption)
     low_w, high_w = exchange(ahead, behind, "gx")
     again = everyone(rows)
-    rows, ahead, behind = middle(middle_kernel, 2, again, told, coarse_inverse, image, low_w, high_w)
-    strips_w = exchange(ahead, behind, "gy")
-    coarse = everyone(rows)
-    second_sum = smooth((0, LEVELS, 2), place, table, told, image, low_w, high_w, strips_w, *coef)
+    strips_w = exchange(*pack(pack_kernel, [VMEM_SPEC] * 3, 2, image, low_w, high_w), "gy")
+    coarse = everyone(solve_rows(again, told, coarse_inverse))
+    second_sum = smooth(place, table, told, image, low_w, high_w, strips_w, absorption, edges)
     residual, precond, precond_image, rows = pl.pallas_call(
         second_coarse_kernel,
-        in_specs=[smem] + [vmem] * 14,
+        in_specs=[SMEM_SPEC] + [VMEM_SPEC] * 2 + [hbm] + [VMEM_SPEC] * 11,
         out_shape=[block, block, block, message],
         scratch_shapes=coarse_scratch,
         compiler_params=params,

time: 172 us -> 168 us (0.977)
  blocking collectives: 58.3 us -> 19.1 us
  waiting for transfers between devices: 0.03 us -> 20.5 us
  starting transfers between devices: 35.5 us -> 55.6 us
  Pallas kernels: 64.9 us -> 59.7 us
    all_to_all x3 -> x1, blocking collectives: 58.3 us -> 19.1 us  [everyone(): return lax.all_to_all(rows, AXES, 0, 0, tiled=True)]
    all_to_all x2 -> x4, starting transfers between devices: 15.4 us -> 33.5 us  [everyone(): return lax.all_to_all(rows, AXES, 0, 0, tiled=True)]
    all_to_all x2 -> x4, waiting for transfers between devices: 0.01 us -> 11.7 us  [everyone(): return lax.all_to_all(rows, AXES, 0, 0, tiled=True)]
    ppermute x4, waiting for transfers between devices: 0.01 us -> 4.5 us  [exchange(): lax.ppermute(forward_value, axis, forward)]
    ppermute x4, waiting for transfers between devices: 0.01 us -> 4.3 us  [exchange(): lax.ppermute(backward_value, axis, backward)]
    pallas_call x6 -> x8, Pallas kernels: 53.5 us -> 50.6 us  [the longest x2 31.9 us: smooth(): pl.pallas_call(functools.partial(smooth_kernel, not more), grid=(1,), in_...]
    pallas_call x1, Pallas kernels: 8.53 us -> 6.24 us  [first_projection(): pl.pallas_call(first_kernel, grid=(VECTORS // group,), in_specs=[block_sp...]
    ppermute x4, starting transfers between devices: 13.7 us -> 15.7 us  [exchange(): lax.ppermute(forward_value, axis, forward)]
  transfers between devices with their start and end apart: 10 -> 12, of which waited for: 0 -> 4; matrix products, arithmetic and copies ran while one was open for 0% -> 0% of each run, Pallas kernels for 22% -> 22%
where the time goes in v4:
time: 168 us; the launch traced here: 167 us
  Pallas kernels  59.7 us (36%)
  starting transfers between devices  55.6 us (33%)
  waiting for transfers between devices  20.5 us (12%)
  blocking collectives  19.1 us (11%)
  local copies, waits for them, and re-layouts  10.4 us (6%)
    all_to_all x4, starting transfers between devices, everyone(): return lax.all_to_all(rows, AXES, 0, 0, tiled=True)  33.5 us
    pallas_call x2, Pallas kernels, smooth(): pl.pallas_call(functools.partial(smooth_kernel, not more), grid=(1,), in_...  31.9 us
    all_to_all x1, blocking collectives, everyone(): return lax.all_to_all(rows, AXES, 0, 0, tiled=True)  19.1 us
    ppermute x4, starting transfers between devices, exchange(): lax.ppermute(forward_value, axis, forward)  15.7 us
    all_to_all x4, waiting for transfers between devices, everyone(): return lax.all_to_all(rows, AXES, 0, 0, tiled=True)  11.7 us
    unnamed x26, local copies, waits for them, and re-layouts  10.4 us
    pallas_call x1, Pallas kernels, shards(): pl.pallas_call(first_coarse_kernel, in_specs=[SMEM_SPEC] + [VMEM_SPEC] *...  6.94 us
    ppermute x4, starting transfers between devices, exchange(): lax.ppermute(backward_value, axis, backward)  6.41 us
  transfers between devices with their start and end apart: 12, of which 4 were waited for; matrix products, arithmetic and copies ran while one was open for 0% of the time, Pallas kernels for 22%

profile of v4, /device:TPU:1, one launch (start us, length us, event | category | flops | bytes accessed | tf_op | source)
XLA Modules:
  0.0 167.0 jit_solution(14084611527158302966)
XLA Ops:
  0.6 0.0 copy-start.12
  0.7 0.0 copy-start.6
  1.4 6.2 %first_projection.1 = (f32[128,128]{1,0:T(8,128)}, f32[64,16,128]{2,1,0:T(8,128)}, f32[64,16,128]{2,1,0:T(8,128)}, f32[4,32,128]{2,1,0:T(8,128)}, f32[4,32,128]{2,1,0:T(8,128)}) custom-call(f32[16,32,128]{2,1,0:T(8,128)} %source_ref.5, f32[16,32,128]{2,1,0:T(8,128)} %absorption_ref.9, bf16[32,16,32,128]{3,2,1,0:T(8,128)(2,1)} %basis_hbm.3, ...), custom_call_target="tpu_custom_call" | custom-call | tf_op jit(solution)/shard_map/first_projection/pallas_call | solution.py:148
  7.6 4.6 %collective-permute-start = (f32[64,16,128]{2,1,0:T(8,128)}, f32[64,16,128]{2,1,0:T(8,128)S(1)}, u32[]{:S(2)}, u32[]{:S(2)}) collective-permute-start(f32[64,16,128]{2,1,0:T(8,128)} %get-tuple-element.21), channel_id=1, source_target_pairs={{0,16},{16,32},{32,48},{48,64},{64,80},{80,96},{96,112},{1,17},{17... | collective-permute-start | bytes 1572872 | tf_op jit(solution)/shard_map/ppermute | solution.py:52
  12.2 1.9 %collective-permute-start.1 = (f32[64,16,128]{2,1,0:T(8,128)}, f32[64,16,128]{2,1,0:T(8,128)S(1)}, u32[]{:S(2)}, u32[]{:S(2)}) collective-permute-start(f32[64,16,128]{2,1,0:T(8,128)} %get-tuple-element.22), channel_id=1, source_target_pairs={{16,0},{32,16},{48,32},{64,48},{80,64},{96,80},{112,96},{17,1},{33... | collective-permute-start | bytes 1572872 | tf_op jit(solution)/shard_map/ppermute | solution.py:52
  14.2 4.5 %collective-permute-done.low_ref.refs_0_ = f32[64,16,128]{2,1,0:T(8,128)S(1)} collective-permute-done((f32[64,16,128]{2,1,0:T(8,128)}, f32[64,16,128]{2,1,0:T(8,128)S(1)}, u32[]{:S(2)}, u32[]{:S(2)}) %collective-permute-start) | collective-permute-done | bytes 524320 | tf_op jit(solution)/shard_map/ppermute | solution.py:52
  18.7 4.3 %collective-permute-done.1.high_ref.refs_1_ = f32[64,16,128]{2,1,0:T(8,128)S(1)} collective-permute-done((f32[64,16,128]{2,1,0:T(8,128)}, f32[64,16,128]{2,1,0:T(8,128)S(1)}, u32[]{:S(2)}, u32[]{:S(2)}) %collective-permute-start.1) | collective-permute-done | bytes 524320 | tf_op jit(solution)/shard_map/ppermute | solution.py:52
  23.0 0.8 copy-done.10
  23.8 0.8 copy-done.11
  24.6 0.7 strips.2
  25.4 3.6 %collective-permute-start.2 = (f32[6,64,128]{2,1,0:T(8,128)S(1)}, f32[6,64,128]{2,1,0:T(8,128)S(1)}, u32[]{:S(2)}, u32[]{:S(2)}) collective-permute-start(f32[6,64,128]{2,1,0:T(8,128)S(1)} %get-tuple-element.25), channel_id=1, source_target_pairs={{0,1},{1,2},{2,3},{3,4},{4,5},{5,6},{6,7},{7,8},{8,9},{9,10},{10,1... | collective-permute-start | bytes 589832 | tf_op jit(solution)/shard_map/ppermute | solution.py:52
  28.9 1.3 collective-permute-start.3
  30.2 10.3 %all-to-all-start = ((f32[128,1,128]{2,1,0:T(1,128)}), f32[128,1,128]{2,1,0:T(1,128)S(1)}, u32[]{:S(2)}, u32[]{:S(2)}) async-start(f32[128,1,128]{2,1,0:T(1,128)} %bitcast.37), calls=%async_computation | async-start | bytes 131072 | tf_op jit(solution)/shard_map/all_to_all | solution.py:56
  40.5 9.4 %all-to-all-done = f32[128,1,128]{2,1,0:T(1,128)S(1)} async-done(((f32[128,1,128]{2,1,0:T(1,128)}), f32[128,1,128]{2,1,0:T(1,128)S(1)}, u32[]{:S(2)}, u32[]{:S(2)}) %all-to-all-start) | async-done | bytes 65568 | tf_op jit(solution)/shard_map/all_to_all | solution.py:56
  50.0 1.8 %coarse_rows.2 = f32[128,128]{1,0:T(8,128)} custom-call(f32[128,128]{1,0:T(8,128)S(1)} %bitcast.22, f32[128,128]{1,0:T(8,128)S(1)} %bitcast.23, f32[32,4096]{1,0:T(8,128)S(1)} %copy-done.6), custom_call_target="tpu_custom_call" | custom-call | tf_op jit(solution)/shard_map/coarse_rows/pallas_call | solution.py:251
  51.8 4.5 %all-to-all-start.1 = ((f32[128,1,128]{2,1,0:T(1,128)}), f32[128,1,128]{2,1,0:T(1,128)S(1)}, u32[]{:S(2)}, u32[]{:S(2)}) async-start(f32[128,1,128]{2,1,0:T(1,128)} %bitcast.6), calls=%async_computation.1 | async-start | bytes 131072 | tf_op jit(solution)/shard_map/all_to_all | solution.py:56
  56.3 0.1 pad_add_fusion.place_ref
  56.4 0.0 collective-permute-done.2.left_ref.refs_2_
  56.4 0.0 collective-permute-done.3.right_ref.refs_3_
  56.4 15.8 %smoother.2.sum_ref.first_sum_ref = f32[16,48,256]{2,1,0:T(8,128)S(1)} custom-call(s32[4]{0:T(128)S(1)} %pad_add_fusion.place_ref, f32[2,8]{1,0:T(2,128)S(1)} %copy-done.12, f32[128,128]{1,0:T(8,128)S(1)} %bitcast.24, f32[16,32,128]{2,1,0:T(8,128)S(1)} %copy-done.3, f32[64,16,128]{2,1,0:T(8,128)S(1)} %collective-permute-done.low_ref.refs_0_, ...), custom_call_target="tpu_custom_call" | custom-call | flops 60000000 | bytes 4000000 | tf_op jit(solution)/shard_map/smoother/pallas_call | solution.py:495
  72.2 0.0 all-to-all-done.1
  72.2 0.0 copy-start
  72.2 2.2 %copy-done = bf16[32,16,32,128]{3,2,1,0:T(8,128)(2,1)S(1)} copy-done((bf16[32,16,32,128]{3,2,1,0:T(8,128)(2,1)S(1)}, bf16[32,16,32,128]{3,2,1,0:T(8,128)(2,1)}, u32[]{:S(2)}) %copy-start) | copy-done | bytes 4194328
  74.4 6.9 %direction_and_image.1 = (f32[16,32,128]{2,1,0:T(8,128)S(1)}, f32[16,32,128]{2,1,0:T(8,128)S(1)}, f32[16,16,128]{2,1,0:T(8,128)}, f32[16,16,128]{2,1,0:T(8,128)}, f32[128,128]{1,0:T(8,128)S(1)}) custom-call(s32[4]{0:T(128)S(1)} %pad_add_fusion.place_ref, f32[128,128]{1,0:T(8,128)S(1)} %bitcast.25, f32[128,128]{1,0:T(8,128)S(1)} %bitcast.32, ...), custom_call_target="tpu_custom_call" | custom-call | tf_op jit(solution)/shard_map/direction_and_image/pallas_call | solution.py:753
  81.4 0.6 copy-done.9
  82.0 3.5 %collective-permute-start.4 = (f32[16,16,128]{2,1,0:T(8,128)}, f32[16,16,128]{2,1,0:T(8,128)S(1)}, u32[]{:S(2)}, u32[]{:S(2)}) collective-permute-start(f32[16,16,128]{2,1,0:T(8,128)} %get-tuple-element.29), channel_id=1, source_target_pairs={{0,16},{16,32},{32,48},{48,64},{64,80},{80,96},{96,112},{1,17},{17... | collective-permute-start | bytes 393224 | tf_op jit(solution)/shard_map/ppermute | solution.py:52
  85.5 1.9 %collective-permute-start.5 = (f32[16,16,128]{2,1,0:T(8,128)}, f32[16,16,128]{2,1,0:T(8,128)}, u32[]{:S(2)}, u32[]{:S(2)}) collective-permute-start(f32[16,16,128]{2,1,0:T(8,128)} %get-tuple-element.30), channel_id=1, source_target_pairs={{16,0},{32,16},{48,32},{64,48},{80,64},{96,80},{112,96},{17,1},{33... | collective-permute-start | bytes 393224 | tf_op jit(solution)/shard_map/ppermute | solution.py:52
  87.4 9.9 %all-to-all-start.2 = ((f32[128,1,128]{2,1,0:T(1,128)}), f32[128,1,128]{2,1,0:T(1,128)S(1)}, u32[]{:S(2)}, u32[]{:S(2)}) async-start(f32[128,1,128]{2,1,0:T(1,128)} %bitcast.35), calls=%async_computation.2 | async-start | bytes 131072 | tf_op jit(solution)/shard_map/all_to_all | solution.py:56
  97.3 0.0 collective-permute-done.4.low_ref
  97.4 1.9 %strips.3 = (f32[2,64,128]{2,1,0:T(8,128)}, f32[2,64,128]{2,1,0:T(8,128)}) custom-call(f32[16,32,128]{2,1,0:T(8,128)S(1)} %get-tuple-element.28.block_ref.first_ref, f32[16,16,128]{2,1,0:T(8,128)S(1)} %collective-permute-done.4.low_ref, f32[16,16,128]{2,1,0:T(8,128)} %collective-permute-done.5.high_ref), custom_call_target="tpu_custom_call" | custom-call | flops 2000000 | bytes 2000000 | tf_op jit(solution)/shard_map/strips/pallas_call | solution.py:239
  99.3 4.0 %collective-permute-start.6 = (f32[2,64,128]{2,1,0:T(8,128)}, f32[2,64,128]{2,1,0:T(8,128)}, u32[]{:S(2)}, u32[]{:S(2)}) collective-permute-start(f32[2,64,128]{2,1,0:T(8,128)} %get-tuple-element.31), channel_id=1, source_target_pairs={{0,1},{1,2},{2,3},{3,4},{4,5},{5,6},{6,7},{7,8},{8,9},{9,10},{10,1... | collective-permute-start | bytes 196616 | tf_op jit(solution)/shard_map/ppermute | solution.py:52
  103.3 1.3 collective-permute-start.7
  104.6 2.3 %all-to-all-done.2 = f32[128,1,128]{2,1,0:T(1,128)S(1)} async-done(((f32[128,1,128]{2,1,0:T(1,128)}), f32[128,1,128]{2,1,0:T(1,128)S(1)}, u32[]{:S(2)}, u32[]{:S(2)}) %all-to-all-start.2) | async-done | bytes 65568 | tf_op jit(solution)/shard_map/all_to_all | solution.py:56
  106.8 1.0 copy-done.7
  107.9 1.2 coarse_rows.3
  109.1 0.0 copy-start.8
  109.1 0.6 copy-done.8
  109.7 8.8 %all-to-all-start.3 = ((f32[128,1,128]{2,1,0:T(1,128)}), f32[128,1,128]{2,1,0:T(1,128)}, u32[]{:S(2)}, u32[]{:S(2)}) async-start(f32[128,1,128]{2,1,0:T(1,128)} %bitcast.34), calls=%async_computation.3 | async-start | bytes 131072 | tf_op jit(solution)/shard_map/all_to_all | solution.py:56
  118.5 0.0 collective-permute-done.6.left_ref
  118.5 0.0 collective-permute-done.7.right_ref
  118.6 16.2 %smoother.3.sum_ref = f32[16,48,256]{2,1,0:T(8,128)S(1)} custom-call(s32[4]{0:T(128)S(1)} %pad_add_fusion.place_ref, f32[2,8]{1,0:T(2,128)S(1)} %copy-done.12, f32[128,128]{1,0:T(8,128)S(1)} %bitcast.27, f32[16,32,128]{2,1,0:T(8,128)S(1)} %get-tuple-element.28.block_ref.first_ref, f32[16,16,128]{2,1,0:T(8,128)S(1)} %collective-permute-done.4.low_ref, ...), custom_call_target="tpu_custom_call" | custom-call | flops 60000000 | bytes 4000000 | tf_op jit(solution)/shard_map/smoother/pallas_call | solution.py:495
  134.7 0.9 copy-done.4
  135.6 0.0 all-to-all-done.3
  135.7 2.2 %copy-done.1 = bf16[32,16,32,128]{3,2,1,0:T(8,128)(2,1)S(1)} copy-done((bf16[32,16,32,128]{3,2,1,0:T(8,128)(2,1)S(1)}, bf16[32,16,32,128]{3,2,1,0:T(8,128)(2,1)}, u32[]{:S(2)}) %copy-start.1) | copy-done | bytes 4194328
  137.8 1.1 copy-done.5
  139.0 6.0 %second_images.1 = (f32[16,32,128]{2,1,0:T(8,128)S(1)}, f32[16,32,128]{2,1,0:T(8,128)S(1)}, f32[16,32,128]{2,1,0:T(8,128)S(1)}, f32[128,128]{1,0:T(8,128)S(1)}) custom-call(s32[4]{0:T(128)S(1)} %pad_add_fusion.place_ref, f32[128,128]{1,0:T(8,128)S(1)} %bitcast.28, f32[128,128]{1,0:T(8,128)} %bitcast.13.coarse_ref, bf16[32,16,32,128]{3,2,1,0:T(8,128)(2,1)S(1)} %copy-done.1, ...), custom_call_target="tpu_custom_call" | custom-call | tf_op jit(solution)/shard_map/second_images/pallas_call | solution.py:766
  145.0 19.1 %all_to_all.55 = f32[128,1,128]{2,1,0:T(1,128)S(1)} all-to-all(f32[128,1,128]{2,1,0:T(1,128)S(1)} %bitcast.36), channel_id=1, replica_groups=mesh['gx'=8,'gy'=16] {'gx','gy'}, dimensions={0} | all-to-all | bytes 131072 | tf_op jit(solution)/shard_map/all_to_all | solution.py:56
  164.1 2.9 %update.1 = (f32[16,32,128]{2,1,0:T(8,128)}, f32[16,32,128]{2,1,0:T(8,128)}) custom-call(f32[128,128]{1,0:T(8,128)S(1)} %bitcast.31, f32[128,128]{1,0:T(8,128)S(1)} %bitcast.33, f32[16,32,128]{2,1,0:T(8,128)S(1)} %get-tuple-element.33.direction_ref, f32[16,32,128]{2,1,0:T(8,128)S(1)} %get-tuple-element.28.block_ref.first_ref, ...), custom_call_target="tpu_custom_call" | custom-call | tf_op jit(solution)/shard_map/update/pallas_call | solution.py:775
  (14 shorter events, 0.0 us)
Async XLA Ops:
  0.6 55.8 %copy-start.12 = (f32[2,8]{1,0:T(2,128)S(1)}, f32[2,8]{1,0:T(2,128)}, u32[]{:S(2)}) copy-start(f32[2,8]{1,0:T(2,128)} %constant.15.clone.table_ref) | copy-start | bytes 196
  0.6 22.3 %copy-start.2 = (f32[16,32,128]{2,1,0:T(8,128)S(1)}, f32[16,32,128]{2,1,0:T(8,128)}, u32[]{:S(2)}) copy-start(f32[16,32,128]{2,1,0:T(8,128)} %absorption_ref.9) | copy-start | bytes 786436
  0.7 22.3 %copy-start.3 = (f32[16,32,128]{2,1,0:T(8,128)S(1)}, f32[16,32,128]{2,1,0:T(8,128)}, u32[]{:S(2)}) copy-start(f32[16,32,128]{2,1,0:T(8,128)} %source_ref.5) | copy-start | bytes 786436
  0.7 49.3 %copy-start.6 = (f32[32,4096]{1,0:T(8,128)S(1)}, f32[32,4096]{1,0:T(8,128)}, u32[]{:S(2)}) copy-start(f32[32,4096]{1,0:T(8,128)} %inverse_ref.3) | copy-start | bytes 1572868
  7.6 11.0 %collective-permute-start = (f32[64,16,128]{2,1,0:T(8,128)}, f32[64,16,128]{2,1,0:T(8,128)S(1)}, u32[]{:S(2)}, u32[]{:S(2)}) collective-permute-start(f32[64,16,128]{2,1,0:T(8,128)} %get-tuple-element.21), channel_id=1, source_target_pairs={{0,16},{16,32},{32,48},{48,64},{64,80},{80,96},{96,112},{1,17},{17... | collective-permute-start | bytes 1572872 | tf_op jit(solution)/shard_map/ppermute | solution.py:52
  12.2 10.7 %collective-permute-start.1 = (f32[64,16,128]{2,1,0:T(8,128)}, f32[64,16,128]{2,1,0:T(8,128)S(1)}, u32[]{:S(2)}, u32[]{:S(2)}) collective-permute-start(f32[64,16,128]{2,1,0:T(8,128)} %get-tuple-element.22), channel_id=1, source_target_pairs={{16,0},{32,16},{48,32},{64,48},{80,64},{96,80},{112,96},{17,1},{33... | collective-permute-start | bytes 1572872 | tf_op jit(solution)/shard_map/ppermute | solution.py:52
  23.0 0.8 copy-start.10
  23.8 0.8 copy-start.11
  25.4 31.0 %collective-permute-start.2 = (f32[6,64,128]{2,1,0:T(8,128)S(1)}, f32[6,64,128]{2,1,0:T(8,128)S(1)}, u32[]{:S(2)}, u32[]{:S(2)}) collective-permute-start(f32[6,64,128]{2,1,0:T(8,128)S(1)} %get-tuple-element.25), channel_id=1, source_target_pairs={{0,1},{1,2},{2,3},{3,4},{4,5},{5,6},{6,7},{7,8},{8,9},{9,10},{10,1... | collective-permute-start | bytes 589832 | tf_op jit(solution)/shard_map/ppermute | solution.py:52
  28.9 27.5 %collective-permute-start.3 = (f32[6,64,128]{2,1,0:T(8,128)S(1)}, f32[6,64,128]{2,1,0:T(8,128)S(1)}, u32[]{:S(2)}, u32[]{:S(2)}) collective-permute-start(f32[6,64,128]{2,1,0:T(8,128)S(1)} %get-tuple-element.26), channel_id=1, source_target_pairs={{1,0},{2,1},{3,2},{4,3},{5,4},{6,5},{7,6},{8,7},{9,8},{10,9},{11,1... | collective-permute-start | bytes 589832 | tf_op jit(solution)/shard_map/ppermute | solution.py:52
  30.2 19.7 %all-to-all-start = ((f32[128,1,128]{2,1,0:T(1,128)}), f32[128,1,128]{2,1,0:T(1,128)S(1)}, u32[]{:S(2)}, u32[]{:S(2)}) async-start(f32[128,1,128]{2,1,0:T(1,128)} %bitcast.37), calls=%async_computation | async-start | bytes 131072 | tf_op jit(solution)/shard_map/all_to_all | solution.py:56
  51.8 20.4 %all-to-all-start.1 = ((f32[128,1,128]{2,1,0:T(1,128)}), f32[128,1,128]{2,1,0:T(1,128)S(1)}, u32[]{:S(2)}, u32[]{:S(2)}) async-start(f32[128,1,128]{2,1,0:T(1,128)} %bitcast.6), calls=%async_computation.1 | async-start | bytes 131072 | tf_op jit(solution)/shard_map/all_to_all | solution.py:56
  72.2 2.2 %copy-start = (bf16[32,16,32,128]{3,2,1,0:T(8,128)(2,1)S(1)}, bf16[32,16,32,128]{3,2,1,0:T(8,128)(2,1)}, u32[]{:S(2)}) copy-start(bf16[32,16,32,128]{3,2,1,0:T(8,128)(2,1)} %basis_hbm.3) | copy-start | bytes 12582916
  81.4 0.6 copy-start.9
  82.0 15.4 %collective-permute-start.4 = (f32[16,16,128]{2,1,0:T(8,128)}, f32[16,16,128]{2,1,0:T(8,128)S(1)}, u32[]{:S(2)}, u32[]{:S(2)}) collective-permute-start(f32[16,16,128]{2,1,0:T(8,128)} %get-tuple-element.29), channel_id=1, source_target_pairs={{0,16},{16,32},{32,48},{48,64},{64,80},{80,96},{96,112},{1,17},{17... | collective-permute-start | bytes 393224 | tf_op jit(solution)/shard_map/ppermute | solution.py:52
  85.5 11.8 %collective-permute-start.5 = (f32[16,16,128]{2,1,0:T(8,128)}, f32[16,16,128]{2,1,0:T(8,128)}, u32[]{:S(2)}, u32[]{:S(2)}) collective-permute-start(f32[16,16,128]{2,1,0:T(8,128)} %get-tuple-element.30), channel_id=1, source_target_pairs={{16,0},{32,16},{48,32},{64,48},{80,64},{96,80},{112,96},{17,1},{33... | collective-permute-start | bytes 393224 | tf_op jit(solution)/shard_map/ppermute | solution.py:52
  87.4 19.4 %all-to-all-start.2 = ((f32[128,1,128]{2,1,0:T(1,128)}), f32[128,1,128]{2,1,0:T(1,128)S(1)}, u32[]{:S(2)}, u32[]{:S(2)}) async-start(f32[128,1,128]{2,1,0:T(1,128)} %bitcast.35), calls=%async_computation.2 | async-start | bytes 131072 | tf_op jit(solution)/shard_map/all_to_all | solution.py:56
  99.3 19.3 %collective-permute-start.6 = (f32[2,64,128]{2,1,0:T(8,128)}, f32[2,64,128]{2,1,0:T(8,128)}, u32[]{:S(2)}, u32[]{:S(2)}) collective-permute-start(f32[2,64,128]{2,1,0:T(8,128)} %get-tuple-element.31), channel_id=1, source_target_pairs={{0,1},{1,2},{2,3},{3,4},{4,5},{5,6},{6,7},{7,8},{8,9},{9,10},{10,1... | collective-permute-start | bytes 196616 | tf_op jit(solution)/shard_map/ppermute | solution.py:52
  103.3 15.2 %collective-permute-start.7 = (f32[2,64,128]{2,1,0:T(8,128)}, f32[2,64,128]{2,1,0:T(8,128)}, u32[]{:S(2)}, u32[]{:S(2)}) collective-permute-start(f32[2,64,128]{2,1,0:T(8,128)} %get-tuple-element.32), channel_id=1, source_target_pairs={{1,0},{2,1},{3,2},{4,3},{5,4},{6,5},{7,6},{8,7},{9,8},{10,9},{11,1... | collective-permute-start | bytes 196616 | tf_op jit(solution)/shard_map/ppermute | solution.py:52
  106.8 1.0 copy-start.7
  109.1 0.6 copy-start.8
  109.7 25.9 %all-to-all-start.3 = ((f32[128,1,128]{2,1,0:T(1,128)}), f32[128,1,128]{2,1,0:T(1,128)}, u32[]{:S(2)}, u32[]{:S(2)}) async-start(f32[128,1,128]{2,1,0:T(1,128)} %bitcast.34), calls=%async_computation.3 | async-start | bytes 131072 | tf_op jit(solution)/shard_map/all_to_all | solution.py:56
  134.7 0.9 copy-start.4
  135.7 2.2 %copy-start.1 = (bf16[32,16,32,128]{3,2,1,0:T(8,128)(2,1)S(1)}, bf16[32,16,32,128]{3,2,1,0:T(8,128)(2,1)}, u32[]{:S(2)}) copy-start(bf16[32,16,32,128]{3,2,1,0:T(8,128)(2,1)} %basis_hbm.3) | copy-start | bytes 12582916
  137.8 1.1 copy-start.5

commit v5 on v4

--- a/solution.py
+++ b/solution.py
@@ -22,7 +22,7 @@
 vertical = 2.0
 theta = 0.5 * (highest_rate + lowest_rate)
 delta = 0.5 * (highest_rate - lowest_rate)
-VMEM_LIMIT = 30 * 1024 * 1024
+VMEM_LIMIT = 24 * 1024 * 1024
 FIRST_LIMIT = 58 * 1024 * 1024
 
 
@@ -70,7 +70,7 @@
 
 def first_kernel(
     field_ref, coefficient_ref, basis_ref, slots_ref, margin_ref,
-    out_ref, ahead_ref, behind_ref, left_ref, right_ref, sums_ref, edges_ref,
+    out_ref, ahead_ref, behind_ref, sides_ref, sums_ref, edges_ref,
 ):
     step = pl.program_id(0)
     group = basis_ref.shape[0]
@@ -133,15 +133,15 @@
                 value = edges_ref[z * ROWS : (z + 1) * ROWS]
                 left = jnp.where(place == q, roll(value, VECTORS * q), left)
                 right = jnp.where(place == q, roll(value, VECTORS * (q - 1)), right)
-            left_ref[n] = left
-            right_ref[n] = right
+            sides_ref[n] = left
+            sides_ref[LEVELS // 4 + n] = right
 
 
 def first_projection(field, coefficient, basis, slots, margin):
     group = 8
     rows = 2 * LEVELS + VECTORS
     edge_rows = jax.ShapeDtypeStruct((rows, LEVELS, COLS), jnp.float32)
-    edge_cols = jax.ShapeDtypeStruct((LEVELS // 4, ROWS, COLS), jnp.float32)
+    edge_cols = jax.ShapeDtypeStruct((LEVELS // 2, ROWS, COLS), jnp.float32)
     block_spec = pl.BlockSpec((LEVELS, ROWS, COLS), lambda i: (0, 0, 0))
     rows_spec = pl.BlockSpec(edge_rows.shape, lambda i: (0, 0, 0))
     cols_spec = pl.BlockSpec(edge_cols.shape, lambda i: (0, 0, 0))
@@ -155,8 +155,8 @@
             pl.BlockSpec(slots.shape, lambda i: (0, 0, 0)),
             pl.BlockSpec(margin.shape, lambda i: (0, 0)),
         ],
-        out_specs=[pl.BlockSpec((COLS, COLS), lambda i: (0, 0)), rows_spec, rows_spec, cols_spec, cols_spec],
-        out_shape=[jax.ShapeDtypeStruct((COLS, COLS), jnp.float32), edge_rows, edge_rows, edge_cols, edge_cols],
+        out_specs=[pl.BlockSpec((COLS, COLS), lambda i: (0, 0)), rows_spec, rows_spec, cols_spec],
+        out_shape=[jax.ShapeDtypeStruct((COLS, COLS), jnp.float32), edge_rows, edge_rows, edge_cols],
         scratch_shapes=[
             pltpu.VMEM((VECTORS, COLS), jnp.float32), pltpu.VMEM((LEVELS * ROWS, COLS), jnp.float32)
         ],
@@ -214,15 +214,15 @@
 
 
 def first_pack_kernel(
-    source_ref, absorption_ref, low_ref, high_ref, left_ref, right_ref, forward_ref, backward_ref
+    told_ref, source_ref, absorption_ref, low_ref, high_ref, sides_ref, forward_ref, backward_ref
 ):
     for f, block in enumerate((source_ref, absorption_ref)):
         pack_strips(((low_ref, LEVELS * f), (block, 0), (high_ref, LEVELS * f)), forward_ref, backward_ref, 2 * f)
     for n in range(LEVELS // 8):
         for half in range(2):
             rows = slice(half * ROWS, (half + 1) * ROWS)
-            forward_ref[4 + n, rows, :] = right_ref[2 * n + half]
-            backward_ref[4 + n, rows, :] = left_ref[2 * n + half]
+            forward_ref[4 + n, rows, :] = sides_ref[LEVELS // 4 + 2 * n + half]
+            backward_ref[4 + n, rows, :] = sides_ref[2 * n + half]
 
 
 def pack_kernel(block_ref, low_ref, high_ref, forward_ref, backward_ref):
@@ -505,7 +505,7 @@
             scratch(LEVELS, *wide), scratch(LEVELS, *thin),
         ],
         compiler_params=pltpu.CompilerParams(vmem_limit_bytes=VMEM_LIMIT),
-        cost_estimate=pl.CostEstimate(flops=60000000, bytes_accessed=4000000, transcendentals=0),
+        cost_estimate=pl.CostEstimate(flops=2000000, bytes_accessed=54000000, transcendentals=0),
         name="smoother",
     )(place, table, told, block, low, high, *strips, absorption, *more)
 
@@ -529,14 +529,8 @@
     return jnp.sum(found, axis=0, keepdims=True)
 
 
-def add_coarse(place, told_ref, coarse_ref, basis_hbm, basis_ref, sems, low_ref, high_ref, left_ref, right_ref, at, sum_ref, x,
+def add_coarse(place, told_ref, coarse_ref, basis_ref, low_ref, high_ref, left_ref, right_ref, at, sum_ref, x,
                own_c, edge_c, ring_ref, side_ref):
-    def part(q):
-        levels = pl.ds(q * 4, 4)
-        return pltpu.make_async_copy(basis_hbm.at[:, levels], basis_ref.at[:, levels], sems.at[q])
-
-    for q in range(LEVELS // 4):
-        part(q).start()
     turned = coarse_ref[...].T[:VECTORS]
     row = coarse_at(turned, slots_of(place, told_ref, ((0, 0), (-1, 0), (1, 0), (0, -1))))
     other = coarse_at(turned, slots_of(place, told_ref, ((0, 1),)))
@@ -579,11 +573,7 @@
             x[here, t, COLS : 2 * COLS] = sum_ref[z, t, COLS : 2 * COLS] + value
         return carry
 
-    def levels(q, carry):
-        part(q).wait()
-        return lax.fori_loop(4 * q, 4 * q + 4, level, carry)
-
-    lax.fori_loop(0, LEVELS // 4, levels, 0)
+    lax.fori_loop(0, LEVELS, level, 0, unroll=2)
     zero = jnp.zeros((ROWS, COLS), jnp.float32)
     x[0, 8 : 8 + ROWS, 0:COLS] = zero
     x[PLANES - 1, 8 : 8 + ROWS, 0:COLS] = zero
@@ -615,11 +605,11 @@
 
 
 def first_coarse_kernel(
-    place_ref, told_ref, coarse_ref, basis_hbm, low_ref, high_ref, left_ref, right_ref, sum_ref, source_ref, absorption_ref,
-    direction_ref, image_ref, ahead_ref, behind_ref, out_ref, x, own_c, edge_c, ring_ref, side_ref, basis_ref, sems, sums_ref,
+    place_ref, told_ref, coarse_ref, basis_ref, low_ref, high_ref, left_ref, right_ref, sum_ref, source_ref, absorption_ref,
+    direction_ref, image_ref, ahead_ref, behind_ref, out_ref, x, own_c, edge_c, ring_ref, side_ref, sums_ref,
 ):
     place = Place(place_ref, told_ref)
-    row = add_coarse(place, told_ref, coarse_ref, basis_hbm, basis_ref, sems, low_ref, high_ref, left_ref, right_ref, 4, sum_ref, x,
+    row = add_coarse(place, told_ref, coarse_ref, basis_ref, low_ref, high_ref, left_ref, right_ref, 4, sum_ref, x,
                      own_c, edge_c, ring_ref, side_ref)
     zero = jnp.zeros((8, COLS), jnp.float32)
 
@@ -638,7 +628,7 @@
             curve = curve + now * image
         return weight, curve
 
-    weight, curve = lax.fori_loop(0, LEVELS, images, (zero, zero))
+    weight, curve = lax.fori_loop(0, LEVELS, images, (zero, zero), unroll=2)
     half = VECTORS // 2
     for part in range(2):
 
@@ -661,12 +651,12 @@
 
 
 def second_coarse_kernel(
-    place_ref, told_ref, coarse_ref, basis_hbm, low_ref, high_ref, left_ref, right_ref, sum_ref, source_ref, absorption_ref,
+    place_ref, told_ref, coarse_ref, basis_ref, low_ref, high_ref, left_ref, right_ref, sum_ref, source_ref, absorption_ref,
     again_ref, first_sum_ref, direction_ref, first_ref,
-    residual_ref, precond_ref, image_ref, out_ref, x, own_c, edge_c, ring_ref, side_ref, basis_ref, sems,
+    residual_ref, precond_ref, image_ref, out_ref, x, own_c, edge_c, ring_ref, side_ref,
 ):
     place = Place(place_ref, told_ref)
-    row = add_coarse(place, told_ref, coarse_ref, basis_hbm, basis_ref, sems, low_ref, high_ref, left_ref, right_ref, 4, sum_ref, x,
+    row = add_coarse(place, told_ref, coarse_ref, basis_ref, low_ref, high_ref, left_ref, right_ref, 4, sum_ref, x,
                      own_c, edge_c, ring_ref, side_ref)
     weight0, curve0 = scalars(again_ref)
     step = weight0 / curve0
@@ -690,7 +680,7 @@
             cross = cross + (precond * first + direction * image)
         return weight, own, cross
 
-    weight, own, cross = lax.fori_loop(0, LEVELS, images, (zero, zero, zero))
+    weight, own, cross = lax.fori_loop(0, LEVELS, images, (zero, zero, zero), unroll=2)
     mine = pl.ds(place.index(0, 0), 1)
     lane = iota((1, COLS), 1)
     again = again_ref[mine, :]
@@ -716,7 +706,7 @@
         r_ref[z] = residual_ref[z] - step1 * (image_ref[z] + ratio * first_ref[z])
         return carry
 
-    lax.fori_loop(0, LEVELS, level, 0)
+    lax.fori_loop(0, LEVELS, level, 0, unroll=4)
 
 
 def shards(source, absorption, basis, coarse_inverse, margin_width, coarse_slot):
@@ -724,7 +714,6 @@
     slab = jax.ShapeDtypeStruct((LEVELS, EDGE, COLS), jnp.float32)
     message = jax.ShapeDtypeStruct((COLS, COLS), jnp.float32)
     params = pltpu.CompilerParams(vmem_limit_bytes=VMEM_LIMIT)
-    hbm = pl.BlockSpec(memory_space=pltpu.HBM)
 
     def scratch(*shape):
         return pltpu.VMEM(shape, jnp.float32)
@@ -732,27 +721,26 @@
     coarse_scratch = [
         scratch(PLANES, INNER, 2 * COLS), scratch(VECTORS, COLS), scratch(2 * VECTORS, COLS),
         scratch(2, LEVELS, COLS), scratch(2, 2 * TALL, COLS),
-        pltpu.VMEM(basis.shape, basis.dtype), pltpu.SemaphoreType.DMA((LEVELS // 4,)),
     ]
     place = jnp.stack(
         [lax.axis_index("gx"), lax.axis_index("gy"), lax.axis_size("gx"), lax.axis_size("gy")]
     ).astype(jnp.int32)
     table = jnp.array(list(zip(*chebyshev_table())), jnp.float32)
-    rows, ahead, behind, left_edge, right_edge = first_projection(
+    rows, ahead, behind, sides = first_projection(
         source, absorption, basis, coarse_slot, margin_width
     )
     low, high = exchange(ahead, behind, "gx")
     told = everyone(rows)
-    fields = [VMEM_SPEC] * 2 + [FIELDS_SPEC] * 2 + [VMEM_SPEC] * 2
+    fields = [pl.BlockSpec(memory_space=pltpu.HBM)] + [VMEM_SPEC] * 2 + [FIELDS_SPEC] * 2 + [VMEM_SPEC]
     strips = exchange(
-        *pack(first_pack_kernel, fields, 6, source, absorption, low, high, left_edge, right_edge), "gy"
+        *pack(first_pack_kernel, fields, 6, told, source, absorption, low, high, sides), "gy"
     )
     coarse = everyone(solve_rows(told, told, coarse_inverse))
     first_sum = smooth(place, table, told, source, low, high, strips, absorption)
     edges = (low, high, *strips)
     direction, image, ahead, behind, rows = pl.pallas_call(
         first_coarse_kernel,
-        in_specs=[SMEM_SPEC] + [VMEM_SPEC] * 2 + [hbm] + [VMEM_SPEC] * 7,
+        in_specs=[SMEM_SPEC] + [VMEM_SPEC] * 10,
         out_shape=[block, block, slab, slab, message],
         scratch_shapes=coarse_scratch + [scratch(VECTORS, COLS)],
         compiler_params=params,
@@ -765,7 +753,7 @@
     second_sum = smooth(place, table, told, image, low_w, high_w, strips_w, absorption, edges)
     residual, precond, precond_image, rows = pl.pallas_call(
         second_coarse_kernel,
-        in_specs=[SMEM_SPEC] + [VMEM_SPEC] * 2 + [hbm] + [VMEM_SPEC] * 11,
+        in_specs=[SMEM_SPEC] + [VMEM_SPEC] * 14,
         out_shape=[block, block, block, message],
         scratch_shapes=coarse_scratch,
         compiler_params=params,

time: 168 us -> 153 us (0.911)
  blocking collectives: 19.1 us -> 39.1 us
  waiting for transfers between devices: 20.5 us -> 2.29 us
  starting transfers between devices: 55.6 us -> 47.4 us
  Pallas kernels: 59.7 us -> 52.2 us
    all_to_all x1 -> x2, blocking collectives: 19.1 us -> 39.1 us  [everyone(): return lax.all_to_all(rows, AXES, 0, 0, tiled=True)]
    all_to_all x4 -> x3, waiting for transfers between devices: 11.7 us -> 2.27 us  [everyone(): return lax.all_to_all(rows, AXES, 0, 0, tiled=True)]
    all_to_all x4 -> x3, starting transfers between devices: 33.5 us -> 26.4 us  [everyone(): return lax.all_to_all(rows, AXES, 0, 0, tiled=True)]
    ppermute x4, waiting for transfers between devices: 4.5 us -> 0.01 us  [exchange(): lax.ppermute(forward_value, axis, forward)]
    ppermute x4, waiting for transfers between devices: 4.3 us -> 0.01 us  [exchange(): lax.ppermute(backward_value, axis, backward)]
    pallas_call x2, Pallas kernels: 31.9 us -> 28.9 us  [smooth(): pl.pallas_call(functools.partial(smooth_kernel, not more), grid=(1,), in_...]
    pallas_call x1, Pallas kernels: 6.02 us -> 4.31 us  [shards(): pl.pallas_call(second_coarse_kernel, in_specs=[SMEM_SPEC] + [VMEM_SPEC] *...]
    unnamed x26 -> x24, local copies, waits for them, and re-layouts: 10.4 us -> 9.61 us
  transfers between devices with their start and end apart: 12 -> 11, of which waited for: 4 -> 1; matrix products, arithmetic and copies ran while one was open for 0% -> 0% of each run, Pallas kernels for 22% -> 22%
where the time goes in v5:
time: 153 us; the launch traced here: 152 us
  Pallas kernels  52.2 us (34%)
  starting transfers between devices  47.4 us (31%)
  blocking collectives  39.1 us (26%)
  local copies, waits for them, and re-layouts  9.61 us (6%)
  waiting for transfers between devices  2.29 us (1%)
  between operations  1.62 us (1%)
    all_to_all x2, blocking collectives, everyone(): return lax.all_to_all(rows, AXES, 0, 0, tiled=True)  39.1 us
    pallas_call x2, Pallas kernels, smooth(): pl.pallas_call(functools.partial(smooth_kernel, not more), grid=(1,), in_...  28.9 us
    all_to_all x3, starting transfers between devices, everyone(): return lax.all_to_all(rows, AXES, 0, 0, tiled=True)  26.4 us
    ppermute x4, starting transfers between devices, exchange(): lax.ppermute(forward_value, axis, forward)  14.6 us
    unnamed x24, local copies, waits for them, and re-layouts  9.61 us
    ppermute x4, starting transfers between devices, exchange(): lax.ppermute(backward_value, axis, backward)  6.41 us
    pallas_call x1, Pallas kernels, first_projection(): pl.pallas_call(first_kernel, grid=(VECTORS // group,), in_specs=[block_sp...  6.23 us
    pallas_call x1, Pallas kernels, shards(): pl.pallas_call(first_coarse_kernel, in_specs=[SMEM_SPEC] + [VMEM_SPEC] *...  5.35 us
  transfers between devices with their start and end apart: 11, of which 1 were waited for; matrix products, arithmetic and copies ran while one was open for 0% of the time, Pallas kernels for 22%

profile of v5, /device:TPU:1, one launch (start us, length us, event | category | flops | bytes accessed | tf_op | source)
XLA Modules:
  0.0 152.3 jit_solution(15784078170414765106)
XLA Ops:
  0.6 0.0 copy-start.11
  0.7 0.0 copy-start.6
  1.4 6.2 %first_projection.1 = (f32[128,128]{1,0:T(8,128)}, f32[64,16,128]{2,1,0:T(8,128)}, f32[64,16,128]{2,1,0:T(8,128)}, f32[8,32,128]{2,1,0:T(8,128)}) custom-call(f32[16,32,128]{2,1,0:T(8,128)} %source_ref.5, f32[16,32,128]{2,1,0:T(8,128)} %absorption_ref.9, bf16[32,16,32,128]{3,2,1,0:T(8,128)(2,1)} %basis_ref.5, s32[1,1,32]{2,1,0:T(1,128)} %slots_ref.1, ...), custom_call_target="tpu_custom_call" | custom-call | tf_op jit(solution)/shard_map/first_projection/pallas_call | solution.py:148
  7.6 4.6 %collective-permute-start = (f32[64,16,128]{2,1,0:T(8,128)}, f32[64,16,128]{2,1,0:T(8,128)S(1)}, u32[]{:S(2)}, u32[]{:S(2)}) collective-permute-start(f32[64,16,128]{2,1,0:T(8,128)} %get-tuple-element.20), channel_id=1, source_target_pairs={{0,16},{16,32},{32,48},{48,64},{64,80},{80,96},{96,112},{1,17},{17... | collective-permute-start | bytes 1572872 | tf_op jit(solution)/shard_map/ppermute | solution.py:52
  12.2 1.9 %collective-permute-start.1 = (f32[64,16,128]{2,1,0:T(8,128)}, f32[64,16,128]{2,1,0:T(8,128)S(1)}, u32[]{:S(2)}, u32[]{:S(2)}) collective-permute-start(f32[64,16,128]{2,1,0:T(8,128)} %get-tuple-element.21), channel_id=1, source_target_pairs={{16,0},{32,16},{48,32},{64,48},{80,64},{96,80},{112,96},{17,1},{33... | collective-permute-start | bytes 1572872 | tf_op jit(solution)/shard_map/ppermute | solution.py:52
  14.2 20.0 %all_to_all.55 = f32[128,1,128]{2,1,0:T(1,128)S(1)} all-to-all(f32[128,1,128]{2,1,0:T(1,128)} %bitcast.38), channel_id=1, replica_groups=mesh['gx'=8,'gy'=16] {'gx','gy'}, dimensions={0} | all-to-all | bytes 131072 | tf_op jit(solution)/shard_map/all_to_all | solution.py:56
  34.2 0.0 collective-permute-done.low_ref.refs_0_
  34.2 0.0 collective-permute-done.1.high_ref.refs_1_
  34.2 0.0 copy-start.9
  34.2 0.9 copy-done.9
  35.1 0.7 strips.2
  35.9 2.5 %collective-permute-start.2 = (f32[6,64,128]{2,1,0:T(8,128)S(1)}, f32[6,64,128]{2,1,0:T(8,128)S(1)}, u32[]{:S(2)}, u32[]{:S(2)}) collective-permute-start(f32[6,64,128]{2,1,0:T(8,128)S(1)} %get-tuple-element.23), channel_id=1, source_target_pairs={{0,1},{1,2},{2,3},{3,4},{4,5},{5,6},{6,7},{7,8},{8,9},{9,10},{10,1... | collective-permute-start | bytes 589832 | tf_op jit(solution)/shard_map/ppermute | solution.py:52
  38.3 1.3 collective-permute-start.3
  39.6 1.8 %coarse_rows.2 = f32[128,128]{1,0:T(8,128)} custom-call(f32[128,128]{1,0:T(8,128)S(1)} %bitcast.23, f32[128,128]{1,0:T(8,128)S(1)} %bitcast.24, f32[32,4096]{1,0:T(8,128)S(1)} %copy-done.6), custom_call_target="tpu_custom_call" | custom-call | tf_op jit(solution)/shard_map/coarse_rows/pallas_call | solution.py:251
  41.5 7.8 %all-to-all-start.1 = ((f32[128,1,128]{2,1,0:T(1,128)}), f32[128,1,128]{2,1,0:T(1,128)S(1)}, u32[]{:S(2)}, u32[]{:S(2)}) async-start(f32[128,1,128]{2,1,0:T(1,128)} %bitcast.6), calls=%async_computation.1 | async-start | bytes 131072 | tf_op jit(solution)/shard_map/all_to_all | solution.py:56
  49.3 0.1 pad_add_fusion.place_ref
  49.3 0.0 collective-permute-done.2.left_ref.refs_2_
  49.3 0.0 collective-permute-done.3.right_ref.refs_3_
  49.3 14.3 %smoother.2.sum_ref.first_sum_ref = f32[16,48,256]{2,1,0:T(8,128)S(1)} custom-call(s32[4]{0:T(128)S(1)} %pad_add_fusion.place_ref, f32[2,8]{1,0:T(2,128)S(1)} %copy-done.11, f32[128,128]{1,0:T(8,128)S(1)} %bitcast.25, f32[16,32,128]{2,1,0:T(8,128)S(1)} %copy-done.3, f32[64,16,128]{2,1,0:T(8,128)S(1)} %collective-permute-done.low_ref.refs_0_, ...), custom_call_target="tpu_custom_call" | custom-call | flops 2000000 | bytes 54000000 | tf_op jit(solution)/shard_map/smoother/pallas_call | solution.py:495
  63.6 0.0 all-to-all-done.1
  63.6 0.0 copy-start
  63.6 2.2 %copy-done = bf16[32,16,32,128]{3,2,1,0:T(8,128)(2,1)S(1)} copy-done((bf16[32,16,32,128]{3,2,1,0:T(8,128)(2,1)S(1)}, bf16[32,16,32,128]{3,2,1,0:T(8,128)(2,1)}, u32[]{:S(2)}) %copy-start) | copy-done | bytes 4194328
  65.8 5.3 %direction_and_image.1 = (f32[16,32,128]{2,1,0:T(8,128)S(1)}, f32[16,32,128]{2,1,0:T(8,128)S(1)}, f32[16,16,128]{2,1,0:T(8,128)}, f32[16,16,128]{2,1,0:T(8,128)}, f32[128,128]{1,0:T(8,128)S(1)}) custom-call(s32[4]{0:T(128)S(1)} %pad_add_fusion.place_ref, f32[128,128]{1,0:T(8,128)S(1)} %bitcast.26, f32[128,128]{1,0:T(8,128)S(1)} %bitcast.33, ...), custom_call_target="tpu_custom_call" | custom-call | tf_op jit(solution)/shard_map/direction_and_image/pallas_call | solution.py:741
  71.2 0.6 copy-done.10
  71.8 3.5 %collective-permute-start.4 = (f32[16,16,128]{2,1,0:T(8,128)}, f32[16,16,128]{2,1,0:T(8,128)S(1)}, u32[]{:S(2)}, u32[]{:S(2)}) collective-permute-start(f32[16,16,128]{2,1,0:T(8,128)} %get-tuple-element.27), channel_id=1, source_target_pairs={{0,16},{16,32},{32,48},{48,64},{64,80},{80,96},{96,112},{1,17},{17... | collective-permute-start | bytes 393224 | tf_op jit(solution)/shard_map/ppermute | solution.py:52
  75.3 1.9 %collective-permute-start.5 = (f32[16,16,128]{2,1,0:T(8,128)}, f32[16,16,128]{2,1,0:T(8,128)}, u32[]{:S(2)}, u32[]{:S(2)}) collective-permute-start(f32[16,16,128]{2,1,0:T(8,128)} %get-tuple-element.28), channel_id=1, source_target_pairs={{16,0},{32,16},{48,32},{64,48},{80,64},{96,80},{112,96},{17,1},{33... | collective-permute-start | bytes 393224 | tf_op jit(solution)/shard_map/ppermute | solution.py:52
  77.2 9.9 %all-to-all-start.2 = ((f32[128,1,128]{2,1,0:T(1,128)}), f32[128,1,128]{2,1,0:T(1,128)S(1)}, u32[]{:S(2)}, u32[]{:S(2)}) async-start(f32[128,1,128]{2,1,0:T(1,128)} %bitcast.36), calls=%async_computation.2 | async-start | bytes 131072 | tf_op jit(solution)/shard_map/all_to_all | solution.py:56
  87.1 0.0 collective-permute-done.4.low_ref
  87.1 0.0 collective-permute-done.5.high_ref
  87.1 1.9 %strips.3 = (f32[2,64,128]{2,1,0:T(8,128)}, f32[2,64,128]{2,1,0:T(8,128)}) custom-call(f32[16,32,128]{2,1,0:T(8,128)S(1)} %get-tuple-element.26.block_ref.first_ref, f32[16,16,128]{2,1,0:T(8,128)S(1)} %collective-permute-done.4.low_ref, f32[16,16,128]{2,1,0:T(8,128)} %collective-permute-done.5.high_ref), custom_call_target="tpu_custom_call" | custom-call | flops 2000000 | bytes 2000000 | tf_op jit(solution)/shard_map/strips/pallas_call | solution.py:239
  89.1 4.0 %collective-permute-start.6 = (f32[2,64,128]{2,1,0:T(8,128)}, f32[2,64,128]{2,1,0:T(8,128)}, u32[]{:S(2)}, u32[]{:S(2)}) collective-permute-start(f32[2,64,128]{2,1,0:T(8,128)} %get-tuple-element.29), channel_id=1, source_target_pairs={{0,1},{1,2},{2,3},{3,4},{4,5},{5,6},{6,7},{7,8},{8,9},{9,10},{10,1... | collective-permute-start | bytes 196616 | tf_op jit(solution)/shard_map/ppermute | solution.py:52
  93.1 1.3 collective-permute-start.7
  94.4 2.3 %all-to-all-done.2 = f32[128,1,128]{2,1,0:T(1,128)S(1)} async-done(((f32[128,1,128]{2,1,0:T(1,128)}), f32[128,1,128]{2,1,0:T(1,128)S(1)}, u32[]{:S(2)}, u32[]{:S(2)}) %all-to-all-start.2) | async-done | bytes 65568 | tf_op jit(solution)/shard_map/all_to_all | solution.py:56
  96.6 1.0 copy-done.7
  97.7 1.2 coarse_rows.3
  98.9 0.0 copy-start.8
  98.9 0.6 copy-done.8
  99.5 8.8 %all-to-all-start.3 = ((f32[128,1,128]{2,1,0:T(1,128)}), f32[128,1,128]{2,1,0:T(1,128)}, u32[]{:S(2)}, u32[]{:S(2)}) async-start(f32[128,1,128]{2,1,0:T(1,128)} %bitcast.35), calls=%async_computation.3 | async-start | bytes 131072 | tf_op jit(solution)/shard_map/all_to_all | solution.py:56
  108.3 0.0 collective-permute-done.6.left_ref
  108.3 0.0 collective-permute-done.7.right_ref
  108.4 14.7 %smoother.3.sum_ref = f32[16,48,256]{2,1,0:T(8,128)S(1)} custom-call(s32[4]{0:T(128)S(1)} %pad_add_fusion.place_ref, f32[2,8]{1,0:T(2,128)S(1)} %copy-done.11, f32[128,128]{1,0:T(8,128)S(1)} %bitcast.28, f32[16,32,128]{2,1,0:T(8,128)S(1)} %get-tuple-element.26.block_ref.first_ref, f32[16,16,128]{2,1,0:T(8,128)S(1)} %collective-permute-done.4.low_ref, ...), custom_call_target="tpu_custom_call" | custom-call | flops 2000000 | bytes 54000000 | tf_op jit(solution)/shard_map/smoother/pallas_call | solution.py:495
  123.0 0.9 copy-done.4
  123.9 0.0 all-to-all-done.3
  123.9 2.2 %copy-done.1 = bf16[32,16,32,128]{3,2,1,0:T(8,128)(2,1)S(1)} copy-done((bf16[32,16,32,128]{3,2,1,0:T(8,128)(2,1)S(1)}, bf16[32,16,32,128]{3,2,1,0:T(8,128)(2,1)}, u32[]{:S(2)}) %copy-start.1) | copy-done | bytes 4194328
  126.1 1.1 copy-done.5
  127.3 4.3 %second_images.1 = (f32[16,32,128]{2,1,0:T(8,128)S(1)}, f32[16,32,128]{2,1,0:T(8,128)S(1)}, f32[16,32,128]{2,1,0:T(8,128)S(1)}, f32[128,128]{1,0:T(8,128)S(1)}) custom-call(s32[4]{0:T(128)S(1)} %pad_add_fusion.place_ref, f32[128,128]{1,0:T(8,128)S(1)} %bitcast.29, f32[128,128]{1,0:T(8,128)} %bitcast.13.coarse_ref, bf16[32,16,32,128]{3,2,1,0:T(8,128)(2,1)S(1)} %copy-done.1, ...), custom_call_target="tpu_custom_call" | custom-call | tf_op jit(solution)/shard_map/second_images/pallas_call | solution.py:754
  131.6 19.1 %all_to_all.56 = f32[128,1,128]{2,1,0:T(1,128)S(1)} all-to-all(f32[128,1,128]{2,1,0:T(1,128)S(1)} %bitcast.37), channel_id=1, replica_groups=mesh['gx'=8,'gy'=16] {'gx','gy'}, dimensions={0} | all-to-all | bytes 131072 | tf_op jit(solution)/shard_map/all_to_all | solution.py:56
  150.7 1.7 %update.1 = (f32[16,32,128]{2,1,0:T(8,128)}, f32[16,32,128]{2,1,0:T(8,128)}) custom-call(f32[128,128]{1,0:T(8,128)S(1)} %bitcast.32, f32[128,128]{1,0:T(8,128)S(1)} %bitcast.34, f32[16,32,128]{2,1,0:T(8,128)S(1)} %get-tuple-element.31.direction_ref, f32[16,32,128]{2,1,0:T(8,128)S(1)} %get-tuple-element.26.block_ref.first_ref, ...), custom_call_target="tpu_custom_call" | custom-call | tf_op jit(solution)/shard_map/update/pallas_call | solution.py:763
  (11 shorter events, 0.0 us)
Async XLA Ops:
  0.6 48.7 %copy-start.11 = (f32[2,8]{1,0:T(2,128)S(1)}, f32[2,8]{1,0:T(2,128)}, u32[]{:S(2)}) copy-start(f32[2,8]{1,0:T(2,128)} %constant.15.clone.table_ref) | copy-start | bytes 196
  0.6 33.5 %copy-start.2 = (f32[16,32,128]{2,1,0:T(8,128)S(1)}, f32[16,32,128]{2,1,0:T(8,128)}, u32[]{:S(2)}) copy-start(f32[16,32,128]{2,1,0:T(8,128)} %absorption_ref.9) | copy-start | bytes 786436
  0.7 33.5 %copy-start.3 = (f32[16,32,128]{2,1,0:T(8,128)S(1)}, f32[16,32,128]{2,1,0:T(8,128)}, u32[]{:S(2)}) copy-start(f32[16,32,128]{2,1,0:T(8,128)} %source_ref.5) | copy-start | bytes 786436
  0.7 39.0 %copy-start.6 = (f32[32,4096]{1,0:T(8,128)S(1)}, f32[32,4096]{1,0:T(8,128)}, u32[]{:S(2)}) copy-start(f32[32,4096]{1,0:T(8,128)} %inverse_ref.3) | copy-start | bytes 1572868
  7.6 26.5 %collective-permute-start = (f32[64,16,128]{2,1,0:T(8,128)}, f32[64,16,128]{2,1,0:T(8,128)S(1)}, u32[]{:S(2)}, u32[]{:S(2)}) collective-permute-start(f32[64,16,128]{2,1,0:T(8,128)} %get-tuple-element.20), channel_id=1, source_target_pairs={{0,16},{16,32},{32,48},{48,64},{64,80},{80,96},{96,112},{1,17},{17... | collective-permute-start | bytes 1572872 | tf_op jit(solution)/shard_map/ppermute | solution.py:52
  12.2 22.0 %collective-permute-start.1 = (f32[64,16,128]{2,1,0:T(8,128)}, f32[64,16,128]{2,1,0:T(8,128)S(1)}, u32[]{:S(2)}, u32[]{:S(2)}) collective-permute-start(f32[64,16,128]{2,1,0:T(8,128)} %get-tuple-element.21), channel_id=1, source_target_pairs={{16,0},{32,16},{48,32},{64,48},{80,64},{96,80},{112,96},{17,1},{33... | collective-permute-start | bytes 1572872 | tf_op jit(solution)/shard_map/ppermute | solution.py:52
  34.2 0.9 copy-start.9
  35.9 13.5 %collective-permute-start.2 = (f32[6,64,128]{2,1,0:T(8,128)S(1)}, f32[6,64,128]{2,1,0:T(8,128)S(1)}, u32[]{:S(2)}, u32[]{:S(2)}) collective-permute-start(f32[6,64,128]{2,1,0:T(8,128)S(1)} %get-tuple-element.23), channel_id=1, source_target_pairs={{0,1},{1,2},{2,3},{3,4},{4,5},{5,6},{6,7},{7,8},{8,9},{9,10},{10,1... | collective-permute-start | bytes 589832 | tf_op jit(solution)/shard_map/ppermute | solution.py:52
  38.3 11.0 %collective-permute-start.3 = (f32[6,64,128]{2,1,0:T(8,128)S(1)}, f32[6,64,128]{2,1,0:T(8,128)S(1)}, u32[]{:S(2)}, u32[]{:S(2)}) collective-permute-start(f32[6,64,128]{2,1,0:T(8,128)S(1)} %get-tuple-element.24), channel_id=1, source_target_pairs={{1,0},{2,1},{3,2},{4,3},{5,4},{6,5},{7,6},{8,7},{9,8},{10,9},{11,1... | collective-permute-start | bytes 589832 | tf_op jit(solution)/shard_map/ppermute | solution.py:52
  41.5 22.1 %all-to-all-start.1 = ((f32[128,1,128]{2,1,0:T(1,128)}), f32[128,1,128]{2,1,0:T(1,128)S(1)}, u32[]{:S(2)}, u32[]{:S(2)}) async-start(f32[128,1,128]{2,1,0:T(1,128)} %bitcast.6), calls=%async_computation.1 | async-start | bytes 131072 | tf_op jit(solution)/shard_map/all_to_all | solution.py:56
  63.6 2.2 %copy-start = (bf16[32,16,32,128]{3,2,1,0:T(8,128)(2,1)S(1)}, bf16[32,16,32,128]{3,2,1,0:T(8,128)(2,1)}, u32[]{:S(2)}) copy-start(bf16[32,16,32,128]{3,2,1,0:T(8,128)(2,1)} %basis_ref.5) | copy-start | bytes 12582916
  71.2 0.6 copy-start.10
  71.8 15.3 %collective-permute-start.4 = (f32[16,16,128]{2,1,0:T(8,128)}, f32[16,16,128]{2,1,0:T(8,128)S(1)}, u32[]{:S(2)}, u32[]{:S(2)}) collective-permute-start(f32[16,16,128]{2,1,0:T(8,128)} %get-tuple-element.27), channel_id=1, source_target_pairs={{0,16},{16,32},{32,48},{48,64},{64,80},{80,96},{96,112},{1,17},{17... | collective-permute-start | bytes 393224 | tf_op jit(solution)/shard_map/ppermute | solution.py:52
  75.3 11.8 %collective-permute-start.5 = (f32[16,16,128]{2,1,0:T(8,128)}, f32[16,16,128]{2,1,0:T(8,128)}, u32[]{:S(2)}, u32[]{:S(2)}) collective-permute-start(f32[16,16,128]{2,1,0:T(8,128)} %get-tuple-element.28), channel_id=1, source_target_pairs={{16,0},{32,16},{48,32},{64,48},{80,64},{96,80},{112,96},{17,1},{33... | collective-permute-start | bytes 393224 | tf_op jit(solution)/shard_map/ppermute | solution.py:52
  77.2 19.4 %all-to-all-start.2 = ((f32[128,1,128]{2,1,0:T(1,128)}), f32[128,1,128]{2,1,0:T(1,128)S(1)}, u32[]{:S(2)}, u32[]{:S(2)}) async-start(f32[128,1,128]{2,1,0:T(1,128)} %bitcast.36), calls=%async_computation.2 | async-start | bytes 131072 | tf_op jit(solution)/shard_map/all_to_all | solution.py:56
  89.1 19.3 %collective-permute-start.6 = (f32[2,64,128]{2,1,0:T(8,128)}, f32[2,64,128]{2,1,0:T(8,128)}, u32[]{:S(2)}, u32[]{:S(2)}) collective-permute-start(f32[2,64,128]{2,1,0:T(8,128)} %get-tuple-element.29), channel_id=1, source_target_pairs={{0,1},{1,2},{2,3},{3,4},{4,5},{5,6},{6,7},{7,8},{8,9},{9,10},{10,1... | collective-permute-start | bytes 196616 | tf_op jit(solution)/shard_map/ppermute | solution.py:52
  93.1 15.3 %collective-permute-start.7 = (f32[2,64,128]{2,1,0:T(8,128)}, f32[2,64,128]{2,1,0:T(8,128)}, u32[]{:S(2)}, u32[]{:S(2)}) collective-permute-start(f32[2,64,128]{2,1,0:T(8,128)} %get-tuple-element.30), channel_id=1, source_target_pairs={{1,0},{2,1},{3,2},{4,3},{5,4},{6,5},{7,6},{8,7},{9,8},{10,9},{11,1... | collective-permute-start | bytes 196616 | tf_op jit(solution)/shard_map/ppermute | solution.py:52
  96.6 1.0 copy-start.7
  98.9 0.6 copy-start.8
  99.5 24.4 %all-to-all-start.3 = ((f32[128,1,128]{2,1,0:T(1,128)}), f32[128,1,128]{2,1,0:T(1,128)}, u32[]{:S(2)}, u32[]{:S(2)}) async-start(f32[128,1,128]{2,1,0:T(1,128)} %bitcast.35), calls=%async_computation.3 | async-start | bytes 131072 | tf_op jit(solution)/shard_map/all_to_all | solution.py:56
  123.0 0.9 copy-start.4
  123.9 2.2 %copy-start.1 = (bf16[32,16,32,128]{3,2,1,0:T(8,128)(2,1)S(1)}, bf16[32,16,32,128]{3,2,1,0:T(8,128)(2,1)}, u32[]{:S(2)}) copy-start(bf16[32,16,32,128]{3,2,1,0:T(8,128)(2,1)} %basis_ref.5) | copy-start | bytes 12582916
  126.1 1.1 copy-start.5

commit v6 on v5

--- a/solution.py
+++ b/solution.py
@@ -250,7 +250,7 @@
 def solve_rows(*operands):
     return pl.pallas_call(
         coarse_rows,
-        out_shape=jax.ShapeDtypeStruct((COLS, COLS), jnp.float32),
+        out_shape=pltpu.HBM((COLS, COLS), jnp.float32),
         compiler_params=pltpu.CompilerParams(vmem_limit_bytes=VMEM_LIMIT),
         name="coarse_rows",
     )(*operands)
@@ -496,7 +496,7 @@
         functools.partial(smooth_kernel, not more),
         grid=(1,),
         in_specs=specs,
-        out_shape=jax.ShapeDtypeStruct((LEVELS, INNER, 2 * COLS), jnp.float32),
+        out_shape=(pltpu.HBM if more else jax.ShapeDtypeStruct)((LEVELS, INNER, 2 * COLS), jnp.float32),
         scratch_shapes=[
             scratch(*wide), scratch(*wide), scratch(TALL, COLS),
             scratch(PLANES, *wide), scratch(PLANES, *wide), scratch(PLANES, *thin),
@@ -529,8 +529,14 @@
     return jnp.sum(found, axis=0, keepdims=True)
 
 
-def add_coarse(place, told_ref, coarse_ref, basis_ref, low_ref, high_ref, left_ref, right_ref, at, sum_ref, x,
+def add_coarse(place, told_ref, coarse_ref, basis_hbm, basis_ref, sems, low_ref, high_ref, left_ref, right_ref, at, sum_ref, x,
                own_c, edge_c, ring_ref, side_ref):
+    def part(q):
+        levels = pl.ds(q * 4, 4)
+        return pltpu.make_async_copy(basis_hbm.at[:, levels], basis_ref.at[:, levels], sems.at[q])
+
+    for q in range(LEVELS // 4):
+        part(q).start()
     turned = coarse_ref[...].T[:VECTORS]
     row = coarse_at(turned, slots_of(place, told_ref, ((0, 0), (-1, 0), (1, 0), (0, -1))))
     other = coarse_at(turned, slots_of(place, told_ref, ((0, 1),)))
@@ -573,7 +579,11 @@
             x[here, t, COLS : 2 * COLS] = sum_ref[z, t, COLS : 2 * COLS] + value
         return carry
 
-    lax.fori_loop(0, LEVELS, level, 0, unroll=2)
+    def levels(q, carry):
+        part(q).wait()
+        return lax.fori_loop(0, 2, lambda n, c: level(4 * q + 2 * n + 1, level(4 * q + 2 * n, c)), carry)
+
+    lax.fori_loop(0, LEVELS // 4, levels, 0)
     zero = jnp.zeros((ROWS, COLS), jnp.float32)
     x[0, 8 : 8 + ROWS, 0:COLS] = zero
     x[PLANES - 1, 8 : 8 + ROWS, 0:COLS] = zero
@@ -605,11 +615,11 @@
 
 
 def first_coarse_kernel(
-    place_ref, told_ref, coarse_ref, basis_ref, low_ref, high_ref, left_ref, right_ref, sum_ref, source_ref, absorption_ref,
-    direction_ref, image_ref, ahead_ref, behind_ref, out_ref, x, own_c, edge_c, ring_ref, side_ref, sums_ref,
+    place_ref, told_ref, coarse_ref, basis_hbm, low_ref, high_ref, left_ref, right_ref, sum_ref, source_ref, absorption_ref,
+    direction_ref, image_ref, ahead_ref, behind_ref, out_ref, x, own_c, edge_c, ring_ref, side_ref, basis_ref, sems, sums_ref,
 ):
     place = Place(place_ref, told_ref)
-    row = add_coarse(place, told_ref, coarse_ref, basis_ref, low_ref, high_ref, left_ref, right_ref, 4, sum_ref, x,
+    row = add_coarse(place, told_ref, coarse_ref, basis_hbm, basis_ref, sems, low_ref, high_ref, left_ref, right_ref, 4, sum_ref, x,
                      own_c, edge_c, ring_ref, side_ref)
     zero = jnp.zeros((8, COLS), jnp.float32)
 
@@ -651,12 +661,12 @@
 
 
 def second_coarse_kernel(
-    place_ref, told_ref, coarse_ref, basis_ref, low_ref, high_ref, left_ref, right_ref, sum_ref, source_ref, absorption_ref,
+    place_ref, told_ref, coarse_ref, basis_hbm, low_ref, high_ref, left_ref, right_ref, sum_ref, source_ref, absorption_ref,
     again_ref, first_sum_ref, direction_ref, first_ref,
-    residual_ref, precond_ref, image_ref, out_ref, x, own_c, edge_c, ring_ref, side_ref,
+    residual_ref, precond_ref, image_ref, out_ref, x, own_c, edge_c, ring_ref, side_ref, basis_ref, sems,
 ):
     place = Place(place_ref, told_ref)
-    row = add_coarse(place, told_ref, coarse_ref, basis_ref, low_ref, high_ref, left_ref, right_ref, 4, sum_ref, x,
+    row = add_coarse(place, told_ref, coarse_ref, basis_hbm, basis_ref, sems, low_ref, high_ref, left_ref, right_ref, 4, sum_ref, x,
                      own_c, edge_c, ring_ref, side_ref)
     weight0, curve0 = scalars(again_ref)
     step = weight0 / curve0
@@ -712,7 +722,7 @@
 def shards(source, absorption, basis, coarse_inverse, margin_width, coarse_slot):
     block = jax.ShapeDtypeStruct((LEVELS, ROWS, COLS), jnp.float32)
     slab = jax.ShapeDtypeStruct((LEVELS, EDGE, COLS), jnp.float32)
-    message = jax.ShapeDtypeStruct((COLS, COLS), jnp.float32)
+    message = pltpu.HBM((COLS, COLS), jnp.float32)
     params = pltpu.CompilerParams(vmem_limit_bytes=VMEM_LIMIT)
 
     def scratch(*shape):
@@ -721,7 +731,12 @@
     coarse_scratch = [
         scratch(PLANES, INNER, 2 * COLS), scratch(VECTORS, COLS), scratch(2 * VECTORS, COLS),
         scratch(2, LEVELS, COLS), scratch(2, 2 * TALL, COLS),
+        pltpu.VMEM(basis.shape, basis.dtype), pltpu.SemaphoreType.DMA((LEVELS // 4,)),
     ]
+    hbm = pl.BlockSpec(memory_space=pltpu.HBM)
+    def in_hbm(value):
+        return pltpu.with_memory_space_constraint(value, pltpu.HBM)
+
     place = jnp.stack(
         [lax.axis_index("gx"), lax.axis_index("gy"), lax.axis_size("gx"), lax.axis_size("gy")]
     ).astype(jnp.int32)
@@ -733,32 +748,32 @@
     told = everyone(rows)
     fields = [pl.BlockSpec(memory_space=pltpu.HBM)] + [VMEM_SPEC] * 2 + [FIELDS_SPEC] * 2 + [VMEM_SPEC]
     strips = exchange(
-        *pack(first_pack_kernel, fields, 6, told, source, absorption, low, high, sides), "gy"
+        *pack(first_pack_kernel, fields, 6, told, source, absorption, low, high, in_hbm(sides)), "gy"
     )
     coarse = everyone(solve_rows(told, told, coarse_inverse))
     first_sum = smooth(place, table, told, source, low, high, strips, absorption)
     edges = (low, high, *strips)
     direction, image, ahead, behind, rows = pl.pallas_call(
         first_coarse_kernel,
-        in_specs=[SMEM_SPEC] + [VMEM_SPEC] * 10,
+        in_specs=[SMEM_SPEC] + [VMEM_SPEC] * 2 + [hbm] + [VMEM_SPEC] * 7,
         out_shape=[block, block, slab, slab, message],
         scratch_shapes=coarse_scratch + [scratch(VECTORS, COLS)],
         compiler_params=params,
         name="direction_and_image",
-    )(place, told, coarse, basis, *edges, first_sum, source, absorption)
+    )(place, told, coarse, in_hbm(basis), *edges, first_sum, source, absorption)
     low_w, high_w = exchange(ahead, behind, "gx")
     again = everyone(rows)
     strips_w = exchange(*pack(pack_kernel, [VMEM_SPEC] * 3, 2, image, low_w, high_w), "gy")
-    coarse = everyone(solve_rows(again, told, coarse_inverse))
+    coarse = everyone(solve_rows(again, told, in_hbm(coarse_inverse)))
     second_sum = smooth(place, table, told, image, low_w, high_w, strips_w, absorption, edges)
     residual, precond, precond_image, rows = pl.pallas_call(
         second_coarse_kernel,
-        in_specs=[SMEM_SPEC] + [VMEM_SPEC] * 14,
+        in_specs=[SMEM_SPEC] + [VMEM_SPEC] * 2 + [hbm] + [VMEM_SPEC] * 11,
         out_shape=[block, block, block, message],
         scratch_shapes=coarse_scratch,
         compiler_params=params,
         name="second_images",
-    )(place, told, coarse, basis, *edges, second_sum, source, absorption, again, first_sum, direction, image)
+    )(place, told, coarse, in_hbm(basis), *edges, in_hbm(second_sum), source, absorption, again, first_sum, direction, image)
     last = everyone(rows)
     concentration, residual = pl.pallas_call(
         last_kernel, out_shape=[block, block], compiler_params=params, name="update"

time: 153 us -> 152 us (level)
  local copies, waits for them, and re-layouts: 9.61 us -> 0.02 us
  Pallas kernels: 52.2 us -> 60.4 us
    unnamed x24 -> x8, local copies, waits for them, and re-layouts: 9.61 us -> 0.02 us
    pallas_call x2, Pallas kernels: 28.9 us -> 32.8 us  [smooth(): pl.pallas_call(functools.partial(smooth_kernel, not more), grid=(1,), in_...]
    pallas_call x2, Pallas kernels: 3.03 us -> 4.72 us  [solve_rows(): pl.pallas_call(coarse_rows, out_shape=pltpu.HBM((COLS, COLS), jnp.float32...]
  transfers between devices with their start and end apart: 11 -> 11, of which waited for: 1 -> 1; matrix products, arithmetic and copies ran while one was open for 0% -> 0% of each run, Pallas kernels for 22% -> 26%
where the time goes in v6:
time: 152 us; the launch traced here: 151 us
  Pallas kernels  60.4 us (40%)
  starting transfers between devices  47.5 us (31%)
  blocking collectives  39.2 us (26%)
  waiting for transfers between devices  2.31 us (2%)
  between operations  1.58 us (1%)
    all_to_all x2, blocking collectives, everyone(): return lax.all_to_all(rows, AXES, 0, 0, tiled=True)  39.2 us
    pallas_call x2, Pallas kernels, smooth(): pl.pallas_call(functools.partial(smooth_kernel, not more), grid=(1,), in_...  32.8 us
    all_to_all x3, starting transfers between devices, everyone(): return lax.all_to_all(rows, AXES, 0, 0, tiled=True)  26.4 us
    ppermute x4, starting transfers between devices, exchange(): lax.ppermute(forward_value, axis, forward)  14.6 us
    ppermute x4, starting transfers between devices, exchange(): lax.ppermute(backward_value, axis, backward)  6.41 us
    pallas_call x1, Pallas kernels, first_projection(): pl.pallas_call(first_kernel, grid=(VECTORS // group,), in_specs=[block_sp...  6.23 us
    pallas_call x1, Pallas kernels, shards(): pl.pallas_call(first_coarse_kernel, in_specs=[SMEM_SPEC] + [VMEM_SPEC] *...  5.88 us
    pallas_call x1, Pallas kernels, shards(): pl.pallas_call(second_coarse_kernel, in_specs=[SMEM_SPEC] + [VMEM_SPEC] *...  5.55 us
  transfers between devices with their start and end apart: 11, of which 1 were waited for; matrix products, arithmetic and copies ran while one was open for 0% of the time, Pallas kernels for 26%

profile of v6, /device:TPU:1, one launch (start us, length us, event | category | flops | bytes accessed | tf_op | source)
XLA Modules:
  0.0 151.1 jit_solution(3023616902503795672)
XLA Ops:
  0.6 0.0 copy-start.3
  0.6 0.0 copy-start
  0.7 0.0 copy-start.1
  0.7 0.0 copy-start.2
  1.4 6.2 %first_projection.1 = (f32[128,128]{1,0:T(8,128)}, f32[64,16,128]{2,1,0:T(8,128)}, f32[64,16,128]{2,1,0:T(8,128)}, f32[8,32,128]{2,1,0:T(8,128)}) custom-call(f32[16,32,128]{2,1,0:T(8,128)} %source_ref.5, f32[16,32,128]{2,1,0:T(8,128)} %absorption_ref.9, bf16[32,16,32,128]{3,2,1,0:T(8,128)(2,1)} %basis_hbm.3, s32[1,1,32]{2,1,0:T(1,128)} %slots_ref.1, ...), custom_call_target="tpu_custom_call" | custom-call | tf_op jit(solution)/shard_map/first_projection/pallas_call | solution.py:148
  7.6 4.6 %collective-permute-start = (f32[64,16,128]{2,1,0:T(8,128)}, f32[64,16,128]{2,1,0:T(8,128)S(1)}, u32[]{:S(2)}, u32[]{:S(2)}) collective-permute-start(f32[64,16,128]{2,1,0:T(8,128)} %get-tuple-element.20), channel_id=1, source_target_pairs={{0,16},{16,32},{32,48},{48,64},{64,80},{80,96},{96,112},{1,17},{17... | collective-permute-start | bytes 1572872 | tf_op jit(solution)/shard_map/ppermute | solution.py:52
  12.2 1.9 %collective-permute-start.1 = (f32[64,16,128]{2,1,0:T(8,128)}, f32[64,16,128]{2,1,0:T(8,128)S(1)}, u32[]{:S(2)}, u32[]{:S(2)}) collective-permute-start(f32[64,16,128]{2,1,0:T(8,128)} %get-tuple-element.21), channel_id=1, source_target_pairs={{16,0},{32,16},{48,32},{64,48},{80,64},{96,80},{112,96},{17,1},{33... | collective-permute-start | bytes 1572872 | tf_op jit(solution)/shard_map/ppermute | solution.py:52
  14.2 20.0 %all_to_all.55 = f32[128,1,128]{2,1,0:T(1,128)S(1)} all-to-all(f32[128,1,128]{2,1,0:T(1,128)} %bitcast.38), channel_id=1, replica_groups=mesh['gx'=8,'gy'=16] {'gx','gy'}, dimensions={0} | all-to-all | bytes 131072 | tf_op jit(solution)/shard_map/all_to_all | solution.py:56
  34.2 0.0 collective-permute-done.low_ref.refs_0_
  34.2 0.0 collective-permute-done.1.high_ref.refs_1_
  34.2 0.0 copy-done
  34.2 0.0 copy-done.1
  34.2 1.6 %strips.2 = (f32[6,64,128]{2,1,0:T(8,128)S(1)}, f32[6,64,128]{2,1,0:T(8,128)S(1)}) custom-call(f32[128,128]{1,0:T(8,128)S(1)} %bitcast.22, f32[16,32,128]{2,1,0:T(8,128)S(1)} %copy-done.1, f32[16,32,128]{2,1,0:T(8,128)S(1)} %copy-done, f32[64,16,128]{2,1,0:T(8,128)S(1)} %collective-permute-done.low_ref.refs_0_, ...), custom_call_target="tpu_custom_call" | custom-call | flops 2000000 | bytes 2000000 | tf_op jit(solution)/shard_map/strips/pallas_call | solution.py:239
  35.9 2.5 %collective-permute-start.2 = (f32[6,64,128]{2,1,0:T(8,128)S(1)}, f32[6,64,128]{2,1,0:T(8,128)S(1)}, u32[]{:S(2)}, u32[]{:S(2)}) collective-permute-start(f32[6,64,128]{2,1,0:T(8,128)S(1)} %get-tuple-element.23), channel_id=1, source_target_pairs={{0,1},{1,2},{2,3},{3,4},{4,5},{5,6},{6,7},{7,8},{8,9},{9,10},{10,1... | collective-permute-start | bytes 589832 | tf_op jit(solution)/shard_map/ppermute | solution.py:52
  38.3 1.3 collective-permute-start.3
  39.6 0.0 copy-done.2
  39.6 1.8 %coarse_rows.2 = f32[128,128]{1,0:T(8,128)} custom-call(f32[128,128]{1,0:T(8,128)S(1)} %bitcast.23, f32[128,128]{1,0:T(8,128)S(1)} %bitcast.24, f32[32,4096]{1,0:T(8,128)S(1)} %copy-done.2), custom_call_target="tpu_custom_call" | custom-call | tf_op jit(solution)/shard_map/coarse_rows/pallas_call | solution.py:251
  41.5 7.8 %all-to-all-start.1 = ((f32[128,1,128]{2,1,0:T(1,128)}), f32[128,1,128]{2,1,0:T(1,128)S(1)}, u32[]{:S(2)}, u32[]{:S(2)}) async-start(f32[128,1,128]{2,1,0:T(1,128)} %bitcast.35), calls=%async_computation.1 | async-start | bytes 131072 | tf_op jit(solution)/shard_map/all_to_all | solution.py:56
  49.3 0.1 pad_add_fusion.place_ref
  49.3 0.0 collective-permute-done.2.left_ref.refs_2_
  49.3 0.0 collective-permute-done.3.right_ref.refs_3_
  49.3 0.0 copy-done.3
  49.4 15.8 %smoother.2.sum_ref.first_sum_ref = f32[16,48,256]{2,1,0:T(8,128)S(1)} custom-call(s32[4]{0:T(128)S(1)} %pad_add_fusion.place_ref, f32[2,8]{1,0:T(2,128)S(1)} %copy-done.3, f32[128,128]{1,0:T(8,128)S(1)} %bitcast.25, f32[16,32,128]{2,1,0:T(8,128)S(1)} %copy-done.1, f32[64,16,128]{2,1,0:T(8,128)S(1)} %collective-permute-done.low_ref.refs_0_, ...), custom_call_target="tpu_custom_call" | custom-call | flops 2000000 | bytes 54000000 | tf_op jit(solution)/shard_map/smoother/pallas_call | solution.py:495
  65.1 0.0 all-to-all-done.1
  65.1 5.9 %direction_and_image.1 = (f32[16,32,128]{2,1,0:T(8,128)S(1)}, f32[16,32,128]{2,1,0:T(8,128)S(1)}, f32[16,16,128]{2,1,0:T(8,128)}, f32[16,16,128]{2,1,0:T(8,128)}, f32[128,128]{1,0:T(8,128)}) custom-call(s32[4]{0:T(128)S(1)} %pad_add_fusion.place_ref, f32[128,128]{1,0:T(8,128)S(1)} %bitcast.26, f32[128,128]{1,0:T(8,128)S(1)} %bitcast.33, ...), custom_call_target="tpu_custom_call" | custom-call | tf_op jit(solution)/shard_map/direction_and_image/pallas_call | solution.py:756
  71.0 3.5 %collective-permute-start.4 = (f32[16,16,128]{2,1,0:T(8,128)}, f32[16,16,128]{2,1,0:T(8,128)S(1)}, u32[]{:S(2)}, u32[]{:S(2)}) collective-permute-start(f32[16,16,128]{2,1,0:T(8,128)} %get-tuple-element.27), channel_id=1, source_target_pairs={{0,16},{16,32},{32,48},{48,64},{64,80},{80,96},{96,112},{1,17},{17... | collective-permute-start | bytes 393224 | tf_op jit(solution)/shard_map/ppermute | solution.py:52
  74.6 1.9 %collective-permute-start.5 = (f32[16,16,128]{2,1,0:T(8,128)}, f32[16,16,128]{2,1,0:T(8,128)}, u32[]{:S(2)}, u32[]{:S(2)}) collective-permute-start(f32[16,16,128]{2,1,0:T(8,128)} %get-tuple-element.28), channel_id=1, source_target_pairs={{16,0},{32,16},{48,32},{64,48},{80,64},{96,80},{112,96},{17,1},{33... | collective-permute-start | bytes 393224 | tf_op jit(solution)/shard_map/ppermute | solution.py:52
  76.5 9.9 %all-to-all-start.2 = ((f32[128,1,128]{2,1,0:T(1,128)}), f32[128,1,128]{2,1,0:T(1,128)S(1)}, u32[]{:S(2)}, u32[]{:S(2)}) async-start(f32[128,1,128]{2,1,0:T(1,128)} %bitcast.37), calls=%async_computation.2 | async-start | bytes 131072 | tf_op jit(solution)/shard_map/all_to_all | solution.py:56
  86.4 0.0 collective-permute-done.4.low_ref
  86.4 0.0 collective-permute-done.5.high_ref
  86.4 1.9 %strips.3 = (f32[2,64,128]{2,1,0:T(8,128)}, f32[2,64,128]{2,1,0:T(8,128)}) custom-call(f32[16,32,128]{2,1,0:T(8,128)S(1)} %get-tuple-element.26.block_ref.first_ref, f32[16,16,128]{2,1,0:T(8,128)S(1)} %collective-permute-done.4.low_ref, f32[16,16,128]{2,1,0:T(8,128)} %collective-permute-done.5.high_ref), custom_call_target="tpu_custom_call" | custom-call | flops 2000000 | bytes 2000000 | tf_op jit(solution)/shard_map/strips/pallas_call | solution.py:239
  88.3 4.0 %collective-permute-start.6 = (f32[2,64,128]{2,1,0:T(8,128)}, f32[2,64,128]{2,1,0:T(8,128)}, u32[]{:S(2)}, u32[]{:S(2)}) collective-permute-start(f32[2,64,128]{2,1,0:T(8,128)} %get-tuple-element.29), channel_id=1, source_target_pairs={{0,1},{1,2},{2,3},{3,4},{4,5},{5,6},{6,7},{7,8},{8,9},{9,10},{10,1... | collective-permute-start | bytes 196616 | tf_op jit(solution)/shard_map/ppermute | solution.py:52
  92.3 1.3 collective-permute-start.7
  93.6 2.3 %all-to-all-done.2 = f32[128,1,128]{2,1,0:T(1,128)S(1)} async-done(((f32[128,1,128]{2,1,0:T(1,128)}), f32[128,1,128]{2,1,0:T(1,128)S(1)}, u32[]{:S(2)}, u32[]{:S(2)}) %all-to-all-start.2) | async-done | bytes 65568 | tf_op jit(solution)/shard_map/all_to_all | solution.py:56
  95.9 2.9 %coarse_rows.3 = f32[128,128]{1,0:T(8,128)} custom-call(f32[128,128]{1,0:T(8,128)S(1)} %bitcast.30, f32[128,128]{1,0:T(8,128)S(1)} %bitcast.27, f32[32,4096]{1,0:T(8,128)} %inverse_ref.3), custom_call_target="tpu_custom_call" | custom-call | tf_op jit(solution)/shard_map/coarse_rows/pallas_call | solution.py:251
  98.8 8.8 %all-to-all-start.3 = ((f32[128,1,128]{2,1,0:T(1,128)}), f32[128,1,128]{2,1,0:T(1,128)}, u32[]{:S(2)}, u32[]{:S(2)}) async-start(f32[128,1,128]{2,1,0:T(1,128)} %bitcast.36), calls=%async_computation.3 | async-start | bytes 131072 | tf_op jit(solution)/shard_map/all_to_all | solution.py:56
  107.6 0.0 collective-permute-done.6.left_ref
  107.6 0.0 collective-permute-done.7.right_ref
  107.6 17.1 %smoother.3.sum_ref = f32[16,48,256]{2,1,0:T(8,128)} custom-call(s32[4]{0:T(128)S(1)} %pad_add_fusion.place_ref, f32[2,8]{1,0:T(2,128)S(1)} %copy-done.3, f32[128,128]{1,0:T(8,128)S(1)} %bitcast.28, f32[16,32,128]{2,1,0:T(8,128)S(1)} %get-tuple-element.26.block_ref.first_ref, f32[16,16,128]{2,1,0:T(8,128)S(1)} %collective-permute-done.4.low_ref, ...), custom_call_target="tpu_custom_call" | custom-call | flops 2000000 | bytes 54000000 | tf_op jit(solution)/shard_map/smoother/pallas_call | solution.py:495
  124.7 0.0 all-to-all-done.3
  124.7 5.5 %second_images.1 = (f32[16,32,128]{2,1,0:T(8,128)S(1)}, f32[16,32,128]{2,1,0:T(8,128)S(1)}, f32[16,32,128]{2,1,0:T(8,128)S(1)}, f32[128,128]{1,0:T(8,128)}) custom-call(s32[4]{0:T(128)S(1)} %pad_add_fusion.place_ref, f32[128,128]{1,0:T(8,128)S(1)} %bitcast.29, f32[128,128]{1,0:T(8,128)} %bitcast.13.coarse_ref, bf16[32,16,32,128]{3,2,1,0:T(8,128)(2,1)} %basis_hbm.3, ...), custom_call_target="tpu_custom_call" | custom-call | tf_op jit(solution)/shard_map/second_images/pallas_call | solution.py:769
  130.2 19.2 %all_to_all.56 = f32[128,1,128]{2,1,0:T(1,128)S(1)} all-to-all(f32[128,1,128]{2,1,0:T(1,128)} %bitcast.39), channel_id=1, replica_groups=mesh['gx'=8,'gy'=16] {'gx','gy'}, dimensions={0} | all-to-all | bytes 131072 | tf_op jit(solution)/shard_map/all_to_all | solution.py:56
  149.5 1.7 %update.1 = (f32[16,32,128]{2,1,0:T(8,128)}, f32[16,32,128]{2,1,0:T(8,128)}) custom-call(f32[128,128]{1,0:T(8,128)S(1)} %bitcast.32, f32[128,128]{1,0:T(8,128)S(1)} %bitcast.34, f32[16,32,128]{2,1,0:T(8,128)S(1)} %get-tuple-element.31.direction_ref, f32[16,32,128]{2,1,0:T(8,128)S(1)} %get-tuple-element.26.block_ref.first_ref, ...), custom_call_target="tpu_custom_call" | custom-call | tf_op jit(solution)/shard_map/update/pallas_call | solution.py:778
Async XLA Ops:
  0.6 48.7 %copy-start.3 = (f32[2,8]{1,0:T(2,128)S(1)}, f32[2,8]{1,0:T(2,128)}, u32[]{:S(2)}) copy-start(f32[2,8]{1,0:T(2,128)} %constant.15.clone.table_ref) | copy-start | bytes 196
  0.6 33.5 %copy-start = (f32[16,32,128]{2,1,0:T(8,128)S(1)}, f32[16,32,128]{2,1,0:T(8,128)}, u32[]{:S(2)}) copy-start(f32[16,32,128]{2,1,0:T(8,128)} %absorption_ref.9) | copy-start | bytes 786436
  0.7 33.5 %copy-start.1 = (f32[16,32,128]{2,1,0:T(8,128)S(1)}, f32[16,32,128]{2,1,0:T(8,128)}, u32[]{:S(2)}) copy-start(f32[16,32,128]{2,1,0:T(8,128)} %source_ref.5) | copy-start | bytes 786436
  0.7 39.0 %copy-start.2 = (f32[32,4096]{1,0:T(8,128)S(1)}, f32[32,4096]{1,0:T(8,128)}, u32[]{:S(2)}) copy-start(f32[32,4096]{1,0:T(8,128)} %inverse_ref.3) | copy-start | bytes 1572868
  7.6 26.5 %collective-permute-start = (f32[64,16,128]{2,1,0:T(8,128)}, f32[64,16,128]{2,1,0:T(8,128)S(1)}, u32[]{:S(2)}, u32[]{:S(2)}) collective-permute-start(f32[64,16,128]{2,1,0:T(8,128)} %get-tuple-element.20), channel_id=1, source_target_pairs={{0,16},{16,32},{32,48},{48,64},{64,80},{80,96},{96,112},{1,17},{17... | collective-permute-start | bytes 1572872 | tf_op jit(solution)/shard_map/ppermute | solution.py:52
  12.2 22.0 %collective-permute-start.1 = (f32[64,16,128]{2,1,0:T(8,128)}, f32[64,16,128]{2,1,0:T(8,128)S(1)}, u32[]{:S(2)}, u32[]{:S(2)}) collective-permute-start(f32[64,16,128]{2,1,0:T(8,128)} %get-tuple-element.21), channel_id=1, source_target_pairs={{16,0},{32,16},{48,32},{64,48},{80,64},{96,80},{112,96},{17,1},{33... | collective-permute-start | bytes 1572872 | tf_op jit(solution)/shard_map/ppermute | solution.py:52
  35.9 13.5 %collective-permute-start.2 = (f32[6,64,128]{2,1,0:T(8,128)S(1)}, f32[6,64,128]{2,1,0:T(8,128)S(1)}, u32[]{:S(2)}, u32[]{:S(2)}) collective-permute-start(f32[6,64,128]{2,1,0:T(8,128)S(1)} %get-tuple-element.23), channel_id=1, source_target_pairs={{0,1},{1,2},{2,3},{3,4},{4,5},{5,6},{6,7},{7,8},{8,9},{9,10},{10,1... | collective-permute-start | bytes 589832 | tf_op jit(solution)/shard_map/ppermute | solution.py:52
  38.3 11.0 %collective-permute-start.3 = (f32[6,64,128]{2,1,0:T(8,128)S(1)}, f32[6,64,128]{2,1,0:T(8,128)S(1)}, u32[]{:S(2)}, u32[]{:S(2)}) collective-permute-start(f32[6,64,128]{2,1,0:T(8,128)S(1)} %get-tuple-element.24), channel_id=1, source_target_pairs={{1,0},{2,1},{3,2},{4,3},{5,4},{6,5},{7,6},{8,7},{9,8},{10,9},{11,1... | collective-permute-start | bytes 589832 | tf_op jit(solution)/shard_map/ppermute | solution.py:52
  41.5 23.7 %all-to-all-start.1 = ((f32[128,1,128]{2,1,0:T(1,128)}), f32[128,1,128]{2,1,0:T(1,128)S(1)}, u32[]{:S(2)}, u32[]{:S(2)}) async-start(f32[128,1,128]{2,1,0:T(1,128)} %bitcast.35), calls=%async_computation.1 | async-start | bytes 131072 | tf_op jit(solution)/shard_map/all_to_all | solution.py:56
  71.0 15.4 %collective-permute-start.4 = (f32[16,16,128]{2,1,0:T(8,128)}, f32[16,16,128]{2,1,0:T(8,128)S(1)}, u32[]{:S(2)}, u32[]{:S(2)}) collective-permute-start(f32[16,16,128]{2,1,0:T(8,128)} %get-tuple-element.27), channel_id=1, source_target_pairs={{0,16},{16,32},{32,48},{48,64},{64,80},{80,96},{96,112},{1,17},{17... | collective-permute-start | bytes 393224 | tf_op jit(solution)/shard_map/ppermute | solution.py:52
  74.6 11.8 %collective-permute-start.5 = (f32[16,16,128]{2,1,0:T(8,128)}, f32[16,16,128]{2,1,0:T(8,128)}, u32[]{:S(2)}, u32[]{:S(2)}) collective-permute-start(f32[16,16,128]{2,1,0:T(8,128)} %get-tuple-element.28), channel_id=1, source_target_pairs={{16,0},{32,16},{48,32},{64,48},{80,64},{96,80},{112,96},{17,1},{33... | collective-permute-start | bytes 393224 | tf_op jit(solution)/shard_map/ppermute | solution.py:52
  76.5 19.4 %all-to-all-start.2 = ((f32[128,1,128]{2,1,0:T(1,128)}), f32[128,1,128]{2,1,0:T(1,128)S(1)}, u32[]{:S(2)}, u32[]{:S(2)}) async-start(f32[128,1,128]{2,1,0:T(1,128)} %bitcast.37), calls=%async_computation.2 | async-start | bytes 131072 | tf_op jit(solution)/shard_map/all_to_all | solution.py:56
  88.3 19.3 %collective-permute-start.6 = (f32[2,64,128]{2,1,0:T(8,128)}, f32[2,64,128]{2,1,0:T(8,128)}, u32[]{:S(2)}, u32[]{:S(2)}) collective-permute-start(f32[2,64,128]{2,1,0:T(8,128)} %get-tuple-element.29), channel_id=1, source_target_pairs={{0,1},{1,2},{2,3},{3,4},{4,5},{5,6},{6,7},{7,8},{8,9},{9,10},{10,1... | collective-permute-start | bytes 196616 | tf_op jit(solution)/shard_map/ppermute | solution.py:52
  92.3 15.3 %collective-permute-start.7 = (f32[2,64,128]{2,1,0:T(8,128)}, f32[2,64,128]{2,1,0:T(8,128)}, u32[]{:S(2)}, u32[]{:S(2)}) collective-permute-start(f32[2,64,128]{2,1,0:T(8,128)} %get-tuple-element.30), channel_id=1, source_target_pairs={{1,0},{2,1},{3,2},{4,3},{5,4},{6,5},{7,6},{8,7},{9,8},{10,9},{11,1... | collective-permute-start | bytes 196616 | tf_op jit(solution)/shard_map/ppermute | solution.py:52
  98.8 25.9 %all-to-all-start.3 = ((f32[128,1,128]{2,1,0:T(1,128)}), f32[128,1,128]{2,1,0:T(1,128)}, u32[]{:S(2)}, u32[]{:S(2)}) async-start(f32[128,1,128]{2,1,0:T(1,128)} %bitcast.36), calls=%async_computation.3 | async-start | bytes 131072 | tf_op jit(solution)/shard_map/all_to_all | solution.py:56

commit v7 on v6

--- a/solution.py
+++ b/solution.py
@@ -26,15 +26,16 @@
 FIRST_LIMIT = 58 * 1024 * 1024
 
 
+def chebyshev_values():
+    ratio = theta / delta
+    values = [1.0, ratio]
+    while len(values) <= KCHEB:
+        values.append(2.0 * ratio * values[-1] - values[-2])
+    return values
+
+
 def chebyshev_table():
-    ratio = theta / delta
-    rho_old = 1.0 / ratio
-    table = []
-    for _ in range(KCHEB - 1):
-        rho_new = 1.0 / (2.0 * ratio - rho_old)
-        table.append((rho_new * rho_old, 2.0 * rho_new / delta))
-        rho_old = rho_new
-    return table
+    return chebyshev_values()[1:KCHEB]
 
 
 def iota(shape, dim):
@@ -165,7 +166,9 @@
     )(field, coefficient, basis, slots, margin)
 
 
-def coarse_rows(told_ref, slots_ref, inverse_ref, out_ref):
+def coarse_rows(told_ref, slots_ref, inverse_hbm, out_ref, inverse_ref, sem):
+    copy = pltpu.make_async_copy(inverse_hbm, inverse_ref, sem)
+    copy.start()
     told = told_ref[...]
     slots = slots_ref[...]
     turned = told.T
@@ -187,6 +190,7 @@
         placed = placed + jnp.dot(parts, ones, preferred_element_type=jnp.float32)
     placed = placed[:VECTORS] + placed[VECTORS : 2 * VECTORS] + placed[2 * VECTORS :]
     total = jnp.zeros((VECTORS, COLS), jnp.float32)
+    copy.wait()
     for high in range(VECTORS):
         total = total + inverse_ref[:, high * COLS : (high + 1) * COLS] * placed[high : high + 1]
     out_ref[...] = row_of_sums(total)
@@ -214,10 +218,13 @@
 
 
 def first_pack_kernel(
-    told_ref, source_ref, absorption_ref, low_ref, high_ref, sides_ref, forward_ref, backward_ref
+    told_ref, source_ref, absorption_ref, low_ref, high_ref, sides_hbm, forward_ref, backward_ref, sides_ref, sem
 ):
+    copy = pltpu.make_async_copy(sides_hbm, sides_ref, sem)
+    copy.start()
     for f, block in enumerate((source_ref, absorption_ref)):
         pack_strips(((low_ref, LEVELS * f), (block, 0), (high_ref, LEVELS * f)), forward_ref, backward_ref, 2 * f)
+    copy.wait()
     for n in range(LEVELS // 8):
         for half in range(2):
             rows = slice(half * ROWS, (half + 1) * ROWS)
@@ -231,16 +238,18 @@
 
 FIELDS_SPEC = pl.BlockSpec((2 * LEVELS, EDGE, COLS), lambda i: (0, 0, 0))
 VMEM_SPEC = pl.BlockSpec(memory_space=pltpu.VMEM)
+HBM_SPEC = pl.BlockSpec(memory_space=pltpu.HBM)
 SMEM_SPEC = pl.BlockSpec(memory_space=pltpu.SMEM)
 
 
-def pack(kernel, specs, strips, *operands):
+def pack(kernel, specs, strips, scratch, *operands):
     strips = jax.ShapeDtypeStruct((strips, TALL, COLS), jnp.float32)
     return pl.pallas_call(
         kernel,
         grid=(1,),
         in_specs=specs,
         out_shape=[strips, strips],
+        scratch_shapes=scratch,
         compiler_params=pltpu.CompilerParams(vmem_limit_bytes=VMEM_LIMIT),
         cost_estimate=pl.CostEstimate(flops=2000000, bytes_accessed=2000000, transcendentals=0),
         name="strips",
@@ -250,7 +259,9 @@
 def solve_rows(*operands):
     return pl.pallas_call(
         coarse_rows,
+        in_specs=[VMEM_SPEC] * 2 + [HBM_SPEC],
         out_shape=pltpu.HBM((COLS, COLS), jnp.float32),
+        scratch_shapes=[pltpu.VMEM((VECTORS, COLS * VECTORS), jnp.float32), pltpu.SemaphoreType.DMA],
         compiler_params=pltpu.CompilerParams(vmem_limit_bytes=VMEM_LIMIT),
         name="coarse_rows",
     )(*operands)
@@ -364,7 +375,8 @@
     ) = refs
     field_start, coef_start, coef_at = 0, LEVELS, 2
     masks(Place(place_ref, told_ref), own_m, beside_m, strip_m)
-    base = 4.0 + 2.0 * vertical
+    base = 2.0 * (theta - (4.0 + 2.0 * vertical)) / delta
+    last = 1.0 / chebyshev_values()[KCHEB]
     zero = jnp.zeros((8, COLS), jnp.float32)
     lane = iota((8, COLS), 1)
     lanes = [slice(0, COLS), slice(COLS, 2 * COLS)]
@@ -389,28 +401,29 @@
             tiles = tiles_of((low_ref, block_ref, high_ref), field_start, (left_ref, right_ref), 0, z, i)
             inner = 1 <= i < 7
             for t in range(2):
-                guess = tiles[t] * (1.0 / theta)
+                guess = tiles[t] * (1.0 / delta)
                 value = guess if t == 0 and 2 <= i < 6 else guess * own_m[t, s]
                 own[at, t, s] = value
                 own_y[at, t, s] = zero
                 if inner:
-                    wide_r[z, t, s] = tiles[t]
+                    wide_r[z, t, s] = guess + guess
                 beside_y[at, t, s] = zero
                 beside[at, t, s] = zero if i in (3, 4) else guess * beside_m[t, s]
-            strip[at, 0, s] = tiles[2] * (strip_m[s] * (1.0 / theta))
+            guess = tiles[2] * (1.0 / delta)
+            strip[at, 0, s] = guess * strip_m[s]
             strip_y[at, 0, s] = zero
             if inner:
-                strip_r[z, 0, s] = tiles[2]
+                strip_r[z, 0, s] = guess + guess
                 tiles = tiles_of((low_c, absorption_ref, high_c), coef_start, (left_c, right_c), coef_at, z, i)
-                diag[z, 0, s] = tiles[0] + base
-                diag[z, 1, s] = tiles[1] + base
-                strip_diag[z, 0, s] = tiles[2] + base
+                diag[z, 0, s] = base - (2.0 / delta) * tiles[0]
+                diag[z, 1, s] = base - (2.0 / delta) * tiles[1]
+                strip_diag[z, 0, s] = base - (2.0 / delta) * tiles[2]
         return carry
 
     lax.fori_loop(0, LEVELS, begin, 0, unroll=UNROLL_BEGIN)
     at_first, at_last = lane == 0, lane == COLS - 1
 
-    def step(here, x, y, r, a, mask, width, i, keep, scale):
+    def step(here, x, y, r, a, mask, width, i, amount):
         s = slice(i * 8, i * 8 + 8)
         up, down = slice(i * 8 - 1, i * 8 + 7), slice(i * 8 + 1, i * 8 + 9)
         z = here - 1
@@ -424,9 +437,7 @@
             high = x[here - 1, t, s] + x[here + 1, t, s]
             around = (x[here, t, up] + x[here, t, down]) + (back[t] + fore[t])
             around = around + (high + high)
-            defect = (r[z, t, s] + around) - a[z, t, s] * now[t]
-            move = keep * (now[t] - y[here, t, s]) + scale * defect
-            after = now[t] + move
+            after = (a[z, t, s] * now[t] + amount * r[z, t, s]) + ((2.0 / delta) * around - y[here, t, s])
             if mask[t] is not None:
                 after = after * mask[t]
             y[here, t, s] = after
@@ -435,7 +446,7 @@
     second = tuple((y, x) for x, y in first)
 
     def sweep(n, arrays):
-        keep, scale = table_ref[0, n], table_ref[1, n]
+        amount = table_ref[n]
         own, beside, strip = arrays
 
         def level(z, carry):
@@ -443,10 +454,10 @@
             for i in range(1, 7):
                 s = slice(i * 8, i * 8 + 8)
                 free = None if 2 <= i < 6 else own_m[0, s]
-                step(here, *own, wide_r, diag, [free, own_m[1, s]], 2, i, keep, scale)
+                step(here, *own, wide_r, diag, [free, own_m[1, s]], 2, i, amount)
                 if i in BESIDE_TILES:
-                    step(here, *beside, wide_r, diag, [beside_m[0, s], beside_m[1, s]], 2, i, keep, scale)
-                step(here, *strip, strip_r, strip_diag, [strip_m[s]], 1, i, keep, scale)
+                    step(here, *beside, wide_r, diag, [beside_m[0, s], beside_m[1, s]], 2, i, amount)
+                step(here, *strip, strip_r, strip_diag, [strip_m[s]], 1, i, amount)
             return carry
 
         lax.fori_loop(0, LEVELS, level, 0, unroll=UNROLL)
@@ -474,8 +485,8 @@
             if i in BESIDE_TILES:
                 first = first + beside[at, 0, s]
                 second = second + beside[at, 1, s]
-            out_ref[z, out, lanes[0]] = first
-            out_ref[z, out, lanes[1]] = second
+            out_ref[z, out, lanes[0]] = first * last
+            out_ref[z, out, lanes[1]] = second * last
         return carry
 
     lax.fori_loop(0, LEVELS, finish, 0, unroll=UNROLL_FINISH)
@@ -530,7 +541,7 @@
 
 
 def add_coarse(place, told_ref, coarse_ref, basis_hbm, basis_ref, sems, low_ref, high_ref, left_ref, right_ref, at, sum_ref, x,
-               own_c, edge_c, ring_ref, side_ref):
+               own_c, edge_c, ring_ref, side_ref, ready=None):
     def part(q):
         levels = pl.ds(q * 4, 4)
         return pltpu.make_async_copy(basis_hbm.at[:, levels], basis_ref.at[:, levels], sems.at[q])
@@ -579,6 +590,9 @@
             x[here, t, COLS : 2 * COLS] = sum_ref[z, t, COLS : 2 * COLS] + value
         return carry
 
+    if ready is not None:
+        ready.wait()
+
     def levels(q, carry):
         part(q).wait()
         return lax.fori_loop(0, 2, lambda n, c: level(4 * q + 2 * n + 1, level(4 * q + 2 * n, c)), carry)
@@ -661,13 +675,16 @@
 
 
 def second_coarse_kernel(
-    place_ref, told_ref, coarse_ref, basis_hbm, low_ref, high_ref, left_ref, right_ref, sum_ref, source_ref, absorption_ref,
+    place_ref, told_ref, coarse_ref, basis_hbm, low_ref, high_ref, left_ref, right_ref, sum_hbm, source_ref, absorption_ref,
     again_ref, first_sum_ref, direction_ref, first_ref,
     residual_ref, precond_ref, image_ref, out_ref, x, own_c, edge_c, ring_ref, side_ref, basis_ref, sems,
+    sum_ref, sum_sem,
 ):
+    copy = pltpu.make_async_copy(sum_hbm, sum_ref, sum_sem)
+    copy.start()
     place = Place(place_ref, told_ref)
     row = add_coarse(place, told_ref, coarse_ref, basis_hbm, basis_ref, sems, low_ref, high_ref, left_ref, right_ref, 4, sum_ref, x,
-                     own_c, edge_c, ring_ref, side_ref)
+                     own_c, edge_c, ring_ref, side_ref, copy)
     weight0, curve0 = scalars(again_ref)
     step = weight0 / curve0
     zero = jnp.zeros((8, COLS), jnp.float32)
@@ -740,17 +757,17 @@
     place = jnp.stack(
         [lax.axis_index("gx"), lax.axis_index("gy"), lax.axis_size("gx"), lax.axis_size("gy")]
     ).astype(jnp.int32)
-    table = jnp.array(list(zip(*chebyshev_table())), jnp.float32)
+    table = jnp.array(chebyshev_table(), jnp.float32)
     rows, ahead, behind, sides = first_projection(
         source, absorption, basis, coarse_slot, margin_width
     )
     low, high = exchange(ahead, behind, "gx")
     told = everyone(rows)
-    fields = [pl.BlockSpec(memory_space=pltpu.HBM)] + [VMEM_SPEC] * 2 + [FIELDS_SPEC] * 2 + [VMEM_SPEC]
+    fields = [pl.BlockSpec(memory_space=pltpu.HBM)] + [VMEM_SPEC] * 2 + [FIELDS_SPEC] * 2 + [HBM_SPEC]
     strips = exchange(
-        *pack(first_pack_kernel, fields, 6, told, source, absorption, low, high, in_hbm(sides)), "gy"
+        *pack(first_pack_kernel, fields, 6, [scratch(LEVELS // 2, ROWS, COLS), pltpu.SemaphoreType.DMA], told, source, absorption, low, high, in_hbm(sides)), "gy"
     )
-    coarse = everyone(solve_rows(told, told, coarse_inverse))
+    coarse = everyone(solve_rows(told, told, in_hbm(coarse_inverse)))
     first_sum = smooth(place, table, told, source, low, high, strips, absorption)
     edges = (low, high, *strips)
     direction, image, ahead, behind, rows = pl.pallas_call(
@@ -763,14 +780,14 @@
     )(place, told, coarse, in_hbm(basis), *edges, first_sum, source, absorption)
     low_w, high_w = exchange(ahead, behind, "gx")
     again = everyone(rows)
-    strips_w = exchange(*pack(pack_kernel, [VMEM_SPEC] * 3, 2, image, low_w, high_w), "gy")
+    strips_w = exchange(*pack(pack_kernel, [VMEM_SPEC] * 3, 2, [], image, low_w, high_w), "gy")
     coarse = everyone(solve_rows(again, told, in_hbm(coarse_inverse)))
     second_sum = smooth(place, table, told, image, low_w, high_w, strips_w, absorption, edges)
     residual, precond, precond_image, rows = pl.pallas_call(
         second_coarse_kernel,
-        in_specs=[SMEM_SPEC] + [VMEM_SPEC] * 2 + [hbm] + [VMEM_SPEC] * 11,
+        in_specs=[SMEM_SPEC] + [VMEM_SPEC] * 2 + [hbm] + [VMEM_SPEC] * 4 + [hbm] + [VMEM_SPEC] * 6,
         out_shape=[block, block, block, message],
-        scratch_shapes=coarse_scratch,
+        scratch_shapes=coarse_scratch + [scratch(LEVELS, INNER, 2 * COLS), pltpu.SemaphoreType.DMA],
         compiler_params=params,
         name="second_images",
     )(place, told, coarse, in_hbm(basis), *edges, in_hbm(second_sum), source, absorption, again, first_sum, direction, image)

time: 152 us -> 148 us (0.974)
  Pallas kernels: 60.4 us -> 56.2 us
    pallas_call x2, Pallas kernels: 32.8 us -> 29.8 us  [smooth(): pl.pallas_call(functools.partial(smooth_kernel, not more), grid=(1,), in_...]
  transfers between devices with their start and end apart: 11 -> 11, of which waited for: 1 -> 1; matrix products, arithmetic and copies ran while one was open for 0% -> 0% of each run, Pallas kernels for 26% -> 24%
where the time goes in v7:
time: 148 us; the launch traced here: 147 us
  Pallas kernels  56.2 us (38%)
  starting transfers between devices  47.5 us (32%)
  blocking collectives  39.2 us (26%)
  waiting for transfers between devices  2.29 us (2%)
  between operations  1.55 us (1%)
    all_to_all x2, blocking collectives, everyone(): return lax.all_to_all(rows, AXES, 0, 0, tiled=True)  39.2 us
    pallas_call x2, Pallas kernels, smooth(): pl.pallas_call(functools.partial(smooth_kernel, not more), grid=(1,), in_...  29.8 us
    all_to_all x3, starting transfers between devices, everyone(): return lax.all_to_all(rows, AXES, 0, 0, tiled=True)  26.4 us
    ppermute x4, starting transfers between devices, exchange(): lax.ppermute(forward_value, axis, forward)  14.6 us
    ppermute x4, starting transfers between devices, exchange(): lax.ppermute(backward_value, axis, backward)  6.41 us
    pallas_call x1, Pallas kernels, first_projection(): pl.pallas_call(first_kernel, grid=(VECTORS // group,), in_specs=[block_sp...  6.23 us
    pallas_call x1, Pallas kernels, shards(): pl.pallas_call(second_coarse_kernel, in_specs=[SMEM_SPEC] + [VMEM_SPEC] *...  5.88 us
    pallas_call x1, Pallas kernels, shards(): pl.pallas_call(first_coarse_kernel, in_specs=[SMEM_SPEC] + [VMEM_SPEC] *...  5.88 us
  transfers between devices with their start and end apart: 11, of which 1 were waited for; matrix products, arithmetic and copies ran while one was open for 0% of the time, Pallas kernels for 24%

profile of v7, /device:TPU:1, one launch (start us, length us, event | category | flops | bytes accessed | tf_op | source)
XLA Modules:
  0.0 146.8 jit_solution(4033979612177911010)
XLA Ops:
  0.6 0.0 copy-start.2
  0.6 0.0 copy-start
  0.7 0.0 copy-start.1
  1.4 6.2 %first_projection.1 = (f32[128,128]{1,0:T(8,128)}, f32[64,16,128]{2,1,0:T(8,128)}, f32[64,16,128]{2,1,0:T(8,128)}, f32[8,32,128]{2,1,0:T(8,128)}) custom-call(f32[16,32,128]{2,1,0:T(8,128)} %source_ref.5, f32[16,32,128]{2,1,0:T(8,128)} %absorption_ref.9, bf16[32,16,32,128]{3,2,1,0:T(8,128)(2,1)} %basis_hbm.3, s32[1,1,32]{2,1,0:T(1,128)} %slots_ref.1, ...), custom_call_target="tpu_custom_call" | custom-call | tf_op jit(solution)/shard_map/first_projection/pallas_call | solution.py:149
  7.6 4.6 %collective-permute-start = (f32[64,16,128]{2,1,0:T(8,128)}, f32[64,16,128]{2,1,0:T(8,128)S(1)}, u32[]{:S(2)}, u32[]{:S(2)}) collective-permute-start(f32[64,16,128]{2,1,0:T(8,128)} %get-tuple-element.20), channel_id=1, source_target_pairs={{0,16},{16,32},{32,48},{48,64},{64,80},{80,96},{96,112},{1,17},{17... | collective-permute-start | bytes 1572872 | tf_op jit(solution)/shard_map/ppermute | solution.py:53
  12.2 1.9 %collective-permute-start.1 = (f32[64,16,128]{2,1,0:T(8,128)}, f32[64,16,128]{2,1,0:T(8,128)S(1)}, u32[]{:S(2)}, u32[]{:S(2)}) collective-permute-start(f32[64,16,128]{2,1,0:T(8,128)} %get-tuple-element.21), channel_id=1, source_target_pairs={{16,0},{32,16},{48,32},{64,48},{80,64},{96,80},{112,96},{17,1},{33... | collective-permute-start | bytes 1572872 | tf_op jit(solution)/shard_map/ppermute | solution.py:53
  14.1 20.0 %all_to_all.55 = f32[128,1,128]{2,1,0:T(1,128)S(1)} all-to-all(f32[128,1,128]{2,1,0:T(1,128)} %bitcast.38), channel_id=1, replica_groups=mesh['gx'=8,'gy'=16] {'gx','gy'}, dimensions={0} | all-to-all | bytes 131072 | tf_op jit(solution)/shard_map/all_to_all | solution.py:57
  34.1 0.0 collective-permute-done.low_ref.refs_0_
  34.1 0.0 collective-permute-done.1.high_ref.refs_1_
  34.1 0.0 copy-done
  34.1 0.0 copy-done.1
  34.2 0.9 strips.2
  35.1 2.5 %collective-permute-start.2 = (f32[6,64,128]{2,1,0:T(8,128)S(1)}, f32[6,64,128]{2,1,0:T(8,128)S(1)}, u32[]{:S(2)}, u32[]{:S(2)}) collective-permute-start(f32[6,64,128]{2,1,0:T(8,128)S(1)} %get-tuple-element.23), channel_id=1, source_target_pairs={{0,1},{1,2},{2,3},{3,4},{4,5},{5,6},{6,7},{7,8},{8,9},{9,10},{10,1... | collective-permute-start | bytes 589832 | tf_op jit(solution)/shard_map/ppermute | solution.py:53
  37.6 1.3 collective-permute-start.3
  38.9 2.0 %coarse_rows.2 = f32[128,128]{1,0:T(8,128)} custom-call(f32[128,128]{1,0:T(8,128)S(1)} %bitcast.23, f32[128,128]{1,0:T(8,128)S(1)} %bitcast.24, f32[32,4096]{1,0:T(8,128)} %inverse_hbm.3), custom_call_target="tpu_custom_call" | custom-call | tf_op jit(solution)/shard_map/coarse_rows/pallas_call | solution.py:260
  40.8 7.8 %all-to-all-start.1 = ((f32[128,1,128]{2,1,0:T(1,128)}), f32[128,1,128]{2,1,0:T(1,128)S(1)}, u32[]{:S(2)}, u32[]{:S(2)}) async-start(f32[128,1,128]{2,1,0:T(1,128)} %bitcast.35), calls=%async_computation.1 | async-start | bytes 131072 | tf_op jit(solution)/shard_map/all_to_all | solution.py:57
  48.6 0.1 pad_add_fusion.place_ref
  48.7 0.0 collective-permute-done.2.left_ref.refs_2_
  48.7 0.0 collective-permute-done.3.right_ref.refs_3_
  48.7 0.0 copy-done.2
  48.7 14.2 %smoother.2.sum_ref.first_sum_ref = f32[16,48,256]{2,1,0:T(8,128)S(1)} custom-call(s32[4]{0:T(128)S(1)} %pad_add_fusion.place_ref, f32[8]{0:T(128)S(1)} %copy-done.2, f32[128,128]{1,0:T(8,128)S(1)} %bitcast.25, f32[16,32,128]{2,1,0:T(8,128)S(1)} %copy-done.1, f32[64,16,128]{2,1,0:T(8,128)S(1)} %collective-permute-done.low_ref.refs_0_, ...), custom_call_target="tpu_custom_call" | custom-call | flops 2000000 | bytes 54000000 | tf_op jit(solution)/shard_map/smoother/pallas_call | solution.py:506
  63.0 0.0 all-to-all-done.1
  63.0 5.9 %direction_and_image.1 = (f32[16,32,128]{2,1,0:T(8,128)S(1)}, f32[16,32,128]{2,1,0:T(8,128)S(1)}, f32[16,16,128]{2,1,0:T(8,128)}, f32[16,16,128]{2,1,0:T(8,128)}, f32[128,128]{1,0:T(8,128)}) custom-call(s32[4]{0:T(128)S(1)} %pad_add_fusion.place_ref, f32[128,128]{1,0:T(8,128)S(1)} %bitcast.26, f32[128,128]{1,0:T(8,128)S(1)} %bitcast.33, ...), custom_call_target="tpu_custom_call" | custom-call | tf_op jit(solution)/shard_map/direction_and_image/pallas_call | solution.py:773
  68.9 3.5 %collective-permute-start.4 = (f32[16,16,128]{2,1,0:T(8,128)}, f32[16,16,128]{2,1,0:T(8,128)S(1)}, u32[]{:S(2)}, u32[]{:S(2)}) collective-permute-start(f32[16,16,128]{2,1,0:T(8,128)} %get-tuple-element.27), channel_id=1, source_target_pairs={{0,16},{16,32},{32,48},{48,64},{64,80},{80,96},{96,112},{1,17},{17... | collective-permute-start | bytes 393224 | tf_op jit(solution)/shard_map/ppermute | solution.py:53
  72.4 1.9 %collective-permute-start.5 = (f32[16,16,128]{2,1,0:T(8,128)}, f32[16,16,128]{2,1,0:T(8,128)}, u32[]{:S(2)}, u32[]{:S(2)}) collective-permute-start(f32[16,16,128]{2,1,0:T(8,128)} %get-tuple-element.28), channel_id=1, source_target_pairs={{16,0},{32,16},{48,32},{64,48},{80,64},{96,80},{112,96},{17,1},{33... | collective-permute-start | bytes 393224 | tf_op jit(solution)/shard_map/ppermute | solution.py:53
  74.3 9.9 %all-to-all-start.2 = ((f32[128,1,128]{2,1,0:T(1,128)}), f32[128,1,128]{2,1,0:T(1,128)S(1)}, u32[]{:S(2)}, u32[]{:S(2)}) async-start(f32[128,1,128]{2,1,0:T(1,128)} %bitcast.37), calls=%async_computation.2 | async-start | bytes 131072 | tf_op jit(solution)/shard_map/all_to_all | solution.py:57
  84.2 0.0 collective-permute-done.4.low_ref
  84.2 0.0 collective-permute-done.5.high_ref
  84.2 1.9 %strips.3 = (f32[2,64,128]{2,1,0:T(8,128)}, f32[2,64,128]{2,1,0:T(8,128)}) custom-call(f32[16,32,128]{2,1,0:T(8,128)S(1)} %get-tuple-element.26.block_ref.first_ref, f32[16,16,128]{2,1,0:T(8,128)S(1)} %collective-permute-done.4.low_ref, f32[16,16,128]{2,1,0:T(8,128)} %collective-permute-done.5.high_ref), custom_call_target="tpu_custom_call" | custom-call | flops 2000000 | bytes 2000000 | tf_op jit(solution)/shard_map/strips/pallas_call | solution.py:247
  86.1 4.0 %collective-permute-start.6 = (f32[2,64,128]{2,1,0:T(8,128)}, f32[2,64,128]{2,1,0:T(8,128)}, u32[]{:S(2)}, u32[]{:S(2)}) collective-permute-start(f32[2,64,128]{2,1,0:T(8,128)} %get-tuple-element.29), channel_id=1, source_target_pairs={{0,1},{1,2},{2,3},{3,4},{4,5},{5,6},{6,7},{7,8},{8,9},{9,10},{10,1... | collective-permute-start | bytes 196616 | tf_op jit(solution)/shard_map/ppermute | solution.py:53
  90.2 1.3 collective-permute-start.7
  91.5 2.3 %all-to-all-done.2 = f32[128,1,128]{2,1,0:T(1,128)S(1)} async-done(((f32[128,1,128]{2,1,0:T(1,128)}), f32[128,1,128]{2,1,0:T(1,128)S(1)}, u32[]{:S(2)}, u32[]{:S(2)}) %all-to-all-start.2) | async-done | bytes 65568 | tf_op jit(solution)/shard_map/all_to_all | solution.py:57
  93.7 2.0 %coarse_rows.3 = f32[128,128]{1,0:T(8,128)} custom-call(f32[128,128]{1,0:T(8,128)S(1)} %bitcast.30, f32[128,128]{1,0:T(8,128)S(1)} %bitcast.27, f32[32,4096]{1,0:T(8,128)} %inverse_hbm.3), custom_call_target="tpu_custom_call" | custom-call | tf_op jit(solution)/shard_map/coarse_rows/pallas_call | solution.py:260
  95.7 8.8 %all-to-all-start.3 = ((f32[128,1,128]{2,1,0:T(1,128)}), f32[128,1,128]{2,1,0:T(1,128)}, u32[]{:S(2)}, u32[]{:S(2)}) async-start(f32[128,1,128]{2,1,0:T(1,128)} %bitcast.36), calls=%async_computation.3 | async-start | bytes 131072 | tf_op jit(solution)/shard_map/all_to_all | solution.py:57
  104.5 0.0 collective-permute-done.6.left_ref
  104.5 0.0 collective-permute-done.7.right_ref
  104.5 15.5 %smoother.3.sum_hbm = f32[16,48,256]{2,1,0:T(8,128)} custom-call(s32[4]{0:T(128)S(1)} %pad_add_fusion.place_ref, f32[8]{0:T(128)S(1)} %copy-done.2, f32[128,128]{1,0:T(8,128)S(1)} %bitcast.28, f32[16,32,128]{2,1,0:T(8,128)S(1)} %get-tuple-element.26.block_ref.first_ref, f32[16,16,128]{2,1,0:T(8,128)S(1)} %collective-permute-done.4.low_ref, ...), custom_call_target="tpu_custom_call" | custom-call | flops 2000000 | bytes 54000000 | tf_op jit(solution)/shard_map/smoother/pallas_call | solution.py:506
  120.1 0.0 all-to-all-done.3
  120.1 5.9 %second_images.1 = (f32[16,32,128]{2,1,0:T(8,128)S(1)}, f32[16,32,128]{2,1,0:T(8,128)S(1)}, f32[16,32,128]{2,1,0:T(8,128)S(1)}, f32[128,128]{1,0:T(8,128)}) custom-call(s32[4]{0:T(128)S(1)} %pad_add_fusion.place_ref, f32[128,128]{1,0:T(8,128)S(1)} %bitcast.29, f32[128,128]{1,0:T(8,128)} %bitcast.13.coarse_ref, bf16[32,16,32,128]{3,2,1,0:T(8,128)(2,1)} %basis_hbm.3, ...), custom_call_target="tpu_custom_call" | custom-call | tf_op jit(solution)/shard_map/second_images/pallas_call | solution.py:786
  125.9 19.2 %all_to_all.56 = f32[128,1,128]{2,1,0:T(1,128)S(1)} all-to-all(f32[128,1,128]{2,1,0:T(1,128)} %bitcast.39), channel_id=1, replica_groups=mesh['gx'=8,'gy'=16] {'gx','gy'}, dimensions={0} | all-to-all | bytes 131072 | tf_op jit(solution)/shard_map/all_to_all | solution.py:57
  145.2 1.7 %update.1 = (f32[16,32,128]{2,1,0:T(8,128)}, f32[16,32,128]{2,1,0:T(8,128)}) custom-call(f32[128,128]{1,0:T(8,128)S(1)} %bitcast.32, f32[128,128]{1,0:T(8,128)S(1)} %bitcast.34, f32[16,32,128]{2,1,0:T(8,128)S(1)} %get-tuple-element.31.direction_ref, f32[16,32,128]{2,1,0:T(8,128)S(1)} %get-tuple-element.26.block_ref.first_ref, ...), custom_call_target="tpu_custom_call" | custom-call | tf_op jit(solution)/shard_map/update/pallas_call | solution.py:795
Async XLA Ops:
  0.6 48.1 %copy-start.2 = (f32[8]{0:T(128)S(1)}, f32[8]{0:T(128)}, u32[]{:S(2)}) copy-start(f32[8]{0:T(128)} %constant.15.clone.table_ref) | copy-start | bytes 100
  0.6 33.5 %copy-start = (f32[16,32,128]{2,1,0:T(8,128)S(1)}, f32[16,32,128]{2,1,0:T(8,128)}, u32[]{:S(2)}) copy-start(f32[16,32,128]{2,1,0:T(8,128)} %absorption_ref.9) | copy-start | bytes 786436
  0.7 33.5 %copy-start.1 = (f32[16,32,128]{2,1,0:T(8,128)S(1)}, f32[16,32,128]{2,1,0:T(8,128)}, u32[]{:S(2)}) copy-start(f32[16,32,128]{2,1,0:T(8,128)} %source_ref.5) | copy-start | bytes 786436
  7.6 26.5 %collective-permute-start = (f32[64,16,128]{2,1,0:T(8,128)}, f32[64,16,128]{2,1,0:T(8,128)S(1)}, u32[]{:S(2)}, u32[]{:S(2)}) collective-permute-start(f32[64,16,128]{2,1,0:T(8,128)} %get-tuple-element.20), channel_id=1, source_target_pairs={{0,16},{16,32},{32,48},{48,64},{64,80},{80,96},{96,112},{1,17},{17... | collective-permute-start | bytes 1572872 | tf_op jit(solution)/shard_map/ppermute | solution.py:53
  12.2 21.9 %collective-permute-start.1 = (f32[64,16,128]{2,1,0:T(8,128)}, f32[64,16,128]{2,1,0:T(8,128)S(1)}, u32[]{:S(2)}, u32[]{:S(2)}) collective-permute-start(f32[64,16,128]{2,1,0:T(8,128)} %get-tuple-element.21), channel_id=1, source_target_pairs={{16,0},{32,16},{48,32},{64,48},{80,64},{96,80},{112,96},{17,1},{33... | collective-permute-start | bytes 1572872 | tf_op jit(solution)/shard_map/ppermute | solution.py:53
  35.1 13.6 %collective-permute-start.2 = (f32[6,64,128]{2,1,0:T(8,128)S(1)}, f32[6,64,128]{2,1,0:T(8,128)S(1)}, u32[]{:S(2)}, u32[]{:S(2)}) collective-permute-start(f32[6,64,128]{2,1,0:T(8,128)S(1)} %get-tuple-element.23), channel_id=1, source_target_pairs={{0,1},{1,2},{2,3},{3,4},{4,5},{5,6},{6,7},{7,8},{8,9},{9,10},{10,1... | collective-permute-start | bytes 589832 | tf_op jit(solution)/shard_map/ppermute | solution.py:53
  37.6 11.1 %collective-permute-start.3 = (f32[6,64,128]{2,1,0:T(8,128)S(1)}, f32[6,64,128]{2,1,0:T(8,128)S(1)}, u32[]{:S(2)}, u32[]{:S(2)}) collective-permute-start(f32[6,64,128]{2,1,0:T(8,128)S(1)} %get-tuple-element.24), channel_id=1, source_target_pairs={{1,0},{2,1},{3,2},{4,3},{5,4},{6,5},{7,6},{8,7},{9,8},{10,9},{11,1... | collective-permute-start | bytes 589832 | tf_op jit(solution)/shard_map/ppermute | solution.py:53
  40.8 22.1 %all-to-all-start.1 = ((f32[128,1,128]{2,1,0:T(1,128)}), f32[128,1,128]{2,1,0:T(1,128)S(1)}, u32[]{:S(2)}, u32[]{:S(2)}) async-start(f32[128,1,128]{2,1,0:T(1,128)} %bitcast.35), calls=%async_computation.1 | async-start | bytes 131072 | tf_op jit(solution)/shard_map/all_to_all | solution.py:57
  68.9 15.4 %collective-permute-start.4 = (f32[16,16,128]{2,1,0:T(8,128)}, f32[16,16,128]{2,1,0:T(8,128)S(1)}, u32[]{:S(2)}, u32[]{:S(2)}) collective-permute-start(f32[16,16,128]{2,1,0:T(8,128)} %get-tuple-element.27), channel_id=1, source_target_pairs={{0,16},{16,32},{32,48},{48,64},{64,80},{80,96},{96,112},{1,17},{17... | collective-permute-start | bytes 393224 | tf_op jit(solution)/shard_map/ppermute | solution.py:53
  72.4 11.8 %collective-permute-start.5 = (f32[16,16,128]{2,1,0:T(8,128)}, f32[16,16,128]{2,1,0:T(8,128)}, u32[]{:S(2)}, u32[]{:S(2)}) collective-permute-start(f32[16,16,128]{2,1,0:T(8,128)} %get-tuple-element.28), channel_id=1, source_target_pairs={{16,0},{32,16},{48,32},{64,48},{80,64},{96,80},{112,96},{17,1},{33... | collective-permute-start | bytes 393224 | tf_op jit(solution)/shard_map/ppermute | solution.py:53
  74.3 19.4 %all-to-all-start.2 = ((f32[128,1,128]{2,1,0:T(1,128)}), f32[128,1,128]{2,1,0:T(1,128)S(1)}, u32[]{:S(2)}, u32[]{:S(2)}) async-start(f32[128,1,128]{2,1,0:T(1,128)} %bitcast.37), calls=%async_computation.2 | async-start | bytes 131072 | tf_op jit(solution)/shard_map/all_to_all | solution.py:57
  86.1 18.4 %collective-permute-start.6 = (f32[2,64,128]{2,1,0:T(8,128)}, f32[2,64,128]{2,1,0:T(8,128)}, u32[]{:S(2)}, u32[]{:S(2)}) collective-permute-start(f32[2,64,128]{2,1,0:T(8,128)} %get-tuple-element.29), channel_id=1, source_target_pairs={{0,1},{1,2},{2,3},{3,4},{4,5},{5,6},{6,7},{7,8},{8,9},{9,10},{10,1... | collective-permute-start | bytes 196616 | tf_op jit(solution)/shard_map/ppermute | solution.py:53
  90.2 14.3 %collective-permute-start.7 = (f32[2,64,128]{2,1,0:T(8,128)}, f32[2,64,128]{2,1,0:T(8,128)}, u32[]{:S(2)}, u32[]{:S(2)}) collective-permute-start(f32[2,64,128]{2,1,0:T(8,128)} %get-tuple-element.30), channel_id=1, source_target_pairs={{1,0},{2,1},{3,2},{4,3},{5,4},{6,5},{7,6},{8,7},{9,8},{10,9},{11,1... | collective-permute-start | bytes 196616 | tf_op jit(solution)/shard_map/ppermute | solution.py:53
  95.7 24.4 %all-to-all-start.3 = ((f32[128,1,128]{2,1,0:T(1,128)}), f32[128,1,128]{2,1,0:T(1,128)}, u32[]{:S(2)}, u32[]{:S(2)}) async-start(f32[128,1,128]{2,1,0:T(1,128)} %bitcast.36), calls=%async_computation.3 | async-start | bytes 131072 | tf_op jit(solution)/shard_map/all_to_all | solution.py:57

commit v8 on v7

--- a/solution.py
+++ b/solution.py
@@ -139,7 +139,7 @@
 
 
 def first_projection(field, coefficient, basis, slots, margin):
-    group = 8
+    group = 16
     rows = 2 * LEVELS + VECTORS
     edge_rows = jax.ShapeDtypeStruct((rows, LEVELS, COLS), jnp.float32)
     edge_cols = jax.ShapeDtypeStruct((LEVELS // 2, ROWS, COLS), jnp.float32)
@@ -218,7 +218,7 @@
 
 
 def first_pack_kernel(
-    told_ref, source_ref, absorption_ref, low_ref, high_ref, sides_hbm, forward_ref, backward_ref, sides_ref, sem
+    source_ref, absorption_ref, low_ref, high_ref, sides_hbm, forward_ref, backward_ref, sides_ref, sem
 ):
     copy = pltpu.make_async_copy(sides_hbm, sides_ref, sem)
     copy.start()
@@ -251,7 +251,7 @@
         out_shape=[strips, strips],
         scratch_shapes=scratch,
         compiler_params=pltpu.CompilerParams(vmem_limit_bytes=VMEM_LIMIT),
-        cost_estimate=pl.CostEstimate(flops=2000000, bytes_accessed=2000000, transcendentals=0),
+        cost_estimate=pl.CostEstimate(flops=3000000000, bytes_accessed=1000000, transcendentals=0),
         name="strips",
     )(*operands)
 
@@ -263,6 +263,7 @@
         out_shape=pltpu.HBM((COLS, COLS), jnp.float32),
         scratch_shapes=[pltpu.VMEM((VECTORS, COLS * VECTORS), jnp.float32), pltpu.SemaphoreType.DMA],
         compiler_params=pltpu.CompilerParams(vmem_limit_bytes=VMEM_LIMIT),
+        cost_estimate=pl.CostEstimate(flops=9200000000, bytes_accessed=1000000, transcendentals=0),
         name="coarse_rows",
     )(*operands)
 
@@ -763,9 +764,9 @@
     )
     low, high = exchange(ahead, behind, "gx")
     told = everyone(rows)
-    fields = [pl.BlockSpec(memory_space=pltpu.HBM)] + [VMEM_SPEC] * 2 + [FIELDS_SPEC] * 2 + [HBM_SPEC]
+    fields = [VMEM_SPEC] * 2 + [FIELDS_SPEC] * 2 + [HBM_SPEC]
     strips = exchange(
-        *pack(first_pack_kernel, fields, 6, [scratch(LEVELS // 2, ROWS, COLS), pltpu.SemaphoreType.DMA], told, source, absorption, low, high, in_hbm(sides)), "gy"
+        *pack(first_pack_kernel, fields, 6, [scratch(LEVELS // 2, ROWS, COLS), pltpu.SemaphoreType.DMA], source, absorption, low, high, in_hbm(sides)), "gy"
     )
     coarse = everyone(solve_rows(told, told, in_hbm(coarse_inverse)))
     first_sum = smooth(place, table, told, source, low, high, strips, absorption)

time: 148 us -> 139 us (0.939)
  blocking collectives: 39.2 us -> 19.2 us
  starting transfers between devices: 47.5 us -> 57.3 us
  waiting for transfers between devices: 2.29 us -> 6.59 us
  Pallas kernels: 56.2 us -> 52.7 us
    all_to_all x2 -> x1, blocking collectives: 39.2 us -> 19.2 us  [everyone(): return lax.all_to_all(rows, AXES, 0, 0, tiled=True)]
    all_to_all x3 -> x4, starting transfers between devices: 26.4 us -> 36 us  [everyone(): return lax.all_to_all(rows, AXES, 0, 0, tiled=True)]
    all_to_all x3 -> x4, waiting for transfers between devices: 2.27 us -> 6.57 us  [everyone(): return lax.all_to_all(rows, AXES, 0, 0, tiled=True)]
    pallas_call x2, Pallas kernels: 29.8 us -> 27.2 us  [smooth(): pl.pallas_call(functools.partial(smooth_kernel, not more), grid=(1,), in_...]
  transfers between devices with their start and end apart: 11 -> 12, of which waited for: 1 -> 2; matrix products, arithmetic and copies ran while one was open for 0% -> 0% of each run, Pallas kernels for 24% -> 25%
where the time goes in v8:
time: 139 us; the launch traced here: 138 us
  starting transfers between devices  57.3 us (41%)
  Pallas kernels  52.7 us (38%)
  blocking collectives  19.2 us (14%)
  waiting for transfers between devices  6.59 us (5%)
  between operations  1.59 us (1%)
    all_to_all x4, starting transfers between devices, everyone(): return lax.all_to_all(rows, AXES, 0, 0, tiled=True)  36 us
    pallas_call x2, Pallas kernels, smooth(): pl.pallas_call(functools.partial(smooth_kernel, not more), grid=(1,), in_...  27.2 us
    all_to_all x1, blocking collectives, everyone(): return lax.all_to_all(rows, AXES, 0, 0, tiled=True)  19.2 us
    ppermute x4, starting transfers between devices, exchange(): lax.ppermute(forward_value, axis, forward)  14.9 us
    all_to_all x4, waiting for transfers between devices, everyone(): return lax.all_to_all(rows, AXES, 0, 0, tiled=True)  6.57 us
    ppermute x4, starting transfers between devices, exchange(): lax.ppermute(backward_value, axis, backward)  6.43 us
    pallas_call x1, Pallas kernels, first_projection(): pl.pallas_call(first_kernel, grid=(VECTORS // group,), in_specs=[block_sp...  5.88 us
    pallas_call x1, Pallas kernels, shards(): pl.pallas_call(first_coarse_kernel, in_specs=[SMEM_SPEC] + [VMEM_SPEC] *...  5.85 us
  transfers between devices with their start and end apart: 12, of which 2 were waited for; matrix products, arithmetic and copies ran while one was open for 0% of the time, Pallas kernels for 25%

profile of v8, /device:TPU:1, one launch (start us, length us, event | category | flops | bytes accessed | tf_op | source)
XLA Modules:
  0.0 138.4 jit_solution(195846328301907803)
XLA Ops:
  0.6 0.0 copy-start
  0.6 0.0 copy-start.1
  1.4 5.9 %first_projection.1 = (f32[128,128]{1,0:T(8,128)}, f32[64,16,128]{2,1,0:T(8,128)}, f32[64,16,128]{2,1,0:T(8,128)}, f32[8,32,128]{2,1,0:T(8,128)}) custom-call(f32[16,32,128]{2,1,0:T(8,128)} %source_ref.5, f32[16,32,128]{2,1,0:T(8,128)} %absorption_ref.9, bf16[32,16,32,128]{3,2,1,0:T(8,128)(2,1)} %basis_hbm.3, s32[1,1,32]{2,1,0:T(1,128)} %slots_ref.1, ...), custom_call_target="tpu_custom_call" | custom-call | tf_op jit(solution)/shard_map/first_projection/pallas_call | solution.py:149
  7.2 4.6 %collective-permute-start = (f32[64,16,128]{2,1,0:T(8,128)}, f32[64,16,128]{2,1,0:T(8,128)S(1)}, u32[]{:S(2)}, u32[]{:S(2)}) collective-permute-start(f32[64,16,128]{2,1,0:T(8,128)} %get-tuple-element.20), channel_id=1, source_target_pairs={{0,16},{16,32},{32,48},{48,64},{64,80},{80,96},{96,112},{1,17},{17... | collective-permute-start | bytes 1572872 | tf_op jit(solution)/shard_map/ppermute | solution.py:53
  11.8 1.9 %collective-permute-start.1 = (f32[64,16,128]{2,1,0:T(8,128)}, f32[64,16,128]{2,1,0:T(8,128)S(1)}, u32[]{:S(2)}, u32[]{:S(2)}) collective-permute-start(f32[64,16,128]{2,1,0:T(8,128)} %get-tuple-element.21), channel_id=1, source_target_pairs={{16,0},{32,16},{48,32},{64,48},{80,64},{96,80},{112,96},{17,1},{33... | collective-permute-start | bytes 1572872 | tf_op jit(solution)/shard_map/ppermute | solution.py:53
  13.8 10.5 %all-to-all-start = ((f32[128,1,128]{2,1,0:T(1,128)}), f32[128,1,128]{2,1,0:T(1,128)S(1)}, u32[]{:S(2)}, u32[]{:S(2)}) async-start(f32[128,1,128]{2,1,0:T(1,128)} %bitcast.35), calls=%async_computation | async-start | bytes 131072 | tf_op jit(solution)/shard_map/all_to_all | solution.py:57
  24.3 0.0 collective-permute-done.low_ref.refs_0_
  24.3 0.0 collective-permute-done.1.high_ref.refs_1_
  24.3 0.0 copy-done
  24.3 0.0 copy-done.1
  24.4 0.9 strips.2
  25.3 3.4 %collective-permute-start.2 = (f32[6,64,128]{2,1,0:T(8,128)S(1)}, f32[6,64,128]{2,1,0:T(8,128)S(1)}, u32[]{:S(2)}, u32[]{:S(2)}) collective-permute-start(f32[6,64,128]{2,1,0:T(8,128)S(1)} %get-tuple-element.23), channel_id=1, source_target_pairs={{0,1},{1,2},{2,3},{3,4},{4,5},{5,6},{6,7},{7,8},{8,9},{9,10},{10,1... | collective-permute-start | bytes 589832 | tf_op jit(solution)/shard_map/ppermute | solution.py:53
  28.7 1.3 collective-permute-start.3
  30.0 3.7 %all-to-all-done = f32[128,1,128]{2,1,0:T(1,128)S(1)} async-done(((f32[128,1,128]{2,1,0:T(1,128)}), f32[128,1,128]{2,1,0:T(1,128)S(1)}, u32[]{:S(2)}, u32[]{:S(2)}) %all-to-all-start) | async-done | bytes 65568 | tf_op jit(solution)/shard_map/all_to_all | solution.py:57
  33.8 0.0 copy-start.4
  33.8 2.0 %coarse_rows.2 = f32[128,128]{1,0:T(8,128)} custom-call(f32[128,128]{1,0:T(8,128)S(1)} %bitcast.22, f32[128,128]{1,0:T(8,128)S(1)} %bitcast.23, f32[32,4096]{1,0:T(8,128)} %inverse_hbm.3), custom_call_target="tpu_custom_call" | custom-call | flops 9200000000 | bytes 1000000 | tf_op jit(solution)/shard_map/coarse_rows/pallas_call | solution.py:260
  35.7 7.2 %all-to-all-start.1 = ((f32[128,1,128]{2,1,0:T(1,128)}), f32[128,1,128]{2,1,0:T(1,128)S(1)}, u32[]{:S(2)}, u32[]{:S(2)}) async-start(f32[128,1,128]{2,1,0:T(1,128)} %bitcast.37), calls=%async_computation.1 | async-start | bytes 131072 | tf_op jit(solution)/shard_map/all_to_all | solution.py:57
  42.9 0.1 pad_add_fusion.place_ref
  43.0 0.0 collective-permute-done.2.left_ref.refs_2_
  43.0 0.0 collective-permute-done.3.right_ref.refs_3_
  43.0 0.0 copy-done.4
  43.0 13.0 %smoother.2.sum_ref.first_sum_ref = f32[16,48,256]{2,1,0:T(8,128)S(1)} custom-call(s32[4]{0:T(128)S(1)} %pad_add_fusion.place_ref, f32[8]{0:T(128)S(1)} %copy-done.4, f32[128,128]{1,0:T(8,128)S(1)} %bitcast.24, f32[16,32,128]{2,1,0:T(8,128)S(1)} %copy-done.1, f32[64,16,128]{2,1,0:T(8,128)S(1)} %collective-permute-done.low_ref.refs_0_, ...), custom_call_target="tpu_custom_call" | custom-call | flops 2000000 | bytes 54000000 | tf_op jit(solution)/shard_map/smoother/pallas_call | solution.py:507
  56.0 0.0 all-to-all-done.1
  56.0 5.9 %direction_and_image.1 = (f32[16,32,128]{2,1,0:T(8,128)S(1)}, f32[16,32,128]{2,1,0:T(8,128)S(1)}, f32[16,16,128]{2,1,0:T(8,128)}, f32[16,16,128]{2,1,0:T(8,128)}, f32[128,128]{1,0:T(8,128)}) custom-call(s32[4]{0:T(128)S(1)} %pad_add_fusion.place_ref, f32[128,128]{1,0:T(8,128)S(1)} %bitcast.25, f32[128,128]{1,0:T(8,128)S(1)} %bitcast.33, ...), custom_call_target="tpu_custom_call" | custom-call | tf_op jit(solution)/shard_map/direction_and_image/pallas_call | solution.py:774
  61.9 3.5 %collective-permute-start.4 = (f32[16,16,128]{2,1,0:T(8,128)}, f32[16,16,128]{2,1,0:T(8,128)S(1)}, u32[]{:S(2)}, u32[]{:S(2)}) collective-permute-start(f32[16,16,128]{2,1,0:T(8,128)} %get-tuple-element.27), channel_id=1, source_target_pairs={{0,16},{16,32},{32,48},{48,64},{64,80},{80,96},{96,112},{1,17},{17... | collective-permute-start | bytes 393224 | tf_op jit(solution)/shard_map/ppermute | solution.py:53
  65.4 1.9 %collective-permute-start.5 = (f32[16,16,128]{2,1,0:T(8,128)}, f32[16,16,128]{2,1,0:T(8,128)}, u32[]{:S(2)}, u32[]{:S(2)}) collective-permute-start(f32[16,16,128]{2,1,0:T(8,128)} %get-tuple-element.28), channel_id=1, source_target_pairs={{16,0},{32,16},{48,32},{64,48},{80,64},{96,80},{112,96},{17,1},{33... | collective-permute-start | bytes 393224 | tf_op jit(solution)/shard_map/ppermute | solution.py:53
  67.4 9.9 %all-to-all-start.2 = ((f32[128,1,128]{2,1,0:T(1,128)}), f32[128,1,128]{2,1,0:T(1,128)S(1)}, u32[]{:S(2)}, u32[]{:S(2)}) async-start(f32[128,1,128]{2,1,0:T(1,128)} %bitcast.36), calls=%async_computation.2 | async-start | bytes 131072 | tf_op jit(solution)/shard_map/all_to_all | solution.py:57
  77.2 0.0 collective-permute-done.4.low_ref
  77.2 0.0 copy-start.2
  77.3 0.0 collective-permute-done.5.high_ref
  77.3 2.0 %strips.3 = (f32[2,64,128]{2,1,0:T(8,128)}, f32[2,64,128]{2,1,0:T(8,128)}) custom-call(f32[16,32,128]{2,1,0:T(8,128)S(1)} %get-tuple-element.26.block_ref.first_ref, f32[16,16,128]{2,1,0:T(8,128)S(1)} %collective-permute-done.4.low_ref, f32[16,16,128]{2,1,0:T(8,128)} %collective-permute-done.5.high_ref), custom_call_target="tpu_custom_call" | custom-call | flops 3000000000 | bytes 1000000 | tf_op jit(solution)/shard_map/strips/pallas_call | solution.py:247
  79.2 0.0 copy-done.2
  79.2 3.4 %collective-permute-start.6 = (f32[2,64,128]{2,1,0:T(8,128)}, f32[2,64,128]{2,1,0:T(8,128)S(1)}, u32[]{:S(2)}, u32[]{:S(2)}) collective-permute-start(f32[2,64,128]{2,1,0:T(8,128)} %get-tuple-element.29), channel_id=1, source_target_pairs={{0,1},{1,2},{2,3},{3,4},{4,5},{5,6},{6,7},{7,8},{8,9},{9,10},{10,1... | collective-permute-start | bytes 196616 | tf_op jit(solution)/shard_map/ppermute | solution.py:53
  82.6 1.3 collective-permute-start.7
  83.9 2.8 %all-to-all-done.2 = f32[128,1,128]{2,1,0:T(1,128)S(1)} async-done(((f32[128,1,128]{2,1,0:T(1,128)}), f32[128,1,128]{2,1,0:T(1,128)S(1)}, u32[]{:S(2)}, u32[]{:S(2)}) %all-to-all-start.2) | async-done | bytes 65568 | tf_op jit(solution)/shard_map/all_to_all | solution.py:57
  86.8 2.0 %coarse_rows.3 = f32[128,128]{1,0:T(8,128)} custom-call(f32[128,128]{1,0:T(8,128)S(1)} %bitcast.29, f32[128,128]{1,0:T(8,128)S(1)} %bitcast.26, f32[32,4096]{1,0:T(8,128)} %inverse_hbm.3), custom_call_target="tpu_custom_call" | custom-call | flops 9200000000 | bytes 1000000 | tf_op jit(solution)/shard_map/coarse_rows/pallas_call | solution.py:260
  88.7 8.4 %all-to-all-start.3 = ((f32[128,1,128]{2,1,0:T(1,128)}), f32[128,1,128]{2,1,0:T(1,128)S(1)}, u32[]{:S(2)}, u32[]{:S(2)}) async-start(f32[128,1,128]{2,1,0:T(1,128)} %bitcast.38), calls=%async_computation.3 | async-start | bytes 131072 | tf_op jit(solution)/shard_map/all_to_all | solution.py:57
  97.1 0.0 collective-permute-done.6.left_ref
  97.1 0.0 collective-permute-done.7.right_ref
  97.2 0.0 copy-start.3
  97.2 0.9 copy-done.3
  98.1 14.3 %smoother.3.sum_hbm = f32[16,48,256]{2,1,0:T(8,128)} custom-call(s32[4]{0:T(128)S(1)} %pad_add_fusion.place_ref, f32[8]{0:T(128)S(1)} %copy-done.4, f32[128,128]{1,0:T(8,128)S(1)} %bitcast.27, f32[16,32,128]{2,1,0:T(8,128)S(1)} %get-tuple-element.26.block_ref.first_ref, f32[16,16,128]{2,1,0:T(8,128)S(1)} %copy-done.3, ...), custom_call_target="tpu_custom_call" | custom-call | flops 2000000 | bytes 54000000 | tf_op jit(solution)/shard_map/smoother/pallas_call | solution.py:507
  112.3 0.0 all-to-all-done.3
  112.3 5.2 %second_images.1 = (f32[16,32,128]{2,1,0:T(8,128)S(1)}, f32[16,32,128]{2,1,0:T(8,128)S(1)}, f32[16,32,128]{2,1,0:T(8,128)S(1)}, f32[128,128]{1,0:T(8,128)}) custom-call(s32[4]{0:T(128)S(1)} %pad_add_fusion.place_ref, f32[128,128]{1,0:T(8,128)S(1)} %bitcast.28, f32[128,128]{1,0:T(8,128)S(1)} %bitcast.32, bf16[32,16,32,128]{3,2,1,0:T(8,128)(2,1)} %basis_hbm.3, ...), custom_call_target="tpu_custom_call" | custom-call | tf_op jit(solution)/shard_map/second_images/pallas_call | solution.py:787
  117.5 19.2 %all_to_all.55 = f32[128,1,128]{2,1,0:T(1,128)S(1)} all-to-all(f32[128,1,128]{2,1,0:T(1,128)} %bitcast.39), channel_id=1, replica_groups=mesh['gx'=8,'gy'=16] {'gx','gy'}, dimensions={0} | all-to-all | bytes 131072 | tf_op jit(solution)/shard_map/all_to_all | solution.py:57
  136.8 1.7 %update.1 = (f32[16,32,128]{2,1,0:T(8,128)}, f32[16,32,128]{2,1,0:T(8,128)}) custom-call(f32[128,128]{1,0:T(8,128)S(1)} %bitcast.31, f32[128,128]{1,0:T(8,128)S(1)} %bitcast.34, f32[16,32,128]{2,1,0:T(8,128)S(1)} %get-tuple-element.31.direction_ref, f32[16,32,128]{2,1,0:T(8,128)S(1)} %get-tuple-element.26.block_ref.first_ref, ...), custom_call_target="tpu_custom_call" | custom-call | tf_op jit(solution)/shard_map/update/pallas_call | solution.py:796
Async XLA Ops:
  0.6 23.7 %copy-start = (f32[16,32,128]{2,1,0:T(8,128)S(1)}, f32[16,32,128]{2,1,0:T(8,128)}, u32[]{:S(2)}) copy-start(f32[16,32,128]{2,1,0:T(8,128)} %absorption_ref.9) | copy-start | bytes 786436
  0.6 23.7 %copy-start.1 = (f32[16,32,128]{2,1,0:T(8,128)S(1)}, f32[16,32,128]{2,1,0:T(8,128)}, u32[]{:S(2)}) copy-start(f32[16,32,128]{2,1,0:T(8,128)} %source_ref.5) | copy-start | bytes 786436
  7.2 17.1 %collective-permute-start = (f32[64,16,128]{2,1,0:T(8,128)}, f32[64,16,128]{2,1,0:T(8,128)S(1)}, u32[]{:S(2)}, u32[]{:S(2)}) collective-permute-start(f32[64,16,128]{2,1,0:T(8,128)} %get-tuple-element.20), channel_id=1, source_target_pairs={{0,16},{16,32},{32,48},{48,64},{64,80},{80,96},{96,112},{1,17},{17... | collective-permute-start | bytes 1572872 | tf_op jit(solution)/shard_map/ppermute | solution.py:53
  11.8 12.5 %collective-permute-start.1 = (f32[64,16,128]{2,1,0:T(8,128)}, f32[64,16,128]{2,1,0:T(8,128)S(1)}, u32[]{:S(2)}, u32[]{:S(2)}) collective-permute-start(f32[64,16,128]{2,1,0:T(8,128)} %get-tuple-element.21), channel_id=1, source_target_pairs={{16,0},{32,16},{48,32},{64,48},{80,64},{96,80},{112,96},{17,1},{33... | collective-permute-start | bytes 1572872 | tf_op jit(solution)/shard_map/ppermute | solution.py:53
  13.8 20.0 %all-to-all-start = ((f32[128,1,128]{2,1,0:T(1,128)}), f32[128,1,128]{2,1,0:T(1,128)S(1)}, u32[]{:S(2)}, u32[]{:S(2)}) async-start(f32[128,1,128]{2,1,0:T(1,128)} %bitcast.35), calls=%async_computation | async-start | bytes 131072 | tf_op jit(solution)/shard_map/all_to_all | solution.py:57
  25.3 17.7 %collective-permute-start.2 = (f32[6,64,128]{2,1,0:T(8,128)S(1)}, f32[6,64,128]{2,1,0:T(8,128)S(1)}, u32[]{:S(2)}, u32[]{:S(2)}) collective-permute-start(f32[6,64,128]{2,1,0:T(8,128)S(1)} %get-tuple-element.23), channel_id=1, source_target_pairs={{0,1},{1,2},{2,3},{3,4},{4,5},{5,6},{6,7},{7,8},{8,9},{9,10},{10,1... | collective-permute-start | bytes 589832 | tf_op jit(solution)/shard_map/ppermute | solution.py:53
  28.7 14.3 %collective-permute-start.3 = (f32[6,64,128]{2,1,0:T(8,128)S(1)}, f32[6,64,128]{2,1,0:T(8,128)S(1)}, u32[]{:S(2)}, u32[]{:S(2)}) collective-permute-start(f32[6,64,128]{2,1,0:T(8,128)S(1)} %get-tuple-element.24), channel_id=1, source_target_pairs={{1,0},{2,1},{3,2},{4,3},{5,4},{6,5},{7,6},{8,7},{9,8},{10,9},{11,1... | collective-permute-start | bytes 589832 | tf_op jit(solution)/shard_map/ppermute | solution.py:53
  33.8 9.2 %copy-start.4 = (f32[8]{0:T(128)S(1)}, f32[8]{0:T(128)}, u32[]{:S(2)}) copy-start(f32[8]{0:T(128)} %constant.15.clone.table_ref) | copy-start | bytes 100
  35.7 20.3 %all-to-all-start.1 = ((f32[128,1,128]{2,1,0:T(1,128)}), f32[128,1,128]{2,1,0:T(1,128)S(1)}, u32[]{:S(2)}, u32[]{:S(2)}) async-start(f32[128,1,128]{2,1,0:T(1,128)} %bitcast.37), calls=%async_computation.1 | async-start | bytes 131072 | tf_op jit(solution)/shard_map/all_to_all | solution.py:57
  61.9 15.4 %collective-permute-start.4 = (f32[16,16,128]{2,1,0:T(8,128)}, f32[16,16,128]{2,1,0:T(8,128)S(1)}, u32[]{:S(2)}, u32[]{:S(2)}) collective-permute-start(f32[16,16,128]{2,1,0:T(8,128)} %get-tuple-element.27), channel_id=1, source_target_pairs={{0,16},{16,32},{32,48},{48,64},{64,80},{80,96},{96,112},{1,17},{17... | collective-permute-start | bytes 393224 | tf_op jit(solution)/shard_map/ppermute | solution.py:53
  65.4 11.8 %collective-permute-start.5 = (f32[16,16,128]{2,1,0:T(8,128)}, f32[16,16,128]{2,1,0:T(8,128)}, u32[]{:S(2)}, u32[]{:S(2)}) collective-permute-start(f32[16,16,128]{2,1,0:T(8,128)} %get-tuple-element.28), channel_id=1, source_target_pairs={{16,0},{32,16},{48,32},{64,48},{80,64},{96,80},{112,96},{17,1},{33... | collective-permute-start | bytes 393224 | tf_op jit(solution)/shard_map/ppermute | solution.py:53
  67.4 19.4 %all-to-all-start.2 = ((f32[128,1,128]{2,1,0:T(1,128)}), f32[128,1,128]{2,1,0:T(1,128)S(1)}, u32[]{:S(2)}, u32[]{:S(2)}) async-start(f32[128,1,128]{2,1,0:T(1,128)} %bitcast.36), calls=%async_computation.2 | async-start | bytes 131072 | tf_op jit(solution)/shard_map/all_to_all | solution.py:57
  77.2 2.0 %copy-start.2 = (f32[16,16,128]{2,1,0:T(8,128)}, f32[16,16,128]{2,1,0:T(8,128)S(1)}, u32[]{:S(2)}) copy-start(f32[16,16,128]{2,1,0:T(8,128)S(1)} %collective-permute-done.4.low_ref) | copy-start | bytes 393220
  79.2 17.9 %collective-permute-start.6 = (f32[2,64,128]{2,1,0:T(8,128)}, f32[2,64,128]{2,1,0:T(8,128)S(1)}, u32[]{:S(2)}, u32[]{:S(2)}) collective-permute-start(f32[2,64,128]{2,1,0:T(8,128)} %get-tuple-element.29), channel_id=1, source_target_pairs={{0,1},{1,2},{2,3},{3,4},{4,5},{5,6},{6,7},{7,8},{8,9},{9,10},{10,1... | collective-permute-start | bytes 196616 | tf_op jit(solution)/shard_map/ppermute | solution.py:53
  82.6 14.5 %collective-permute-start.7 = (f32[2,64,128]{2,1,0:T(8,128)}, f32[2,64,128]{2,1,0:T(8,128)}, u32[]{:S(2)}, u32[]{:S(2)}) collective-permute-start(f32[2,64,128]{2,1,0:T(8,128)} %get-tuple-element.30), channel_id=1, source_target_pairs={{1,0},{2,1},{3,2},{4,3},{5,4},{6,5},{7,6},{8,7},{9,8},{10,9},{11,1... | collective-permute-start | bytes 196616 | tf_op jit(solution)/shard_map/ppermute | solution.py:53
  88.7 23.6 %all-to-all-start.3 = ((f32[128,1,128]{2,1,0:T(1,128)}), f32[128,1,128]{2,1,0:T(1,128)S(1)}, u32[]{:S(2)}, u32[]{:S(2)}) async-start(f32[128,1,128]{2,1,0:T(1,128)} %bitcast.38), calls=%async_computation.3 | async-start | bytes 131072 | tf_op jit(solution)/shard_map/all_to_all | solution.py:57
  97.2 0.9 copy-start.3

commit v9 on v8

--- a/solution.py
+++ b/solution.py
@@ -357,9 +357,9 @@
     return center, margin, packed
 
 
-UNROLL = 8
+UNROLL = 16
 UNROLL_BEGIN = 2
-UNROLL_FINISH = 2
+UNROLL_FINISH = 4
 PLANES = LEVELS + 2
 BESIDE_TILES = (1, 2, 5, 6)
 

time: 139 us -> 136 us (0.978)
  Pallas kernels: 52.7 us -> 49.9 us
    pallas_call x2, Pallas kernels: 27.2 us -> 24.5 us  [smooth(): pl.pallas_call(functools.partial(smooth_kernel, not more), grid=(1,), in_...]
  transfers between devices with their start and end apart: 12 -> 12, of which waited for: 2 -> 2; matrix products, arithmetic and copies ran while one was open for 0% -> 0% of each run, Pallas kernels for 25% -> 23%
where the time goes in v9:
time: 136 us
  starting transfers between devices  57.4 us (42%)
  Pallas kernels  49.9 us (37%)
  blocking collectives  19.2 us (14%)
  waiting for transfers between devices  6.59 us (5%)
  between operations  1.59 us (1%)
    all_to_all x4, starting transfers between devices, everyone(): return lax.all_to_all(rows, AXES, 0, 0, tiled=True)  36 us
    pallas_call x2, Pallas kernels, smooth(): pl.pallas_call(functools.partial(smooth_kernel, not more), grid=(1,), in_...  24.5 us
    all_to_all x1, blocking collectives, everyone(): return lax.all_to_all(rows, AXES, 0, 0, tiled=True)  19.2 us
    ppermute x4, starting transfers between devices, exchange(): lax.ppermute(forward_value, axis, forward)  14.9 us
    all_to_all x4, waiting for transfers between devices, everyone(): return lax.all_to_all(rows, AXES, 0, 0, tiled=True)  6.57 us
    ppermute x4, starting transfers between devices, exchange(): lax.ppermute(backward_value, axis, backward)  6.43 us
    pallas_call x1, Pallas kernels, first_projection(): pl.pallas_call(first_kernel, grid=(VECTORS // group,), in_specs=[block_sp...  5.88 us
    pallas_call x1, Pallas kernels, shards(): pl.pallas_call(first_coarse_kernel, in_specs=[SMEM_SPEC] + [VMEM_SPEC] *...  5.85 us
  transfers between devices with their start and end apart: 12, of which 2 were waited for; matrix products, arithmetic and copies ran while one was open for 0% of the time, Pallas kernels for 23%

profile of v9, /device:TPU:1, one launch (start us, length us, event | category | flops | bytes accessed | tf_op | source)
XLA Modules:
  0.0 135.7 jit_solution(2542397424381976077)
XLA Ops:
  0.6 0.0 copy-start
  0.6 0.0 copy-start.1
  1.4 5.9 %first_projection.1 = (f32[128,128]{1,0:T(8,128)}, f32[64,16,128]{2,1,0:T(8,128)}, f32[64,16,128]{2,1,0:T(8,128)}, f32[8,32,128]{2,1,0:T(8,128)}) custom-call(f32[16,32,128]{2,1,0:T(8,128)} %source_ref.5, f32[16,32,128]{2,1,0:T(8,128)} %absorption_ref.9, bf16[32,16,32,128]{3,2,1,0:T(8,128)(2,1)} %basis_hbm.3, s32[1,1,32]{2,1,0:T(1,128)} %slots_ref.1, ...), custom_call_target="tpu_custom_call" | custom-call | tf_op jit(solution)/shard_map/first_projection/pallas_call | solution.py:149
  7.2 4.6 %collective-permute-start = (f32[64,16,128]{2,1,0:T(8,128)}, f32[64,16,128]{2,1,0:T(8,128)S(1)}, u32[]{:S(2)}, u32[]{:S(2)}) collective-permute-start(f32[64,16,128]{2,1,0:T(8,128)} %get-tuple-element.20), channel_id=1, source_target_pairs={{0,16},{16,32},{32,48},{48,64},{64,80},{80,96},{96,112},{1,17},{17... | collective-permute-start | bytes 1572872 | tf_op jit(solution)/shard_map/ppermute | solution.py:53
  11.8 1.9 %collective-permute-start.1 = (f32[64,16,128]{2,1,0:T(8,128)}, f32[64,16,128]{2,1,0:T(8,128)S(1)}, u32[]{:S(2)}, u32[]{:S(2)}) collective-permute-start(f32[64,16,128]{2,1,0:T(8,128)} %get-tuple-element.21), channel_id=1, source_target_pairs={{16,0},{32,16},{48,32},{64,48},{80,64},{96,80},{112,96},{17,1},{33... | collective-permute-start | bytes 1572872 | tf_op jit(solution)/shard_map/ppermute | solution.py:53
  13.8 10.6 %all-to-all-start = ((f32[128,1,128]{2,1,0:T(1,128)}), f32[128,1,128]{2,1,0:T(1,128)S(1)}, u32[]{:S(2)}, u32[]{:S(2)}) async-start(f32[128,1,128]{2,1,0:T(1,128)} %bitcast.35), calls=%async_computation | async-start | bytes 131072 | tf_op jit(solution)/shard_map/all_to_all | solution.py:57
  24.3 0.0 collective-permute-done.low_ref.refs_0_
  24.3 0.0 collective-permute-done.1.high_ref.refs_1_
  24.3 0.0 copy-done
  24.3 0.0 copy-done.1
  24.4 0.9 strips.2
  25.3 3.4 %collective-permute-start.2 = (f32[6,64,128]{2,1,0:T(8,128)S(1)}, f32[6,64,128]{2,1,0:T(8,128)S(1)}, u32[]{:S(2)}, u32[]{:S(2)}) collective-permute-start(f32[6,64,128]{2,1,0:T(8,128)S(1)} %get-tuple-element.23), channel_id=1, source_target_pairs={{0,1},{1,2},{2,3},{3,4},{4,5},{5,6},{6,7},{7,8},{8,9},{9,10},{10,1... | collective-permute-start | bytes 589832 | tf_op jit(solution)/shard_map/ppermute | solution.py:53
  28.7 1.3 collective-permute-start.3
  30.0 3.7 %all-to-all-done = f32[128,1,128]{2,1,0:T(1,128)S(1)} async-done(((f32[128,1,128]{2,1,0:T(1,128)}), f32[128,1,128]{2,1,0:T(1,128)S(1)}, u32[]{:S(2)}, u32[]{:S(2)}) %all-to-all-start) | async-done | bytes 65568 | tf_op jit(solution)/shard_map/all_to_all | solution.py:57
  33.8 0.0 copy-start.4
  33.8 2.0 %coarse_rows.2 = f32[128,128]{1,0:T(8,128)} custom-call(f32[128,128]{1,0:T(8,128)S(1)} %bitcast.22, f32[128,128]{1,0:T(8,128)S(1)} %bitcast.23, f32[32,4096]{1,0:T(8,128)} %inverse_hbm.3), custom_call_target="tpu_custom_call" | custom-call | flops 9200000000 | bytes 1000000 | tf_op jit(solution)/shard_map/coarse_rows/pallas_call | solution.py:260
  35.7 7.2 %all-to-all-start.1 = ((f32[128,1,128]{2,1,0:T(1,128)}), f32[128,1,128]{2,1,0:T(1,128)S(1)}, u32[]{:S(2)}, u32[]{:S(2)}) async-start(f32[128,1,128]{2,1,0:T(1,128)} %bitcast.37), calls=%async_computation.1 | async-start | bytes 131072 | tf_op jit(solution)/shard_map/all_to_all | solution.py:57
  42.9 0.1 pad_add_fusion.place_ref
  43.0 0.0 collective-permute-done.2.left_ref.refs_2_
  43.0 0.0 collective-permute-done.3.right_ref.refs_3_
  43.0 0.0 copy-done.4
  43.0 11.6 %smoother.2.sum_ref.first_sum_ref = f32[16,48,256]{2,1,0:T(8,128)S(1)} custom-call(s32[4]{0:T(128)S(1)} %pad_add_fusion.place_ref, f32[8]{0:T(128)S(1)} %copy-done.4, f32[128,128]{1,0:T(8,128)S(1)} %bitcast.24, f32[16,32,128]{2,1,0:T(8,128)S(1)} %copy-done.1, f32[64,16,128]{2,1,0:T(8,128)S(1)} %collective-permute-done.low_ref.refs_0_, ...), custom_call_target="tpu_custom_call" | custom-call | flops 2000000 | bytes 54000000 | tf_op jit(solution)/shard_map/smoother/pallas_call | solution.py:507
  54.6 0.0 all-to-all-done.1
  54.7 5.9 %direction_and_image.1 = (f32[16,32,128]{2,1,0:T(8,128)S(1)}, f32[16,32,128]{2,1,0:T(8,128)S(1)}, f32[16,16,128]{2,1,0:T(8,128)}, f32[16,16,128]{2,1,0:T(8,128)}, f32[128,128]{1,0:T(8,128)}) custom-call(s32[4]{0:T(128)S(1)} %pad_add_fusion.place_ref, f32[128,128]{1,0:T(8,128)S(1)} %bitcast.25, f32[128,128]{1,0:T(8,128)S(1)} %bitcast.33, ...), custom_call_target="tpu_custom_call" | custom-call | tf_op jit(solution)/shard_map/direction_and_image/pallas_call | solution.py:774
  60.5 3.5 %collective-permute-start.4 = (f32[16,16,128]{2,1,0:T(8,128)}, f32[16,16,128]{2,1,0:T(8,128)S(1)}, u32[]{:S(2)}, u32[]{:S(2)}) collective-permute-start(f32[16,16,128]{2,1,0:T(8,128)} %get-tuple-element.27), channel_id=1, source_target_pairs={{0,16},{16,32},{32,48},{48,64},{64,80},{80,96},{96,112},{1,17},{17... | collective-permute-start | bytes 393224 | tf_op jit(solution)/shard_map/ppermute | solution.py:53
  64.1 1.9 %collective-permute-start.5 = (f32[16,16,128]{2,1,0:T(8,128)}, f32[16,16,128]{2,1,0:T(8,128)}, u32[]{:S(2)}, u32[]{:S(2)}) collective-permute-start(f32[16,16,128]{2,1,0:T(8,128)} %get-tuple-element.28), channel_id=1, source_target_pairs={{16,0},{32,16},{48,32},{64,48},{80,64},{96,80},{112,96},{17,1},{33... | collective-permute-start | bytes 393224 | tf_op jit(solution)/shard_map/ppermute | solution.py:53
  66.0 9.9 %all-to-all-start.2 = ((f32[128,1,128]{2,1,0:T(1,128)}), f32[128,1,128]{2,1,0:T(1,128)S(1)}, u32[]{:S(2)}, u32[]{:S(2)}) async-start(f32[128,1,128]{2,1,0:T(1,128)} %bitcast.36), calls=%async_computation.2 | async-start | bytes 131072 | tf_op jit(solution)/shard_map/all_to_all | solution.py:57
  75.9 0.0 collective-permute-done.4.low_ref
  75.9 0.0 copy-start.2
  75.9 0.0 collective-permute-done.5.high_ref
  75.9 2.0 %strips.3 = (f32[2,64,128]{2,1,0:T(8,128)}, f32[2,64,128]{2,1,0:T(8,128)}) custom-call(f32[16,32,128]{2,1,0:T(8,128)S(1)} %get-tuple-element.26.block_ref.first_ref, f32[16,16,128]{2,1,0:T(8,128)S(1)} %collective-permute-done.4.low_ref, f32[16,16,128]{2,1,0:T(8,128)} %collective-permute-done.5.high_ref), custom_call_target="tpu_custom_call" | custom-call | flops 3000000000 | bytes 1000000 | tf_op jit(solution)/shard_map/strips/pallas_call | solution.py:247
  77.9 0.0 copy-done.2
  77.9 3.4 %collective-permute-start.6 = (f32[2,64,128]{2,1,0:T(8,128)}, f32[2,64,128]{2,1,0:T(8,128)S(1)}, u32[]{:S(2)}, u32[]{:S(2)}) collective-permute-start(f32[2,64,128]{2,1,0:T(8,128)} %get-tuple-element.29), channel_id=1, source_target_pairs={{0,1},{1,2},{2,3},{3,4},{4,5},{5,6},{6,7},{7,8},{8,9},{9,10},{10,1... | collective-permute-start | bytes 196616 | tf_op jit(solution)/shard_map/ppermute | solution.py:53
  81.3 1.3 collective-permute-start.7
  82.6 2.8 %all-to-all-done.2 = f32[128,1,128]{2,1,0:T(1,128)S(1)} async-done(((f32[128,1,128]{2,1,0:T(1,128)}), f32[128,1,128]{2,1,0:T(1,128)S(1)}, u32[]{:S(2)}, u32[]{:S(2)}) %all-to-all-start.2) | async-done | bytes 65568 | tf_op jit(solution)/shard_map/all_to_all | solution.py:57
  85.4 2.0 %coarse_rows.3 = f32[128,128]{1,0:T(8,128)} custom-call(f32[128,128]{1,0:T(8,128)S(1)} %bitcast.29, f32[128,128]{1,0:T(8,128)S(1)} %bitcast.26, f32[32,4096]{1,0:T(8,128)} %inverse_hbm.3), custom_call_target="tpu_custom_call" | custom-call | flops 9200000000 | bytes 1000000 | tf_op jit(solution)/shard_map/coarse_rows/pallas_call | solution.py:260
  87.4 8.4 %all-to-all-start.3 = ((f32[128,1,128]{2,1,0:T(1,128)}), f32[128,1,128]{2,1,0:T(1,128)S(1)}, u32[]{:S(2)}, u32[]{:S(2)}) async-start(f32[128,1,128]{2,1,0:T(1,128)} %bitcast.38), calls=%async_computation.3 | async-start | bytes 131072 | tf_op jit(solution)/shard_map/all_to_all | solution.py:57
  95.8 0.0 collective-permute-done.6.left_ref
  95.8 0.0 collective-permute-done.7.right_ref
  95.8 0.0 copy-start.3
  95.8 0.9 copy-done.3
  96.7 12.9 %smoother.3.sum_hbm = f32[16,48,256]{2,1,0:T(8,128)} custom-call(s32[4]{0:T(128)S(1)} %pad_add_fusion.place_ref, f32[8]{0:T(128)S(1)} %copy-done.4, f32[128,128]{1,0:T(8,128)S(1)} %bitcast.27, f32[16,32,128]{2,1,0:T(8,128)S(1)} %get-tuple-element.26.block_ref.first_ref, f32[16,16,128]{2,1,0:T(8,128)S(1)} %copy-done.3, ...), custom_call_target="tpu_custom_call" | custom-call | flops 2000000 | bytes 54000000 | tf_op jit(solution)/shard_map/smoother/pallas_call | solution.py:507
  109.6 0.0 all-to-all-done.3
  109.6 5.2 %second_images.1 = (f32[16,32,128]{2,1,0:T(8,128)S(1)}, f32[16,32,128]{2,1,0:T(8,128)S(1)}, f32[16,32,128]{2,1,0:T(8,128)S(1)}, f32[128,128]{1,0:T(8,128)}) custom-call(s32[4]{0:T(128)S(1)} %pad_add_fusion.place_ref, f32[128,128]{1,0:T(8,128)S(1)} %bitcast.28, f32[128,128]{1,0:T(8,128)S(1)} %bitcast.32, bf16[32,16,32,128]{3,2,1,0:T(8,128)(2,1)} %basis_hbm.3, ...), custom_call_target="tpu_custom_call" | custom-call | tf_op jit(solution)/shard_map/second_images/pallas_call | solution.py:787
  114.8 19.2 %all_to_all.55 = f32[128,1,128]{2,1,0:T(1,128)S(1)} all-to-all(f32[128,1,128]{2,1,0:T(1,128)} %bitcast.39), channel_id=1, replica_groups=mesh['gx'=8,'gy'=16] {'gx','gy'}, dimensions={0} | all-to-all | bytes 131072 | tf_op jit(solution)/shard_map/all_to_all | solution.py:57
  134.0 1.7 %update.1 = (f32[16,32,128]{2,1,0:T(8,128)}, f32[16,32,128]{2,1,0:T(8,128)}) custom-call(f32[128,128]{1,0:T(8,128)S(1)} %bitcast.31, f32[128,128]{1,0:T(8,128)S(1)} %bitcast.34, f32[16,32,128]{2,1,0:T(8,128)S(1)} %get-tuple-element.31.direction_ref, f32[16,32,128]{2,1,0:T(8,128)S(1)} %get-tuple-element.26.block_ref.first_ref, ...), custom_call_target="tpu_custom_call" | custom-call | tf_op jit(solution)/shard_map/update/pallas_call | solution.py:796
Async XLA Ops:
  0.6 23.7 %copy-start = (f32[16,32,128]{2,1,0:T(8,128)S(1)}, f32[16,32,128]{2,1,0:T(8,128)}, u32[]{:S(2)}) copy-start(f32[16,32,128]{2,1,0:T(8,128)} %absorption_ref.9) | copy-start | bytes 786436
  0.6 23.7 %copy-start.1 = (f32[16,32,128]{2,1,0:T(8,128)S(1)}, f32[16,32,128]{2,1,0:T(8,128)}, u32[]{:S(2)}) copy-start(f32[16,32,128]{2,1,0:T(8,128)} %source_ref.5) | copy-start | bytes 786436
  7.2 17.1 %collective-permute-start = (f32[64,16,128]{2,1,0:T(8,128)}, f32[64,16,128]{2,1,0:T(8,128)S(1)}, u32[]{:S(2)}, u32[]{:S(2)}) collective-permute-start(f32[64,16,128]{2,1,0:T(8,128)} %get-tuple-element.20), channel_id=1, source_target_pairs={{0,16},{16,32},{32,48},{48,64},{64,80},{80,96},{96,112},{1,17},{17... | collective-permute-start | bytes 1572872 | tf_op jit(solution)/shard_map/ppermute | solution.py:53
  11.8 12.5 %collective-permute-start.1 = (f32[64,16,128]{2,1,0:T(8,128)}, f32[64,16,128]{2,1,0:T(8,128)S(1)}, u32[]{:S(2)}, u32[]{:S(2)}) collective-permute-start(f32[64,16,128]{2,1,0:T(8,128)} %get-tuple-element.21), channel_id=1, source_target_pairs={{16,0},{32,16},{48,32},{64,48},{80,64},{96,80},{112,96},{17,1},{33... | collective-permute-start | bytes 1572872 | tf_op jit(solution)/shard_map/ppermute | solution.py:53
  13.8 20.0 %all-to-all-start = ((f32[128,1,128]{2,1,0:T(1,128)}), f32[128,1,128]{2,1,0:T(1,128)S(1)}, u32[]{:S(2)}, u32[]{:S(2)}) async-start(f32[128,1,128]{2,1,0:T(1,128)} %bitcast.35), calls=%async_computation | async-start | bytes 131072 | tf_op jit(solution)/shard_map/all_to_all | solution.py:57
  25.3 17.7 %collective-permute-start.2 = (f32[6,64,128]{2,1,0:T(8,128)S(1)}, f32[6,64,128]{2,1,0:T(8,128)S(1)}, u32[]{:S(2)}, u32[]{:S(2)}) collective-permute-start(f32[6,64,128]{2,1,0:T(8,128)S(1)} %get-tuple-element.23), channel_id=1, source_target_pairs={{0,1},{1,2},{2,3},{3,4},{4,5},{5,6},{6,7},{7,8},{8,9},{9,10},{10,1... | collective-permute-start | bytes 589832 | tf_op jit(solution)/shard_map/ppermute | solution.py:53
  28.7 14.3 %collective-permute-start.3 = (f32[6,64,128]{2,1,0:T(8,128)S(1)}, f32[6,64,128]{2,1,0:T(8,128)S(1)}, u32[]{:S(2)}, u32[]{:S(2)}) collective-permute-start(f32[6,64,128]{2,1,0:T(8,128)S(1)} %get-tuple-element.24), channel_id=1, source_target_pairs={{1,0},{2,1},{3,2},{4,3},{5,4},{6,5},{7,6},{8,7},{9,8},{10,9},{11,1... | collective-permute-start | bytes 589832 | tf_op jit(solution)/shard_map/ppermute | solution.py:53
  33.8 9.2 %copy-start.4 = (f32[8]{0:T(128)S(1)}, f32[8]{0:T(128)}, u32[]{:S(2)}) copy-start(f32[8]{0:T(128)} %constant.15.clone.table_ref) | copy-start | bytes 100
  35.7 18.9 %all-to-all-start.1 = ((f32[128,1,128]{2,1,0:T(1,128)}), f32[128,1,128]{2,1,0:T(1,128)S(1)}, u32[]{:S(2)}, u32[]{:S(2)}) async-start(f32[128,1,128]{2,1,0:T(1,128)} %bitcast.37), calls=%async_computation.1 | async-start | bytes 131072 | tf_op jit(solution)/shard_map/all_to_all | solution.py:57
  60.5 15.4 %collective-permute-start.4 = (f32[16,16,128]{2,1,0:T(8,128)}, f32[16,16,128]{2,1,0:T(8,128)S(1)}, u32[]{:S(2)}, u32[]{:S(2)}) collective-permute-start(f32[16,16,128]{2,1,0:T(8,128)} %get-tuple-element.27), channel_id=1, source_target_pairs={{0,16},{16,32},{32,48},{48,64},{64,80},{80,96},{96,112},{1,17},{17... | collective-permute-start | bytes 393224 | tf_op jit(solution)/shard_map/ppermute | solution.py:53
  64.1 11.8 %collective-permute-start.5 = (f32[16,16,128]{2,1,0:T(8,128)}, f32[16,16,128]{2,1,0:T(8,128)}, u32[]{:S(2)}, u32[]{:S(2)}) collective-permute-start(f32[16,16,128]{2,1,0:T(8,128)} %get-tuple-element.28), channel_id=1, source_target_pairs={{16,0},{32,16},{48,32},{64,48},{80,64},{96,80},{112,96},{17,1},{33... | collective-permute-start | bytes 393224 | tf_op jit(solution)/shard_map/ppermute | solution.py:53
  66.0 19.4 %all-to-all-start.2 = ((f32[128,1,128]{2,1,0:T(1,128)}), f32[128,1,128]{2,1,0:T(1,128)S(1)}, u32[]{:S(2)}, u32[]{:S(2)}) async-start(f32[128,1,128]{2,1,0:T(1,128)} %bitcast.36), calls=%async_computation.2 | async-start | bytes 131072 | tf_op jit(solution)/shard_map/all_to_all | solution.py:57
  75.9 2.0 %copy-start.2 = (f32[16,16,128]{2,1,0:T(8,128)}, f32[16,16,128]{2,1,0:T(8,128)S(1)}, u32[]{:S(2)}) copy-start(f32[16,16,128]{2,1,0:T(8,128)S(1)} %collective-permute-done.4.low_ref) | copy-start | bytes 393220
  77.9 17.9 %collective-permute-start.6 = (f32[2,64,128]{2,1,0:T(8,128)}, f32[2,64,128]{2,1,0:T(8,128)S(1)}, u32[]{:S(2)}, u32[]{:S(2)}) collective-permute-start(f32[2,64,128]{2,1,0:T(8,128)} %get-tuple-element.29), channel_id=1, source_target_pairs={{0,1},{1,2},{2,3},{3,4},{4,5},{5,6},{6,7},{7,8},{8,9},{9,10},{10,1... | collective-permute-start | bytes 196616 | tf_op jit(solution)/shard_map/ppermute | solution.py:53
  81.3 14.5 %collective-permute-start.7 = (f32[2,64,128]{2,1,0:T(8,128)}, f32[2,64,128]{2,1,0:T(8,128)}, u32[]{:S(2)}, u32[]{:S(2)}) collective-permute-start(f32[2,64,128]{2,1,0:T(8,128)} %get-tuple-element.30), channel_id=1, source_target_pairs={{1,0},{2,1},{3,2},{4,3},{5,4},{6,5},{7,6},{8,7},{9,8},{10,9},{11,1... | collective-permute-start | bytes 196616 | tf_op jit(solution)/shard_map/ppermute | solution.py:53
  87.4 22.2 %all-to-all-start.3 = ((f32[128,1,128]{2,1,0:T(1,128)}), f32[128,1,128]{2,1,0:T(1,128)S(1)}, u32[]{:S(2)}, u32[]{:S(2)}) async-start(f32[128,1,128]{2,1,0:T(1,128)} %bitcast.38), calls=%async_computation.3 | async-start | bytes 131072 | tf_op jit(solution)/shard_map/all_to_all | solution.py:57
  95.8 0.9 copy-start.3

commit v10 on v9

--- a/solution.py
+++ b/solution.py
@@ -653,7 +653,7 @@
             curve = curve + now * image
         return weight, curve
 
-    weight, curve = lax.fori_loop(0, LEVELS, images, (zero, zero), unroll=2)
+    weight, curve = lax.fori_loop(0, LEVELS, images, (zero, zero), unroll=4)
     half = VECTORS // 2
     for part in range(2):
 
@@ -663,7 +663,7 @@
                 sums[k] + fold_rows(basis_ref[part * half + k, z].astype(jnp.float32) * image) for k in range(half)
             )
 
-        sums = lax.fori_loop(0, LEVELS, level, (zero,) * half)
+        sums = lax.fori_loop(0, LEVELS, level, (zero,) * half, unroll=2)
         for k in range(half):
             sums_ref[part * half + k : part * half + k + 1] = jnp.sum(sums[k], axis=0, keepdims=True)
     lane = iota((1, COLS), 1)
@@ -708,7 +708,7 @@
             cross = cross + (precond * first + direction * image)
         return weight, own, cross
 
-    weight, own, cross = lax.fori_loop(0, LEVELS, images, (zero, zero, zero), unroll=2)
+    weight, own, cross = lax.fori_loop(0, LEVELS, images, (zero, zero, zero), unroll=4)
     mine = pl.ds(place.index(0, 0), 1)
     lane = iota((1, COLS), 1)
     again = again_ref[mine, :]

time: 136 us -> 135 us (level)
  no operation moved by 1% of the time
where the time goes in v10:
time: 135 us
  starting transfers between devices  57.4 us (43%)
  Pallas kernels  49.1 us (36%)
  blocking collectives  19.2 us (14%)
  waiting for transfers between devices  6.59 us (5%)
  between operations  1.59 us (1%)
    all_to_all x4, starting transfers between devices, everyone(): return lax.all_to_all(rows, AXES, 0, 0, tiled=True)  36 us
    pallas_call x2, Pallas kernels, smooth(): pl.pallas_call(functools.partial(smooth_kernel, not more), grid=(1,), in_...  24.5 us
    all_to_all x1, blocking collectives, everyone(): return lax.all_to_all(rows, AXES, 0, 0, tiled=True)  19.2 us
    ppermute x4, starting transfers between devices, exchange(): lax.ppermute(forward_value, axis, forward)  14.9 us
    all_to_all x4, waiting for transfers between devices, everyone(): return lax.all_to_all(rows, AXES, 0, 0, tiled=True)  6.57 us
    ppermute x4, starting transfers between devices, exchange(): lax.ppermute(backward_value, axis, backward)  6.43 us
    pallas_call x1, Pallas kernels, first_projection(): pl.pallas_call(first_kernel, grid=(VECTORS // group,), in_specs=[block_sp...  5.88 us
    pallas_call x1, Pallas kernels, shards(): pl.pallas_call(first_coarse_kernel, in_specs=[SMEM_SPEC] + [VMEM_SPEC] *...  5.41 us
  transfers between devices with their start and end apart: 12, of which 2 were waited for; matrix products, arithmetic and copies ran while one was open for 0% of the time, Pallas kernels for 23%

profile of v10, /device:TPU:1, one launch (start us, length us, event | category | flops | bytes accessed | tf_op | source)
XLA Modules:
  0.0 134.9 jit_solution(8706463566681575438)
XLA Ops:
  0.6 0.0 copy-start
  0.6 0.0 copy-start.1
  1.4 5.9 %first_projection.1 = (f32[128,128]{1,0:T(8,128)}, f32[64,16,128]{2,1,0:T(8,128)}, f32[64,16,128]{2,1,0:T(8,128)}, f32[8,32,128]{2,1,0:T(8,128)}) custom-call(f32[16,32,128]{2,1,0:T(8,128)} %source_ref.5, f32[16,32,128]{2,1,0:T(8,128)} %absorption_ref.9, bf16[32,16,32,128]{3,2,1,0:T(8,128)(2,1)} %basis_hbm.3, s32[1,1,32]{2,1,0:T(1,128)} %slots_ref.1, ...), custom_call_target="tpu_custom_call" | custom-call | tf_op jit(solution)/shard_map/first_projection/pallas_call | solution.py:149
  7.2 4.6 %collective-permute-start = (f32[64,16,128]{2,1,0:T(8,128)}, f32[64,16,128]{2,1,0:T(8,128)S(1)}, u32[]{:S(2)}, u32[]{:S(2)}) collective-permute-start(f32[64,16,128]{2,1,0:T(8,128)} %get-tuple-element.20), channel_id=1, source_target_pairs={{0,16},{16,32},{32,48},{48,64},{64,80},{80,96},{96,112},{1,17},{17... | collective-permute-start | bytes 1572872 | tf_op jit(solution)/shard_map/ppermute | solution.py:53
  11.8 1.9 %collective-permute-start.1 = (f32[64,16,128]{2,1,0:T(8,128)}, f32[64,16,128]{2,1,0:T(8,128)S(1)}, u32[]{:S(2)}, u32[]{:S(2)}) collective-permute-start(f32[64,16,128]{2,1,0:T(8,128)} %get-tuple-element.21), channel_id=1, source_target_pairs={{16,0},{32,16},{48,32},{64,48},{80,64},{96,80},{112,96},{17,1},{33... | collective-permute-start | bytes 1572872 | tf_op jit(solution)/shard_map/ppermute | solution.py:53
  13.8 10.6 %all-to-all-start = ((f32[128,1,128]{2,1,0:T(1,128)}), f32[128,1,128]{2,1,0:T(1,128)S(1)}, u32[]{:S(2)}, u32[]{:S(2)}) async-start(f32[128,1,128]{2,1,0:T(1,128)} %bitcast.35), calls=%async_computation | async-start | bytes 131072 | tf_op jit(solution)/shard_map/all_to_all | solution.py:57
  24.3 0.0 collective-permute-done.low_ref.refs_0_
  24.3 0.0 collective-permute-done.1.high_ref.refs_1_
  24.3 0.0 copy-done
  24.3 0.0 copy-done.1
  24.4 0.9 strips.2
  25.3 3.4 %collective-permute-start.2 = (f32[6,64,128]{2,1,0:T(8,128)S(1)}, f32[6,64,128]{2,1,0:T(8,128)S(1)}, u32[]{:S(2)}, u32[]{:S(2)}) collective-permute-start(f32[6,64,128]{2,1,0:T(8,128)S(1)} %get-tuple-element.23), channel_id=1, source_target_pairs={{0,1},{1,2},{2,3},{3,4},{4,5},{5,6},{6,7},{7,8},{8,9},{9,10},{10,1... | collective-permute-start | bytes 589832 | tf_op jit(solution)/shard_map/ppermute | solution.py:53
  28.7 1.3 collective-permute-start.3
  30.0 3.7 %all-to-all-done = f32[128,1,128]{2,1,0:T(1,128)S(1)} async-done(((f32[128,1,128]{2,1,0:T(1,128)}), f32[128,1,128]{2,1,0:T(1,128)S(1)}, u32[]{:S(2)}, u32[]{:S(2)}) %all-to-all-start) | async-done | bytes 65568 | tf_op jit(solution)/shard_map/all_to_all | solution.py:57
  33.8 0.0 copy-start.4
  33.8 2.0 %coarse_rows.2 = f32[128,128]{1,0:T(8,128)} custom-call(f32[128,128]{1,0:T(8,128)S(1)} %bitcast.22, f32[128,128]{1,0:T(8,128)S(1)} %bitcast.23, f32[32,4096]{1,0:T(8,128)} %inverse_hbm.3), custom_call_target="tpu_custom_call" | custom-call | flops 9200000000 | bytes 1000000 | tf_op jit(solution)/shard_map/coarse_rows/pallas_call | solution.py:260
  35.7 7.2 %all-to-all-start.1 = ((f32[128,1,128]{2,1,0:T(1,128)}), f32[128,1,128]{2,1,0:T(1,128)S(1)}, u32[]{:S(2)}, u32[]{:S(2)}) async-start(f32[128,1,128]{2,1,0:T(1,128)} %bitcast.37), calls=%async_computation.1 | async-start | bytes 131072 | tf_op jit(solution)/shard_map/all_to_all | solution.py:57
  42.9 0.1 pad_add_fusion.place_ref
  43.0 0.0 collective-permute-done.2.left_ref.refs_2_
  43.0 0.0 collective-permute-done.3.right_ref.refs_3_
  43.0 0.0 copy-done.4
  43.0 11.6 %smoother.2.sum_ref.first_sum_ref = f32[16,48,256]{2,1,0:T(8,128)S(1)} custom-call(s32[4]{0:T(128)S(1)} %pad_add_fusion.place_ref, f32[8]{0:T(128)S(1)} %copy-done.4, f32[128,128]{1,0:T(8,128)S(1)} %bitcast.24, f32[16,32,128]{2,1,0:T(8,128)S(1)} %copy-done.1, f32[64,16,128]{2,1,0:T(8,128)S(1)} %collective-permute-done.low_ref.refs_0_, ...), custom_call_target="tpu_custom_call" | custom-call | flops 2000000 | bytes 54000000 | tf_op jit(solution)/shard_map/smoother/pallas_call | solution.py:507
  54.6 0.0 all-to-all-done.1
  54.7 5.4 %direction_and_image.1 = (f32[16,32,128]{2,1,0:T(8,128)S(1)}, f32[16,32,128]{2,1,0:T(8,128)S(1)}, f32[16,16,128]{2,1,0:T(8,128)}, f32[16,16,128]{2,1,0:T(8,128)}, f32[128,128]{1,0:T(8,128)}) custom-call(s32[4]{0:T(128)S(1)} %pad_add_fusion.place_ref, f32[128,128]{1,0:T(8,128)S(1)} %bitcast.25, f32[128,128]{1,0:T(8,128)S(1)} %bitcast.33, ...), custom_call_target="tpu_custom_call" | custom-call | tf_op jit(solution)/shard_map/direction_and_image/pallas_call | solution.py:774
  60.1 3.5 %collective-permute-start.4 = (f32[16,16,128]{2,1,0:T(8,128)}, f32[16,16,128]{2,1,0:T(8,128)S(1)}, u32[]{:S(2)}, u32[]{:S(2)}) collective-permute-start(f32[16,16,128]{2,1,0:T(8,128)} %get-tuple-element.27), channel_id=1, source_target_pairs={{0,16},{16,32},{32,48},{48,64},{64,80},{80,96},{96,112},{1,17},{17... | collective-permute-start | bytes 393224 | tf_op jit(solution)/shard_map/ppermute | solution.py:53
  63.6 1.9 %collective-permute-start.5 = (f32[16,16,128]{2,1,0:T(8,128)}, f32[16,16,128]{2,1,0:T(8,128)}, u32[]{:S(2)}, u32[]{:S(2)}) collective-permute-start(f32[16,16,128]{2,1,0:T(8,128)} %get-tuple-element.28), channel_id=1, source_target_pairs={{16,0},{32,16},{48,32},{64,48},{80,64},{96,80},{112,96},{17,1},{33... | collective-permute-start | bytes 393224 | tf_op jit(solution)/shard_map/ppermute | solution.py:53
  65.6 9.9 %all-to-all-start.2 = ((f32[128,1,128]{2,1,0:T(1,128)}), f32[128,1,128]{2,1,0:T(1,128)S(1)}, u32[]{:S(2)}, u32[]{:S(2)}) async-start(f32[128,1,128]{2,1,0:T(1,128)} %bitcast.36), calls=%async_computation.2 | async-start | bytes 131072 | tf_op jit(solution)/shard_map/all_to_all | solution.py:57
  75.4 0.0 collective-permute-done.4.low_ref
  75.4 0.0 copy-start.2
  75.5 0.0 collective-permute-done.5.high_ref
  75.5 2.0 %strips.3 = (f32[2,64,128]{2,1,0:T(8,128)}, f32[2,64,128]{2,1,0:T(8,128)}) custom-call(f32[16,32,128]{2,1,0:T(8,128)S(1)} %get-tuple-element.26.block_ref.first_ref, f32[16,16,128]{2,1,0:T(8,128)S(1)} %collective-permute-done.4.low_ref, f32[16,16,128]{2,1,0:T(8,128)} %collective-permute-done.5.high_ref), custom_call_target="tpu_custom_call" | custom-call | flops 3000000000 | bytes 1000000 | tf_op jit(solution)/shard_map/strips/pallas_call | solution.py:247
  77.4 0.0 copy-done.2
  77.4 3.4 %collective-permute-start.6 = (f32[2,64,128]{2,1,0:T(8,128)}, f32[2,64,128]{2,1,0:T(8,128)S(1)}, u32[]{:S(2)}, u32[]{:S(2)}) collective-permute-start(f32[2,64,128]{2,1,0:T(8,128)} %get-tuple-element.29), channel_id=1, source_target_pairs={{0,1},{1,2},{2,3},{3,4},{4,5},{5,6},{6,7},{7,8},{8,9},{9,10},{10,1... | collective-permute-start | bytes 196616 | tf_op jit(solution)/shard_map/ppermute | solution.py:53
  80.8 1.3 collective-permute-start.7
  82.1 2.8 %all-to-all-done.2 = f32[128,1,128]{2,1,0:T(1,128)S(1)} async-done(((f32[128,1,128]{2,1,0:T(1,128)}), f32[128,1,128]{2,1,0:T(1,128)S(1)}, u32[]{:S(2)}, u32[]{:S(2)}) %all-to-all-start.2) | async-done | bytes 65568 | tf_op jit(solution)/shard_map/all_to_all | solution.py:57
  85.0 2.0 %coarse_rows.3 = f32[128,128]{1,0:T(8,128)} custom-call(f32[128,128]{1,0:T(8,128)S(1)} %bitcast.29, f32[128,128]{1,0:T(8,128)S(1)} %bitcast.26, f32[32,4096]{1,0:T(8,128)} %inverse_hbm.3), custom_call_target="tpu_custom_call" | custom-call | flops 9200000000 | bytes 1000000 | tf_op jit(solution)/shard_map/coarse_rows/pallas_call | solution.py:260
  86.9 8.4 %all-to-all-start.3 = ((f32[128,1,128]{2,1,0:T(1,128)}), f32[128,1,128]{2,1,0:T(1,128)S(1)}, u32[]{:S(2)}, u32[]{:S(2)}) async-start(f32[128,1,128]{2,1,0:T(1,128)} %bitcast.38), calls=%async_computation.3 | async-start | bytes 131072 | tf_op jit(solution)/shard_map/all_to_all | solution.py:57
  95.3 0.0 collective-permute-done.6.left_ref
  95.3 0.0 collective-permute-done.7.right_ref
  95.4 0.0 copy-start.3
  95.4 0.9 copy-done.3
  96.3 12.9 %smoother.3.sum_hbm = f32[16,48,256]{2,1,0:T(8,128)} custom-call(s32[4]{0:T(128)S(1)} %pad_add_fusion.place_ref, f32[8]{0:T(128)S(1)} %copy-done.4, f32[128,128]{1,0:T(8,128)S(1)} %bitcast.27, f32[16,32,128]{2,1,0:T(8,128)S(1)} %get-tuple-element.26.block_ref.first_ref, f32[16,16,128]{2,1,0:T(8,128)S(1)} %copy-done.3, ...), custom_call_target="tpu_custom_call" | custom-call | flops 2000000 | bytes 54000000 | tf_op jit(solution)/shard_map/smoother/pallas_call | solution.py:507
  109.2 0.0 all-to-all-done.3
  109.2 4.8 %second_images.1 = (f32[16,32,128]{2,1,0:T(8,128)S(1)}, f32[16,32,128]{2,1,0:T(8,128)S(1)}, f32[16,32,128]{2,1,0:T(8,128)S(1)}, f32[128,128]{1,0:T(8,128)}) custom-call(s32[4]{0:T(128)S(1)} %pad_add_fusion.place_ref, f32[128,128]{1,0:T(8,128)S(1)} %bitcast.28, f32[128,128]{1,0:T(8,128)S(1)} %bitcast.32, bf16[32,16,32,128]{3,2,1,0:T(8,128)(2,1)} %basis_hbm.3, ...), custom_call_target="tpu_custom_call" | custom-call | tf_op jit(solution)/shard_map/second_images/pallas_call | solution.py:787
  114.0 19.2 %all_to_all.55 = f32[128,1,128]{2,1,0:T(1,128)S(1)} all-to-all(f32[128,1,128]{2,1,0:T(1,128)} %bitcast.39), channel_id=1, replica_groups=mesh['gx'=8,'gy'=16] {'gx','gy'}, dimensions={0} | all-to-all | bytes 131072 | tf_op jit(solution)/shard_map/all_to_all | solution.py:57
  133.2 1.7 %update.1 = (f32[16,32,128]{2,1,0:T(8,128)}, f32[16,32,128]{2,1,0:T(8,128)}) custom-call(f32[128,128]{1,0:T(8,128)S(1)} %bitcast.31, f32[128,128]{1,0:T(8,128)S(1)} %bitcast.34, f32[16,32,128]{2,1,0:T(8,128)S(1)} %get-tuple-element.31.direction_ref, f32[16,32,128]{2,1,0:T(8,128)S(1)} %get-tuple-element.26.block_ref.first_ref, ...), custom_call_target="tpu_custom_call" | custom-call | tf_op jit(solution)/shard_map/update/pallas_call | solution.py:796
Async XLA Ops:
  0.6 23.7 %copy-start = (f32[16,32,128]{2,1,0:T(8,128)S(1)}, f32[16,32,128]{2,1,0:T(8,128)}, u32[]{:S(2)}) copy-start(f32[16,32,128]{2,1,0:T(8,128)} %absorption_ref.9) | copy-start | bytes 786436
  0.6 23.7 %copy-start.1 = (f32[16,32,128]{2,1,0:T(8,128)S(1)}, f32[16,32,128]{2,1,0:T(8,128)}, u32[]{:S(2)}) copy-start(f32[16,32,128]{2,1,0:T(8,128)} %source_ref.5) | copy-start | bytes 786436
  7.2 17.1 %collective-permute-start = (f32[64,16,128]{2,1,0:T(8,128)}, f32[64,16,128]{2,1,0:T(8,128)S(1)}, u32[]{:S(2)}, u32[]{:S(2)}) collective-permute-start(f32[64,16,128]{2,1,0:T(8,128)} %get-tuple-element.20), channel_id=1, source_target_pairs={{0,16},{16,32},{32,48},{48,64},{64,80},{80,96},{96,112},{1,17},{17... | collective-permute-start | bytes 1572872 | tf_op jit(solution)/shard_map/ppermute | solution.py:53
  11.8 12.5 %collective-permute-start.1 = (f32[64,16,128]{2,1,0:T(8,128)}, f32[64,16,128]{2,1,0:T(8,128)S(1)}, u32[]{:S(2)}, u32[]{:S(2)}) collective-permute-start(f32[64,16,128]{2,1,0:T(8,128)} %get-tuple-element.21), channel_id=1, source_target_pairs={{16,0},{32,16},{48,32},{64,48},{80,64},{96,80},{112,96},{17,1},{33... | collective-permute-start | bytes 1572872 | tf_op jit(solution)/shard_map/ppermute | solution.py:53
  13.8 20.0 %all-to-all-start = ((f32[128,1,128]{2,1,0:T(1,128)}), f32[128,1,128]{2,1,0:T(1,128)S(1)}, u32[]{:S(2)}, u32[]{:S(2)}) async-start(f32[128,1,128]{2,1,0:T(1,128)} %bitcast.35), calls=%async_computation | async-start | bytes 131072 | tf_op jit(solution)/shard_map/all_to_all | solution.py:57
  25.3 17.7 %collective-permute-start.2 = (f32[6,64,128]{2,1,0:T(8,128)S(1)}, f32[6,64,128]{2,1,0:T(8,128)S(1)}, u32[]{:S(2)}, u32[]{:S(2)}) collective-permute-start(f32[6,64,128]{2,1,0:T(8,128)S(1)} %get-tuple-element.23), channel_id=1, source_target_pairs={{0,1},{1,2},{2,3},{3,4},{4,5},{5,6},{6,7},{7,8},{8,9},{9,10},{10,1... | collective-permute-start | bytes 589832 | tf_op jit(solution)/shard_map/ppermute | solution.py:53
  28.7 14.3 %collective-permute-start.3 = (f32[6,64,128]{2,1,0:T(8,128)S(1)}, f32[6,64,128]{2,1,0:T(8,128)S(1)}, u32[]{:S(2)}, u32[]{:S(2)}) collective-permute-start(f32[6,64,128]{2,1,0:T(8,128)S(1)} %get-tuple-element.24), channel_id=1, source_target_pairs={{1,0},{2,1},{3,2},{4,3},{5,4},{6,5},{7,6},{8,7},{9,8},{10,9},{11,1... | collective-permute-start | bytes 589832 | tf_op jit(solution)/shard_map/ppermute | solution.py:53
  33.8 9.2 %copy-start.4 = (f32[8]{0:T(128)S(1)}, f32[8]{0:T(128)}, u32[]{:S(2)}) copy-start(f32[8]{0:T(128)} %constant.15.clone.table_ref) | copy-start | bytes 100
  35.7 18.9 %all-to-all-start.1 = ((f32[128,1,128]{2,1,0:T(1,128)}), f32[128,1,128]{2,1,0:T(1,128)S(1)}, u32[]{:S(2)}, u32[]{:S(2)}) async-start(f32[128,1,128]{2,1,0:T(1,128)} %bitcast.37), calls=%async_computation.1 | async-start | bytes 131072 | tf_op jit(solution)/shard_map/all_to_all | solution.py:57
  60.1 15.4 %collective-permute-start.4 = (f32[16,16,128]{2,1,0:T(8,128)}, f32[16,16,128]{2,1,0:T(8,128)S(1)}, u32[]{:S(2)}, u32[]{:S(2)}) collective-permute-start(f32[16,16,128]{2,1,0:T(8,128)} %get-tuple-element.27), channel_id=1, source_target_pairs={{0,16},{16,32},{32,48},{48,64},{64,80},{80,96},{96,112},{1,17},{17... | collective-permute-start | bytes 393224 | tf_op jit(solution)/shard_map/ppermute | solution.py:53
  63.6 11.8 %collective-permute-start.5 = (f32[16,16,128]{2,1,0:T(8,128)}, f32[16,16,128]{2,1,0:T(8,128)}, u32[]{:S(2)}, u32[]{:S(2)}) collective-permute-start(f32[16,16,128]{2,1,0:T(8,128)} %get-tuple-element.28), channel_id=1, source_target_pairs={{16,0},{32,16},{48,32},{64,48},{80,64},{96,80},{112,96},{17,1},{33... | collective-permute-start | bytes 393224 | tf_op jit(solution)/shard_map/ppermute | solution.py:53
  65.6 19.4 %all-to-all-start.2 = ((f32[128,1,128]{2,1,0:T(1,128)}), f32[128,1,128]{2,1,0:T(1,128)S(1)}, u32[]{:S(2)}, u32[]{:S(2)}) async-start(f32[128,1,128]{2,1,0:T(1,128)} %bitcast.36), calls=%async_computation.2 | async-start | bytes 131072 | tf_op jit(solution)/shard_map/all_to_all | solution.py:57
  75.4 2.0 %copy-start.2 = (f32[16,16,128]{2,1,0:T(8,128)}, f32[16,16,128]{2,1,0:T(8,128)S(1)}, u32[]{:S(2)}) copy-start(f32[16,16,128]{2,1,0:T(8,128)S(1)} %collective-permute-done.4.low_ref) | copy-start | bytes 393220
  77.4 17.9 %collective-permute-start.6 = (f32[2,64,128]{2,1,0:T(8,128)}, f32[2,64,128]{2,1,0:T(8,128)S(1)}, u32[]{:S(2)}, u32[]{:S(2)}) collective-permute-start(f32[2,64,128]{2,1,0:T(8,128)} %get-tuple-element.29), channel_id=1, source_target_pairs={{0,1},{1,2},{2,3},{3,4},{4,5},{5,6},{6,7},{7,8},{8,9},{9,10},{10,1... | collective-permute-start | bytes 196616 | tf_op jit(solution)/shard_map/ppermute | solution.py:53
  80.8 14.5 %collective-permute-start.7 = (f32[2,64,128]{2,1,0:T(8,128)}, f32[2,64,128]{2,1,0:T(8,128)}, u32[]{:S(2)}, u32[]{:S(2)}) collective-permute-start(f32[2,64,128]{2,1,0:T(8,128)} %get-tuple-element.30), channel_id=1, source_target_pairs={{1,0},{2,1},{3,2},{4,3},{5,4},{6,5},{7,6},{8,7},{9,8},{10,9},{11,1... | collective-permute-start | bytes 196616 | tf_op jit(solution)/shard_map/ppermute | solution.py:53
  86.9 22.2 %all-to-all-start.3 = ((f32[128,1,128]{2,1,0:T(1,128)}), f32[128,1,128]{2,1,0:T(1,128)S(1)}, u32[]{:S(2)}, u32[]{:S(2)}) async-start(f32[128,1,128]{2,1,0:T(1,128)} %bitcast.38), calls=%async_computation.3 | async-start | bytes 131072 | tf_op jit(solution)/shard_map/all_to_all | solution.py:57
  95.4 0.9 copy-start.3

commit v11 on v10

--- a/solution.py
+++ b/solution.py
@@ -562,7 +562,7 @@
         def vector(k, total):
             return total + edge[2 * LEVELS + k] * edge_c[pl.ds(n * VECTORS + k, 1), :]
 
-        ring_ref[n] = lax.fori_loop(0, VECTORS, vector, jnp.zeros((LEVELS, COLS), jnp.float32))
+        ring_ref[n] = lax.fori_loop(0, VECTORS, vector, jnp.zeros((LEVELS, COLS), jnp.float32), unroll=8)
     which = iota((COLS, COLS), 0) >> 5
     for n, (edge, values) in enumerate(((left_ref, roll(row, VECTORS)), (right_ref, other))):
         values = jnp.where(lane_row < VECTORS, values, 0.0)

time: 135 us -> 135 us (level)
  no operation moved by 1% of the time
where the time goes in v11:
time: 135 us
  starting transfers between devices  57.4 us (43%)
  Pallas kernels  49.1 us (36%)
  blocking collectives  19.2 us (14%)
  waiting for transfers between devices  6.59 us (5%)
  between operations  1.59 us (1%)
    all_to_all x4, starting transfers between devices, everyone(): return lax.all_to_all(rows, AXES, 0, 0, tiled=True)  36 us
    pallas_call x2, Pallas kernels, smooth(): pl.pallas_call(functools.partial(smooth_kernel, not more), grid=(1,), in_...  24.5 us
    all_to_all x1, blocking collectives, everyone(): return lax.all_to_all(rows, AXES, 0, 0, tiled=True)  19.2 us
    ppermute x4, starting transfers between devices, exchange(): lax.ppermute(forward_value, axis, forward)  14.9 us
    all_to_all x4, waiting for transfers between devices, everyone(): return lax.all_to_all(rows, AXES, 0, 0, tiled=True)  6.57 us
    ppermute x4, starting transfers between devices, exchange(): lax.ppermute(backward_value, axis, backward)  6.43 us
    pallas_call x1, Pallas kernels, first_projection(): pl.pallas_call(first_kernel, grid=(VECTORS // group,), in_specs=[block_sp...  5.88 us
    pallas_call x1, Pallas kernels, shards(): pl.pallas_call(first_coarse_kernel, in_specs=[SMEM_SPEC] + [VMEM_SPEC] *...  5.41 us
  transfers between devices with their start and end apart: 12, of which 2 were waited for; matrix products, arithmetic and copies ran while one was open for 0% of the time, Pallas kernels for 23%

profile of v11, /device:TPU:1, one launch (start us, length us, event | category | flops | bytes accessed | tf_op | source)
XLA Modules:
  0.0 134.9 jit_solution(7979562655577595021)
XLA Ops:
  0.6 0.0 copy-start
  0.6 0.0 copy-start.1
  1.4 5.9 %first_projection.1 = (f32[128,128]{1,0:T(8,128)}, f32[64,16,128]{2,1,0:T(8,128)}, f32[64,16,128]{2,1,0:T(8,128)}, f32[8,32,128]{2,1,0:T(8,128)}) custom-call(f32[16,32,128]{2,1,0:T(8,128)} %source_ref.5, f32[16,32,128]{2,1,0:T(8,128)} %absorption_ref.9, bf16[32,16,32,128]{3,2,1,0:T(8,128)(2,1)} %basis_hbm.3, s32[1,1,32]{2,1,0:T(1,128)} %slots_ref.1, ...), custom_call_target="tpu_custom_call" | custom-call | tf_op jit(solution)/shard_map/first_projection/pallas_call | solution.py:149
  7.2 4.6 %collective-permute-start = (f32[64,16,128]{2,1,0:T(8,128)}, f32[64,16,128]{2,1,0:T(8,128)S(1)}, u32[]{:S(2)}, u32[]{:S(2)}) collective-permute-start(f32[64,16,128]{2,1,0:T(8,128)} %get-tuple-element.20), channel_id=1, source_target_pairs={{0,16},{16,32},{32,48},{48,64},{64,80},{80,96},{96,112},{1,17},{17... | collective-permute-start | bytes 1572872 | tf_op jit(solution)/shard_map/ppermute | solution.py:53
  11.8 1.9 %collective-permute-start.1 = (f32[64,16,128]{2,1,0:T(8,128)}, f32[64,16,128]{2,1,0:T(8,128)S(1)}, u32[]{:S(2)}, u32[]{:S(2)}) collective-permute-start(f32[64,16,128]{2,1,0:T(8,128)} %get-tuple-element.21), channel_id=1, source_target_pairs={{16,0},{32,16},{48,32},{64,48},{80,64},{96,80},{112,96},{17,1},{33... | collective-permute-start | bytes 1572872 | tf_op jit(solution)/shard_map/ppermute | solution.py:53
  13.8 10.6 %all-to-all-start = ((f32[128,1,128]{2,1,0:T(1,128)}), f32[128,1,128]{2,1,0:T(1,128)S(1)}, u32[]{:S(2)}, u32[]{:S(2)}) async-start(f32[128,1,128]{2,1,0:T(1,128)} %bitcast.35), calls=%async_computation | async-start | bytes 131072 | tf_op jit(solution)/shard_map/all_to_all | solution.py:57
  24.3 0.0 collective-permute-done.low_ref.refs_0_
  24.3 0.0 collective-permute-done.1.high_ref.refs_1_
  24.3 0.0 copy-done
  24.3 0.0 copy-done.1
  24.4 0.9 strips.2
  25.3 3.4 %collective-permute-start.2 = (f32[6,64,128]{2,1,0:T(8,128)S(1)}, f32[6,64,128]{2,1,0:T(8,128)S(1)}, u32[]{:S(2)}, u32[]{:S(2)}) collective-permute-start(f32[6,64,128]{2,1,0:T(8,128)S(1)} %get-tuple-element.23), channel_id=1, source_target_pairs={{0,1},{1,2},{2,3},{3,4},{4,5},{5,6},{6,7},{7,8},{8,9},{9,10},{10,1... | collective-permute-start | bytes 589832 | tf_op jit(solution)/shard_map/ppermute | solution.py:53
  28.7 1.3 collective-permute-start.3
  30.0 3.7 %all-to-all-done = f32[128,1,128]{2,1,0:T(1,128)S(1)} async-done(((f32[128,1,128]{2,1,0:T(1,128)}), f32[128,1,128]{2,1,0:T(1,128)S(1)}, u32[]{:S(2)}, u32[]{:S(2)}) %all-to-all-start) | async-done | bytes 65568 | tf_op jit(solution)/shard_map/all_to_all | solution.py:57
  33.8 0.0 copy-start.4
  33.8 2.0 %coarse_rows.2 = f32[128,128]{1,0:T(8,128)} custom-call(f32[128,128]{1,0:T(8,128)S(1)} %bitcast.22, f32[128,128]{1,0:T(8,128)S(1)} %bitcast.23, f32[32,4096]{1,0:T(8,128)} %inverse_hbm.3), custom_call_target="tpu_custom_call" | custom-call | flops 9200000000 | bytes 1000000 | tf_op jit(solution)/shard_map/coarse_rows/pallas_call | solution.py:260
  35.7 7.2 %all-to-all-start.1 = ((f32[128,1,128]{2,1,0:T(1,128)}), f32[128,1,128]{2,1,0:T(1,128)S(1)}, u32[]{:S(2)}, u32[]{:S(2)}) async-start(f32[128,1,128]{2,1,0:T(1,128)} %bitcast.37), calls=%async_computation.1 | async-start | bytes 131072 | tf_op jit(solution)/shard_map/all_to_all | solution.py:57
  42.9 0.1 pad_add_fusion.place_ref
  43.0 0.0 collective-permute-done.2.left_ref.refs_2_
  43.0 0.0 collective-permute-done.3.right_ref.refs_3_
  43.0 0.0 copy-done.4
  43.0 11.6 %smoother.2.sum_ref.first_sum_ref = f32[16,48,256]{2,1,0:T(8,128)S(1)} custom-call(s32[4]{0:T(128)S(1)} %pad_add_fusion.place_ref, f32[8]{0:T(128)S(1)} %copy-done.4, f32[128,128]{1,0:T(8,128)S(1)} %bitcast.24, f32[16,32,128]{2,1,0:T(8,128)S(1)} %copy-done.1, f32[64,16,128]{2,1,0:T(8,128)S(1)} %collective-permute-done.low_ref.refs_0_, ...), custom_call_target="tpu_custom_call" | custom-call | flops 2000000 | bytes 54000000 | tf_op jit(solution)/shard_map/smoother/pallas_call | solution.py:507
  54.6 0.0 all-to-all-done.1
  54.7 5.4 %direction_and_image.1 = (f32[16,32,128]{2,1,0:T(8,128)S(1)}, f32[16,32,128]{2,1,0:T(8,128)S(1)}, f32[16,16,128]{2,1,0:T(8,128)}, f32[16,16,128]{2,1,0:T(8,128)}, f32[128,128]{1,0:T(8,128)}) custom-call(s32[4]{0:T(128)S(1)} %pad_add_fusion.place_ref, f32[128,128]{1,0:T(8,128)S(1)} %bitcast.25, f32[128,128]{1,0:T(8,128)S(1)} %bitcast.33, ...), custom_call_target="tpu_custom_call" | custom-call | tf_op jit(solution)/shard_map/direction_and_image/pallas_call | solution.py:774
  60.1 3.5 %collective-permute-start.4 = (f32[16,16,128]{2,1,0:T(8,128)}, f32[16,16,128]{2,1,0:T(8,128)S(1)}, u32[]{:S(2)}, u32[]{:S(2)}) collective-permute-start(f32[16,16,128]{2,1,0:T(8,128)} %get-tuple-element.27), channel_id=1, source_target_pairs={{0,16},{16,32},{32,48},{48,64},{64,80},{80,96},{96,112},{1,17},{17... | collective-permute-start | bytes 393224 | tf_op jit(solution)/shard_map/ppermute | solution.py:53
  63.6 1.9 %collective-permute-start.5 = (f32[16,16,128]{2,1,0:T(8,128)}, f32[16,16,128]{2,1,0:T(8,128)}, u32[]{:S(2)}, u32[]{:S(2)}) collective-permute-start(f32[16,16,128]{2,1,0:T(8,128)} %get-tuple-element.28), channel_id=1, source_target_pairs={{16,0},{32,16},{48,32},{64,48},{80,64},{96,80},{112,96},{17,1},{33... | collective-permute-start | bytes 393224 | tf_op jit(solution)/shard_map/ppermute | solution.py:53
  65.6 9.9 %all-to-all-start.2 = ((f32[128,1,128]{2,1,0:T(1,128)}), f32[128,1,128]{2,1,0:T(1,128)S(1)}, u32[]{:S(2)}, u32[]{:S(2)}) async-start(f32[128,1,128]{2,1,0:T(1,128)} %bitcast.36), calls=%async_computation.2 | async-start | bytes 131072 | tf_op jit(solution)/shard_map/all_to_all | solution.py:57
  75.4 0.0 collective-permute-done.4.low_ref
  75.4 0.0 copy-start.2
  75.5 0.0 collective-permute-done.5.high_ref
  75.5 2.0 %strips.3 = (f32[2,64,128]{2,1,0:T(8,128)}, f32[2,64,128]{2,1,0:T(8,128)}) custom-call(f32[16,32,128]{2,1,0:T(8,128)S(1)} %get-tuple-element.26.block_ref.first_ref, f32[16,16,128]{2,1,0:T(8,128)S(1)} %collective-permute-done.4.low_ref, f32[16,16,128]{2,1,0:T(8,128)} %collective-permute-done.5.high_ref), custom_call_target="tpu_custom_call" | custom-call | flops 3000000000 | bytes 1000000 | tf_op jit(solution)/shard_map/strips/pallas_call | solution.py:247
  77.4 0.0 copy-done.2
  77.4 3.4 %collective-permute-start.6 = (f32[2,64,128]{2,1,0:T(8,128)}, f32[2,64,128]{2,1,0:T(8,128)S(1)}, u32[]{:S(2)}, u32[]{:S(2)}) collective-permute-start(f32[2,64,128]{2,1,0:T(8,128)} %get-tuple-element.29), channel_id=1, source_target_pairs={{0,1},{1,2},{2,3},{3,4},{4,5},{5,6},{6,7},{7,8},{8,9},{9,10},{10,1... | collective-permute-start | bytes 196616 | tf_op jit(solution)/shard_map/ppermute | solution.py:53
  80.8 1.3 collective-permute-start.7
  82.1 2.8 %all-to-all-done.2 = f32[128,1,128]{2,1,0:T(1,128)S(1)} async-done(((f32[128,1,128]{2,1,0:T(1,128)}), f32[128,1,128]{2,1,0:T(1,128)S(1)}, u32[]{:S(2)}, u32[]{:S(2)}) %all-to-all-start.2) | async-done | bytes 65568 | tf_op jit(solution)/shard_map/all_to_all | solution.py:57
  85.0 2.0 %coarse_rows.3 = f32[128,128]{1,0:T(8,128)} custom-call(f32[128,128]{1,0:T(8,128)S(1)} %bitcast.29, f32[128,128]{1,0:T(8,128)S(1)} %bitcast.26, f32[32,4096]{1,0:T(8,128)} %inverse_hbm.3), custom_call_target="tpu_custom_call" | custom-call | flops 9200000000 | bytes 1000000 | tf_op jit(solution)/shard_map/coarse_rows/pallas_call | solution.py:260
  86.9 8.4 %all-to-all-start.3 = ((f32[128,1,128]{2,1,0:T(1,128)}), f32[128,1,128]{2,1,0:T(1,128)S(1)}, u32[]{:S(2)}, u32[]{:S(2)}) async-start(f32[128,1,128]{2,1,0:T(1,128)} %bitcast.38), calls=%async_computation.3 | async-start | bytes 131072 | tf_op jit(solution)/shard_map/all_to_all | solution.py:57
  95.3 0.0 collective-permute-done.6.left_ref
  95.3 0.0 collective-permute-done.7.right_ref
  95.4 0.0 copy-start.3
  95.4 0.9 copy-done.3
  96.3 12.9 %smoother.3.sum_hbm = f32[16,48,256]{2,1,0:T(8,128)} custom-call(s32[4]{0:T(128)S(1)} %pad_add_fusion.place_ref, f32[8]{0:T(128)S(1)} %copy-done.4, f32[128,128]{1,0:T(8,128)S(1)} %bitcast.27, f32[16,32,128]{2,1,0:T(8,128)S(1)} %get-tuple-element.26.block_ref.first_ref, f32[16,16,128]{2,1,0:T(8,128)S(1)} %copy-done.3, ...), custom_call_target="tpu_custom_call" | custom-call | flops 2000000 | bytes 54000000 | tf_op jit(solution)/shard_map/smoother/pallas_call | solution.py:507
  109.2 0.0 all-to-all-done.3
  109.2 4.8 %second_images.1 = (f32[16,32,128]{2,1,0:T(8,128)S(1)}, f32[16,32,128]{2,1,0:T(8,128)S(1)}, f32[16,32,128]{2,1,0:T(8,128)S(1)}, f32[128,128]{1,0:T(8,128)}) custom-call(s32[4]{0:T(128)S(1)} %pad_add_fusion.place_ref, f32[128,128]{1,0:T(8,128)S(1)} %bitcast.28, f32[128,128]{1,0:T(8,128)S(1)} %bitcast.32, bf16[32,16,32,128]{3,2,1,0:T(8,128)(2,1)} %basis_hbm.3, ...), custom_call_target="tpu_custom_call" | custom-call | tf_op jit(solution)/shard_map/second_images/pallas_call | solution.py:787
  114.0 19.2 %all_to_all.55 = f32[128,1,128]{2,1,0:T(1,128)S(1)} all-to-all(f32[128,1,128]{2,1,0:T(1,128)} %bitcast.39), channel_id=1, replica_groups=mesh['gx'=8,'gy'=16] {'gx','gy'}, dimensions={0} | all-to-all | bytes 131072 | tf_op jit(solution)/shard_map/all_to_all | solution.py:57
  133.2 1.7 %update.1 = (f32[16,32,128]{2,1,0:T(8,128)}, f32[16,32,128]{2,1,0:T(8,128)}) custom-call(f32[128,128]{1,0:T(8,128)S(1)} %bitcast.31, f32[128,128]{1,0:T(8,128)S(1)} %bitcast.34, f32[16,32,128]{2,1,0:T(8,128)S(1)} %get-tuple-element.31.direction_ref, f32[16,32,128]{2,1,0:T(8,128)S(1)} %get-tuple-element.26.block_ref.first_ref, ...), custom_call_target="tpu_custom_call" | custom-call | tf_op jit(solution)/shard_map/update/pallas_call | solution.py:796
Async XLA Ops:
  0.6 23.7 %copy-start = (f32[16,32,128]{2,1,0:T(8,128)S(1)}, f32[16,32,128]{2,1,0:T(8,128)}, u32[]{:S(2)}) copy-start(f32[16,32,128]{2,1,0:T(8,128)} %absorption_ref.9) | copy-start | bytes 786436
  0.6 23.7 %copy-start.1 = (f32[16,32,128]{2,1,0:T(8,128)S(1)}, f32[16,32,128]{2,1,0:T(8,128)}, u32[]{:S(2)}) copy-start(f32[16,32,128]{2,1,0:T(8,128)} %source_ref.5) | copy-start | bytes 786436
  7.2 17.1 %collective-permute-start = (f32[64,16,128]{2,1,0:T(8,128)}, f32[64,16,128]{2,1,0:T(8,128)S(1)}, u32[]{:S(2)}, u32[]{:S(2)}) collective-permute-start(f32[64,16,128]{2,1,0:T(8,128)} %get-tuple-element.20), channel_id=1, source_target_pairs={{0,16},{16,32},{32,48},{48,64},{64,80},{80,96},{96,112},{1,17},{17... | collective-permute-start | bytes 1572872 | tf_op jit(solution)/shard_map/ppermute | solution.py:53
  11.8 12.5 %collective-permute-start.1 = (f32[64,16,128]{2,1,0:T(8,128)}, f32[64,16,128]{2,1,0:T(8,128)S(1)}, u32[]{:S(2)}, u32[]{:S(2)}) collective-permute-start(f32[64,16,128]{2,1,0:T(8,128)} %get-tuple-element.21), channel_id=1, source_target_pairs={{16,0},{32,16},{48,32},{64,48},{80,64},{96,80},{112,96},{17,1},{33... | collective-permute-start | bytes 1572872 | tf_op jit(solution)/shard_map/ppermute | solution.py:53
  13.8 20.0 %all-to-all-start = ((f32[128,1,128]{2,1,0:T(1,128)}), f32[128,1,128]{2,1,0:T(1,128)S(1)}, u32[]{:S(2)}, u32[]{:S(2)}) async-start(f32[128,1,128]{2,1,0:T(1,128)} %bitcast.35), calls=%async_computation | async-start | bytes 131072 | tf_op jit(solution)/shard_map/all_to_all | solution.py:57
  25.3 17.7 %collective-permute-start.2 = (f32[6,64,128]{2,1,0:T(8,128)S(1)}, f32[6,64,128]{2,1,0:T(8,128)S(1)}, u32[]{:S(2)}, u32[]{:S(2)}) collective-permute-start(f32[6,64,128]{2,1,0:T(8,128)S(1)} %get-tuple-element.23), channel_id=1, source_target_pairs={{0,1},{1,2},{2,3},{3,4},{4,5},{5,6},{6,7},{7,8},{8,9},{9,10},{10,1... | collective-permute-start | bytes 589832 | tf_op jit(solution)/shard_map/ppermute | solution.py:53
  28.7 14.3 %collective-permute-start.3 = (f32[6,64,128]{2,1,0:T(8,128)S(1)}, f32[6,64,128]{2,1,0:T(8,128)S(1)}, u32[]{:S(2)}, u32[]{:S(2)}) collective-permute-start(f32[6,64,128]{2,1,0:T(8,128)S(1)} %get-tuple-element.24), channel_id=1, source_target_pairs={{1,0},{2,1},{3,2},{4,3},{5,4},{6,5},{7,6},{8,7},{9,8},{10,9},{11,1... | collective-permute-start | bytes 589832 | tf_op jit(solution)/shard_map/ppermute | solution.py:53
  33.8 9.2 %copy-start.4 = (f32[8]{0:T(128)S(1)}, f32[8]{0:T(128)}, u32[]{:S(2)}) copy-start(f32[8]{0:T(128)} %constant.15.clone.table_ref) | copy-start | bytes 100
  35.7 18.9 %all-to-all-start.1 = ((f32[128,1,128]{2,1,0:T(1,128)}), f32[128,1,128]{2,1,0:T(1,128)S(1)}, u32[]{:S(2)}, u32[]{:S(2)}) async-start(f32[128,1,128]{2,1,0:T(1,128)} %bitcast.37), calls=%async_computation.1 | async-start | bytes 131072 | tf_op jit(solution)/shard_map/all_to_all | solution.py:57
  60.1 15.4 %collective-permute-start.4 = (f32[16,16,128]{2,1,0:T(8,128)}, f32[16,16,128]{2,1,0:T(8,128)S(1)}, u32[]{:S(2)}, u32[]{:S(2)}) collective-permute-start(f32[16,16,128]{2,1,0:T(8,128)} %get-tuple-element.27), channel_id=1, source_target_pairs={{0,16},{16,32},{32,48},{48,64},{64,80},{80,96},{96,112},{1,17},{17... | collective-permute-start | bytes 393224 | tf_op jit(solution)/shard_map/ppermute | solution.py:53
  63.6 11.8 %collective-permute-start.5 = (f32[16,16,128]{2,1,0:T(8,128)}, f32[16,16,128]{2,1,0:T(8,128)}, u32[]{:S(2)}, u32[]{:S(2)}) collective-permute-start(f32[16,16,128]{2,1,0:T(8,128)} %get-tuple-element.28), channel_id=1, source_target_pairs={{16,0},{32,16},{48,32},{64,48},{80,64},{96,80},{112,96},{17,1},{33... | collective-permute-start | bytes 393224 | tf_op jit(solution)/shard_map/ppermute | solution.py:53
  65.6 19.4 %all-to-all-start.2 = ((f32[128,1,128]{2,1,0:T(1,128)}), f32[128,1,128]{2,1,0:T(1,128)S(1)}, u32[]{:S(2)}, u32[]{:S(2)}) async-start(f32[128,1,128]{2,1,0:T(1,128)} %bitcast.36), calls=%async_computation.2 | async-start | bytes 131072 | tf_op jit(solution)/shard_map/all_to_all | solution.py:57
  75.4 2.0 %copy-start.2 = (f32[16,16,128]{2,1,0:T(8,128)}, f32[16,16,128]{2,1,0:T(8,128)S(1)}, u32[]{:S(2)}) copy-start(f32[16,16,128]{2,1,0:T(8,128)S(1)} %collective-permute-done.4.low_ref) | copy-start | bytes 393220
  77.4 17.9 %collective-permute-start.6 = (f32[2,64,128]{2,1,0:T(8,128)}, f32[2,64,128]{2,1,0:T(8,128)S(1)}, u32[]{:S(2)}, u32[]{:S(2)}) collective-permute-start(f32[2,64,128]{2,1,0:T(8,128)} %get-tuple-element.29), channel_id=1, source_target_pairs={{0,1},{1,2},{2,3},{3,4},{4,5},{5,6},{6,7},{7,8},{8,9},{9,10},{10,1... | collective-permute-start | bytes 196616 | tf_op jit(solution)/shard_map/ppermute | solution.py:53
  80.8 14.5 %collective-permute-start.7 = (f32[2,64,128]{2,1,0:T(8,128)}, f32[2,64,128]{2,1,0:T(8,128)}, u32[]{:S(2)}, u32[]{:S(2)}) collective-permute-start(f32[2,64,128]{2,1,0:T(8,128)} %get-tuple-element.30), channel_id=1, source_target_pairs={{1,0},{2,1},{3,2},{4,3},{5,4},{6,5},{7,6},{8,7},{9,8},{10,9},{11,1... | collective-permute-start | bytes 196616 | tf_op jit(solution)/shard_map/ppermute | solution.py:53
  86.9 22.2 %all-to-all-start.3 = ((f32[128,1,128]{2,1,0:T(1,128)}), f32[128,1,128]{2,1,0:T(1,128)S(1)}, u32[]{:S(2)}, u32[]{:S(2)}) async-start(f32[128,1,128]{2,1,0:T(1,128)} %bitcast.38), calls=%async_computation.3 | async-start | bytes 131072 | tf_op jit(solution)/shard_map/all_to_all | solution.py:57
  95.4 0.9 copy-start.3
